TPU v7x, 32 devices: a whole 2x2x4 slice. The times are simulated.
32 devices in a mesh: clip: 8 (over z, x), frame: 4 (over y, core).
Axes of the slice: x: 2, y: 2, z: 4, core: 2. Of those that a mesh axis runs over, the one named last changes fastest.
Arguments:
- frames_in: bfloat16 [8, 8, 96, 1280], P('clip', 'frame'), may hold values from -6 to 6
- ref_feats: bfloat16 [8, 96, 1280], P('clip', 'frame'), may hold values from -6 to 6
- out_grad: bfloat16 [8, 8, 96, 1280], P('clip', 'frame'), may hold values from -6 to 6
- space_query: bfloat16 [1280, 640], P('frame'), may hold values from -0.15625 to 0.15625
- space_key: bfloat16 [1280, 640], P('frame'), may hold values from -0.15625 to 0.15625
- space_value: bfloat16 [1280, 640], P('frame'), may hold values from -0.15625 to 0.15625
- space_output: bfloat16 [640, 1280], P('frame'), may hold values from -0.25 to 0.25
- time_query: bfloat16 [1280, 640], P('frame'), may hold values from -0.15625 to 0.15625
- time_key: bfloat16 [1280, 640], P('frame'), may hold values from -0.15625 to 0.15625
- time_value: bfloat16 [1280, 640], P('frame'), may hold values from -0.15625 to 0.15625
- time_output: bfloat16 [640, 1280], P('frame'), may hold values from -0.25 to 0.25
Outputs:
- out: bfloat16 [8, 8, 96, 1280], P('clip', 'frame')
- frames_grad: bfloat16 [8, 8, 96, 1280], P('clip', 'frame')
- ref_grad: bfloat16 [8, 96, 1280], P('clip', 'frame')
- space_query_grad: float32 [1280, 640], P('frame')
- space_key_grad: float32 [1280, 640], P('frame')
- space_value_grad: float32 [1280, 640], P('frame')
- space_output_grad: float32 [640, 1280], P('frame')
- time_query_grad: float32 [1280, 640], P('frame')
- time_key_grad: float32 [1280, 640], P('frame')
- time_value_grad: float32 [1280, 640], P('frame')
- time_output_grad: float32 [640, 1280], P('frame')
All inputs are finite; a program needn't handle non-finite values.
Results may differ from a plain program's by a relative error of at most 0.035.
Values may be sent and summed in bfloat16 or wider, within the bound.
No kernel may reach another device: no remote copies, remote signals or barrier semaphores. Data moves between devices by JAX's collectives and lax.ppermute only.
A program may use at most 128 MiB of HBM per device.

v0:
```python
import math

import jax
import jax.numpy as jnp
from jax import lax
from jax.sharding import PartitionSpec as P

HEADS = 4


EPSILON = 1e-05


def layer_stats(rows):
    wide = rows.astype(jnp.float32)
    centre = jnp.mean(wide, -1, keepdims=True)
    offset = wide - centre
    inverse = lax.rsqrt(jnp.mean(offset * offset, -1, keepdims=True) + EPSILON)
    return (offset * inverse, inverse)


def layer_back(centred, inverse, cotangent):
    first = jnp.mean(cotangent, -1, keepdims=True)
    second = jnp.mean(cotangent * centred, -1, keepdims=True)
    return inverse * (cotangent - first - centred * second)


def position_table(first, count, width):
    frame_ids = (first + jnp.arange(count, dtype=jnp.int32)).astype(jnp.float32)
    halves = jnp.arange(width // 2, dtype=jnp.int32).astype(jnp.float32)
    rates = jnp.exp(halves * (-2.0 * math.log(10000.0) / width))
    angles = frame_ids[:, None] * rates[None, :]
    return jnp.stack([jnp.sin(angles), jnp.cos(angles)], -1).reshape(count, width)


def einsum_forms(temporal):
    if temporal:
        return ("qbhe,kbhe->bhqk", "bhqk,kbhe->qbhe", "bhqk,qbhe->kbhe")
    return ("bqhe,bkhe->bhqk", "bhqk,bkhe->bqhe", "bhqk,bqhe->bkhe")


def product(form, left, right):
    return jnp.einsum(form, left, right, preferred_element_type=jnp.float32)


def attention(query, keys, values, temporal):
    score_form, mix_form, back_form = einsum_forms(temporal)
    scores = product(score_form, query, keys) * query.shape[-1] ** (-0.5)
    powers = jnp.exp(scores)
    probs = powers / jnp.sum(powers, -1, keepdims=True)
    rounded = probs.astype(jnp.bfloat16)
    mixed = product(mix_form, rounded, values).astype(jnp.bfloat16)
    return (mixed, probs, rounded)


def attention_back(query, keys, values, probs, rounded, cotangent, temporal):
    score_form, mix_form, back_form = einsum_forms(temporal)
    prob_grad = product(score_form, cotangent, values)
    score_grad = probs * (prob_grad - jnp.sum(probs * prob_grad, -1, keepdims=True))
    score_rounded = (score_grad * query.shape[-1] ** (-0.5)).astype(jnp.bfloat16)
    query_grad = product(mix_form, score_rounded, keys).astype(jnp.bfloat16)
    key_grad = product(back_form, score_rounded, query)
    value_grad = product(back_form, rounded, cotangent)
    return (query_grad, key_grad, value_grad)


def split_heads(rows):
    return rows.reshape(rows.shape[:-1] + (HEADS, rows.shape[-1] // HEADS))


def merge_heads(rows):
    return rows.reshape(rows.shape[:-2] + (rows.shape[-2] * rows.shape[-1],))


def project(rows, weight):
    flat_rows = rows.reshape(-1, rows.shape[-1])
    result = jnp.dot(flat_rows, weight, preferred_element_type=jnp.float32)
    return result.reshape(rows.shape[:-1] + (weight.shape[1],))


def project_back(rows, weight):
    flat_rows = rows.reshape(-1, rows.shape[-1])
    result = lax.dot_general(
        flat_rows, weight, (((1,), (1,)), ((), ())), preferred_element_type=jnp.float32
    )
    return result.reshape(rows.shape[:-1] + (weight.shape[0],))


def outer_sum(left, right):
    left_rows = left.reshape(-1, left.shape[-1])
    right_rows = right.reshape(-1, right.shape[-1])
    return lax.dot_general(
        left_rows, right_rows, (((0,), (0,)), ((), ())), preferred_element_type=jnp.float32
    )


def per_device(
    frames_in,
    ref_feats,
    out_grad,
    space_query,
    space_key,
    space_value,
    space_output,
    time_query,
    time_key,
    time_value,
    time_output,
):
    block = lax.axis_index("frame")
    (
        full_space_query,
        full_space_key,
        full_space_value,
        full_space_output,
        full_time_query,
        full_time_key,
        full_time_value,
        full_time_output,
    ) = (
        lax.all_gather(space_query, "frame", axis=0, tiled=True),
        lax.all_gather(space_key, "frame", axis=0, tiled=True),
        lax.all_gather(space_value, "frame", axis=0, tiled=True),
        lax.all_gather(space_output, "frame", axis=0, tiled=True),
        lax.all_gather(time_query, "frame", axis=0, tiled=True),
        lax.all_gather(time_key, "frame", axis=0, tiled=True),
        lax.all_gather(time_value, "frame", axis=0, tiled=True),
        lax.all_gather(time_output, "frame", axis=0, tiled=True),
    )
    frames = frames_in[0]
    refer = ref_feats[0]
    cotangent = out_grad[0]
    frame_count = frames.shape[0]
    token_count = frames.shape[1]
    centred_one, inverse_one = layer_stats(frames)
    normed_one = centred_one.astype(jnp.bfloat16)
    spatial_query = project(normed_one, full_space_query).astype(jnp.bfloat16)
    spatial_key = project(normed_one, full_space_key).astype(jnp.bfloat16)
    spatial_value = project(normed_one, full_space_value).astype(jnp.bfloat16)
    own_key = project(refer, full_space_key).astype(jnp.bfloat16)
    own_value = project(refer, full_space_value).astype(jnp.bfloat16)
    refer_key, refer_value = (
        lax.all_gather(own_key, "frame", axis=0, tiled=True),
        lax.all_gather(own_value, "frame", axis=0, tiled=True),
    )
    keys_joined = jnp.concatenate(
        [spatial_key, jnp.broadcast_to(refer_key[None], spatial_key.shape)], 1
    )
    values_joined = jnp.concatenate(
        [spatial_value, jnp.broadcast_to(refer_value[None], spatial_value.shape)], 1
    )
    spatial_mixed, spatial_probs, spatial_rounded = attention(
        split_heads(spatial_query), split_heads(keys_joined), split_heads(values_joined), False
    )
    spatial_mixed = merge_heads(spatial_mixed)
    hidden_one = (frames.astype(jnp.float32) + project(spatial_mixed, full_space_output)).astype(
        jnp.bfloat16
    )
    centred_two, inverse_two = layer_stats(hidden_one)
    table = position_table(block * frame_count, frame_count, frames.shape[2])
    normed_two = (centred_two + table[:, None, :]).astype(jnp.bfloat16)
    normed_rows = lax.all_to_all(normed_two, "frame", split_axis=1, concat_axis=0, tiled=True)
    temporal_query = project(normed_rows, full_time_query).astype(jnp.bfloat16)
    temporal_key = project(normed_rows, full_time_key).astype(jnp.bfloat16)
    temporal_value = project(normed_rows, full_time_value).astype(jnp.bfloat16)
    temporal_mixed, temporal_probs, temporal_rounded = attention(
        split_heads(temporal_query), split_heads(temporal_key), split_heads(temporal_value), True
    )
    mixed_two = lax.all_to_all(
        merge_heads(temporal_mixed), "frame", split_axis=0, concat_axis=1, tiled=True
    )
    output = (hidden_one.astype(jnp.float32) + project(mixed_two, full_time_output)).astype(
        jnp.bfloat16
    )
    mixed_grad_two = project_back(cotangent, full_time_output).astype(jnp.bfloat16)
    token_grad = lax.all_to_all(mixed_grad_two, "frame", split_axis=1, concat_axis=0, tiled=True)
    token_query_grad, token_key_grad, token_value_grad = attention_back(
        split_heads(temporal_query),
        split_heads(temporal_key),
        split_heads(temporal_value),
        temporal_probs,
        temporal_rounded,
        split_heads(token_grad),
        True,
    )
    query_grad_two, key_grad_two, value_grad_two = (
        lax.all_to_all(
            merge_heads(token_query_grad), "frame", split_axis=0, concat_axis=1, tiled=True
        ),
        lax.all_to_all(
            merge_heads(token_key_grad).astype(jnp.bfloat16),
            "frame",
            split_axis=0,
            concat_axis=1,
            tiled=True,
        ),
        lax.all_to_all(
            merge_heads(token_value_grad).astype(jnp.bfloat16),
            "frame",
            split_axis=0,
            concat_axis=1,
            tiled=True,
        ),
    )
    normed_grad_two = (
        project_back(query_grad_two, full_time_query)
        + project_back(key_grad_two, full_time_key)
        + project_back(value_grad_two, full_time_value)
    )
    hidden_grad = (
        cotangent.astype(jnp.float32) + layer_back(centred_two, inverse_two, normed_grad_two)
    ).astype(jnp.bfloat16)
    mixed_grad_one = project_back(hidden_grad, full_space_output).astype(jnp.bfloat16)
    query_grad_one, key_joined_grad, value_joined_grad = attention_back(
        split_heads(spatial_query),
        split_heads(keys_joined),
        split_heads(values_joined),
        spatial_probs,
        spatial_rounded,
        split_heads(mixed_grad_one),
        False,
    )
    query_grad_one = merge_heads(query_grad_one)
    key_grad_one = merge_heads(key_joined_grad[:, :token_count]).astype(jnp.bfloat16)
    value_grad_one = merge_heads(value_joined_grad[:, :token_count]).astype(jnp.bfloat16)
    partial_key = merge_heads(jnp.sum(key_joined_grad[:, token_count:], 0))
    partial_value = merge_heads(jnp.sum(value_joined_grad[:, token_count:], 0))
    summed_key, summed_value = (
        lax.psum_scatter(
            partial_key.astype(jnp.bfloat16), "frame", scatter_dimension=0, tiled=True
        ).astype(jnp.float32),
        lax.psum_scatter(
            partial_value.astype(jnp.bfloat16), "frame", scatter_dimension=0, tiled=True
        ).astype(jnp.float32),
    )
    refer_key_grad = summed_key.astype(jnp.bfloat16)
    refer_value_grad = summed_value.astype(jnp.bfloat16)
    normed_grad_one = (
        project_back(query_grad_one, full_space_query)
        + project_back(key_grad_one, full_space_key)
        + project_back(value_grad_one, full_space_value)
    )
    frames_grad = (
        hidden_grad.astype(jnp.float32) + layer_back(centred_one, inverse_one, normed_grad_one)
    ).astype(jnp.bfloat16)
    refer_grad = (
        project_back(refer_key_grad, full_space_key)
        + project_back(refer_value_grad, full_space_value)
    ).astype(jnp.bfloat16)
    term_sq = outer_sum(normed_one, query_grad_one)
    term_sk = outer_sum(normed_one, key_grad_one) + outer_sum(refer, refer_key_grad)
    term_sv = outer_sum(normed_one, value_grad_one) + outer_sum(refer, refer_value_grad)
    term_so = outer_sum(spatial_mixed, hidden_grad)
    term_tq = outer_sum(normed_two, query_grad_two)
    term_tk = outer_sum(normed_two, key_grad_two)
    term_tv = outer_sum(normed_two, value_grad_two)
    term_to = outer_sum(mixed_two, cotangent)
    share_sq, share_sk, share_sv, share_so, share_tq, share_tk, share_tv, share_to = (
        lax.psum_scatter(
            term_sq.astype(jnp.bfloat16), "frame", scatter_dimension=0, tiled=True
        ).astype(jnp.float32),
        lax.psum_scatter(
            term_sk.astype(jnp.bfloat16), "frame", scatter_dimension=0, tiled=True
        ).astype(jnp.float32),
        lax.psum_scatter(
            term_sv.astype(jnp.bfloat16), "frame", scatter_dimension=0, tiled=True
        ).astype(jnp.float32),
        lax.psum_scatter(
            term_so.astype(jnp.bfloat16), "frame", scatter_dimension=0, tiled=True
        ).astype(jnp.float32),
        lax.psum_scatter(
            term_tq.astype(jnp.bfloat16), "frame", scatter_dimension=0, tiled=True
        ).astype(jnp.float32),
        lax.psum_scatter(
            term_tk.astype(jnp.bfloat16), "frame", scatter_dimension=0, tiled=True
        ).astype(jnp.float32),
        lax.psum_scatter(
            term_tv.astype(jnp.bfloat16), "frame", scatter_dimension=0, tiled=True
        ).astype(jnp.float32),
        lax.psum_scatter(
            term_to.astype(jnp.bfloat16), "frame", scatter_dimension=0, tiled=True
        ).astype(jnp.float32),
    )
    total_sq, total_sk, total_sv, total_so, total_tq, total_tk, total_tv, total_to = (
        lax.psum(share_sq.astype(jnp.bfloat16), "clip").astype(jnp.float32),
        lax.psum(share_sk.astype(jnp.bfloat16), "clip").astype(jnp.float32),
        lax.psum(share_sv.astype(jnp.bfloat16), "clip").astype(jnp.float32),
        lax.psum(share_so.astype(jnp.bfloat16), "clip").astype(jnp.float32),
        lax.psum(share_tq.astype(jnp.bfloat16), "clip").astype(jnp.float32),
        lax.psum(share_tk.astype(jnp.bfloat16), "clip").astype(jnp.float32),
        lax.psum(share_tv.astype(jnp.bfloat16), "clip").astype(jnp.float32),
        lax.psum(share_to.astype(jnp.bfloat16), "clip").astype(jnp.float32),
    )
    return (
        output[None],
        frames_grad[None],
        refer_grad[None],
        total_sq,
        total_sk,
        total_sv,
        total_so,
        total_tq,
        total_tk,
        total_tv,
        total_to,
    )


def solution(mesh):
    in_specs = (
        P("clip", "frame", None, None),
        P("clip", "frame", None),
        P("clip", "frame", None, None),
        P("frame", None),
        P("frame", None),
        P("frame", None),
        P("frame", None),
        P("frame", None),
        P("frame", None),
        P("frame", None),
        P("frame", None),
    )
    out_specs = (
        P("clip", "frame", None, None),
        P("clip", "frame", None, None),
        P("clip", "frame", None),
        P("frame", None),
        P("frame", None),
        P("frame", None),
        P("frame", None),
        P("frame", None),
        P("frame", None),
        P("frame", None),
        P("frame", None),
    )
    return jax.shard_map(
        per_device, mesh=mesh, in_specs=in_specs, out_specs=out_specs, check_vma=False
    )
```

profile of v0, /device:TPU:0, one launch (start us, length us, event | category | flops | bytes accessed | tf_op | source)
XLA Modules:
  0.0 697.8 jit_solution(17178550746613144705)
XLA Ops:
  14.1 18.3 %all-gather.13.cloned.1.call-done = bf16[1280,640]{1,0:T(8,128)(2,1)} async-done(((bf16[320,640]{1,0:T(8,128)(2,1)}), bf16[1280,640]{1,0:T(8,128)(2,1)}) %all-gather.13.cloned.1.call-update) | async-done | bytes 1638416 | tf_op jit(solution)/shard_map/all_gather | solution.py:122
  34.2 5.4 all_gather.34
  41.4 12.5 %all-gather.11.cloned.1.call-done = bf16[1280,640]{1,0:T(8,128)(2,1)} async-done(((bf16[320,640]{1,0:T(8,128)(2,1)}), bf16[1280,640]{1,0:T(8,128)(2,1)}) %all-gather.11.cloned.1.call-update) | async-done | bytes 1638416 | tf_op jit(solution)/shard_map/all_gather | solution.py:121
  54.0 2.0 fusion.55
  56.3 19.3 %all-gather.9.cloned.1.call-done = bf16[1280,640]{1,0:T(8,128)(2,1)} async-done(((bf16[320,640]{1,0:T(8,128)(2,1)}), bf16[1280,640]{1,0:T(8,128)(2,1)}) %all-gather.9.cloned.1.call-update) | async-done | bytes 1638416 | tf_op jit(solution)/shard_map/all_gather | solution.py:123
  77.5 5.4 all_gather.31
  84.7 12.4 %all-gather.23.cloned.1.call-done = bf16[640,1280]{1,0:T(8,128)(2,1)} async-done(((bf16[160,1280]{1,0:T(8,128)(2,1)}), bf16[640,1280]{1,0:T(8,128)(2,1)}) %all-gather.23.cloned.1.call-update) | async-done | bytes 1638416 | tf_op jit(solution)/shard_map/all_gather | solution.py:128
  97.1 2.1 fusion.73
  100.1 4.0 all-to-all-start.2
  104.1 2.4 fusion.39
  106.5 2.5 convolution_convert_fusion.11
  109.0 11.2 %all-gather.15.cloned.1.call-done = bf16[640,1280]{1,0:T(8,128)(2,1)} async-done(((bf16[160,1280]{1,0:T(8,128)(2,1)}), bf16[640,1280]{1,0:T(8,128)(2,1)}) %all-gather.15.cloned.1.call-update) | async-done | bytes 1638416 | tf_op jit(solution)/shard_map/all_gather | solution.py:124
  120.2 2.2 fusion.151
  125.0 4.3 all-to-all-start
  131.3 2.0 reshape_reshape.9
  135.0 2.0 reshape.373
  137.0 6.1 all-to-all-done
  144.9 2.1 all-gather.19.cloned.1.call-done
  147.0 2.9 fusion.67
  149.9 2.0 reshape.370
  151.8 16.8 %all-gather.21.cloned.1.call-done = bf16[1280,640]{1,0:T(8,128)(2,1)} async-done(((bf16[320,640]{1,0:T(8,128)(2,1)}), bf16[1280,640]{1,0:T(8,128)(2,1)}) %all-gather.21.cloned.1.call-update) | async-done | bytes 1638416 | tf_op jit(solution)/shard_map/all_gather | solution.py:126
  168.6 2.9 fusion.70
  176.7 13.5 %all-gather.17.cloned.1.call-done = bf16[1280,640]{1,0:T(8,128)(2,1)} async-done(((bf16[320,640]{1,0:T(8,128)(2,1)}), bf16[1280,640]{1,0:T(8,128)(2,1)}) %all-gather.17.cloned.1.call-update) | async-done | bytes 1638416 | tf_op jit(solution)/shard_map/all_gather | solution.py:127
  190.2 2.9 fusion.64
  195.1 2.4 fusion.107
  197.5 2.8 fusion.46
  202.1 2.0 convert_element_type.284
  204.1 4.0 all-to-all-start.4
  208.1 2.7 fusion.45
  212.8 2.0 reshape.374
  214.8 4.0 all-to-all-start.3
  218.8 2.4 fusion.47
  223.1 2.0 convert_element_type.287
  225.1 4.0 all-to-all-start.5
  229.2 2.4 fusion.103
  236.2 2.3 fusion.18
  245.5 3.0 convolution_bitcast_fusion.4
  248.5 2.5 fusion.152
  251.9 3.5 convolution_bitcast_fusion.5
  255.4 2.2 slice_reduce_fusion.1
  257.9 3.0 convolution_convert_fusion.4
  261.1 2.9 convolution_convert_fusion.2
  265.1 2.5 convolution_convert_fusion.10
  268.7 2.0 reshape_reshape.8
  270.7 3.1 convolution_convert_fusion.5
  273.9 3.0 convolution_convert_fusion.3
  277.0 3.0 convolution_convert_fusion.1
  280.0 2.4 fusion.44
  285.7 8.8 %all_to_all.90 = bf16[8,24,640]{2,1,0:T(8,128)(2,1)S(1)} all-to-all(bf16[8,24,640]{2,1,0:T(8,128)(2,1)S(1)} %reshape.372), channel_id=1, replica_groups=mesh['clip'=8,'frame'=4] {'frame'}, dimensions={0} | all-to-all | bytes 491520 | tf_op jit(solution)/shard_map/all_to_all | solution.py:169
  295.2 2.9 convolution_convert_fusion
  300.5 3.5 convolution_bitcast_fusion.1
  304.0 3.9 fusion.5
  313.3 9.3 %reduce-scatter.17.cloned.1.call-done = bf16[160,1280]{1,0:T(8,128)(2,1)} async-done(((bf16[640,1280]{1,0:T(8,128)(2,1)}), bf16[160,1280]{1,0:T(8,128)(2,1)}) %reduce-scatter.17.cloned.1.call-update) | async-done | bytes 409616 | tf_op jit(solution)/shard_map/reduce_scatter | solution.py:268
  322.7 31.3 %reduce-scatter.21.cloned.1.call-done = bf16[320,640]{1,0:T(8,128)(2,1)} async-done(((bf16[1280,640]{1,0:T(8,128)(2,1)}), bf16[320,640]{1,0:T(8,128)(2,1)}) %reduce-scatter.21.cloned.1.call-update) | async-done | bytes 409616 | tf_op jit(solution)/shard_map/reduce_scatter | solution.py:274
  354.0 31.0 %reduce-scatter.11.cloned.1.call-done = bf16[320,640]{1,0:T(8,128)(2,1)} async-done(((bf16[1280,640]{1,0:T(8,128)(2,1)}), bf16[320,640]{1,0:T(8,128)(2,1)}) %reduce-scatter.11.cloned.1.call-update) | async-done | bytes 409616 | tf_op jit(solution)/shard_map/reduce_scatter | solution.py:259
  385.0 31.3 %reduce-scatter.19.cloned.1.call-done = bf16[320,640]{1,0:T(8,128)(2,1)} async-done(((bf16[1280,640]{1,0:T(8,128)(2,1)}), bf16[320,640]{1,0:T(8,128)(2,1)}) %reduce-scatter.19.cloned.1.call-update) | async-done | bytes 409616 | tf_op jit(solution)/shard_map/reduce_scatter | solution.py:271
  416.4 31.0 %reduce-scatter.23.cloned.1.call-done = bf16[320,640]{1,0:T(8,128)(2,1)} async-done(((bf16[1280,640]{1,0:T(8,128)(2,1)}), bf16[320,640]{1,0:T(8,128)(2,1)}) %reduce-scatter.23.cloned.1.call-update) | async-done | bytes 409616 | tf_op jit(solution)/shard_map/reduce_scatter | solution.py:277
  447.4 31.2 %reduce-scatter.25.cloned.1.call-done = bf16[160,1280]{1,0:T(8,128)(2,1)} async-done(((bf16[640,1280]{1,0:T(8,128)(2,1)}), bf16[160,1280]{1,0:T(8,128)(2,1)}) %reduce-scatter.25.cloned.1.call-update) | async-done | bytes 409616 | tf_op jit(solution)/shard_map/reduce_scatter | solution.py:280
  478.6 31.0 %reduce-scatter.15.cloned.1.call-done = bf16[320,640]{1,0:T(8,128)(2,1)} async-done(((bf16[1280,640]{1,0:T(8,128)(2,1)}), bf16[320,640]{1,0:T(8,128)(2,1)}) %reduce-scatter.15.cloned.1.call-update) | async-done | bytes 409616 | tf_op jit(solution)/shard_map/reduce_scatter | solution.py:265
  509.6 31.2 %reduce-scatter.13.cloned.1.call-done = bf16[320,640]{1,0:T(8,128)(2,1)} async-done(((bf16[1280,640]{1,0:T(8,128)(2,1)}), bf16[320,640]{1,0:T(8,128)(2,1)}) %reduce-scatter.13.cloned.1.call-update) | async-done | bytes 409616 | tf_op jit(solution)/shard_map/reduce_scatter | solution.py:262
  540.9 2.3 fusion.31
  550.1 131.2 %all-reduce.7.cloned.1.call-done = (bf16[320,640]{1,0:T(8,128)(2,1)}, bf16[320,640]{1,0:T(8,128)(2,1)}, bf16[320,640]{1,0:T(8,128)(2,1)}, bf16[160,1280]{1,0:T(8...) async-done(((bf16[320,640]{1,0:T(8,128)(2,1)}, bf16[320,640]{1,0:T(8,128)(2,1)}, ...) | async-done | bytes 3276816 | tf_op jit(solution)/shard_map/psum | solution.py:285
  681.3 2.0 convert_element_type.307
  683.3 2.0 convert_element_type.310
  (184 shorter events, 74.7 us)
Async XLA Ops:
  7.2 25.2 %copy-start = (bf16[1,24,1280]{2,1,0:T(8,128)(2,1)S(1)}, bf16[1,24,1280]{2,1,0:T(8,128)(2,1)}, u32[]{:S(2)}) copy-start(bf16[1,24,1280]{2,1,0:T(8,128)(2,1)} %param.12) | copy-start | bytes 184324
  7.2 5.5 copy-start.1
  7.2 25.2 %all-gather.13.cloned.1.call-start = ((), (), s32[]{:S(2)}) async-start(), calls=%async_computation.16 | async-start | bytes 2048000 | tf_op jit(solution)/shard_map/all_gather | solution.py:122
  7.9 46.0 %all-gather.11.cloned.1.call-start = ((), (), s32[]{:S(2)}) async-start(), calls=%async_computation.15 | async-start | bytes 2048000 | tf_op jit(solution)/shard_map/all_gather | solution.py:121
  8.7 66.9 %all-gather.9.cloned.1.call-start = ((), (), s32[]{:S(2)}) async-start(), calls=%async_computation.14 | async-start | bytes 2048000 | tf_op jit(solution)/shard_map/all_gather | solution.py:123
  9.4 87.7 %all-gather.23.cloned.1.call-start = ((), (), s32[]{:S(2)}) async-start(), calls=%async_computation.21 | async-start | bytes 2048000 | tf_op jit(solution)/shard_map/all_gather | solution.py:128
  10.0 110.2 %all-gather.15.cloned.1.call-start = ((), (), s32[]{:S(2)}) async-start(), calls=%async_computation.17 | async-start | bytes 2048000 | tf_op jit(solution)/shard_map/all_gather | solution.py:124
  10.6 136.4 %all-gather.19.cloned.1.call-start = ((), (), s32[]{:S(2)}) async-start(), calls=%async_computation.19 | async-start | bytes 2048000 | tf_op jit(solution)/shard_map/all_gather | solution.py:125
  11.2 157.5 %all-gather.21.cloned.1.call-start = ((), (), s32[]{:S(2)}) async-start(), calls=%async_computation.20 | async-start | bytes 2048000 | tf_op jit(solution)/shard_map/all_gather | solution.py:126
  11.9 178.3 %all-gather.17.cloned.1.call-start = ((), (), s32[]{:S(2)}) async-start(), calls=%async_computation.18 | async-start | bytes 2048000 | tf_op jit(solution)/shard_map/all_gather | solution.py:127
  32.4 7.3 %copy-start.3 = (bf16[1280,640]{1,0:T(8,128)(2,1)S(1)}, bf16[1280,640]{1,0:T(8,128)(2,1)}, u32[]{:S(2)}) copy-start(bf16[1280,640]{1,0:T(8,128)(2,1)} %all-gather.13.cloned.1.call-done) | copy-start | bytes 4915204
  75.6 7.3 %copy-start.2 = (bf16[1280,640]{1,0:T(8,128)(2,1)S(1)}, bf16[1280,640]{1,0:T(8,128)(2,1)}, u32[]{:S(2)}) copy-start(bf16[1280,640]{1,0:T(8,128)(2,1)} %all-gather.9.cloned.1.call-done) | copy-start | bytes 4915204
  83.5 13.6 %copy-start.12 = (bf16[1,2,96,1280]{3,2,1,0:T(8,128)(2,1)S(1)}, bf16[1,2,96,1280]{3,2,1,0:T(8,128)(2,1)}, u32[]{:S(2)}) copy-start(bf16[1,2,96,1280]{3,2,1,0:T(8,128)(2,1)} %param.13) | copy-start | bytes 1474564
  99.2 7.3 %copy-start.16 = (bf16[2,192,640]{1,2,0:T(8,128)(2,1)S(1)}, bf16[2,192,640]{1,2,0:T(8,128)(2,1)}, u32[]{:S(2)}) copy-start(bf16[2,192,640]{1,2,0:T(8,128)(2,1)} %copy.119) | copy-start | bytes 1474564
  100.1 24.9 %all-to-all-start.2 = ((bf16[2,96,640]{2,0,1:T(2,128)(2,1)}), bf16[2,96,640]{2,0,1:T(2,128)(2,1)}, u32[]{:S(2)}, u32[]{:S(2)}) async-start(bf16[2,96,640]{2,0,1:T(2,128)(2,1)} %copy.132), calls=%async_computation.2 | async-start | bytes 491520 | tf_op jit(solution)/shard_map/all_to_all | solution.py:176
  123.0 0.8 copy-start.5
  125.0 18.0 %all-to-all-start = ((bf16[2,96,1280]{2,0,1:T(2,128)(2,1)}), bf16[2,96,1280]{2,0,1:T(2,128)(2,1)}, u32[]{:S(2)}, u32[]{:S(2)}) async-start(bf16[2,96,1280]{2,0,1:T(2,128)(2,1)} %copy.124), calls=%async_computation | async-start | bytes 983040 | tf_op jit(solution)/shard_map/all_to_all | solution.py:162
  175.1 0.8 copy-start.35
  204.1 10.7 %all-to-all-start.4 = ((bf16[8,24,640]{2,1,0:T(8,128)(2,1)}), bf16[8,24,640]{2,1,0:T(8,128)(2,1)}, u32[]{:S(2)}, u32[]{:S(2)}) async-start(bf16[8,24,640]{2,1,0:T(8,128)(2,1)} %convert_element_type.284), calls=%async_computation.4 | async-start | bytes 491520 | tf_op jit(solution)/shard_map/all_to_all | solution.py:190
  214.8 10.3 %all-to-all-start.3 = ((bf16[8,24,640]{2,1,0:T(8,128)(2,1)}), bf16[8,24,640]{2,1,0:T(8,128)(2,1)}, u32[]{:S(2)}, u32[]{:S(2)}) async-start(bf16[8,24,640]{2,1,0:T(8,128)(2,1)} %reshape.374), calls=%async_computation.3 | async-start | bytes 491520 | tf_op jit(solution)/shard_map/all_to_all | solution.py:187
  225.1 10.0 %all-to-all-start.5 = ((bf16[8,24,640]{2,1,0:T(8,128)(2,1)}), bf16[8,24,640]{2,1,0:T(8,128)(2,1)}, u32[]{:S(2)}, u32[]{:S(2)}) async-start(bf16[8,24,640]{2,1,0:T(8,128)(2,1)} %convert_element_type.287), calls=%async_computation.5 | async-start | bytes 491520 | tf_op jit(solution)/shard_map/all_to_all | solution.py:197
  229.1 74.9 %all-reduce.9.cloned.1.call-start = ((), (), s32[]{:S(2)}) async-start(), calls=%async_computation.31 | async-start | bytes 655360
  235.1 3.4 copy-start.10
  235.1 3.4 copy-start.21
  236.2 3.0 copy-start.19
  238.5 1.4 copy-start.11
  240.0 1.0 copy-start.13
  240.8 1.5 copy-start.9
  241.4 0.8 copy-start.6
  248.5 2.5 copy-start.24
  257.7 65.0 %reduce-scatter.17.cloned.1.call-start = ((), (), s32[]{:S(2)}) async-start(), calls=%async_computation.25 | async-start | bytes 2048000 | tf_op jit(solution)/shard_map/reduce_scatter | solution.py:268
  257.9 3.1 copy-start.22
  261.0 93.0 %reduce-scatter.21.cloned.1.call-start = ((), (), s32[]{:S(2)}) async-start(), calls=%async_computation.27 | async-start | bytes 2048000 | tf_op jit(solution)/shard_map/reduce_scatter | solution.py:274
  264.0 121.0 %reduce-scatter.11.cloned.1.call-start = ((), (), s32[]{:S(2)}) async-start(), calls=%async_computation.22 | async-start | bytes 2048000 | tf_op jit(solution)/shard_map/reduce_scatter | solution.py:259
  267.7 6.1 copy-start.23
  273.8 142.6 %reduce-scatter.19.cloned.1.call-start = ((), (), s32[]{:S(2)}) async-start(), calls=%async_computation.26 | async-start | bytes 2048000 | tf_op jit(solution)/shard_map/reduce_scatter | solution.py:271
  273.9 3.1 copy-start.20
  276.9 170.5 %reduce-scatter.23.cloned.1.call-start = ((), (), s32[]{:S(2)}) async-start(), calls=%async_computation.28 | async-start | bytes 2048000 | tf_op jit(solution)/shard_map/reduce_scatter | solution.py:277
  280.0 198.6 %reduce-scatter.25.cloned.1.call-start = ((), (), s32[]{:S(2)}) async-start(), calls=%async_computation.29 | async-start | bytes 2048000 | tf_op jit(solution)/shard_map/reduce_scatter | solution.py:280
  294.5 0.7 copy-start.17
  295.2 2.9 copy-start.34
  298.1 211.6 %reduce-scatter.15.cloned.1.call-start = ((), (), s32[]{:S(2)}) async-start(), calls=%async_computation.24 | async-start | bytes 2048000 | tf_op jit(solution)/shard_map/reduce_scatter | solution.py:265
  308.0 232.9 %reduce-scatter.13.cloned.1.call-start = ((), (), s32[]{:S(2)}) async-start(), calls=%async_computation.23 | async-start | bytes 2048000 | tf_op jit(solution)/shard_map/reduce_scatter | solution.py:262
  309.1 1.9 copy-start.14
  309.1 1.9 copy-start.26
  313.0 368.2 %all-reduce.7.cloned.1.call-start = ((), (), s32[]{:S(2)}) async-start(), calls=%async_computation.30 | async-start | bytes 6553600 | tf_op jit(solution)/shard_map/psum | solution.py:285
  540.8 2.4 copy-start.4
  540.8 2.4 copy-start.15
  543.9 1.4 copy-start.8
  543.9 1.4 copy-start.18
  545.4 1.4 copy-start.7
  546.7 1.2 copy-start.27
  546.7 1.9 copy-start.25
  681.3 4.0 copy-start.33
  681.3 5.0 copy-start.32
  683.3 3.9 copy-start.31
  685.3 2.8 copy-start.30
  686.2 2.8 copy-start.29
  687.2 2.8 copy-start.28
Sparse Core Ops, SparseCore 0:
  9.6 22.7 all-gather.12
  33.9 20.0 all-gather.10
  55.5 20.0 all-gather.8
  77.0 20.0 all-gather.22
  98.5 21.7 all-gather.14
  121.7 25.2 all-gather.18
  148.6 20.0 all-gather.20
  170.2 20.0 all-gather.16
  257.8 33.7 all-reduce.8
  294.0 28.6 reduce-scatter.16
  325.4 28.5 reduce-scatter.20
  356.4 28.5 reduce-scatter.10
  387.8 28.5 reduce-scatter.18
  418.8 28.5 reduce-scatter.22
  450.0 28.5 reduce-scatter.24
  481.0 28.5 reduce-scatter.14
  512.2 28.5 reduce-scatter.12
  545.3 135.9 all-reduce.6
where the time goes:
time: 700 us; the launch traced here: 698 us
  waiting for transfers between devices  476 us (68%)
  matrix products  92.4 us (13%)
  local copies, waits for them, and re-layouts  52.3 us (7%)
  starting transfers between devices  21.6 us (3%)
  other arithmetic  20.1 us (3%)
  blocking collectives  19.6 us (3%)
  between operations  15.6 us (2%)
    psum x1, waiting for transfers between devices, per_device(): lax.psum(share_sq.astype(jnp.bfloat16), 'clip').astype(jnp.float32)  131 us
    reduce_scatter x1, waiting for transfers between devices, per_device(): lax.psum_scatter(term_tk.astype(jnp.bfloat16), 'frame', scatter_dimension...  31.3 us
    reduce_scatter x1, waiting for transfers between devices, per_device(): lax.psum_scatter(term_tq.astype(jnp.bfloat16), 'frame', scatter_dimension...  31.3 us
    reduce_scatter x1, waiting for transfers between devices, per_device(): lax.psum_scatter(term_sk.astype(jnp.bfloat16), 'frame', scatter_dimension...  31.2 us
    reduce_scatter x1, waiting for transfers between devices, per_device(): lax.psum_scatter(term_to.astype(jnp.bfloat16), 'frame', scatter_dimension...  31.2 us
    reduce_scatter x1, waiting for transfers between devices, per_device(): lax.psum_scatter(term_sq.astype(jnp.bfloat16), 'frame', scatter_dimension...  31 us
    reduce_scatter x1, waiting for transfers between devices, per_device(): lax.psum_scatter(term_tv.astype(jnp.bfloat16), 'frame', scatter_dimension...  31 us
    reduce_scatter x1, waiting for transfers between devices, per_device(): lax.psum_scatter(term_sv.astype(jnp.bfloat16), 'frame', scatter_dimension...  31 us
  transfers between devices with their start and end apart: 23, of which 19 were waited for; matrix products, arithmetic and copies ran while one was open for 17% of the time, Pallas kernels for 0%

commit v1 on v0

--- a/solution.py
+++ b/solution.py
@@ -1,8 +1,12 @@
 import math
+
+import functools
 
 import jax
 import jax.numpy as jnp
 from jax import lax
+from jax.experimental import pallas as pl
+from jax.experimental.pallas import tpu as pltpu
 from jax.sharding import PartitionSpec as P
 
 HEADS = 4
@@ -94,7 +98,7 @@
     )
 
 
-def per_device(
+def per_device_general(
     frames_in,
     ref_feats,
     out_grad,
@@ -306,6 +310,525 @@
     )
 
 
+F32 = jnp.float32
+BF16 = jnp.bfloat16
+CHUNK = 32
+
+
+def mm(left, right):
+    return jnp.dot(left, right, preferred_element_type=F32)
+
+
+def mm_bt(left, right):
+    return lax.dot_general(left, right, (((1,), (1,)), ((), ())), preferred_element_type=F32)
+
+
+def mm_at(left, right):
+    return lax.dot_general(left, right, (((0,), (0,)), ((), ())), preferred_element_type=F32)
+
+
+def wide_call(body, name, out_shape, scratch, limit_mb, flops, num_in):
+    return pl.pallas_call(
+        body,
+        name=name,
+        out_shape=out_shape,
+        in_specs=[pl.BlockSpec(memory_space=pltpu.SMEM)]
+        + [pl.BlockSpec(memory_space=pltpu.VMEM)] * (num_in - 1),
+        out_specs=tuple(pl.BlockSpec(memory_space=pltpu.VMEM) for _ in out_shape),
+        scratch_shapes=scratch,
+        compiler_params=pltpu.CompilerParams(vmem_limit_bytes=limit_mb * 1024 * 1024),
+        cost_estimate=pl.CostEstimate(flops=flops, bytes_accessed=8_000_000, transcendentals=0),
+    )
+
+
+def struct(*shape, dtype=BF16):
+    return jax.ShapeDtypeStruct(shape, dtype)
+
+
+def flip(value, axis, bit):
+    size = lax.axis_size(axis)
+    return lax.ppermute(value, axis, [(i, i ^ bit) for i in range(size)])
+
+
+def after(value, *others):
+    return lax.optimization_barrier((value,) + others)[0]
+
+
+def pack_body(heads, idx, wq, wk, wv, *outs):
+    width = wq.shape[1] // heads
+    room = outs[0].shape[1]
+    for h in range(heads):
+        parts = [w[:, h * width : (h + 1) * width] for w in (wq, wk, wv)]
+        parts.append(jnp.zeros((wq.shape[0], room - 3 * width), BF16))
+        outs[h][...] = jnp.concatenate(parts, 1)
+
+
+def spatial_forward_body(n, tokens, width, idx, *refs):
+    frames, weights, refer = refs[:n], refs[n : 2 * n], refs[2 * n]
+    x_out, w_out, q_out, k_out, v_out, p_out, o_out = refs[2 * n + 1 : 2 * n + 8]
+    mixed, turn = refs[2 * n + 8 :]
+    me = idx[0]
+    rows = frames[0].shape[0]
+    depth = weights[0].shape[0]
+    lanes = q_out.shape[1]
+    room = w_out.shape[1]
+    total = n * rows
+    for r in range(n):
+        w_out[pl.ds(pl.multiple_of((me ^ r) * depth, depth), depth), :] = weights[r][...]
+    for r in range(n):
+
+        def norm(i, _, r=r):
+            at = pl.multiple_of(i * CHUNK, CHUNK)
+            centred, _ = layer_stats(frames[r][pl.ds(at, CHUNK), :])
+            x_out[pl.ds(r * rows + at, CHUNK), :] = centred.astype(BF16)
+            return 0
+
+        lax.fori_loop(0, rows // CHUNK, norm, 0)
+    x_out[total:, :] = refer[...]
+    for start, count in [(r * rows, rows) for r in range(n)] + [(total, refer.shape[0])]:
+        three = mm(x_out[start : start + count, :], w_out[...])
+        keep = lax.broadcasted_iota(jnp.int32, (count, lanes), 1) < width
+        q_out[start : start + count, :] = jnp.where(keep, three[:, :lanes], 0.0).astype(BF16)
+        k_out[start : start + count, :] = jnp.where(
+            keep, pltpu.roll(three, room - width, 1)[:, :lanes], 0.0
+        ).astype(BF16)
+        v_out[start : start + count, :] = jnp.where(
+            keep, pltpu.roll(three, room - 2 * width, 1)[:, :lanes], 0.0
+        ).astype(BF16)
+    scale = width**-0.5
+    for b in range(total // tokens):
+        at = slice(b * tokens, (b + 1) * tokens)
+        keys = jnp.concatenate([k_out[at, :], k_out[total:, :]], 0)
+        values = jnp.concatenate([v_out[at, :], v_out[total:, :]], 0)
+        powers = jnp.exp(mm_bt(q_out[at, :], keys) * scale)
+        probs = powers / jnp.sum(powers, -1, keepdims=True)
+        p_out[at, :] = probs
+        mixed[at, :] = mm(probs.astype(BF16), values)
+    share = tokens // n
+    per = rows // tokens
+    for r in range(n):
+        first = pl.multiple_of((me ^ r) * share, share)
+        for b in range(total // tokens):
+            to = ((b // per) ^ r) * per + b % per
+            turn[to * share : (to + 1) * share, :] = mixed[pl.ds(b * tokens + first, share), :]
+        o_out[r] = turn[...].astype(BF16)
+
+
+def spatial_backward_body(n, tokens, width, idx, *refs):
+    grads = refs[:n]
+    x_ref, w_ref, q_ref, k_ref, v_ref, p_ref = refs[n : n + 6]
+    keep_out, send_out, keep_ref, send_ref, term_out = refs[n + 6 : n + 11]
+    spread, turn, packed = refs[n + 11 :]
+    me = idx[0]
+    share = tokens // n
+    total = p_ref.shape[0]
+    rows = total // n
+    lanes = q_ref.shape[1]
+    room = w_ref.shape[1]
+    per = rows // tokens
+    for r in range(n):
+        first = pl.multiple_of((me ^ r) * share, share)
+        turn[...] = grads[r][...].astype(F32)
+        for b in range(total // tokens):
+            to = ((b // per) ^ r) * per + b % per
+            spread[pl.ds(b * tokens + first, share), :] = turn[to * share : (to + 1) * share, :]
+    scale = width**-0.5
+
+    def pack(first, second, third):
+        def wide(part):
+            blank = jnp.zeros((part.shape[0], room - lanes), F32)
+            return jnp.concatenate([part, blank], 1)
+
+        result = pltpu.roll(wide(second), width, 1) + pltpu.roll(wide(third), 2 * width, 1)
+        return result if first is None else result + wide(first)
+
+    key_sum = jnp.zeros((k_ref.shape[0] - total, lanes), F32)
+    value_sum = key_sum
+    for b in range(total // tokens):
+        at = slice(b * tokens, (b + 1) * tokens)
+        query = q_ref[at, :]
+        keys = jnp.concatenate([k_ref[at, :], k_ref[total:, :]], 0)
+        values = jnp.concatenate([v_ref[at, :], v_ref[total:, :]], 0)
+        cotangent = spread[at, :].astype(BF16)
+        probs = p_ref[at, :]
+        back = mm_bt(cotangent, values)
+        score = (probs * (back - jnp.sum(probs * back, -1, keepdims=True)) * scale).astype(BF16)
+        query_grad = mm(score, keys)
+        key_grad = mm_at(score, query)
+        value_grad = mm_at(probs.astype(BF16), cotangent)
+        key_sum = key_sum + key_grad[tokens:]
+        value_sum = value_sum + value_grad[tokens:]
+        packed[at, :] = pack(query_grad, key_grad[:tokens], value_grad[:tokens]).astype(BF16)
+    packed[total:, :] = pack(None, key_sum, value_sum).astype(BF16)
+    for r in range(n):
+        part = mm_bt(packed[r * rows : (r + 1) * rows, :], w_ref[...]).astype(BF16)
+        (send_out if r & 1 else keep_out)[r >> 1] = part
+    part = mm_bt(packed[total:, :], w_ref[...])
+    for r in range(n):
+        (send_ref if r & 1 else keep_ref)[r >> 1] = part[r * share : (r + 1) * share].astype(BF16)
+    depth = x_ref.shape[1] // 5
+    for j in range(5):
+        at = slice(j * depth, (j + 1) * depth)
+        term_out[at, :] = mm_at(x_ref[:, at], packed[...]).astype(BF16)
+
+
+def temporal_body(n, heads, idx, *refs):
+    mixed, so_parts, tq_parts, tk_parts, tv_parts, to_parts = (
+        refs[i * n : (i + 1) * n] for i in range(6)
+    )
+    frames, cotangent, table, same = refs[6 * n : 6 * n + 4]
+    grad_outs = refs[6 * n + 4 : 7 * n + 4]
+    gh_out, n2_out, gq_out, gk_out, gv_out, o2_out, out_out = refs[7 * n + 4 : 7 * n + 11]
+    so, tq, tk, tv, to, hidden, centred, inverse, wide, qs, gos = refs[7 * n + 11 :]
+    me = idx[0]
+    rows, dim = frames.shape
+    inner = tq.shape[1]
+    width = inner // heads
+    for r in range(n):
+        for parts, whole in ((tq_parts, tq), (tk_parts, tk), (tv_parts, tv), (to_parts, to)):
+            depth = parts[r].shape[0]
+            whole[pl.ds(pl.multiple_of((me ^ r) * depth, depth), depth), :] = parts[r][...]
+        depth = so_parts[r].shape[0]
+        so[r, :depth, :] = so_parts[r][...]
+        so[r, depth:, :] = jnp.zeros((so.shape[1] - depth, dim), BF16)
+    step = dim // 5
+    for j in range(5):
+        at = slice(j * step, (j + 1) * step)
+        acc = frames[:, at].astype(F32)
+        for r in range(n):
+            acc = acc + mm(mixed[r][...], so[r, :, at])
+        hidden[:, at] = acc.astype(BF16).astype(F32)
+
+    def norm(i, _):
+        at = pl.ds(pl.multiple_of(i * CHUNK, CHUNK), CHUNK)
+        offset, scale = layer_stats(hidden[at, :])
+        centred[at, :] = offset
+        inverse[at, :] = jnp.broadcast_to(scale, (CHUNK, inverse.shape[1]))
+        n2_out[at, :] = (offset + table[at, :]).astype(BF16)
+        return 0
+
+    lax.fori_loop(0, rows // CHUNK, norm, 0)
+    lane_head = lax.broadcasted_iota(jnp.int32, (rows, inner), 1)
+
+    def own(h, value):
+        inside = (lane_head >= h * width) & (lane_head < (h + 1) * width)
+        return jnp.where(inside, value, 0.0)
+
+    scale = width**-0.5
+    query = mm(n2_out[...], tq[...])
+    for h in range(heads):
+        qs[h * rows : (h + 1) * rows, :] = own(h, query).astype(BF16)
+    keys = mm(n2_out[...], tk[...]).astype(BF16)
+    values = mm(n2_out[...], tv[...]).astype(BF16)
+    mixed_grad = mm_bt(cotangent[...], to[...])
+    for h in range(heads):
+        gos[h * rows : (h + 1) * rows, :] = own(h, mixed_grad).astype(BF16)
+    key_grad = jnp.zeros((rows, inner), F32)
+    value_grad = jnp.zeros((rows, inner), F32)
+    query_grad = jnp.zeros((rows, inner), F32)
+    o2 = jnp.zeros((rows, inner), F32)
+    for h in range(heads):
+        at = slice(h * rows, (h + 1) * rows)
+        scores = mm_bt(qs[at, :], keys) * scale
+        powers = jnp.where(same[...] > 0.5, jnp.exp(scores), 0.0)
+        probs = powers / jnp.sum(powers, -1, keepdims=True)
+        rounded = probs.astype(BF16)
+        o2 = o2 + own(h, mm(rounded, values))
+        back = mm_bt(gos[at, :], values)
+        score = (probs * (back - jnp.sum(probs * back, -1, keepdims=True)) * scale).astype(BF16)
+        query_grad = query_grad + own(h, mm(score, keys))
+        key_grad = key_grad + mm_at(score, qs[at, :])
+        value_grad = value_grad + mm_at(rounded, gos[at, :])
+    o2_out[...] = o2.astype(BF16)
+    gq_out[...] = query_grad.astype(BF16)
+    gk_out[...] = key_grad.astype(BF16)
+    gv_out[...] = value_grad.astype(BF16)
+    for j in range(5):
+        at = slice(j * step, (j + 1) * step)
+        wide[:, at] = (
+            mm_bt(gq_out[...], tq[at, :]) + mm_bt(gk_out[...], tk[at, :]) + mm_bt(gv_out[...], tv[at, :])
+        )
+
+    def back_norm(i, _):
+        at = pl.ds(pl.multiple_of(i * CHUNK, CHUNK), CHUNK)
+        back = layer_back(centred[at, :], inverse[at, :1], wide[at, :])
+        gh_out[at, :] = (cotangent[at, :].astype(F32) + back).astype(BF16)
+        return 0
+
+    lax.fori_loop(0, rows // CHUNK, back_norm, 0)
+    for r in range(n):
+        grad_outs[r][...] = mm_bt(gh_out[...], so[r]).astype(BF16)
+    for j in range(5):
+        at = slice(j * step, (j + 1) * step)
+        out_out[:, at] = (hidden[:, at] + mm(o2_out[...], to[:, at])).astype(BF16)
+
+
+def terms_body(n, idx, *refs):
+    mixed = refs[:n]
+    gh, n2, gq, gk, gv, o2, cotangent = refs[n : n + 7]
+    keep_a, send_a, keep_b, send_b = refs[n + 7 : n + 11]
+    tall, flat = refs[n + 11 :]
+    me = idx[0]
+    dim, inner = tall.shape
+    depth, low = dim // n, inner // n
+
+    for i, grad in enumerate((gq, gk, gv)):
+        for j in range(5):
+            at = slice(j * (dim // 5), (j + 1) * (dim // 5))
+            tall[at, :] = mm_at(n2[:, at], grad[...]).astype(BF16)
+        for r in range(n):
+            to = send_a if r & 1 else keep_a
+            to[r >> 1, i * depth : (i + 1) * depth, :] = tall[
+                pl.ds(pl.multiple_of((me ^ r) * depth, depth), depth), :
+            ]
+    for j in range(5):
+        at = slice(j * (inner // 5), (j + 1) * (inner // 5))
+        flat[at, :] = mm_at(o2[:, at], cotangent[...]).astype(BF16)
+    for r in range(n):
+        to = send_b if r & 1 else keep_b
+        to[r >> 1, :low, :] = flat[pl.ds(pl.multiple_of((me ^ r) * low, low), low), :]
+        to[r >> 1, low:, :] = mm_at(mixed[r][...], gh[...])[:low].astype(BF16)
+
+
+def finish_body(idx, frames, hidden_grad, first, second, out):
+    def step(i, _):
+        at = pl.ds(pl.multiple_of(i * CHUNK, CHUNK), CHUNK)
+        centred, inverse = layer_stats(frames[at, :])
+        grad = first[at, :].astype(F32) + second[at, :].astype(F32)
+        back = layer_back(centred, inverse, grad)
+        out[at, :] = (hidden_grad[at, :].astype(F32) + back).astype(BF16)
+        return 0
+
+    lax.fori_loop(0, frames.shape[0] // CHUNK, step, 0)
+
+
+def add(left, right):
+    return (left.astype(F32) + right.astype(F32)).astype(BF16)
+
+
+def pick(value, index, axis=0):
+    return lax.dynamic_index_in_dim(value, index, axis, keepdims=False)
+
+
+def clip_scatter(value, clip, bits):
+    for place in reversed(range(bits)):
+        axis = bits - 1 - place
+        bit = (clip >> place) & 1
+        moved = flip(pick(value, 1 - bit, axis), "clip", 1 << place)
+        value = add(pick(value, bit, axis), moved)
+        value = jnp.expand_dims(value, axis)
+    return value.reshape(value.shape[bits:])
+
+
+def clip_gather(value, clip, bits):
+    pieces = [value]
+    for place in range(bits):
+        pieces = pieces + [flip(p, "clip", 1 << place) for p in pieces]
+    stack = jnp.stack(pieces)
+    order = jnp.arange(1 << bits) ^ clip
+    return stack, order
+
+
+def per_device(
+    frames_in,
+    ref_feats,
+    out_grad,
+    space_query,
+    space_key,
+    space_value,
+    space_output,
+    time_query,
+    time_key,
+    time_value,
+    time_output,
+):
+    n = lax.axis_size("frame")
+    clips = lax.axis_size("clip")
+    bits = clips.bit_length() - 1
+    me = lax.axis_index("frame")
+    clip = lax.axis_index("clip")
+    idx = jnp.stack([me, clip]).astype(jnp.int32)
+    _, per, tokens, dim = frames_in.shape
+    inner = space_query.shape[1]
+    width = inner // HEADS
+    lanes = -(-width // 128) * 128
+    room = -(-3 * width // 128) * 128
+    depth = dim // n
+    rows = per * tokens
+    total = n * rows
+    share = tokens // n
+    frames = frames_in.reshape(rows, dim)
+    refer = ref_feats[0]
+    cotangent = out_grad[0]
+
+    def gather(value):
+        one, two = flip(value, "frame", 1), flip(value, "frame", 2)
+        return [value, one, two, flip(two, "frame", 1)]
+
+    def relative(parts):
+        return [pick(parts, me ^ r) for r in range(n)]
+
+    def exchange(parts):
+        return [parts[0]] + [flip(parts[r], "frame", r) for r in range(1, n)]
+
+    packs = wide_call(
+        functools.partial(pack_body, HEADS), "pack_heads", [struct(depth, room)] * HEADS, [], 24, 0, 4
+    )(idx, space_query, space_key, space_value)
+    packs = exchange(relative(jnp.stack(packs)))
+    all_frames = gather(frames)
+    all_refer = jnp.concatenate(gather(refer), 0)
+    token_parts = cotangent.reshape(per, n, share, dim)
+    token_grad = jnp.concatenate(
+        [p.reshape(per * share, dim) for p in exchange([pick(token_parts, me ^ r, 1) for r in range(n)])], 0
+    )
+    held = after((space_output, time_query, time_key, time_value, time_output), all_frames[2], packs[2])
+    so_parts, tq_parts, tk_parts, tv_parts, to_parts = [gather(w) for w in held]
+    token_frames = jnp.concatenate(
+        [
+            lax.dynamic_slice_in_dim(f.reshape(per, tokens, dim), me * share, share, 1).reshape(
+                per * share, dim
+            )
+            for f in all_frames
+        ],
+        0,
+    )
+    table = position_table(0, n * per, dim).reshape(n, per, dim)
+    table = jnp.concatenate([pick(table, me ^ r) for r in range(n)], 0)
+    table = jnp.repeat(table, share, 0)
+    token_rows = n * per * share
+    token_of = jnp.arange(token_rows) % share
+    same = (token_of[:, None] == token_of[None, :]).astype(F32)
+
+    x_all, w_all, q_all, k_all, v_all, probs, mixed = wide_call(
+        functools.partial(spatial_forward_body, n, tokens, width),
+        "spatial_forward",
+        [
+            struct(total + tokens, dim),
+            struct(dim, room),
+            struct(total + tokens, lanes),
+            struct(total + tokens, lanes),
+            struct(total + tokens, lanes),
+            struct(total, 2 * tokens, dtype=F32),
+            struct(n, token_rows, lanes),
+        ],
+        [pltpu.VMEM((total, lanes), F32), pltpu.VMEM((token_rows, lanes), F32)],
+        40,
+        2_000_000_000,
+        2 * n + 2,
+    )(idx, *all_frames, *packs, all_refer)
+    mixed = exchange([mixed[r] for r in range(n)])
+
+    outs = wide_call(
+        functools.partial(temporal_body, n, HEADS),
+        "temporal",
+        [struct(token_rows, lanes)] * n
+        + [struct(token_rows, dim)] * 2
+        + [struct(token_rows, inner)] * 4
+        + [struct(token_rows, dim)],
+        [
+            pltpu.VMEM((n, lanes, dim), BF16),
+            pltpu.VMEM((dim, inner), BF16),
+            pltpu.VMEM((dim, inner), BF16),
+            pltpu.VMEM((dim, inner), BF16),
+            pltpu.VMEM((inner, dim), BF16),
+            pltpu.VMEM((token_rows, dim), F32),
+            pltpu.VMEM((token_rows, dim), F32),
+            pltpu.VMEM((token_rows, 128), F32),
+            pltpu.VMEM((token_rows, dim), F32),
+            pltpu.VMEM((HEADS * token_rows, inner), BF16),
+            pltpu.VMEM((HEADS * token_rows, inner), BF16),
+        ],
+        48,
+        5_000_000_000,
+        6 * n + 5,
+    )(idx, *mixed, *so_parts, *tq_parts, *tk_parts, *tv_parts, *to_parts, token_frames, token_grad, table, same)
+    mixed_grads = exchange(list(outs[:n]))
+    hidden_grad, n2, gq, gk, gv, o2, out_tokens = outs[n:]
+
+    keep_a, send_a, keep_b, send_b = wide_call(
+        functools.partial(terms_body, n),
+        "temporal_terms",
+        [struct(n // 2, 3 * depth, inner)] * 2 + [struct(n // 2, 2 * (inner // n), dim)] * 2,
+        [pltpu.VMEM((dim, inner), BF16), pltpu.VMEM((inner, dim), BF16)],
+        40,
+        3_000_000_000,
+        n + 8,
+    )(idx, *mixed, hidden_grad, n2, gq, gk, gv, o2, token_grad)
+
+    keep_out, send_out, keep_ref, send_ref, term = wide_call(
+        functools.partial(spatial_backward_body, n, tokens, width),
+        "spatial_backward",
+        [struct(n // 2, rows, dim)] * 2 + [struct(n // 2, share, dim)] * 2 + [struct(dim, room)],
+        [
+            pltpu.VMEM((total, lanes), F32),
+            pltpu.VMEM((token_rows, lanes), F32),
+            pltpu.VMEM((total + tokens, room), BF16),
+        ],
+        40,
+        4_000_000_000,
+        n + 7,
+    )(idx, *mixed_grads, x_all, w_all, q_all, k_all, v_all, probs)
+
+    def to_frames(value):
+        parts = exchange(list(value.reshape(n, per * share, dim)))
+        stack = jnp.stack([p.reshape(per, share, dim) for p in parts], 1)
+        order = jnp.arange(n) ^ me
+        return jnp.take(stack, order, 1).reshape(per, tokens, dim)
+
+    output = to_frames(out_tokens)
+    hidden_frames = to_frames(hidden_grad).reshape(rows, dim)
+
+    near = add(keep_out, flip(send_out, "frame", 1))
+    far = flip(near[1], "frame", 2)
+    near_ref = add(keep_ref, flip(send_ref, "frame", 1))
+    refer_grad = add(near_ref[0], flip(near_ref[1], "frame", 2))
+    frames_grad = wide_call(finish_body, "finish", [struct(rows, dim)], [], 24, 0, 5)(
+        idx, frames, hidden_frames, near[0], far
+    )[0].reshape(per, tokens, dim)
+
+    split = (2,) * bits
+
+    def over_frame(keep, send):
+        near = add(keep, flip(send, "frame", 1))
+        return add(near[0], flip(near[1], "frame", 2))
+
+    sum_a = over_frame(keep_a, send_a)
+    sum_b = over_frame(keep_b, send_b)
+    sum_a = clip_scatter(sum_a.reshape(split + (-1, inner)), clip, bits)
+    sum_b = clip_scatter(sum_b.reshape(split + (-1, dim)), clip, bits)
+    term = term.reshape(n, clips, depth // clips, room).swapaxes(0, 1)
+    sum_c = clip_scatter(term.reshape(split + (n, depth // clips, room)), clip, bits)
+    heads = exchange(relative(sum_c))
+    heads = jnp.take(jnp.stack(heads), jnp.arange(n) ^ me, 0)
+    sum_c = jnp.stack(
+        [
+            heads[:, :, i * width : (i + 1) * width].swapaxes(0, 1).reshape(-1, inner)
+            for i in range(3)
+        ]
+    )
+
+    def whole(value):
+        stack, order = clip_gather(value, clip, bits)
+        return jnp.take(stack, order, 0)
+
+    all_a = whole(sum_a).reshape(3, depth, inner).astype(F32)
+    all_b = whole(sum_b).reshape(2, inner // n, dim).astype(F32)
+    all_c = whole(sum_c).swapaxes(0, 1).reshape(3, depth, inner).astype(F32)
+    return (
+        output[None],
+        frames_grad[None],
+        refer_grad[None],
+        all_c[0],
+        all_c[1],
+        all_c[2],
+        all_b[1],
+        all_a[0],
+        all_a[1],
+        all_a[2],
+        all_b[0],
+    )
+
+
 def solution(mesh):
     in_specs = (
         P("clip", "frame", None, None),
@@ -333,6 +856,8 @@
         P("frame", None),
         P("frame", None),
     )
+    clips = mesh.shape["clip"]
+    by_heads = mesh.shape["frame"] == HEADS == 4 and clips & (clips - 1) == 0
     return jax.shard_map(
-        per_device, mesh=mesh, in_specs=in_specs, out_specs=out_specs, check_vma=False
-    )
+        per_device if by_heads else per_device_general, mesh=mesh, in_specs=in_specs, out_specs=out_specs, check_vma=False
+    )

time: 700 us -> 368 us (0.53)
  waiting for transfers between devices: 476 us -> 171 us
  matrix products: 92.4 us -> 0 us
  starting transfers between devices: 21.6 us -> 81 us
  Pallas kernels: 0 us -> 42 us
  blocking collectives: 19.6 us -> 0 us
  between operations: 15.6 us -> 1.51 us
    reduce_scatter x8 -> x0, waiting for transfers between devices: 227 us -> none  [the longest x1 31.3 us: per_device(): lax.psum_scatter(term_tk.astype(jnp.bfloat16), 'frame', scatter_dimension...]
    ppermute x0 -> x80, waiting for transfers between devices: none -> 171 us  [flip(): return lax.ppermute(value, axis, [(i, i ^ bit) for i in range(size)])]
    psum x1 -> x0, waiting for transfers between devices: 131 us -> none  [per_device(): lax.psum(share_sq.astype(jnp.bfloat16), 'clip').astype(jnp.float32)]
    all_gather x8 -> x0, waiting for transfers between devices: 106 us -> none  [the longest x1 19.3 us: per_device(): lax.all_gather(space_value, 'frame', axis=0, tiled=True)]
    dot_general x42 -> x0, matrix products: 92.4 us -> none  [the longest x12 30.7 us: product(): return jnp.einsum(form, left, right, preferred_element_type=jnp.float32)]
    ppermute x0 -> x80, starting transfers between devices: none -> 81 us  [flip(): return lax.ppermute(value, axis, [(i, i ^ bit) for i in range(size)])]
    pallas_call x0 -> x6, Pallas kernels: none -> 42 us  [the longest x1 15.1 us: per_device(): wide_call(functools.partial(temporal_body, n, HEADS), 'temporal', [struct...]
    all_to_all x5 -> x0, starting transfers between devices: 20.4 us -> none  [the longest x1 4.32 us: per_device(): lax.all_to_all(normed_two, 'frame', split_axis=1, concat_axis=0, tiled=True)]
  transfers between devices with their start and end apart: 23 -> 80, of which waited for: 19 -> 37; matrix products, arithmetic and copies ran while one was open for 17% -> 17% of each run, Pallas kernels for 0% -> 7%
where the time goes in v1:
time: 368 us; the launch traced here: 367 us
  waiting for transfers between devices  171 us (46%)
  starting transfers between devices  81 us (22%)
  local copies, waits for them, and re-layouts  50.4 us (14%)
  Pallas kernels  42 us (11%)
  other arithmetic  21.6 us (6%)
    ppermute x80, waiting for transfers between devices, flip(): return lax.ppermute(value, axis, [(i, i ^ bit) for i in range(size)])  171 us
    ppermute x80, starting transfers between devices, flip(): return lax.ppermute(value, axis, [(i, i ^ bit) for i in range(size)])  81 us
    pallas_call x1, Pallas kernels, per_device(): wide_call(functools.partial(temporal_body, n, HEADS), 'temporal', [struct...  15.1 us
    unnamed x87, local copies, waits for them, and re-layouts  12 us
    convert_element_type x13, other arithmetic, add(): return (left.astype(F32) + right.astype(F32)).astype(BF16)  10.3 us
    pallas_call x1, Pallas kernels, per_device(): wide_call(functools.partial(spatial_forward_body, n, tokens, width), 'spa...  9.87 us
  transfers between devices with their start and end apart: 80, of which 37 were waited for; matrix products, arithmetic and copies ran while one was open for 17% of the time, Pallas kernels for 7%

profile of v1, /device:TPU:0, one launch (start us, length us, event | category | flops | bytes accessed | tf_op | source)
XLA Modules:
  0.0 367.4 jit_solution(10259779781482181746)
XLA Ops:
  0.6 3.0 collective-permute-start.7
  9.1 1.9 collective-permute-start.4
  12.0 2.3 copy.44
  14.3 3.5 reshape_reshape.7
  18.4 1.9 collective-permute-start.28
  20.9 6.0 %collective-permute-done.29 = bf16[2,24,1280]{2,1,0:T(8,128)(2,1)} collective-permute-done((bf16[2,24,1280]{2,1,0:T(8,128)(2,1)S(1)}, bf16[2,24,1280]{2,1,0:T(8,128)(2,1)}, u32[]{:S(2)}, u32[]{:S(2)}) %collective-permute-start.29) | collective-permute-done | bytes 122912 | tf_op jit(solution)/shard_map/ppermute | solution.py:350
  27.5 1.5 collective-permute-start.5
  30.4 1.8 pad_maximum_fusion.2.refs_25_.refs_10_
  33.2 4.2 %collective-permute-done.5.refs_7_ = bf16[320,512]{1,0:T(8,128)(2,1)} collective-permute-done((bf16[320,512]{1,0:T(8,128)(2,1)}, bf16[320,512]{1,0:T(8,128)(2,1)}, u32[]{:S(2)}, u32[]{:S(2)}) %collective-permute-start.5) | collective-permute-done | bytes 327712 | tf_op jit(solution)/shard_map/ppermute | solution.py:350
  40.7 6.4 %collective-permute-done.13.refs_6_ = bf16[160,1280]{1,0:T(8,128)(2,1)S(1)} collective-permute-done((bf16[160,1280]{1,0:T(8,128)(2,1)S(1)}, bf16[160,1280]{1,0:T(8,128)(2,1)S(1)}, u32[]{:S(2)}, u32[]{:S(2)}) %collective-permute-start.13) | collective-permute-done | bytes 409632 | tf_op jit(solution)/shard_map/ppermute | solution.py:350
  49.2 9.9 %spatial_forward.1 = (bf16[864,1280]{1,0:T(8,128)(2,1)S(1)}, bf16[1280,512]{1,0:T(8,128)(2,1)S(1)}, bf16[864,256]{1,0:T(8,128)(2,1)S(1)}, bf16[864,256]{1,0:T(8,...) custom-call(s32[2]{0:T(128)S(1)} %pad_add_fusion.idx, ...), custom_call_target="tpu_custom_call" | custom-call | flops 2000000000 | bytes 8000000 | tf_op jit(solution)/shard_map/spatial_forward/pallas_call | solution.py:702
  60.8 3.9 %collective-permute-done.19.refs_14_ = bf16[320,640]{1,0:T(8,128)(2,1)S(1)} collective-permute-done((bf16[320,640]{1,0:T(8,128)(2,1)S(1)}, bf16[320,640]{1,0:T(8,128)(2,1)S(1)}, u32[]{:S(2)}, u32[]{:S(2)}) %collective-permute-start.19) | collective-permute-done | bytes 409632 | tf_op jit(solution)/shard_map/ppermute | solution.py:350
  66.2 7.3 %collective-permute-done.22.refs_18_ = bf16[320,640]{1,0:T(8,128)(2,1)S(1)} collective-permute-done((bf16[320,640]{1,0:T(8,128)(2,1)S(1)}, bf16[320,640]{1,0:T(8,128)(2,1)S(1)}, u32[]{:S(2)}, u32[]{:S(2)}) %collective-permute-start.22) | collective-permute-done | bytes 409632 | tf_op jit(solution)/shard_map/ppermute | solution.py:350
  73.5 1.6 collective-permute-start.14
  75.1 7.2 %collective-permute-done.25.refs_22_ = bf16[160,1280]{1,0:T(8,128)(2,1)S(1)} collective-permute-done((bf16[160,1280]{1,0:T(8,128)(2,1)S(1)}, bf16[160,1280]{1,0:T(8,128)(2,1)S(1)}, u32[]{:S(2)}, u32[]{:S(2)}) %collective-permute-start.25) | collective-permute-done | bytes 409632 | tf_op jit(solution)/shard_map/ppermute | solution.py:350
  82.8 1.6 collective-permute-done.10.refs_2_
  88.2 15.1 %temporal.1 = (bf16[192,256]{1,0:T(8,128)(2,1)S(1)}, bf16[192,256]{1,0:T(8,128)(2,1)S(1)}, bf16[192,256]{1,0:T(8,128)(2,1)S(1)}, bf16[192,256]{1,0:T(8,128)(2,1)...) custom-call(s32[2]{0:T(128)S(1)} %pad_add_fusion.idx, ...), custom_call_target="tpu_custom_call" | custom-call | flops 5000000000 | bytes 8000000 | tf_op jit(solution)/shard_map/temporal/pallas_call | solution.py:721
  106.6 1.8 fusion.14
  110.3 5.5 %temporal_terms.1 = (bf16[2,960,640]{2,1,0:T(8,128)(2,1)S(1)}, bf16[2,960,640]{2,1,0:T(8,128)(2,1)}, bf16[2,320,1280]{2,1,0:T(8,128)(2,1)S(1)}, bf16[2,320,1280]{2,1,0:T(8,128)(2,1)}) custom-call(s32[2]{0:T(128)S(1)} %pad_add_fusion.idx, bf16[192,256]{1,0:T(8,128)(2,1)S(1)} %get-tuple-element.115.refs_0_, ...), custom_call_target="tpu_custom_call" | custom-call | flops 3000000000 | bytes 8000000 | tf_op jit(solution)/shard_map/temporal_terms/pallas_call | solution.py:748
  119.2 6.8 %spatial_backward.1 = (bf16[2,192,1280]{2,1,0:T(8,128)(2,1)S(1)}, bf16[2,192,1280]{2,1,0:T(8,128)(2,1)S(1)}, bf16[2,24,1280]{2,1,0:T(8,128)(2,1)S(1)}, bf16[2,24...) custom-call(s32[2]{0:T(128)S(1)} %pad_add_fusion.idx, bf16[192,256]{1,0:T(8,128)(2,1)S(1)} %get-tuple-element.60.refs_0_, ...), custom_call_target="tpu_custom_call" | custom-call | flops 4000000000 | bytes 8000000 | tf_op jit(solution)/shard_map/spatial_backward/pallas_call | solution.py:758
  129.9 1.6 gather_fusion.5
  132.1 2.6 collective-permute-start.43
  134.7 1.9 pad_maximum_fusion.3
  136.5 2.4 gather_fusion.4
  143.4 21.0 %collective-permute-done.43 = bf16[2,2,4,40,512]{4,3,2,1,0:T(8,128)(2,1)} collective-permute-done((bf16[2,2,4,40,512]{4,3,2,1,0:T(8,128)(2,1)}, bf16[2,2,4,40,512]{4,3,2,1,0:T(8,128)(2,1)}, u32[]{:S(2)}, u32[]{:S(2)}) %collective-permute-start.43) | collective-permute-done | bytes 655392 | tf_op jit(solution)/shard_map/ppermute | solution.py:350
  167.2 7.9 %collective-permute-done.44 = bf16[1,2,4,40,512]{4,3,2,1,0:T(8,128)(2,1)S(1)} collective-permute-done((bf16[1,2,4,40,512]{4,3,2,1,0:T(8,128)(2,1)S(1)}, bf16[1,2,4,40,512]{4,3,2,1,0:T(8,128)(2,1)S(1)}, u32[]{:S(2)}, u32[]{:S(2)}) %collective-permute-start.44) | collective-permute-done | bytes 327712 | tf_op jit(solution)/shard_map/ppermute | solution.py:350
  175.2 1.6 collective-permute-start.45
  178.2 2.4 collective-permute-done.45
  180.8 1.5 collective-permute-start.47
  186.3 2.1 gather_fusion
  200.2 2.4 collective-permute-done.49
  202.6 3.0 collective-permute-start.52
  209.6 3.7 %finish.1 = bf16[192,1280]{1,0:T(8,128)(2,1)} custom-call(s32[2]{0:T(128)S(1)} %pad_add_fusion.idx, bf16[192,1280]{1,0:T(8,128)(2,1)S(1)} %bitcast.227, bf16[192,1280]{1,0:T(8,128)(2,1)S(1)} %bitcast.222, bf16[192,1280]{1,0:T(8,128)(2,1)S(1)} %get-tuple-element.99.first, bf16[192,1280]{1,0:T(8,128)(2,1)} %collective-permute-done.40.second), custom_call_target="tpu_custom_call" | custom-call | bytes 8000000 | tf_op jit(solution)/shard_map/finish/pallas_call | solution.py:785
  215.9 1.8 collective-permute-start.55
  217.7 1.8 add_convert_fusion.1
  221.4 4.6 %collective-permute-done.53 = bf16[3,40,640]{2,1,0:T(8,128)(2,1)S(1)} collective-permute-done((bf16[3,40,640]{2,1,0:T(8,128)(2,1)S(1)}, bf16[3,40,640]{2,1,0:T(8,128)(2,1)S(1)}, u32[]{:S(2)}, u32[]{:S(2)}) %collective-permute-start.53) | collective-permute-done | bytes 153632 | tf_op jit(solution)/shard_map/ppermute | solution.py:350
  226.7 2.6 collective-permute-done.54
  230.0 1.6 collective-permute-done.55
  232.3 3.1 gather_fusion.1
  236.5 1.6 fusion.1
  238.2 1.8 collective-permute-start.58
  240.2 1.5 fusion.12
  241.7 15.6 %collective-permute-done.58 = bf16[2,2,40,1280]{3,2,1,0:T(8,128)(2,1)S(1)} collective-permute-done((bf16[2,2,40,1280]{3,2,1,0:T(8,128)(2,1)S(1)}, bf16[2,2,40,1280]{3,2,1,0:T(8,128)(2,1)S(1)}, u32[]{:S(2)}, u32[]{:S(2)}) %collective-permute-start.58) | collective-permute-done | bytes 409632 | tf_op jit(solution)/shard_map/ppermute | solution.py:350
  257.6 2.4 add_convert_fusion
  260.0 3.3 collective-permute-done.59
  263.4 1.5 collective-permute-start.60
  266.2 2.8 collective-permute-done.60
  269.0 1.6 collective-permute-start.61
  270.6 2.1 collective-permute-start.64
  273.8 2.1 collective-permute-start.65
  278.4 3.2 collective-permute-start.67
  281.6 4.8 %collective-permute-done.65 = bf16[40,1280]{1,0:T(8,128)(2,1)S(1)} collective-permute-done((bf16[40,1280]{1,0:T(8,128)(2,1)S(1)}, bf16[40,1280]{1,0:T(8,128)(2,1)S(1)}, u32[]{:S(2)}, u32[]{:S(2)}) %collective-permute-start.65) | collective-permute-done | bytes 102432 | tf_op jit(solution)/shard_map/ppermute | solution.py:350
  286.4 4.8 %collective-permute-done.69 = bf16[960,640]{1,0:T(8,128)(2,1)S(1)} collective-permute-done((bf16[960,640]{1,0:T(8,128)(2,1)S(1)}, bf16[960,640]{1,0:T(8,128)(2,1)S(1)}, u32[]{:S(2)}, u32[]{:S(2)}) %collective-permute-start.69) | collective-permute-done | bytes 1228832 | tf_op jit(solution)/shard_map/ppermute | solution.py:350
  292.4 3.2 collective-permute-start.70
  296.3 25.0 %collective-permute-done.70 = bf16[2,2,120,640]{3,2,1,0:T(8,128)(2,1)S(1)} collective-permute-done((bf16[2,2,120,640]{3,2,1,0:T(8,128)(2,1)}, bf16[2,2,120,640]{3,2,1,0:T(8,128)(2,1)S(1)}, u32[]{:S(2)}, u32[]{:S(2)}) %collective-permute-start.70) | collective-permute-done | bytes 614432 | tf_op jit(solution)/shard_map/ppermute | solution.py:350
  322.3 7.9 %collective-permute-done.71 = bf16[1,2,120,640]{3,2,1,0:T(8,128)(2,1)S(1)} collective-permute-done((bf16[1,2,120,640]{3,2,1,0:T(8,128)(2,1)S(1)}, bf16[1,2,120,640]{3,2,1,0:T(8,128)(2,1)S(1)}, u32[]{:S(2)}, u32[]{:S(2)}) %collective-permute-start.71) | collective-permute-done | bytes 307232 | tf_op jit(solution)/shard_map/ppermute | solution.py:350
  332.2 3.4 collective-permute-done.72
  336.9 3.3 collective-permute-start.76
  341.6 3.3 collective-permute-start.77
  348.0 3.7 %collective-permute-start.79 = (bf16[120,640]{1,0:T(8,128)(2,1)S(1)}, bf16[120,640]{1,0:T(8,128)(2,1)S(1)}, u32[]{:S(2)}, u32[]{:S(2)}) collective-permute-start(bf16[120,640]{1,0:T(8,128)(2,1)S(1)} %collective-permute-done.75), channel_id=1, source_target_pairs={{0,16},{4,20},{8,24},{12,28},{16,0},{20,4},{24,8},{28,12},{1,17},{... | collective-permute-start | bytes 460808 | tf_op jit(solution)/shard_map/ppermute | solution.py:350
  351.7 8.1 %collective-permute-done.77 = bf16[120,640]{1,0:T(8,128)(2,1)S(1)} collective-permute-done((bf16[120,640]{1,0:T(8,128)(2,1)S(1)}, bf16[120,640]{1,0:T(8,128)(2,1)S(1)}, u32[]{:S(2)}, u32[]{:S(2)}) %collective-permute-start.77) | collective-permute-done | bytes 153632 | tf_op jit(solution)/shard_map/ppermute | solution.py:350
  359.9 3.3 collective-permute-done.78
  363.2 1.7 collective-permute-done.79
  365.9 1.5 slice_bitcast_fusion.3
  (290 shorter events, 90.0 us)
Async XLA Ops:
  0.6 17.3 %collective-permute-start.7 = (bf16[24,1280]{1,0:T(8,128)(2,1)}, bf16[24,1280]{1,0:T(8,128)(2,1)S(1)}, u32[]{:S(2)}, u32[]{:S(2)}) collective-permute-start(bf16[24,1280]{1,0:T(8,128)(2,1)} %bitcast.259), channel_id=1, source_target_pairs={{0,2},{1,3},{2,0},{3,1},{4,6},{5,7},{6,4},{7,5},{8,10},{9,11},{10,... | collective-permute-start | bytes 184328 | tf_op jit(solution)/shard_map/ppermute | solution.py:350
  3.7 14.7 %collective-permute-start.6 = (bf16[24,1280]{1,0:T(8,128)(2,1)}, bf16[24,1280]{1,0:T(8,128)(2,1)S(1)}, u32[]{:S(2)}, u32[]{:S(2)}) collective-permute-start(bf16[24,1280]{1,0:T(8,128)(2,1)} %bitcast.260), channel_id=1, source_target_pairs={{0,1},{1,0},{2,3},{3,2},{4,5},{5,4},{6,7},{7,6},{8,9},{9,8},{10,11... | collective-permute-start | bytes 184328 | tf_op jit(solution)/shard_map/ppermute | solution.py:350
  3.7 23.8 %collective-permute-start.1 = (bf16[192,1280]{1,0:T(8,128)(2,1)}, bf16[192,1280]{1,0:T(8,128)(2,1)S(1)}, u32[]{:S(2)}, u32[]{:S(2)}) collective-permute-start(bf16[192,1280]{1,0:T(8,128)(2,1)} %bitcast.224), channel_id=1, source_target_pairs={{0,2},{1,3},{2,0},{3,1},{4,6},{5,7},{6,4},{7,5},{8,10},{9,11},{10,... | collective-permute-start | bytes 1474568 | tf_op jit(solution)/shard_map/ppermute | solution.py:350
  9.1 18.4 %collective-permute-start.4 = (bf16[320,512]{1,0:T(8,128)(2,1)}, bf16[320,512]{1,0:T(8,128)(2,1)}, u32[]{:S(2)}, u32[]{:S(2)}) collective-permute-start(bf16[320,512]{1,0:T(8,128)(2,1)} %get-tuple-element.95), channel_id=1, source_target_pairs={{0,2},{1,3},{2,0},{3,1},{4,6},{5,7},{6,4},{7,5},{8,10},{9,11},{10,... | collective-permute-start | bytes 983048 | tf_op jit(solution)/shard_map/ppermute | solution.py:350
  11.7 15.2 %collective-permute-start.29 = (bf16[2,24,1280]{2,1,0:T(8,128)(2,1)S(1)}, bf16[2,24,1280]{2,1,0:T(8,128)(2,1)}, u32[]{:S(2)}, u32[]{:S(2)}) collective-permute-start(bf16[2,24,1280]{2,1,0:T(8,128)(2,1)S(1)} %get-tuple-element.109), channel_id=1, source_target_pairs={{0,3},{1,2},{2,1},{3,0},{4,7},{5,6},{6,5},{7,4},{8,11},{9,10},{10,... | collective-permute-start | bytes 368648 | tf_op jit(solution)/shard_map/ppermute | solution.py:350
  18.4 11.6 %collective-permute-start.28 = (bf16[2,24,1280]{2,1,0:T(8,128)(2,1)}, bf16[2,24,1280]{2,1,0:T(8,128)(2,1)}, u32[]{:S(2)}, u32[]{:S(2)}) collective-permute-start(bf16[2,24,1280]{2,1,0:T(8,128)(2,1)} %get-tuple-element.110), channel_id=1, source_target_pairs={{0,2},{1,3},{2,0},{3,1},{4,6},{5,7},{6,4},{7,5},{8,10},{9,11},{10,... | collective-permute-start | bytes 368648 | tf_op jit(solution)/shard_map/ppermute | solution.py:350
  20.2 9.7 %collective-permute-start.27 = (bf16[2,24,1280]{2,1,0:T(8,128)(2,1)}, bf16[2,24,1280]{2,1,0:T(8,128)(2,1)}, u32[]{:S(2)}, u32[]{:S(2)}) collective-permute-start(bf16[2,24,1280]{2,1,0:T(8,128)(2,1)} %get-tuple-element.111), channel_id=1, source_target_pairs={{0,1},{1,0},{2,3},{3,2},{4,5},{5,4},{6,7},{7,6},{8,9},{9,8},{10,11... | collective-permute-start | bytes 368648 | tf_op jit(solution)/shard_map/ppermute | solution.py:350
  26.9 12.3 %collective-permute-start = (bf16[192,1280]{1,0:T(8,128)(2,1)S(1)}, bf16[192,1280]{1,0:T(8,128)(2,1)S(1)}, u32[]{:S(2)}, u32[]{:S(2)}) collective-permute-start(bf16[192,1280]{1,0:T(8,128)(2,1)S(1)} %bitcast.225), channel_id=1, source_target_pairs={{0,1},{1,0},{2,3},{3,2},{4,5},{5,4},{6,7},{7,6},{8,9},{9,8},{10,11... | collective-permute-start | bytes 1474568 | tf_op jit(solution)/shard_map/ppermute | solution.py:350
  27.5 9.9 %collective-permute-start.5 = (bf16[320,512]{1,0:T(8,128)(2,1)}, bf16[320,512]{1,0:T(8,128)(2,1)}, u32[]{:S(2)}, u32[]{:S(2)}) collective-permute-start(bf16[320,512]{1,0:T(8,128)(2,1)} %get-tuple-element.94), channel_id=1, source_target_pairs={{0,3},{1,2},{2,1},{3,0},{4,7},{5,6},{6,5},{7,4},{8,11},{9,10},{10,... | collective-permute-start | bytes 983048 | tf_op jit(solution)/shard_map/ppermute | solution.py:350
  29.9 10.8 %collective-permute-start.12 = (bf16[160,1280]{1,0:T(8,128)(2,1)S(1)}, bf16[160,1280]{1,0:T(8,128)(2,1)S(1)}, u32[]{:S(2)}, u32[]{:S(2)}) collective-permute-start(bf16[160,1280]{1,0:T(8,128)(2,1)S(1)} %copy-done.12), channel_id=1, source_target_pairs={{0,1},{1,0},{2,3},{3,2},{4,5},{5,4},{6,7},{7,6},{8,9},{9,8},{10,11... | collective-permute-start | bytes 1228808 | tf_op jit(solution)/shard_map/ppermute | solution.py:350
  29.9 18.6 %collective-permute-start.2 = (bf16[192,1280]{1,0:T(8,128)(2,1)S(1)}, bf16[192,1280]{1,0:T(8,128)(2,1)S(1)}, u32[]{:S(2)}, u32[]{:S(2)}) collective-permute-start(bf16[192,1280]{1,0:T(8,128)(2,1)S(1)} %collective-permute-done.1.refs_2_), channel_id=1, source_target_pairs={{0,1},{1,0},{2,3},{3,2},{4,5},{5,4},{6,7},{7,6},{8,9},{9,8},{10,11... | collective-permute-start | bytes 1474568 | tf_op jit(solution)/shard_map/ppermute | solution.py:350
  32.3 14.9 %collective-permute-start.13 = (bf16[160,1280]{1,0:T(8,128)(2,1)S(1)}, bf16[160,1280]{1,0:T(8,128)(2,1)S(1)}, u32[]{:S(2)}, u32[]{:S(2)}) collective-permute-start(bf16[160,1280]{1,0:T(8,128)(2,1)S(1)} %copy-done.12), channel_id=1, source_target_pairs={{0,2},{1,3},{2,0},{3,1},{4,6},{5,7},{6,4},{7,5},{8,10},{9,11},{10,... | collective-permute-start | bytes 1228808 | tf_op jit(solution)/shard_map/ppermute | solution.py:350
  37.4 11.2 %collective-permute-start.15 = (bf16[320,640]{1,0:T(8,128)(2,1)S(1)}, bf16[320,640]{1,0:T(8,128)(2,1)S(1)}, u32[]{:S(2)}, u32[]{:S(2)}) collective-permute-start(bf16[320,640]{1,0:T(8,128)(2,1)S(1)} %copy-done.13), channel_id=1, source_target_pairs={{0,1},{1,0},{2,3},{3,2},{4,5},{5,4},{6,7},{7,6},{8,9},{9,8},{10,11... | collective-permute-start | bytes 1228808 | tf_op jit(solution)/shard_map/ppermute | solution.py:350
  39.2 19.9 %collective-permute-start.16 = (bf16[320,640]{1,0:T(8,128)(2,1)S(1)}, bf16[320,640]{1,0:T(8,128)(2,1)S(1)}, u32[]{:S(2)}, u32[]{:S(2)}) collective-permute-start(bf16[320,640]{1,0:T(8,128)(2,1)S(1)} %copy-done.13), channel_id=1, source_target_pairs={{0,2},{1,3},{2,0},{3,1},{4,6},{5,7},{6,4},{7,5},{8,10},{9,11},{10,... | collective-permute-start | bytes 1228808 | tf_op jit(solution)/shard_map/ppermute | solution.py:350
  40.7 18.7 %collective-permute-start.18 = (bf16[320,640]{1,0:T(8,128)(2,1)S(1)}, bf16[320,640]{1,0:T(8,128)(2,1)S(1)}, u32[]{:S(2)}, u32[]{:S(2)}) collective-permute-start(bf16[320,640]{1,0:T(8,128)(2,1)S(1)} %copy-done.14), channel_id=1, source_target_pairs={{0,1},{1,0},{2,3},{3,2},{4,5},{5,4},{6,7},{7,6},{8,9},{9,8},{10,11... | collective-permute-start | bytes 1228808 | tf_op jit(solution)/shard_map/ppermute | solution.py:350
  47.1 17.6 %collective-permute-start.19 = (bf16[320,640]{1,0:T(8,128)(2,1)S(1)}, bf16[320,640]{1,0:T(8,128)(2,1)S(1)}, u32[]{:S(2)}, u32[]{:S(2)}) collective-permute-start(bf16[320,640]{1,0:T(8,128)(2,1)S(1)} %copy-done.14), channel_id=1, source_target_pairs={{0,2},{1,3},{2,0},{3,1},{4,6},{5,7},{6,4},{7,5},{8,10},{9,11},{10,... | collective-permute-start | bytes 1228808 | tf_op jit(solution)/shard_map/ppermute | solution.py:350
  48.5 16.2 %collective-permute-start.21 = (bf16[320,640]{1,0:T(8,128)(2,1)S(1)}, bf16[320,640]{1,0:T(8,128)(2,1)S(1)}, u32[]{:S(2)}, u32[]{:S(2)}) collective-permute-start(bf16[320,640]{1,0:T(8,128)(2,1)S(1)} %copy-done.23), channel_id=1, source_target_pairs={{0,1},{1,0},{2,3},{3,2},{4,5},{5,4},{6,7},{7,6},{8,9},{9,8},{10,11... | collective-permute-start | bytes 1228808 | tf_op jit(solution)/shard_map/ppermute | solution.py:350
  48.5 24.9 %collective-permute-start.22 = (bf16[320,640]{1,0:T(8,128)(2,1)S(1)}, bf16[320,640]{1,0:T(8,128)(2,1)S(1)}, u32[]{:S(2)}, u32[]{:S(2)}) collective-permute-start(bf16[320,640]{1,0:T(8,128)(2,1)S(1)} %copy-done.23), channel_id=1, source_target_pairs={{0,2},{1,3},{2,0},{3,1},{4,6},{5,7},{6,4},{7,5},{8,10},{9,11},{10,... | collective-permute-start | bytes 1228808 | tf_op jit(solution)/shard_map/ppermute | solution.py:350
  59.1 14.3 %collective-permute-start.24 = (bf16[160,1280]{1,0:T(8,128)(2,1)S(1)}, bf16[160,1280]{1,0:T(8,128)(2,1)S(1)}, u32[]{:S(2)}, u32[]{:S(2)}) collective-permute-start(bf16[160,1280]{1,0:T(8,128)(2,1)S(1)} %copy-done.24), channel_id=1, source_target_pairs={{0,1},{1,0},{2,3},{3,2},{4,5},{5,4},{6,7},{7,6},{8,9},{9,8},{10,11... | collective-permute-start | bytes 1228808 | tf_op jit(solution)/shard_map/ppermute | solution.py:350
  59.4 22.9 %collective-permute-start.25 = (bf16[160,1280]{1,0:T(8,128)(2,1)S(1)}, bf16[160,1280]{1,0:T(8,128)(2,1)S(1)}, u32[]{:S(2)}, u32[]{:S(2)}) collective-permute-start(bf16[160,1280]{1,0:T(8,128)(2,1)S(1)} %copy-done.24), channel_id=1, source_target_pairs={{0,2},{1,3},{2,0},{3,1},{4,6},{5,7},{6,4},{7,5},{8,10},{9,11},{10,... | collective-permute-start | bytes 1228808 | tf_op jit(solution)/shard_map/ppermute | solution.py:350
  64.7 17.6 %collective-permute-start.9 = (bf16[192,256]{1,0:T(8,128)(2,1)S(1)}, bf16[192,256]{1,0:T(8,128)(2,1)S(1)}, u32[]{:S(2)}, u32[]{:S(2)}) collective-permute-start(bf16[192,256]{1,0:T(8,128)(2,1)S(1)} %get-tuple-element.114), channel_id=1, source_target_pairs={{0,1},{1,0},{2,3},{3,2},{4,5},{5,4},{6,7},{7,6},{8,9},{9,8},{10,11... | collective-permute-start | bytes 294920 | tf_op jit(solution)/shard_map/ppermute | solution.py:350
  64.7 19.6 %collective-permute-start.10 = (bf16[192,256]{1,0:T(8,128)(2,1)S(1)}, bf16[192,256]{1,0:T(8,128)(2,1)S(1)}, u32[]{:S(2)}, u32[]{:S(2)}) collective-permute-start(bf16[192,256]{1,0:T(8,128)(2,1)S(1)} %get-tuple-element.113), channel_id=1, source_target_pairs={{0,2},{1,3},{2,0},{3,1},{4,6},{5,7},{6,4},{7,5},{8,10},{9,11},{10,... | collective-permute-start | bytes 294920 | tf_op jit(solution)/shard_map/ppermute | solution.py:350
  73.5 11.9 %collective-permute-start.11 = (bf16[192,256]{1,0:T(8,128)(2,1)S(1)}, bf16[192,256]{1,0:T(8,128)(2,1)S(1)}, u32[]{:S(2)}, u32[]{:S(2)}) collective-permute-start(bf16[192,256]{1,0:T(8,128)(2,1)S(1)} %get-tuple-element.112), channel_id=1, source_target_pairs={{0,3},{1,2},{2,1},{3,0},{4,7},{5,6},{6,5},{7,4},{8,11},{9,10},{10,... | collective-permute-start | bytes 294920 | tf_op jit(solution)/shard_map/ppermute | solution.py:350
  73.5 13.0 %collective-permute-start.14 = (bf16[160,1280]{1,0:T(8,128)(2,1)S(1)}, bf16[160,1280]{1,0:T(8,128)(2,1)S(1)}, u32[]{:S(2)}, u32[]{:S(2)}) collective-permute-start(bf16[160,1280]{1,0:T(8,128)(2,1)S(1)} %collective-permute-done.13.refs_6_), channel_id=1, source_target_pairs={{0,1},{1,0},{2,3},{3,2},{4,5},{5,4},{6,7},{7,6},{8,9},{9,8},{10,11... | collective-permute-start | bytes 1228808 | tf_op jit(solution)/shard_map/ppermute | solution.py:350
  104.6 23.9 %collective-permute-start.35 = (bf16[48,1280]{1,0:T(8,128)(2,1)S(1)}, bf16[48,1280]{1,0:T(8,128)(2,1)S(1)}, u32[]{:S(2)}, u32[]{:S(2)}) collective-permute-start(bf16[48,1280]{1,0:T(8,128)(2,1)S(1)} %get-tuple-element.101), channel_id=1, source_target_pairs={{0,3},{1,2},{2,1},{3,0},{4,7},{5,6},{6,5},{7,4},{8,11},{9,10},{10,... | collective-permute-start | bytes 368648 | tf_op jit(solution)/shard_map/ppermute | solution.py:350
  106.0 22.5 %collective-permute-start.34 = (bf16[48,1280]{1,0:T(8,128)(2,1)S(1)}, bf16[48,1280]{1,0:T(8,128)(2,1)S(1)}, u32[]{:S(2)}, u32[]{:S(2)}) collective-permute-start(bf16[48,1280]{1,0:T(8,128)(2,1)S(1)} %get-tuple-element.102), channel_id=1, source_target_pairs={{0,2},{1,3},{2,0},{3,1},{4,6},{5,7},{6,4},{7,5},{8,10},{9,11},{10,... | collective-permute-start | bytes 368648 | tf_op jit(solution)/shard_map/ppermute | solution.py:350
  108.4 8.6 %collective-permute-start.36 = (bf16[192,256]{1,0:T(8,128)(2,1)S(1)}, bf16[192,256]{1,0:T(8,128)(2,1)S(1)}, u32[]{:S(2)}, u32[]{:S(2)}) collective-permute-start(bf16[192,256]{1,0:T(8,128)(2,1)S(1)} %get-tuple-element.61), channel_id=1, source_target_pairs={{0,1},{1,0},{2,3},{3,2},{4,5},{5,4},{6,7},{7,6},{8,9},{9,8},{10,11... | collective-permute-start | bytes 294920 | tf_op jit(solution)/shard_map/ppermute | solution.py:350
  108.4 8.9 %collective-permute-start.37 = (bf16[192,256]{1,0:T(8,128)(2,1)S(1)}, bf16[192,256]{1,0:T(8,128)(2,1)S(1)}, u32[]{:S(2)}, u32[]{:S(2)}) collective-permute-start(bf16[192,256]{1,0:T(8,128)(2,1)S(1)} %get-tuple-element.62), channel_id=1, source_target_pairs={{0,2},{1,3},{2,0},{3,1},{4,6},{5,7},{6,4},{7,5},{8,10},{9,11},{10,... | collective-permute-start | bytes 294920 | tf_op jit(solution)/shard_map/ppermute | solution.py:350
  109.8 8.8 %collective-permute-start.38 = (bf16[192,256]{1,0:T(8,128)(2,1)S(1)}, bf16[192,256]{1,0:T(8,128)(2,1)S(1)}, u32[]{:S(2)}, u32[]{:S(2)}) collective-permute-start(bf16[192,256]{1,0:T(8,128)(2,1)S(1)} %get-tuple-element.63), channel_id=1, source_target_pairs={{0,3},{1,2},{2,1},{3,0},{4,7},{5,6},{6,5},{7,4},{8,11},{9,10},{10,... | collective-permute-start | bytes 294920 | tf_op jit(solution)/shard_map/ppermute | solution.py:350
  117.1 11.9 %collective-permute-start.33 = (bf16[48,1280]{1,0:T(8,128)(2,1)S(1)}, bf16[48,1280]{1,0:T(8,128)(2,1)S(1)}, u32[]{:S(2)}, u32[]{:S(2)}) collective-permute-start(bf16[48,1280]{1,0:T(8,128)(2,1)S(1)} %get-tuple-element.103), channel_id=1, source_target_pairs={{0,1},{1,0},{2,3},{3,2},{4,5},{5,4},{6,7},{7,6},{8,9},{9,8},{10,11... | collective-permute-start | bytes 368648 | tf_op jit(solution)/shard_map/ppermute | solution.py:350
  117.4 14.1 %collective-permute-start.32 = (bf16[48,1280]{1,0:T(8,128)(2,1)}, bf16[48,1280]{1,0:T(8,128)(2,1)}, u32[]{:S(2)}, u32[]{:S(2)}) collective-permute-start(bf16[48,1280]{1,0:T(8,128)(2,1)} %get-tuple-element.105), channel_id=1, source_target_pairs={{0,3},{1,2},{2,1},{3,0},{4,7},{5,6},{6,5},{7,4},{8,11},{9,10},{10,... | collective-permute-start | bytes 368648 | tf_op jit(solution)/shard_map/ppermute | solution.py:350
  118.6 13.4 %collective-permute-start.31 = (bf16[48,1280]{1,0:T(8,128)(2,1)}, bf16[48,1280]{1,0:T(8,128)(2,1)}, u32[]{:S(2)}, u32[]{:S(2)}) collective-permute-start(bf16[48,1280]{1,0:T(8,128)(2,1)} %get-tuple-element.106), channel_id=1, source_target_pairs={{0,2},{1,3},{2,0},{3,1},{4,6},{5,7},{6,4},{7,5},{8,10},{9,11},{10,... | collective-permute-start | bytes 368648 | tf_op jit(solution)/shard_map/ppermute | solution.py:350
  128.5 87.4 %collective-permute-start.56 = (bf16[2,320,1280]{2,1,0:T(8,128)(2,1)}, bf16[2,320,1280]{2,1,0:T(8,128)(2,1)}, u32[]{:S(2)}, u32[]{:S(2)}) collective-permute-start(bf16[2,320,1280]{2,1,0:T(8,128)(2,1)} %get-tuple-element.81), channel_id=1, source_target_pairs={{0,1},{1,0},{2,3},{3,2},{4,5},{5,4},{6,7},{7,6},{8,9},{9,8},{10,11... | collective-permute-start | bytes 4915208 | tf_op jit(solution)/shard_map/ppermute | solution.py:350
  129.0 128.6 %collective-permute-start.68 = (bf16[2,960,640]{2,1,0:T(8,128)(2,1)}, bf16[2,960,640]{2,1,0:T(8,128)(2,1)}, u32[]{:S(2)}, u32[]{:S(2)}) collective-permute-start(bf16[2,960,640]{2,1,0:T(8,128)(2,1)} %get-tuple-element.83), channel_id=1, source_target_pairs={{0,1},{1,0},{2,3},{3,2},{4,5},{5,4},{6,7},{7,6},{8,9},{9,8},{10,11... | collective-permute-start | bytes 7372808 | tf_op jit(solution)/shard_map/ppermute | solution.py:350
  131.5 45.3 %collective-permute-start.39 = (bf16[2,192,1280]{2,1,0:T(8,128)(2,1)}, bf16[2,192,1280]{2,1,0:T(8,128)(2,1)}, u32[]{:S(2)}, u32[]{:S(2)}) collective-permute-start(bf16[2,192,1280]{2,1,0:T(8,128)(2,1)} %copy-done.11), channel_id=1, source_target_pairs={{0,1},{1,0},{2,3},{3,2},{4,5},{5,4},{6,7},{7,6},{8,9},{9,8},{10,11... | collective-permute-start | bytes 2949128 | tf_op jit(solution)/shard_map/ppermute | solution.py:350
  132.0 9.0 %collective-permute-start.41 = (bf16[2,24,1280]{2,1,0:T(8,128)(2,1)S(1)}, bf16[2,24,1280]{2,1,0:T(8,128)(2,1)}, u32[]{:S(2)}, u32[]{:S(2)}) collective-permute-start(bf16[2,24,1280]{2,1,0:T(8,128)(2,1)S(1)} %get-tuple-element.73), channel_id=1, source_target_pairs={{0,1},{1,0},{2,3},{3,2},{4,5},{5,4},{6,7},{7,6},{8,9},{9,8},{10,11... | collective-permute-start | bytes 368648 | tf_op jit(solution)/shard_map/ppermute | solution.py:350
  132.1 32.3 %collective-permute-start.43 = (bf16[2,2,4,40,512]{4,3,2,1,0:T(8,128)(2,1)}, bf16[2,2,4,40,512]{4,3,2,1,0:T(8,128)(2,1)}, u32[]{:S(2)}, u32[]{:S(2)}) collective-permute-start(bf16[2,2,4,40,512]{4,3,2,1,0:T(8,128)(2,1)} %bitcast.245), channel_id=1, source_target_pairs={{0,16},{4,20},{8,24},{12,28},{16,0},{20,4},{24,8},{28,12},{1,17},{... | collective-permute-start | bytes 1966088 | tf_op jit(solution)/shard_map/ppermute | solution.py:350
  142.0 24.6 %collective-permute-start.42 = (bf16[24,1280]{1,0:T(8,128)(2,1)S(1)}, bf16[24,1280]{1,0:T(8,128)(2,1)S(1)}, u32[]{:S(2)}, u32[]{:S(2)}) collective-permute-start(bf16[24,1280]{1,0:T(8,128)(2,1)S(1)} %slice_bitcast_fusion.18), channel_id=1, source_target_pairs={{0,2},{1,3},{2,0},{3,1},{4,6},{5,7},{6,4},{7,5},{8,10},{9,11},{10,... | collective-permute-start | bytes 184328 | tf_op jit(solution)/shard_map/ppermute | solution.py:350
  165.8 9.3 %collective-permute-start.44 = (bf16[1,2,4,40,512]{4,3,2,1,0:T(8,128)(2,1)S(1)}, bf16[1,2,4,40,512]{4,3,2,1,0:T(8,128)(2,1)S(1)}, u32[]{:S(2)}, u32[]{:S(2)}) collective-permute-start(bf16[1,2,4,40,512]{4,3,2,1,0:T(8,128)(2,1)S(1)} %constant_dynamic-slice_fusion.5), channel_id=1, source_target_pairs={{0,8},{4,12},{8,0},{12,4},{16,24},{20,28},{24,16},{28,20},{1,9},{5... | collective-permute-start | bytes 983048 | tf_op jit(solution)/shard_map/ppermute | solution.py:350
  184.6 23.7 %collective-permute-start.40 = (bf16[192,1280]{1,0:T(8,128)(2,1)}, bf16[192,1280]{1,0:T(8,128)(2,1)}, u32[]{:S(2)}, u32[]{:S(2)}) collective-permute-start(bf16[192,1280]{1,0:T(8,128)(2,1)} %get-tuple-element.98), channel_id=1, source_target_pairs={{0,2},{1,3},{2,0},{3,1},{4,6},{5,7},{6,4},{7,5},{8,10},{9,11},{10,... | collective-permute-start | bytes 1474568 | tf_op jit(solution)/shard_map/ppermute | solution.py:350
  199.1 7.1 %collective-permute-start.50 = (bf16[3,40,640]{2,1,0:T(8,128)(2,1)S(1)}, bf16[3,40,640]{2,1,0:T(8,128)(2,1)S(1)}, u32[]{:S(2)}, u32[]{:S(2)}) collective-permute-start(bf16[3,40,640]{2,1,0:T(8,128)(2,1)S(1)} %constant_dynamic-update-slice_fusion), channel_id=1, source_target_pairs={{0,8},{4,12},{8,0},{12,4},{16,24},{20,28},{24,16},{28,20},{1,9},{5... | collective-permute-start | bytes 460808 | tf_op jit(solution)/shard_map/ppermute | solution.py:350
  202.6 17.0 %collective-permute-start.52 = (bf16[3,40,640]{2,1,0:T(8,128)(2,1)S(1)}, bf16[3,40,640]{2,1,0:T(8,128)(2,1)S(1)}, u32[]{:S(2)}, u32[]{:S(2)}) collective-permute-start(bf16[3,40,640]{2,1,0:T(8,128)(2,1)S(1)} %constant_dynamic-update-slice_fusion), channel_id=1, source_target_pairs={{0,16},{4,20},{8,24},{12,28},{16,0},{20,4},{24,8},{28,12},{1,17},{... | collective-permute-start | bytes 460808 | tf_op jit(solution)/shard_map/ppermute | solution.py:350
  206.3 7.8 %collective-permute-start.51 = (bf16[3,40,640]{2,1,0:T(8,128)(2,1)S(1)}, bf16[3,40,640]{2,1,0:T(8,128)(2,1)S(1)}, u32[]{:S(2)}, u32[]{:S(2)}) collective-permute-start(bf16[3,40,640]{2,1,0:T(8,128)(2,1)S(1)} %collective-permute-done.49), channel_id=1, source_target_pairs={{0,8},{4,12},{8,0},{12,4},{16,24},{20,28},{24,16},{28,20},{1,9},{5... | collective-permute-start | bytes 460808 | tf_op jit(solution)/shard_map/ppermute | solution.py:350
  208.4 17.7 %collective-permute-start.53 = (bf16[3,40,640]{2,1,0:T(8,128)(2,1)S(1)}, bf16[3,40,640]{2,1,0:T(8,128)(2,1)S(1)}, u32[]{:S(2)}, u32[]{:S(2)}) collective-permute-start(bf16[3,40,640]{2,1,0:T(8,128)(2,1)S(1)} %collective-permute-done.49), channel_id=1, source_target_pairs={{0,16},{4,20},{8,24},{12,28},{16,0},{20,4},{24,8},{28,12},{1,17},{... | collective-permute-start | bytes 460808 | tf_op jit(solution)/shard_map/ppermute | solution.py:350
  214.1 15.3 %collective-permute-start.54 = (bf16[3,40,640]{2,1,0:T(8,128)(2,1)S(1)}, bf16[3,40,640]{2,1,0:T(8,128)(2,1)S(1)}, u32[]{:S(2)}, u32[]{:S(2)}) collective-permute-start(bf16[3,40,640]{2,1,0:T(8,128)(2,1)S(1)} %collective-permute-done.50), channel_id=1, source_target_pairs={{0,16},{4,20},{8,24},{12,28},{16,0},{20,4},{24,8},{28,12},{1,17},{... | collective-permute-start | bytes 460808 | tf_op jit(solution)/shard_map/ppermute | solution.py:350
  215.9 15.7 %collective-permute-start.55 = (bf16[3,40,640]{2,1,0:T(8,128)(2,1)S(1)}, bf16[3,40,640]{2,1,0:T(8,128)(2,1)S(1)}, u32[]{:S(2)}, u32[]{:S(2)}) collective-permute-start(bf16[3,40,640]{2,1,0:T(8,128)(2,1)S(1)} %collective-permute-done.51), channel_id=1, source_target_pairs={{0,16},{4,20},{8,24},{12,28},{16,0},{20,4},{24,8},{28,12},{1,17},{... | collective-permute-start | bytes 460808 | tf_op jit(solution)/shard_map/ppermute | solution.py:350
  219.6 17.0 %collective-permute-start.57 = (bf16[320,1280]{1,0:T(8,128)(2,1)S(1)}, bf16[320,1280]{1,0:T(8,128)(2,1)}, u32[]{:S(2)}, u32[]{:S(2)}) collective-permute-start(bf16[320,1280]{1,0:T(8,128)(2,1)S(1)} %slice_bitcast_fusion.7), channel_id=1, source_target_pairs={{0,2},{1,3},{2,0},{3,1},{4,6},{5,7},{6,4},{7,5},{8,10},{9,11},{10,... | collective-permute-start | bytes 2457608 | tf_op jit(solution)/shard_map/ppermute | solution.py:350
  238.2 19.2 %collective-permute-start.58 = (bf16[2,2,40,1280]{3,2,1,0:T(8,128)(2,1)S(1)}, bf16[2,2,40,1280]{3,2,1,0:T(8,128)(2,1)S(1)}, u32[]{:S(2)}, u32[]{:S(2)}) collective-permute-start(bf16[2,2,40,1280]{3,2,1,0:T(8,128)(2,1)S(1)} %dynamic-slice_bitcast_fusion.1), channel_id=1, source_target_pairs={{0,16},{4,20},{8,24},{12,28},{16,0},{20,4},{24,8},{28,12},{1,17},{... | collective-permute-start | bytes 1228808 | tf_op jit(solution)/shard_map/ppermute | solution.py:350
  257.5 5.8 %collective-permute-start.59 = (bf16[1,2,40,1280]{3,2,1,0:T(8,128)(2,1)S(1)}, bf16[1,2,40,1280]{3,2,1,0:T(8,128)(2,1)S(1)}, u32[]{:S(2)}, u32[]{:S(2)}) collective-permute-start(bf16[1,2,40,1280]{3,2,1,0:T(8,128)(2,1)S(1)} %constant_dynamic-slice_fusion.3), channel_id=1, source_target_pairs={{0,8},{4,12},{8,0},{12,4},{16,24},{20,28},{24,16},{28,20},{1,9},{5... | collective-permute-start | bytes 614408 | tf_op jit(solution)/shard_map/ppermute | solution.py:350
  263.4 5.6 %collective-permute-start.60 = (bf16[1,1,40,1280]{3,2,1,0:T(8,128)(2,1)S(1)}, bf16[1,1,40,1280]{3,2,1,0:T(8,128)(2,1)S(1)}, u32[]{:S(2)}, u32[]{:S(2)}) collective-permute-start(bf16[1,1,40,1280]{3,2,1,0:T(8,128)(2,1)S(1)} %constant_dynamic-slice_fusion.2), channel_id=1, source_target_pairs={{0,4},{4,0},{8,12},{12,8},{16,20},{20,16},{24,28},{28,24},{1,5},{5... | collective-permute-start | bytes 307208 | tf_op jit(solution)/shard_map/ppermute | solution.py:350
  265.0 26.2 %collective-permute-start.69 = (bf16[960,640]{1,0:T(8,128)(2,1)S(1)}, bf16[960,640]{1,0:T(8,128)(2,1)S(1)}, u32[]{:S(2)}, u32[]{:S(2)}) collective-permute-start(bf16[960,640]{1,0:T(8,128)(2,1)S(1)} %slice_bitcast_fusion), channel_id=1, source_target_pairs={{0,2},{1,3},{2,0},{3,1},{4,6},{5,7},{6,4},{7,5},{8,10},{9,11},{10,... | collective-permute-start | bytes 3686408 | tf_op jit(solution)/shard_map/ppermute | solution.py:350
  270.6 6.2 %collective-permute-start.62 = (bf16[40,1280]{1,0:T(8,128)(2,1)S(1)}, bf16[40,1280]{1,0:T(8,128)(2,1)S(1)}, u32[]{:S(2)}, u32[]{:S(2)}) collective-permute-start(bf16[40,1280]{1,0:T(8,128)(2,1)S(1)} %fusion.9), channel_id=1, source_target_pairs={{0,8},{4,12},{8,0},{12,4},{16,24},{20,28},{24,16},{28,20},{1,9},{5... | collective-permute-start | bytes 307208 | tf_op jit(solution)/shard_map/ppermute | solution.py:350
  270.6 11.0 %collective-permute-start.64 = (bf16[40,1280]{1,0:T(8,128)(2,1)S(1)}, bf16[40,1280]{1,0:T(8,128)(2,1)S(1)}, u32[]{:S(2)}, u32[]{:S(2)}) collective-permute-start(bf16[40,1280]{1,0:T(8,128)(2,1)S(1)} %fusion.9), channel_id=1, source_target_pairs={{0,16},{4,20},{8,24},{12,28},{16,0},{20,4},{24,8},{28,12},{1,17},{... | collective-permute-start | bytes 307208 | tf_op jit(solution)/shard_map/ppermute | solution.py:350
  273.8 12.6 %collective-permute-start.65 = (bf16[40,1280]{1,0:T(8,128)(2,1)S(1)}, bf16[40,1280]{1,0:T(8,128)(2,1)S(1)}, u32[]{:S(2)}, u32[]{:S(2)}) collective-permute-start(bf16[40,1280]{1,0:T(8,128)(2,1)S(1)} %collective-permute-done.61), channel_id=1, source_target_pairs={{0,16},{4,20},{8,24},{12,28},{16,0},{20,4},{24,8},{28,12},{1,17},{... | collective-permute-start | bytes 307208 | tf_op jit(solution)/shard_map/ppermute | solution.py:350
  276.8 18.9 %collective-permute-start.66 = (bf16[40,1280]{1,0:T(8,128)(2,1)S(1)}, bf16[40,1280]{1,0:T(8,128)(2,1)S(1)}, u32[]{:S(2)}, u32[]{:S(2)}) collective-permute-start(bf16[40,1280]{1,0:T(8,128)(2,1)S(1)} %collective-permute-done.62), channel_id=1, source_target_pairs={{0,16},{4,20},{8,24},{12,28},{16,0},{20,4},{24,8},{28,12},{1,17},{... | collective-permute-start | bytes 307208 | tf_op jit(solution)/shard_map/ppermute | solution.py:350
  278.4 17.3 %collective-permute-start.67 = (bf16[40,1280]{1,0:T(8,128)(2,1)S(1)}, bf16[40,1280]{1,0:T(8,128)(2,1)S(1)}, u32[]{:S(2)}, u32[]{:S(2)}) collective-permute-start(bf16[40,1280]{1,0:T(8,128)(2,1)S(1)} %collective-permute-done.63), channel_id=1, source_target_pairs={{0,16},{4,20},{8,24},{12,28},{16,0},{20,4},{24,8},{28,12},{1,17},{... | collective-permute-start | bytes 307208 | tf_op jit(solution)/shard_map/ppermute | solution.py:350
  292.4 28.9 %collective-permute-start.70 = (bf16[2,2,120,640]{3,2,1,0:T(8,128)(2,1)}, bf16[2,2,120,640]{3,2,1,0:T(8,128)(2,1)S(1)}, u32[]{:S(2)}, u32[]{:S(2)}) collective-permute-start(bf16[2,2,120,640]{3,2,1,0:T(8,128)(2,1)} %dynamic-slice_bitcast_fusion), channel_id=1, source_target_pairs={{0,16},{4,20},{8,24},{12,28},{16,0},{20,4},{24,8},{28,12},{1,17},{... | collective-permute-start | bytes 1843208 | tf_op jit(solution)/shard_map/ppermute | solution.py:350
  321.6 8.6 %collective-permute-start.71 = (bf16[1,2,120,640]{3,2,1,0:T(8,128)(2,1)S(1)}, bf16[1,2,120,640]{3,2,1,0:T(8,128)(2,1)S(1)}, u32[]{:S(2)}, u32[]{:S(2)}) collective-permute-start(bf16[1,2,120,640]{3,2,1,0:T(8,128)(2,1)S(1)} %constant_dynamic-slice_fusion.1), channel_id=1, source_target_pairs={{0,8},{4,12},{8,0},{12,4},{16,24},{20,28},{24,16},{28,20},{1,9},{5... | collective-permute-start | bytes 921608 | tf_op jit(solution)/shard_map/ppermute | solution.py:350
  336.3 9.8 %collective-permute-start.74 = (bf16[120,640]{1,0:T(8,128)(2,1)S(1)}, bf16[120,640]{1,0:T(8,128)(2,1)S(1)}, u32[]{:S(2)}, u32[]{:S(2)}) collective-permute-start(bf16[120,640]{1,0:T(8,128)(2,1)S(1)} %fusion.8), channel_id=1, source_target_pairs={{0,8},{4,12},{8,0},{12,4},{16,24},{20,28},{24,16},{28,20},{1,9},{5... | collective-permute-start | bytes 460808 | tf_op jit(solution)/shard_map/ppermute | solution.py:350
  336.9 14.8 %collective-permute-start.76 = (bf16[120,640]{1,0:T(8,128)(2,1)S(1)}, bf16[120,640]{1,0:T(8,128)(2,1)S(1)}, u32[]{:S(2)}, u32[]{:S(2)}) collective-permute-start(bf16[120,640]{1,0:T(8,128)(2,1)S(1)} %fusion.8), channel_id=1, source_target_pairs={{0,16},{4,20},{8,24},{12,28},{16,0},{20,4},{24,8},{28,12},{1,17},{... | collective-permute-start | bytes 460808 | tf_op jit(solution)/shard_map/ppermute | solution.py:350
  340.9 7.1 %collective-permute-start.75 = (bf16[120,640]{1,0:T(8,128)(2,1)S(1)}, bf16[120,640]{1,0:T(8,128)(2,1)S(1)}, u32[]{:S(2)}, u32[]{:S(2)}) collective-permute-start(bf16[120,640]{1,0:T(8,128)(2,1)S(1)} %collective-permute-done.73), channel_id=1, source_target_pairs={{0,8},{4,12},{8,0},{12,4},{16,24},{20,28},{24,16},{28,20},{1,9},{5... | collective-permute-start | bytes 460808 | tf_op jit(solution)/shard_map/ppermute | solution.py:350
  341.6 18.3 %collective-permute-start.77 = (bf16[120,640]{1,0:T(8,128)(2,1)S(1)}, bf16[120,640]{1,0:T(8,128)(2,1)S(1)}, u32[]{:S(2)}, u32[]{:S(2)}) collective-permute-start(bf16[120,640]{1,0:T(8,128)(2,1)S(1)} %collective-permute-done.73), channel_id=1, source_target_pairs={{0,16},{4,20},{8,24},{12,28},{16,0},{20,4},{24,8},{28,12},{1,17},{... | collective-permute-start | bytes 460808 | tf_op jit(solution)/shard_map/ppermute | solution.py:350
  346.1 17.1 %collective-permute-start.78 = (bf16[120,640]{1,0:T(8,128)(2,1)S(1)}, bf16[120,640]{1,0:T(8,128)(2,1)S(1)}, u32[]{:S(2)}, u32[]{:S(2)}) collective-permute-start(bf16[120,640]{1,0:T(8,128)(2,1)S(1)} %collective-permute-done.74), channel_id=1, source_target_pairs={{0,16},{4,20},{8,24},{12,28},{16,0},{20,4},{24,8},{28,12},{1,17},{... | collective-permute-start | bytes 460808 | tf_op jit(solution)/shard_map/ppermute | solution.py:350
  348.0 16.8 %collective-permute-start.79 = (bf16[120,640]{1,0:T(8,128)(2,1)S(1)}, bf16[120,640]{1,0:T(8,128)(2,1)S(1)}, u32[]{:S(2)}, u32[]{:S(2)}) collective-permute-start(bf16[120,640]{1,0:T(8,128)(2,1)S(1)} %collective-permute-done.75), channel_id=1, source_target_pairs={{0,16},{4,20},{8,24},{12,28},{16,0},{20,4},{24,8},{28,12},{1,17},{... | collective-permute-start | bytes 460808 | tf_op jit(solution)/shard_map/ppermute | solution.py:350
  (49 other events, 353.4 us)

commit v2 on v1

--- a/solution.py
+++ b/solution.py
@@ -10,6 +10,8 @@
 from jax.sharding import PartitionSpec as P
 
 HEADS = 4
+F32 = jnp.float32
+BF16 = jnp.bfloat16
 
 
 EPSILON = 1e-05
@@ -35,6 +37,13 @@
     rates = jnp.exp(halves * (-2.0 * math.log(10000.0) / width))
     angles = frame_ids[:, None] * rates[None, :]
     return jnp.stack([jnp.sin(angles), jnp.cos(angles)], -1).reshape(count, width)
+
+
+def position_rows(frame_ids, width):
+    lane = jnp.arange(width, dtype=jnp.int32)
+    rates = jnp.exp((lane // 2).astype(F32) * (-2.0 * math.log(10000.0) / width))
+    angles = frame_ids.astype(F32)[:, None] * rates[None, :]
+    return jnp.where(lane % 2 == 0, jnp.sin(angles), jnp.cos(angles))
 
 
 def einsum_forms(temporal):
@@ -310,8 +319,6 @@
     )
 
 
-F32 = jnp.float32
-BF16 = jnp.bfloat16
 CHUNK = 32
 
 
@@ -327,14 +334,18 @@
     return lax.dot_general(left, right, (((0,), (0,)), ((), ())), preferred_element_type=F32)
 
 
-def wide_call(body, name, out_shape, scratch, limit_mb, flops, num_in):
+def wide_call(body, name, out_shape, scratch, limit_mb, flops, num_in, kept=0, out_kept=()):
     return pl.pallas_call(
         body,
         name=name,
         out_shape=out_shape,
         in_specs=[pl.BlockSpec(memory_space=pltpu.SMEM)]
-        + [pl.BlockSpec(memory_space=pltpu.VMEM)] * (num_in - 1),
-        out_specs=tuple(pl.BlockSpec(memory_space=pltpu.VMEM) for _ in out_shape),
+        + [pl.BlockSpec(memory_space=pltpu.HBM)] * kept
+        + [pl.BlockSpec(memory_space=pltpu.VMEM)] * (num_in - 1 - kept),
+        out_specs=tuple(
+            pl.BlockSpec(memory_space=pltpu.HBM if i in out_kept else pltpu.VMEM)
+            for i in range(len(out_shape))
+        ),
         scratch_shapes=scratch,
         compiler_params=pltpu.CompilerParams(vmem_limit_bytes=limit_mb * 1024 * 1024),
         cost_estimate=pl.CostEstimate(flops=flops, bytes_accessed=8_000_000, transcendentals=0),
@@ -354,27 +365,90 @@
     return lax.optimization_barrier((value,) + others)[0]
 
 
-def pack_body(heads, idx, wq, wk, wv, *outs):
-    width = wq.shape[1] // heads
-    room = outs[0].shape[1]
+def load(sources, held, sems):
+    copies = [pltpu.make_async_copy(w, h, sems.at[i]) for i, (w, h) in enumerate(zip(sources, held))]
+    for copy in copies:
+        copy.start()
+    return copies
+
+
+def pack_body(heads, idx, *refs):
+    sources, near, (far, quarter), packs = refs[:8], refs[8:10], refs[10:12], refs[12]
+    held, sems = refs[13:21], refs[21]
+    me, side, mine = idx[0], idx[1] & 1, idx[1] & 3
+    half = far.shape[1]
+    depth, inner = held[0].shape
+    low = held[6].shape[0]
+    width = inner // heads
+    part = depth // 4
+    copies = load(sources, held, sems)
+    for copy in copies[:3]:
+        copy.wait()
     for h in range(heads):
-        parts = [w[:, h * width : (h + 1) * width] for w in (wq, wk, wv)]
-        parts.append(jnp.zeros((wq.shape[0], room - 3 * width), BF16))
-        outs[h][...] = jnp.concatenate(parts, 1)
+        parts = [held[i][:, h * width : (h + 1) * width] for i in range(3)]
+        parts.append(jnp.zeros((depth, packs.shape[2] - 3 * width), BF16))
+        packs[h] = jnp.concatenate(parts, 1)
+    for r in range(2):
+        near[r][...] = packs[me ^ r]
+        far[r] = packs[me ^ (r + 2), pl.ds(pl.multiple_of(side * half, half), half), :]
+    for copy in copies[3:]:
+        copy.wait()
+    at = pl.ds(pl.multiple_of(mine * part, part), part)
+    for i in range(3):
+        quarter[i * part : (i + 1) * part, :] = held[3 + i][at, :]
+    for v in range(4):
+
+        @pl.when(mine == v)
+        def _(v=v):
+            quarter[3 * part :, :] = held[6 + (v >> 1)][:, (v & 1) * inner : (v & 1) * inner + inner]
+
+
+def block_body(n, per, idx, *refs):
+    sources, block, near, across = refs[:6], refs[6], refs[7:9], refs[9]
+    held, (wide, few, sems) = refs[10:16], refs[16:]
+    me = idx[0]
+    depth, inner = held[1].shape
+    low = held[4].shape[0]
+    copies = load(sources, held, sems)
+    copies[0].wait()
+    wide[...] = held[0][...].astype(F32)
+    share = few.shape[0] // per
+    tokens = wide.shape[0] // per
+    for r in range(n):
+        first = pl.multiple_of((me ^ r) * share, share)
+        for j in range(per):
+            few[j * share : (j + 1) * share, :] = wide[pl.ds(j * tokens + first, share), :]
+        if r < 2:
+            near[r][...] = few[...].astype(BF16)
+        else:
+            across[r - 2] = few[...].astype(BF16)
+    for copy in copies[1:]:
+        copy.wait()
+    for i in range(3):
+        block[i * depth : (i + 1) * depth, :] = held[1 + i][...]
+    for v in range(4):
+        at = 3 * depth + v * low
+        block[at : at + low, :] = held[4 + (v >> 1)][:, (v & 1) * inner : (v & 1) * inner + inner]
 
 
 def spatial_forward_body(n, tokens, width, idx, *refs):
-    frames, weights, refer = refs[:n], refs[n : 2 * n], refs[2 * n]
-    x_out, w_out, q_out, k_out, v_out, p_out, o_out = refs[2 * n + 1 : 2 * n + 8]
-    mixed, turn = refs[2 * n + 8 :]
-    me = idx[0]
+    frames, refer, refs = refs[:n], refs[n : 2 * n], refs[2 * n :]
+    near, far = refs[:2], ((refs[2], refs[3]), (refs[4], refs[5]))
+    x_out, w_out, q_out, k_out, v_out, p_out, o_out = refs[6:13]
+    mixed, turn, few = refs[13:]
+    me, side = idx[0], idx[1] & 1
+    share = tokens // n
     rows = frames[0].shape[0]
-    depth = weights[0].shape[0]
+    depth = near[0].shape[0]
+    half = depth // 2
     lanes = q_out.shape[1]
     room = w_out.shape[1]
     total = n * rows
-    for r in range(n):
-        w_out[pl.ds(pl.multiple_of((me ^ r) * depth, depth), depth), :] = weights[r][...]
+    for r in range(2):
+        w_out[pl.ds(pl.multiple_of((me ^ r) * depth, depth), depth), :] = near[r][...]
+        for k in range(2):
+            at = pl.multiple_of((me ^ (r + 2)) * depth + (side ^ k) * half, half)
+            w_out[pl.ds(at, half), :] = far[r][k][r]
     for r in range(n):
 
         def norm(i, _, r=r):
@@ -384,8 +458,9 @@
             return 0
 
         lax.fori_loop(0, rows // CHUNK, norm, 0)
-    x_out[total:, :] = refer[...]
-    for start, count in [(r * rows, rows) for r in range(n)] + [(total, refer.shape[0])]:
+        few[r * share : (r + 1) * share, :] = refer[r][...].astype(F32)
+    x_out[total:, :] = few[...].astype(BF16)
+    for start, count in [(r * rows, rows) for r in range(n)] + [(total, tokens)]:
         three = mm(x_out[start : start + count, :], w_out[...])
         keep = lax.broadcasted_iota(jnp.int32, (count, lanes), 1) < width
         q_out[start : start + count, :] = jnp.where(keep, three[:, :lanes], 0.0).astype(BF16)
@@ -404,7 +479,6 @@
         probs = powers / jnp.sum(powers, -1, keepdims=True)
         p_out[at, :] = probs
         mixed[at, :] = mm(probs.astype(BF16), values)
-    share = tokens // n
     per = rows // tokens
     for r in range(n):
         first = pl.multiple_of((me ^ r) * share, share)
@@ -417,8 +491,8 @@
 def spatial_backward_body(n, tokens, width, idx, *refs):
     grads = refs[:n]
     x_ref, w_ref, q_ref, k_ref, v_ref, p_ref = refs[n : n + 6]
-    keep_out, send_out, keep_ref, send_ref, term_out = refs[n + 6 : n + 11]
-    spread, turn, packed = refs[n + 11 :]
+    keep_out, send_out, keep_term, send_term = refs[n + 6 : n + 10]
+    spread, turn, packed, term = refs[n + 10 :]
     me = idx[0]
     share = tokens // n
     total = p_ref.shape[0]
@@ -462,35 +536,72 @@
     packed[total:, :] = pack(None, key_sum, value_sum).astype(BF16)
     for r in range(n):
         part = mm_bt(packed[r * rows : (r + 1) * rows, :], w_ref[...]).astype(BF16)
-        (send_out if r & 1 else keep_out)[r >> 1] = part
+        (send_out if r & 1 else keep_out)[r >> 1, :rows, :] = part
     part = mm_bt(packed[total:, :], w_ref[...])
     for r in range(n):
-        (send_ref if r & 1 else keep_ref)[r >> 1] = part[r * share : (r + 1) * share].astype(BF16)
+        few = part[r * share : (r + 1) * share].astype(BF16)
+        (send_out if r & 1 else keep_out)[r >> 1, rows:, :] = few
     depth = x_ref.shape[1] // 5
     for j in range(5):
         at = slice(j * depth, (j + 1) * depth)
-        term_out[at, :] = mm_at(x_ref[:, at], packed[...]).astype(BF16)
-
-
-def temporal_body(n, heads, idx, *refs):
-    mixed, so_parts, tq_parts, tk_parts, tv_parts, to_parts = (
-        refs[i * n : (i + 1) * n] for i in range(6)
-    )
-    frames, cotangent, table, same = refs[6 * n : 6 * n + 4]
-    grad_outs = refs[6 * n + 4 : 7 * n + 4]
-    gh_out, n2_out, gq_out, gk_out, gv_out, o2_out, out_out = refs[7 * n + 4 : 7 * n + 11]
-    so, tq, tk, tv, to, hidden, centred, inverse, wide, qs, gos = refs[7 * n + 11 :]
-    me = idx[0]
+        term[at, :] = mm_at(x_ref[:, at], packed[...])
+    side = idx[1] & 1
+    count, piece = keep_term.shape[0], keep_term.shape[2]
+    for j in range(n):
+        for k in range(count):
+            for out, half in ((keep_term, side), (send_term, 1 - side)):
+                at = pl.multiple_of((j * 2 * count + half * count + k) * piece, piece)
+                out[k, j] = term[pl.ds(at, piece), :].astype(BF16)
+
+
+def temporal_body(n, heads, per, idx, *refs):
+    mixed, refs = refs[:n], refs[n:]
+    near, far, refs = refs[:2], (refs[2:6], refs[6:10]), refs[10:]
+    frames, table = refs[0], refs[n + 1]
+    cotangents = refs[1 : n + 1]
+    refs = refs[n + 2 :]
+    grad_outs, back_outs, refs = refs[:n], refs[n : 2 * n], refs[2 * n :]
+    gh_out, n2_out, gq_out, gk_out, gv_out, o2_out, cotangent = refs[:7]
+    so, tq, tk, tv, to, hidden, centred, inverse, wide, qs, gos = refs[7:]
+    me, quarter = idx[0], idx[1] & 3
     rows, dim = frames.shape
     inner = tq.shape[1]
     width = inner // heads
+    depth, low = dim // n, inner // n
+    part = depth // 4
+    few = rows // n
+    share = few // per
     for r in range(n):
-        for parts, whole in ((tq_parts, tq), (tk_parts, tk), (tv_parts, tv), (to_parts, to)):
-            depth = parts[r].shape[0]
-            whole[pl.ds(pl.multiple_of((me ^ r) * depth, depth), depth), :] = parts[r][...]
-        depth = so_parts[r].shape[0]
-        so[r, :depth, :] = so_parts[r][...]
-        so[r, depth:, :] = jnp.zeros((so.shape[1] - depth, dim), BF16)
+        cotangent[r * few : (r + 1) * few, :] = cotangents[r][...] if r < 2 else cotangents[r][r - 2]
+        base = (me ^ r) * depth
+        low_at = pl.ds(pl.multiple_of((me ^ r) * low, low), low)
+
+        def put(v, source, r=r, low_at=low_at):
+            lanes = slice((v & 1) * inner, (v & 1) * inner + inner)
+            if v < 2:
+                so[r, :low, lanes] = source
+            else:
+                to[low_at, lanes] = source
+
+        if r < 2:
+            for i, whole in enumerate((tq, tk, tv)):
+                whole[pl.ds(pl.multiple_of(base, depth), depth), :] = near[r][i * depth : (i + 1) * depth, :]
+            for v in range(4):
+                at = 3 * depth + v * low
+                put(v, near[r][at : at + low, :])
+        else:
+            for s in range(4):
+                source = far[r - 2][s]
+                at = pl.ds(pl.multiple_of(base + (quarter ^ s) * part, part), part)
+                for i, whole in enumerate((tq, tk, tv)):
+                    whole[at, :] = source[i * part : (i + 1) * part, :]
+                for v in range(4):
+
+                    @pl.when((quarter ^ s) == v)
+                    def _(v=v, source=source, put=put):
+                        put(v, source[3 * part :, :])
+
+        so[r, low:, :] = jnp.zeros((so.shape[1] - low, dim), BF16)
     step = dim // 5
     for j in range(5):
         at = slice(j * step, (j + 1) * step)
@@ -500,14 +611,21 @@
         hidden[:, at] = acc.astype(BF16).astype(F32)
 
     def norm(i, _):
-        at = pl.ds(pl.multiple_of(i * CHUNK, CHUNK), CHUNK)
+        at = pl.ds(pl.multiple_of(i * share, share), share)
         offset, scale = layer_stats(hidden[at, :])
         centred[at, :] = offset
-        inverse[at, :] = jnp.broadcast_to(scale, (CHUNK, inverse.shape[1]))
-        n2_out[at, :] = (offset + table[at, :]).astype(BF16)
+        inverse[at, :] = jnp.broadcast_to(scale, (share, inverse.shape[1]))
+        wide[at, :] = offset + table[pl.ds(i, 1), :]
         return 0
 
-    lax.fori_loop(0, rows // CHUNK, norm, 0)
+    lax.fori_loop(0, rows // share, norm, 0)
+    n2_out[...] = wide[...].astype(BF16)
+
+    def token(axis):
+        place = lax.broadcasted_iota(jnp.int32, (rows, rows), axis).astype(F32)
+        return place - share * jnp.floor((place + 0.5) * (1.0 / share))
+
+    same = token(0) == token(1)
     lane_head = lax.broadcasted_iota(jnp.int32, (rows, inner), 1)
 
     def own(h, value):
@@ -530,7 +648,7 @@
     for h in range(heads):
         at = slice(h * rows, (h + 1) * rows)
         scores = mm_bt(qs[at, :], keys) * scale
-        powers = jnp.where(same[...] > 0.5, jnp.exp(scores), 0.0)
+        powers = jnp.where(same, jnp.exp(scores), 0.0)
         probs = powers / jnp.sum(powers, -1, keepdims=True)
         rounded = probs.astype(BF16)
         o2 = o2 + own(h, mm(rounded, values))
@@ -560,73 +678,132 @@
         grad_outs[r][...] = mm_bt(gh_out[...], so[r]).astype(BF16)
     for j in range(5):
         at = slice(j * step, (j + 1) * step)
-        out_out[:, at] = (hidden[:, at] + mm(o2_out[...], to[:, at])).astype(BF16)
+        part = (hidden[:, at] + mm(o2_out[...], to[:, at])).astype(BF16)
+        for r in range(n):
+            back_outs[r][:few, at] = part[r * few : (r + 1) * few]
+    for r in range(n):
+        back_outs[r][few:, :] = gh_out[r * few : (r + 1) * few, :]
 
 
 def terms_body(n, idx, *refs):
     mixed = refs[:n]
     gh, n2, gq, gk, gv, o2, cotangent = refs[n : n + 7]
-    keep_a, send_a, keep_b, send_b = refs[n + 7 : n + 11]
+    talls, flats = refs[n + 7 : n + 9], refs[n + 9 : n + 11]
     tall, flat = refs[n + 11 :]
     me = idx[0]
     dim, inner = tall.shape
     depth, low = dim // n, inner // n
-
+    pieces, piece = talls[0].shape[1], talls[0].shape[3]
     for i, grad in enumerate((gq, gk, gv)):
         for j in range(5):
             at = slice(j * (dim // 5), (j + 1) * (dim // 5))
-            tall[at, :] = mm_at(n2[:, at], grad[...]).astype(BF16)
+            tall[at, :] = mm_at(n2[:, at], grad[...])
         for r in range(n):
-            to = send_a if r & 1 else keep_a
-            to[r >> 1, i * depth : (i + 1) * depth, :] = tall[
-                pl.ds(pl.multiple_of((me ^ r) * depth, depth), depth), :
-            ]
+            for p in range(pieces):
+                at = pl.multiple_of((me ^ r) * depth + p * piece, piece)
+                talls[r & 1][r >> 1, p, i] = tall[pl.ds(at, piece), :].astype(BF16)
     for j in range(5):
         at = slice(j * (inner // 5), (j + 1) * (inner // 5))
         flat[at, :] = mm_at(o2[:, at], cotangent[...]).astype(BF16)
+    half = low // 2
     for r in range(n):
-        to = send_b if r & 1 else keep_b
-        to[r >> 1, :low, :] = flat[pl.ds(pl.multiple_of((me ^ r) * low, low), low), :]
-        to[r >> 1, low:, :] = mm_at(mixed[r][...], gh[...])[:low].astype(BF16)
-
-
-def finish_body(idx, frames, hidden_grad, first, second, out):
+        out = flats[r & 1]
+        mine = mm_at(mixed[r][...], gh[...])[:low].astype(BF16)
+        for j in range(2):
+            lanes = slice(j * inner, (j + 1) * inner)
+            for k in range(2):
+                at = pl.multiple_of((me ^ r) * low + k * half, half)
+                out[r >> 1, 2 * j + k] = mine[k * half : (k + 1) * half, lanes]
+                out[r >> 1, 4 + 2 * j + k] = flat[pl.ds(at, half), lanes]
+
+
+def finish_body(n, per, idx, frames, *refs):
+    parts, near, far = refs[:n], refs[n], refs[n + 1]
+    out, frames_grad, refer_grad, turn, wide = refs[n + 2 :]
+    me = idx[0]
+    rows, few = frames.shape[0], parts[0].shape[0] // 2
+    share, tokens = few // per, rows // per
+    for r in range(n):
+        first = pl.multiple_of((me ^ r) * share, share)
+        turn[...] = parts[r][...].astype(F32)
+        for which in range(2):
+            for j in range(per):
+                at = which * few + j * share
+                wide[which, pl.ds(j * tokens + first, share), :] = turn[at : at + share, :]
+    out[...] = wide[0].astype(BF16)
+
     def step(i, _):
         at = pl.ds(pl.multiple_of(i * CHUNK, CHUNK), CHUNK)
         centred, inverse = layer_stats(frames[at, :])
-        grad = first[at, :].astype(F32) + second[at, :].astype(F32)
+        grad = near[at, :].astype(F32) + far[at, :].astype(F32)
         back = layer_back(centred, inverse, grad)
-        out[at, :] = (hidden_grad[at, :].astype(F32) + back).astype(BF16)
+        frames_grad[at, :] = (wide[1, at, :] + back).astype(BF16)
         return 0
 
-    lax.fori_loop(0, frames.shape[0] // CHUNK, step, 0)
-
-
-def add(left, right):
-    return (left.astype(F32) + right.astype(F32)).astype(BF16)
+    lax.fori_loop(0, rows // CHUNK, step, 0)
+    refer_grad[...] = (near[rows:, :].astype(F32) + far[rows:, :].astype(F32)).astype(BF16)
+
+
+def place_body(idx, near, far, *outs):
+    side, level = idx[1] & 1, idx[1] >> 1
+    count, _, piece = near.shape[:3]
+    for source, half in ((near, side), (far, 1 - side)):
+        for k in range(count):
+            at = pl.multiple_of((half * count + (level ^ k)) * piece, piece)
+            for i, out in enumerate(outs):
+                out[pl.ds(at, piece), :] = source[k, i].astype(F32)
+
+
+def place_flat_body(idx, near, far, *outs):
+    side, level = idx[1] & 1, idx[1] >> 1
+    count, piece, inner = near.shape
+    for source, half in ((near, side), (far, 1 - side)):
+        for k in range(count):
+            place = level ^ k
+            at = pl.multiple_of((place & 1) * piece, piece)
+            for i, out in enumerate(outs):
+                for j in range(2):
+
+                    @pl.when((half == i) & ((place >> 1) == j))
+                    def _(source=source, k=k, at=at, out=out, j=j):
+                        out[pl.ds(at, piece), j * inner : (j + 1) * inner] = source[k].astype(F32)
+
+
+def place_heads_body(width, idx, near, far, *outs):
+    me, side, level = idx[0], idx[1] & 1, idx[1] >> 1
+    count, n, piece = near.shape[:3]
+    for source, half in ((near, side), (far, 1 - side)):
+        for k in range(count):
+            at = pl.multiple_of((half * count + (level ^ k)) * piece, piece)
+            heads = [source[k, me ^ h].astype(F32) for h in range(n)]
+            for i, out in enumerate(outs):
+                parts = [h[:, i * width : (i + 1) * width] for h in heads]
+                out[pl.ds(at, piece), :] = jnp.concatenate(parts, 1)
+
+
+def add(*parts):
+    total = parts[0].astype(F32)
+    for part in parts[1:]:
+        total = total + part.astype(F32)
+    return total.astype(BF16)
 
 
 def pick(value, index, axis=0):
     return lax.dynamic_index_in_dim(value, index, axis, keepdims=False)
 
 
-def clip_scatter(value, clip, bits):
-    for place in reversed(range(bits)):
-        axis = bits - 1 - place
-        bit = (clip >> place) & 1
-        moved = flip(pick(value, 1 - bit, axis), "clip", 1 << place)
-        value = add(pick(value, bit, axis), moved)
-        value = jnp.expand_dims(value, axis)
-    return value.reshape(value.shape[bits:])
-
-
-def clip_gather(value, clip, bits):
-    pieces = [value]
-    for place in range(bits):
-        pieces = pieces + [flip(p, "clip", 1 << place) for p in pieces]
-    stack = jnp.stack(pieces)
-    order = jnp.arange(1 << bits) ^ clip
-    return stack, order
+class Links:
+    def __init__(self, window):
+        self.window = window
+        self.past = {}
+
+    def send(self, link, value, axis, bit):
+        past = self.past.setdefault(link, [])
+        if len(past) >= self.window:
+            value = after(value, past[-self.window])
+        got = flip(value, axis, bit)
+        past.append(got)
+        return got
 
 
 def per_device(
@@ -644,60 +821,87 @@
 ):
     n = lax.axis_size("frame")
     clips = lax.axis_size("clip")
-    bits = clips.bit_length() - 1
     me = lax.axis_index("frame")
     clip = lax.axis_index("clip")
+    side, level = clip & 1, clip >> 1
     idx = jnp.stack([me, clip]).astype(jnp.int32)
     _, per, tokens, dim = frames_in.shape
     inner = space_query.shape[1]
     width = inner // HEADS
     lanes = -(-width // 128) * 128
     room = -(-3 * width // 128) * 128
-    depth = dim // n
+    depth, low = dim // n, inner // n
     rows = per * tokens
     total = n * rows
     share = tokens // n
+    few = per * share
+    token_rows = n * few
+    count, piece = clips // 2, depth // clips
     frames = frames_in.reshape(rows, dim)
-    refer = ref_feats[0]
-    cotangent = out_grad[0]
-
-    def gather(value):
-        one, two = flip(value, "frame", 1), flip(value, "frame", 2)
-        return [value, one, two, flip(two, "frame", 1)]
-
-    def relative(parts):
-        return [pick(parts, me ^ r) for r in range(n)]
+    links = Links(2)
 
     def exchange(parts):
         return [parts[0]] + [flip(parts[r], "frame", r) for r in range(1, n)]
 
-    packs = wide_call(
-        functools.partial(pack_body, HEADS), "pack_heads", [struct(depth, room)] * HEADS, [], 24, 0, 4
-    )(idx, space_query, space_key, space_value)
-    packs = exchange(relative(jnp.stack(packs)))
-    all_frames = gather(frames)
-    all_refer = jnp.concatenate(gather(refer), 0)
-    token_parts = cotangent.reshape(per, n, share, dim)
-    token_grad = jnp.concatenate(
-        [p.reshape(per * share, dim) for p in exchange([pick(token_parts, me ^ r, 1) for r in range(n)])], 0
-    )
-    held = after((space_output, time_query, time_key, time_value, time_output), all_frames[2], packs[2])
-    so_parts, tq_parts, tk_parts, tv_parts, to_parts = [gather(w) for w in held]
+    def gather(value):
+        far = flip(value, "frame", 2)
+        return [value, flip(value, "frame", 1), far, flip(far, "frame", 1)]
+
+    own, near, far_pack, quarter = wide_call(
+        functools.partial(pack_body, HEADS),
+        "pack_heads",
+        [
+            struct(depth, room),
+            struct(depth, room),
+            struct(2, depth // 2, room),
+            struct(3 * depth // 4 + low, inner),
+        ],
+        [pltpu.VMEM((HEADS, depth, room), BF16)]
+        + [pltpu.VMEM((depth, inner), BF16)] * 6
+        + [pltpu.VMEM((low, dim), BF16)] * 2
+        + [pltpu.SemaphoreType.DMA((8,))],
+        60,
+        0,
+        9,
+        8,
+    )(idx, space_query, space_key, space_value, time_query, time_key, time_value, space_output, time_output)
+    far_pack = flip(far_pack, "frame", 2)
+    first = flip(quarter, "frame", 2)
+    far_frames = flip(after(frames, far_pack), "frame", 2)
+    all_refer = gather(ref_feats[0])
+    side_pack = flip(far_pack, "clip", 1)
+    packs = [own, flip(near, "frame", 1), far_pack, side_pack]
+    packs = packs + [flip(p, "frame", 1) for p in packs[2:]]
+    second, third = flip(first, "clip", 1), flip(first, "clip", 2)
+    far = [first, second, third, flip(second, "clip", 2)]
+    far_frames = after(far_frames, second, third)
+    all_frames = [frames, flip(frames, "frame", 1), far_frames, flip(far_frames, "frame", 1)]
+    far = far + [flip(p, "frame", 1) for p in far]
+    block, grad_own, grad_near, across = wide_call(
+        functools.partial(block_body, n, per),
+        "weight_block",
+        [struct(3 * depth + 4 * low, inner)] + [struct(few, dim)] * 2 + [struct(2, few, dim)],
+        [pltpu.VMEM((rows, dim), BF16)]
+        + [pltpu.VMEM((depth, inner), BF16)] * 3
+        + [pltpu.VMEM((low, dim), BF16)] * 2
+        + [pltpu.VMEM((rows, dim), F32), pltpu.VMEM((few, dim), F32), pltpu.SemaphoreType.DMA((6,))],
+        60,
+        0,
+        7,
+        6,
+    )(idx, after(out_grad.reshape(rows, dim), own), time_query, time_key, time_value, space_output, time_output)
+    blocks = [block, flip(block, "frame", 1)] + far
+    across = flip(after(across, first), "frame", 2)
+    token_grad = [grad_own, flip(grad_near, "frame", 1), across, flip(across, "frame", 1)]
     token_frames = jnp.concatenate(
         [
-            lax.dynamic_slice_in_dim(f.reshape(per, tokens, dim), me * share, share, 1).reshape(
-                per * share, dim
-            )
+            lax.dynamic_slice_in_dim(f.reshape(per, tokens, dim), me * share, share, 1).reshape(few, dim)
             for f in all_frames
         ],
         0,
     )
-    table = position_table(0, n * per, dim).reshape(n, per, dim)
-    table = jnp.concatenate([pick(table, me ^ r) for r in range(n)], 0)
-    table = jnp.repeat(table, share, 0)
-    token_rows = n * per * share
-    token_of = jnp.arange(token_rows) % share
-    same = (token_of[:, None] == token_of[None, :]).astype(F32)
+    frame_ids = jnp.concatenate([(me ^ r) * per + jnp.arange(per) for r in range(n)])
+    table = position_rows(frame_ids, dim)
 
     x_all, w_all, q_all, k_all, v_all, probs, mixed = wide_call(
         functools.partial(spatial_forward_body, n, tokens, width),
@@ -711,17 +915,22 @@
             struct(total, 2 * tokens, dtype=F32),
             struct(n, token_rows, lanes),
         ],
-        [pltpu.VMEM((total, lanes), F32), pltpu.VMEM((token_rows, lanes), F32)],
-        40,
+        [
+            pltpu.VMEM((total, lanes), F32),
+            pltpu.VMEM((token_rows, lanes), F32),
+            pltpu.VMEM((tokens, dim), F32),
+        ],
+        26,
         2_000_000_000,
-        2 * n + 2,
-    )(idx, *all_frames, *packs, all_refer)
-    mixed = exchange([mixed[r] for r in range(n)])
+        2 * n + 7,
+    )(idx, *all_frames, *all_refer, *packs)
+    mixed = exchange(list(after([mixed[r] for r in range(n)], across)))
 
     outs = wide_call(
-        functools.partial(temporal_body, n, HEADS),
+        functools.partial(temporal_body, n, HEADS, per),
         "temporal",
         [struct(token_rows, lanes)] * n
+        + [struct(2 * few, dim)] * n
         + [struct(token_rows, dim)] * 2
         + [struct(token_rows, inner)] * 4
         + [struct(token_rows, dim)],
@@ -738,94 +947,112 @@
             pltpu.VMEM((HEADS * token_rows, inner), BF16),
             pltpu.VMEM((HEADS * token_rows, inner), BF16),
         ],
-        48,
+        36,
         5_000_000_000,
-        6 * n + 5,
-    )(idx, *mixed, *so_parts, *tq_parts, *tk_parts, *tv_parts, *to_parts, token_frames, token_grad, table, same)
+        2 * n + 13,
+    )(idx, *mixed, *blocks, token_frames, *token_grad, table)
     mixed_grads = exchange(list(outs[:n]))
-    hidden_grad, n2, gq, gk, gv, o2, out_tokens = outs[n:]
-
-    keep_a, send_a, keep_b, send_b = wide_call(
+    backs = outs[n : 2 * n]
+    hidden_grad, n2, gq, gk, gv, o2, token_grad = outs[2 * n :]
+
+    keep_tall, send_tall, keep_flat, send_flat = wide_call(
         functools.partial(terms_body, n),
         "temporal_terms",
-        [struct(n // 2, 3 * depth, inner)] * 2 + [struct(n // 2, 2 * (inner // n), dim)] * 2,
-        [pltpu.VMEM((dim, inner), BF16), pltpu.VMEM((inner, dim), BF16)],
-        40,
+        [struct(n // 2, clips, 3, piece, inner)] * 2 + [struct(n // 2, clips, low // 2, inner)] * 2,
+        [pltpu.VMEM((dim, inner), F32), pltpu.VMEM((inner, dim), BF16)],
+        26,
         3_000_000_000,
         n + 8,
     )(idx, *mixed, hidden_grad, n2, gq, gk, gv, o2, token_grad)
 
-    keep_out, send_out, keep_ref, send_ref, term = wide_call(
+    tall = add(keep_tall, flip(send_tall, "frame", 1))
+    flat = add(keep_flat, flip(send_flat, "frame", 1))
+    backs = exchange([backs[0]] + [after(t, mixed_grads[2]) for t in backs[1:]])
+    mixed_grads[1] = after(mixed_grads[1], tall, flat)
+    keep_out, send_out, keep_term, send_term = wide_call(
         functools.partial(spatial_backward_body, n, tokens, width),
         "spatial_backward",
-        [struct(n // 2, rows, dim)] * 2 + [struct(n // 2, share, dim)] * 2 + [struct(dim, room)],
+        [struct(n // 2, rows + share, dim)] * 2 + [struct(count, n, piece, room)] * 2,
         [
             pltpu.VMEM((total, lanes), F32),
             pltpu.VMEM((token_rows, lanes), F32),
             pltpu.VMEM((total + tokens, room), BF16),
+            pltpu.VMEM((dim, room), F32),
         ],
-        40,
+        26,
         4_000_000_000,
         n + 7,
     )(idx, *mixed_grads, x_all, w_all, q_all, k_all, v_all, probs)
 
-    def to_frames(value):
-        parts = exchange(list(value.reshape(n, per * share, dim)))
-        stack = jnp.stack([p.reshape(per, share, dim) for p in parts], 1)
-        order = jnp.arange(n) ^ me
-        return jnp.take(stack, order, 1).reshape(per, tokens, dim)
-
-    output = to_frames(out_tokens)
-    hidden_frames = to_frames(hidden_grad).reshape(rows, dim)
-
+    def over_x(value):
+        moved = links.send("x", pick(value, 1 - side), "clip", 1)
+        return add(pick(value, side), moved)
+
+    def over_y(value):
+        return add(value[0], links.send("y", value[1], "frame", 2))
+
+    def over_z(value):
+        moved = [links.send(f"z{k}", pick(value, level ^ k), "clip", 2 * k) for k in range(1, count)]
+        return add(pick(value, level), *moved)
+
+    def spread_z(value):
+        return jnp.stack([value] + [links.send(f"z{k}", value, "clip", 2 * k) for k in range(1, count)])
+
+    def spread_x(value):
+        return value, links.send("x", value, "clip", 1)
+
+    bit = level & 1
+    flat = flat.reshape(n // 2, 2, 2, 2, low // 2, inner)
+    flat = add(pick(flat, bit, 3), links.send("z1", pick(flat, 1 - bit, 3), "clip", 2))
+    tall = over_y(tall).reshape(2, count, 3, piece, inner)
+    head = add(keep_term, links.send("x", send_term, "clip", 1))
+    flat = over_y(flat)
+    head = over_z(head)
+    tall = over_x(tall)
+    flat = over_x(flat)
+    head = jnp.stack(exchange([pick(head, me ^ r) for r in range(n)]))
+    high = level >> 1
+    flat = add(pick(flat, high), links.send("z2", pick(flat, 1 - high), "clip", 4))
+    tall = over_z(tall)
     near = add(keep_out, flip(send_out, "frame", 1))
-    far = flip(near[1], "frame", 2)
-    near_ref = add(keep_ref, flip(send_ref, "frame", 1))
-    refer_grad = add(near_ref[0], flip(near_ref[1], "frame", 2))
-    frames_grad = wide_call(finish_body, "finish", [struct(rows, dim)], [], 24, 0, 5)(
-        idx, frames, hidden_frames, near[0], far
-    )[0].reshape(per, tokens, dim)
-
-    split = (2,) * bits
-
-    def over_frame(keep, send):
-        near = add(keep, flip(send, "frame", 1))
-        return add(near[0], flip(near[1], "frame", 2))
-
-    sum_a = over_frame(keep_a, send_a)
-    sum_b = over_frame(keep_b, send_b)
-    sum_a = clip_scatter(sum_a.reshape(split + (-1, inner)), clip, bits)
-    sum_b = clip_scatter(sum_b.reshape(split + (-1, dim)), clip, bits)
-    term = term.reshape(n, clips, depth // clips, room).swapaxes(0, 1)
-    sum_c = clip_scatter(term.reshape(split + (n, depth // clips, room)), clip, bits)
-    heads = exchange(relative(sum_c))
-    heads = jnp.take(jnp.stack(heads), jnp.arange(n) ^ me, 0)
-    sum_c = jnp.stack(
-        [
-            heads[:, :, i * width : (i + 1) * width].swapaxes(0, 1).reshape(-1, inner)
-            for i in range(3)
-        ]
-    )
-
-    def whole(value):
-        stack, order = clip_gather(value, clip, bits)
-        return jnp.take(stack, order, 0)
-
-    all_a = whole(sum_a).reshape(3, depth, inner).astype(F32)
-    all_b = whole(sum_b).reshape(2, inner // n, dim).astype(F32)
-    all_c = whole(sum_c).swapaxes(0, 1).reshape(3, depth, inner).astype(F32)
+    head = after(head, near, *backs)
+    partial_far = flip(near[1], "frame", 2)
+    head = spread_z(head)
+    flat = spread_z(flat)
+    tall = spread_z(after(tall, partial_far))
+    head = spread_x(head)
+    flat = spread_x(flat)
+    tall = spread_x(tall)
+
+    output, frames_grad, refer_grad = wide_call(
+        functools.partial(finish_body, n, per),
+        "finish",
+        [struct(rows, dim)] * 2 + [struct(share, dim)],
+        [pltpu.VMEM((2 * few, dim), F32), pltpu.VMEM((2, rows, dim), F32)],
+        16,
+        0,
+        n + 4,
+    )(idx, frames, *backs, near[0], partial_far)
+
+    head_grads = wide_call(
+        functools.partial(place_heads_body, width),
+        "place_heads",
+        [struct(depth, inner, dtype=F32)] * 3,
+        [],
+        24,
+        0,
+        3,
+    )(idx, *head)
+    tall_grads = wide_call(place_body, "place_tall", [struct(depth, inner, dtype=F32)] * 3, [], 24, 0, 3)(idx, *tall)
+    flat_grads = wide_call(place_flat_body, "place_flat", [struct(low, dim, dtype=F32)] * 2, [], 24, 0, 3)(idx, *flat)
     return (
-        output[None],
-        frames_grad[None],
+        output.reshape(frames_in.shape),
+        frames_grad.reshape(frames_in.shape),
         refer_grad[None],
-        all_c[0],
-        all_c[1],
-        all_c[2],
-        all_b[1],
-        all_a[0],
-        all_a[1],
-        all_a[2],
-        all_b[0],
+        *head_grads,
+        flat_grads[0],
+        *tall_grads,
+        flat_grads[1],
     )
 
 
@@ -857,7 +1084,7 @@
         P("frame", None),
     )
     clips = mesh.shape["clip"]
-    by_heads = mesh.shape["frame"] == HEADS == 4 and clips & (clips - 1) == 0
+    by_heads = mesh.shape["frame"] == HEADS == 4 and clips == 8
     return jax.shard_map(
         per_device if by_heads else per_device_general, mesh=mesh, in_specs=in_specs, out_specs=out_specs, check_vma=False
     )

time: 368 us -> 261 us (0.71)
  waiting for transfers between devices: 171 us -> 114 us
  local copies, waits for them, and re-layouts: 50.4 us -> 15 us
  starting transfers between devices: 81 us -> 60.8 us
  Pallas kernels: 42 us -> 55.3 us
  other arithmetic: 21.6 us -> 11.1 us
    ppermute x80 -> x64, waiting for transfers between devices: 171 us -> 114 us  [flip(): return lax.ppermute(value, axis, [(i, i ^ bit) for i in range(size)])]
    ppermute x80 -> x64, starting transfers between devices: 81 us -> 60.8 us  [flip(): return lax.ppermute(value, axis, [(i, i ^ bit) for i in range(size)])]
    another operation x11 -> x0, local copies, waits for them, and re-layouts: 12.7 us -> none  [the longest x1 3.47 us: per_device(): table = position_table(0, n * per, dim).reshape(n, per, dim)]
    gather x6 -> x0, local copies, waits for them, and re-layouts: 10.6 us -> none  [the longest x3 4.5 us: whole(): return jnp.take(stack, order, 0)]
    pallas_call x2 -> x6, Pallas kernels: 18.8 us -> 28.1 us  [the longest x1 14.1 us: per_device(): wide_call(functools.partial(temporal_body, n, HEADS, per), 'temporal', [s...]
    convert_element_type x18 -> x13, other arithmetic: 11.1 us -> 9.97 us  [the longest x12 9.89 us: add(): return total.astype(BF16)]
    unnamed x87 -> x86, local copies, waits for them, and re-layouts: 12 us -> 11.9 us
  transfers between devices with their start and end apart: 80 -> 64, of which waited for: 37 -> 23; matrix products, arithmetic and copies ran while one was open for 17% -> 5% of each run, Pallas kernels for 7% -> 11%
where the time goes in v2:
time: 261 us; the launch traced here: 258 us
  waiting for transfers between devices  114 us (44%)
  starting transfers between devices  60.8 us (23%)
  Pallas kernels  55.3 us (21%)
  local copies, waits for them, and re-layouts  15 us (6%)
  other arithmetic  11.1 us (4%)
    ppermute x64, waiting for transfers between devices, flip(): return lax.ppermute(value, axis, [(i, i ^ bit) for i in range(size)])  114 us
    ppermute x64, starting transfers between devices, flip(): return lax.ppermute(value, axis, [(i, i ^ bit) for i in range(size)])  60.8 us
    pallas_call x1, Pallas kernels, per_device(): wide_call(functools.partial(temporal_body, n, HEADS, per), 'temporal', [s...  14.1 us
    unnamed x86, local copies, waits for them, and re-layouts  11.9 us
    convert_element_type x12, other arithmetic, add(): return total.astype(BF16)  9.89 us
    pallas_call x1, Pallas kernels, per_device(): wide_call(functools.partial(spatial_forward_body, n, tokens, width), 'spa...  9.71 us
    pallas_call x1, Pallas kernels, per_device(): wide_call(functools.partial(spatial_backward_body, n, tokens, width), 'sp...  7.72 us
    pallas_call x1, Pallas kernels, per_device(): wide_call(functools.partial(terms_body, n), 'temporal_terms', [struct(n /...  5.91 us
  transfers between devices with their start and end apart: 64, of which 23 were waited for; matrix products, arithmetic and copies ran while one was open for 5% of the time, Pallas kernels for 11%

profile of v2, /device:TPU:0, one launch (start us, length us, event | category | flops | bytes accessed | tf_op | source)
XLA Modules:
  0.0 257.6 jit_solution(13972872636948556637)
XLA Ops:
  1.2 3.9 %pack_heads.1 = (bf16[320,512]{1,0:T(8,128)(2,1)}, bf16[320,512]{1,0:T(8,128)(2,1)}, bf16[2,160,512]{2,1,0:T(8,128)(2,1)}, bf16[400,640]{1,0:T(8,128)(2,1)}) custom-call(s32[2]{0:T(128)} %pad_add_fusion.idx, bf16[320,640]{1,0:T(8,128)(2,1)} %refs_0_.1, bf16[320,640]{1,0:T(8,128)(2,1)} %refs_1_.2, bf16[320,640]{1,0:T(8,128)(2,1)} %refs_2_.2, ...), custom_call_target="tpu_custom_call" | custom-call | bytes 8000000 | tf_op jit(solution)/shard_map/pack_heads/pallas_call | solution.py:850
  5.1 3.0 %collective-permute-start.3 = (bf16[400,640]{1,0:T(8,128)(2,1)}, bf16[400,640]{1,0:T(8,128)(2,1)S(1)}, u32[]{:S(2)}, u32[]{:S(2)}) collective-permute-start(bf16[400,640]{1,0:T(8,128)(2,1)} %get-tuple-element.91), channel_id=1, source_target_pairs={{0,2},{1,3},{2,0},{3,1},{4,6},{5,7},{6,4},{7,5},{8,10},{9,11},{10,... | collective-permute-start | bytes 1536008 | tf_op jit(solution)/shard_map/ppermute | solution.py:361
  8.3 1.9 collective-permute-start.8
  10.2 17.5 %collective-permute-done.1.refs_10_ = bf16[2,160,512]{2,1,0:T(8,128)(2,1)S(1)} collective-permute-done((bf16[2,160,512]{2,1,0:T(8,128)(2,1)}, bf16[2,160,512]{2,1,0:T(8,128)(2,1)S(1)}, u32[]{:S(2)}, u32[]{:S(2)}) %collective-permute-start.1) | collective-permute-done | bytes 327712 | tf_op jit(solution)/shard_map/ppermute | solution.py:361
  27.7 1.7 collective-permute-start.2
  29.5 1.5 collective-permute-start.4
  31.0 1.6 collective-permute-start.5
  32.5 4.0 %weight_block.1 = (bf16[1600,640]{1,0:T(8,128)(2,1)}, bf16[48,1280]{1,0:T(8,128)(2,1)}, bf16[48,1280]{1,0:T(8,128)(2,1)}, bf16[2,48,1280]{2,1,0:T(8,128)(2,1)}) custom-call(s32[2]{0:T(128)} %pad_add_fusion.idx, bf16[192,1280]{1,0:T(8,128)(2,1)} %bitcast.120, bf16[320,640]{1,0:T(8,128)(2,1)} %refs_1_.3, bf16[320,640]{1,0:T(8,128)(2,1)} %refs_2_.3, ...), custom_call_target="tpu_custom_call" | custom-call | bytes 8000000 | tf_op jit(solution)/shard_map/weight_block/pallas_call | solution.py:880
  37.2 1.2 collective-permute-done.9.refs_7_
  38.5 1.4 collective-permute-done.24.refs_16_
  43.7 8.3 %collective-permute-done.11.refs_11_ = bf16[2,160,512]{2,1,0:T(8,128)(2,1)} collective-permute-done((bf16[2,160,512]{2,1,0:T(8,128)(2,1)}, bf16[2,160,512]{2,1,0:T(8,128)(2,1)}, u32[]{:S(2)}, u32[]{:S(2)}) %collective-permute-start.11) | collective-permute-done | bytes 327712 | tf_op jit(solution)/shard_map/ppermute | solution.py:361
  54.5 1.0 copy-done.8
  55.4 1.0 copy-done.10
  56.4 1.0 copy-done.12
  57.4 9.7 %spatial_forward.1 = (bf16[864,1280]{1,0:T(8,128)(2,1)S(1)}, bf16[1280,512]{1,0:T(8,128)(2,1)S(1)}, bf16[864,256]{1,0:T(8,128)(2,1)S(1)}, bf16[864,256]{1,0:T(8,...) custom-call(s32[2]{0:T(128)S(1)} %copy-done.6, ...), custom_call_target="tpu_custom_call" | custom-call | flops 2000000000 | bytes 8000000 | tf_op jit(solution)/shard_map/spatial_forward/pallas_call | solution.py:906
  67.1 1.4 copy-done.25
  72.4 1.0 collective-permute-start.17
  73.4 3.9 %collective-permute-done.16.refs_2_ = bf16[192,256]{1,0:T(8,128)(2,1)S(1)} collective-permute-done((bf16[192,256]{1,0:T(8,128)(2,1)S(1)}, bf16[192,256]{1,0:T(8,128)(2,1)S(1)}, u32[]{:S(2)}, u32[]{:S(2)}) %collective-permute-start.16) | collective-permute-done | bytes 98336 | tf_op jit(solution)/shard_map/ppermute | solution.py:361
  77.3 1.0 collective-permute-done.17.refs_3_
  78.4 14.1 %temporal.1 = (bf16[192,256]{1,0:T(8,128)(2,1)S(1)}, bf16[192,256]{1,0:T(8,128)(2,1)S(1)}, bf16[192,256]{1,0:T(8,128)(2,1)S(1)}, bf16[192,256]{1,0:T(8,128)(2,1)...) custom-call(s32[2]{0:T(128)S(1)} %copy-done.6, ...), custom_call_target="tpu_custom_call" | custom-call | flops 5000000000 | bytes 8000000 | tf_op jit(solution)/shard_map/temporal/pallas_call | solution.py:929
  93.8 5.9 %temporal_terms.1 = (bf16[2,8,3,40,640]{4,3,2,1,0:T(8,128)(2,1)S(1)}, bf16[2,8,3,40,640]{4,3,2,1,0:T(8,128)(2,1)}, bf16[2,8,80,640]{3,2,1,0:T(8,128)(2,1)S(1)}, bf16[2,8,80,640]{3,2,1,0:T(8,128)(2,1)}) custom-call(s32[2]{0:T(128)S(1)} %copy-done.6, bf16[192,256]{1,0:T(8,128)(2,1)S(1)} %get-tuple-element.99.refs_0_, ...), custom_call_target="tpu_custom_call" | custom-call | flops 3000000000 | bytes 8000000 | tf_op jit(solution)/shard_map/temporal_terms/pallas_call | solution.py:958
  99.7 1.1 copy-done
  102.1 6.1 %collective-permute-done.32 = bf16[2,8,80,640]{3,2,1,0:T(8,128)(2,1)} collective-permute-done((bf16[2,8,80,640]{3,2,1,0:T(8,128)(2,1)}, bf16[2,8,80,640]{3,2,1,0:T(8,128)(2,1)}, u32[]{:S(2)}, u32[]{:S(2)}) %collective-permute-start.32) | collective-permute-done | bytes 1638432 | tf_op jit(solution)/shard_map/ppermute | solution.py:361
  108.2 2.3 add_convert_fusion.1
  110.5 1.2 copy-done.39
  111.7 1.0 dynamic-slice_bitcast_fusion
  114.5 2.6 add_convert_fusion
  117.1 1.0 collective-permute-done.33.refs_3_
  118.1 7.7 %spatial_backward.1 = (bf16[2,216,1280]{2,1,0:T(8,128)(2,1)S(1)}, bf16[2,216,1280]{2,1,0:T(8,128)(2,1)S(1)}, bf16[4,4,40,512]{3,2,1,0:T(8,128)(2,1)S(1)}, bf16[4,4,40,512]{3,2,1,0:T(8,128)(2,1)S(1)}) custom-call(s32[2]{0:T(128)S(1)} %copy-done.6, bf16[192,256]{1,0:T(8,128)(2,1)S(1)} %copy-done.38, bf16[192,256]{1,0:T(8,128)(2,1)S(1)} %collective-permute-done.30.refs_1_, ...), custom_call_target="tpu_custom_call" | custom-call | flops 4000000000 | bytes 8000000 | tf_op jit(solution)/shard_map/spatial_backward/pallas_call | solution.py:972
  126.5 7.0 %collective-permute-done.44 = bf16[2,2,2,80,640]{4,3,2,1,0:T(8,128)(2,1)} collective-permute-done((bf16[2,2,2,80,640]{4,3,2,1,0:T(8,128)(2,1)}, bf16[2,2,2,80,640]{4,3,2,1,0:T(8,128)(2,1)}, u32[]{:S(2)}, u32[]{:S(2)}) %collective-permute-start.44) | collective-permute-done | bytes 819232 | tf_op jit(solution)/shard_map/ppermute | solution.py:361
  133.5 1.4 fusion.1
  135.8 1.4 collective-permute-start.50
  137.2 6.2 %collective-permute-done.36 = bf16[4,4,40,512]{3,2,1,0:T(8,128)(2,1)S(1)} collective-permute-done((bf16[4,4,40,512]{3,2,1,0:T(8,128)(2,1)S(1)}, bf16[4,4,40,512]{3,2,1,0:T(8,128)(2,1)S(1)}, u32[]{:S(2)}, u32[]{:S(2)}) %collective-permute-start.36) | collective-permute-done | bytes 655392 | tf_op jit(solution)/shard_map/ppermute | solution.py:361
  143.7 2.7 %collective-permute-start.38 = (bf16[4,40,512]{2,1,0:T(8,128)(2,1)S(1)}, bf16[4,40,512]{2,1,0:T(8,128)(2,1)S(1)}, u32[]{:S(2)}, u32[]{:S(2)}) collective-permute-start(bf16[4,40,512]{2,1,0:T(8,128)(2,1)S(1)} %get-tuple-element.171), channel_id=1, source_target_pairs={{0,16},{4,20},{8,24},{12,28},{16,0},{20,4},{24,8},{28,12},{1,17},{... | collective-permute-start | bytes 491528 | tf_op jit(solution)/shard_map/ppermute | solution.py:361
  146.3 1.2 collective-permute-start.37
  147.5 2.7 %collective-permute-start.39 = (bf16[4,40,512]{2,1,0:T(8,128)(2,1)S(1)}, bf16[4,40,512]{2,1,0:T(8,128)(2,1)S(1)}, u32[]{:S(2)}, u32[]{:S(2)}) collective-permute-start(bf16[4,40,512]{2,1,0:T(8,128)(2,1)S(1)} %get-tuple-element.170), channel_id=1, source_target_pairs={{0,24},{4,28},{8,16},{12,20},{16,8},{20,12},{24,0},{28,4},{1,25},{... | collective-permute-start | bytes 491528 | tf_op jit(solution)/shard_map/ppermute | solution.py:361
  150.4 5.5 %collective-permute-done.38 = bf16[4,40,512]{2,1,0:T(8,128)(2,1)S(1)} collective-permute-done((bf16[4,40,512]{2,1,0:T(8,128)(2,1)S(1)}, bf16[4,40,512]{2,1,0:T(8,128)(2,1)S(1)}, u32[]{:S(2)}, u32[]{:S(2)}) %collective-permute-start.38) | collective-permute-done | bytes 163872 | tf_op jit(solution)/shard_map/ppermute | solution.py:361
  156.5 2.0 collective-permute-done.39
  159.6 2.1 collective-permute-done.46
  161.8 1.8 collective-permute-start.29
  163.6 11.0 %collective-permute-done.41 = bf16[40,512]{1,0:T(8,128)(2,1)S(1)} collective-permute-done((bf16[40,512]{1,0:T(8,128)(2,1)S(1)}, bf16[40,512]{1,0:T(8,128)(2,1)S(1)}, u32[]{:S(2)}, u32[]{:S(2)}) %collective-permute-start.41) | collective-permute-done | bytes 40992 | tf_op jit(solution)/shard_map/ppermute | solution.py:361
  175.6 2.7 %collective-permute-start.47 = (bf16[80,640]{1,0:T(8,128)(2,1)S(1)}, bf16[80,640]{1,0:T(8,128)(2,1)S(1)}, u32[]{:S(2)}, u32[]{:S(2)}) collective-permute-start(bf16[80,640]{1,0:T(8,128)(2,1)S(1)} %dynamic-slice_bitcast_fusion.9), channel_id=1, source_target_pairs={{0,16},{4,20},{8,24},{12,28},{16,0},{20,4},{24,8},{28,12},{1,17},{... | collective-permute-start | bytes 307208 | tf_op jit(solution)/shard_map/ppermute | solution.py:361
  180.5 1.0 collective-permute-start.35
  181.6 4.1 %collective-permute-done.28.refs_2_ = bf16[96,1280]{1,0:T(8,128)(2,1)S(1)} collective-permute-done((bf16[96,1280]{1,0:T(8,128)(2,1)S(1)}, bf16[96,1280]{1,0:T(8,128)(2,1)S(1)}, u32[]{:S(2)}, u32[]{:S(2)}) %collective-permute-start.28) | collective-permute-done | bytes 245792 | tf_op jit(solution)/shard_map/ppermute | solution.py:361
  186.1 2.6 %collective-permute-start.48 = (bf16[4,40,512]{2,1,0:T(8,128)(2,1)S(1)}, bf16[4,40,512]{2,1,0:T(8,128)(2,1)S(1)}, u32[]{:S(2)}, u32[]{:S(2)}) collective-permute-start(bf16[4,40,512]{2,1,0:T(8,128)(2,1)S(1)} %pad_maximum_fusion.4), channel_id=1, source_target_pairs={{0,16},{4,20},{8,24},{12,28},{16,0},{20,4},{24,8},{28,12},{1,17},{... | collective-permute-start | bytes 491528 | tf_op jit(solution)/shard_map/ppermute | solution.py:361
  188.7 1.4 collective-permute-start.49
  190.1 4.4 %collective-permute-done.51 = bf16[4,3,40,640]{3,2,1,0:T(8,128)(2,1)S(1)} collective-permute-done((bf16[4,3,40,640]{3,2,1,0:T(8,128)(2,1)S(1)}, bf16[4,3,40,640]{3,2,1,0:T(8,128)(2,1)S(1)}, u32[]{:S(2)}, u32[]{:S(2)}) %collective-permute-start.51) | collective-permute-done | bytes 614432 | tf_op jit(solution)/shard_map/ppermute | solution.py:361
  196.7 3.6 %collective-permute-done.48 = bf16[4,40,512]{2,1,0:T(8,128)(2,1)S(1)} collective-permute-done((bf16[4,40,512]{2,1,0:T(8,128)(2,1)S(1)}, bf16[4,40,512]{2,1,0:T(8,128)(2,1)S(1)}, u32[]{:S(2)}, u32[]{:S(2)}) %collective-permute-start.48) | collective-permute-done | bytes 163872 | tf_op jit(solution)/shard_map/ppermute | solution.py:361
  200.4 3.3 %collective-permute-start.57 = (bf16[3,40,640]{2,1,0:T(8,128)(2,1)}, bf16[3,40,640]{2,1,0:T(8,128)(2,1)}, u32[]{:S(2)}, u32[]{:S(2)}) collective-permute-start(bf16[3,40,640]{2,1,0:T(8,128)(2,1)} %get-tuple-element.173), channel_id=1, source_target_pairs={{0,24},{4,28},{8,16},{12,20},{16,8},{20,12},{24,0},{28,4},{1,25},{... | collective-permute-start | bytes 460808 | tf_op jit(solution)/shard_map/ppermute | solution.py:361
  204.6 8.7 %collective-permute-done.55 = bf16[3,40,640]{2,1,0:T(8,128)(2,1)} collective-permute-done((bf16[3,40,640]{2,1,0:T(8,128)(2,1)}, bf16[3,40,640]{2,1,0:T(8,128)(2,1)}, u32[]{:S(2)}, u32[]{:S(2)}) %collective-permute-start.55) | collective-permute-done | bytes 153632 | tf_op jit(solution)/shard_map/ppermute | solution.py:361
  213.3 1.2 fusion.10
  214.5 2.3 collective-permute-start.60
  216.8 1.6 collective-permute-start.61
  218.4 1.4 collective-permute-start.62
  219.8 0.9 fusion.11
  221.6 3.6 %collective-permute-start.56 = (bf16[80,640]{1,0:T(8,128)(2,1)S(1)}, bf16[80,640]{1,0:T(8,128)(2,1)S(1)}, u32[]{:S(2)}, u32[]{:S(2)}) collective-permute-start(bf16[80,640]{1,0:T(8,128)(2,1)S(1)} %fusion.11), channel_id=1, source_target_pairs={{0,16},{4,20},{8,24},{12,28},{16,0},{20,4},{24,8},{28,12},{1,17},{... | collective-permute-start | bytes 307208 | tf_op jit(solution)/shard_map/ppermute | solution.py:361
  225.2 7.3 %collective-permute-done.61 = bf16[3,40,640]{2,1,0:T(8,128)(2,1)S(1)} collective-permute-done((bf16[3,40,640]{2,1,0:T(8,128)(2,1)S(1)}, bf16[3,40,640]{2,1,0:T(8,128)(2,1)S(1)}, u32[]{:S(2)}, u32[]{:S(2)}) %collective-permute-start.61) | collective-permute-done | bytes 153632 | tf_op jit(solution)/shard_map/ppermute | solution.py:361
  232.5 3.3 %collective-permute-start.58 = (bf16[80,640]{1,0:T(8,128)(2,1)S(1)}, bf16[80,640]{1,0:T(8,128)(2,1)S(1)}, u32[]{:S(2)}, u32[]{:S(2)}) collective-permute-start(bf16[80,640]{1,0:T(8,128)(2,1)S(1)} %fusion.11), channel_id=1, source_target_pairs={{0,24},{4,28},{8,16},{12,20},{16,8},{20,12},{24,0},{28,4},{1,25},{... | collective-permute-start | bytes 307208 | tf_op jit(solution)/shard_map/ppermute | solution.py:361
  236.5 3.3 %collective-permute-done.56 = bf16[80,640]{1,0:T(8,128)(2,1)S(1)} collective-permute-done((bf16[80,640]{1,0:T(8,128)(2,1)S(1)}, bf16[80,640]{1,0:T(8,128)(2,1)S(1)}, u32[]{:S(2)}, u32[]{:S(2)}) %collective-permute-start.56) | collective-permute-done | bytes 102432 | tf_op jit(solution)/shard_map/ppermute | solution.py:361
  240.3 3.5 %finish.1 = (bf16[192,1280]{1,0:T(8,128)(2,1)}, bf16[192,1280]{1,0:T(8,128)(2,1)}, bf16[24,1280]{1,0:T(8,128)(2,1)}) custom-call(s32[2]{0:T(128)S(1)} %copy-done.6, bf16[192,1280]{1,0:T(8,128)(2,1)S(1)} %bitcast.107, bf16[96,1280]{1,0:T(8,128)(2,1)S(1)} %get-tuple-element.106.refs_0_, bf16[96,1280]{1,0:T(8,128)(2,1)S(1)} %copy-done.5, ...), custom_call_target="tpu_custom_call" | custom-call | bytes 8000000 | tf_op jit(solution)/shard_map/finish/pallas_call | solution.py:1027
  243.8 2.4 place_heads.1
  246.2 7.3 %collective-permute-done.59.far = bf16[4,80,640]{2,1,0:T(8,128)(2,1)S(1)} collective-permute-done((bf16[4,80,640]{2,1,0:T(8,128)(2,1)S(1)}, bf16[4,80,640]{2,1,0:T(8,128)(2,1)S(1)}, u32[]{:S(2)}, u32[]{:S(2)}) %collective-permute-start.59) | collective-permute-done | bytes 409632 | tf_op jit(solution)/shard_map/ppermute | solution.py:361
  253.5 2.0 place_flat.1
  255.5 2.1 place_tall.1
  (199 shorter events, 28.3 us)
Async XLA Ops:
  5.1 24.3 %collective-permute-start.3 = (bf16[400,640]{1,0:T(8,128)(2,1)}, bf16[400,640]{1,0:T(8,128)(2,1)S(1)}, u32[]{:S(2)}, u32[]{:S(2)}) collective-permute-start(bf16[400,640]{1,0:T(8,128)(2,1)} %get-tuple-element.91), channel_id=1, source_target_pairs={{0,2},{1,3},{2,0},{3,1},{4,6},{5,7},{6,4},{7,5},{8,10},{9,11},{10,... | collective-permute-start | bytes 1536008 | tf_op jit(solution)/shard_map/ppermute | solution.py:361
  8.2 19.6 %collective-permute-start.1 = (bf16[2,160,512]{2,1,0:T(8,128)(2,1)}, bf16[2,160,512]{2,1,0:T(8,128)(2,1)S(1)}, u32[]{:S(2)}, u32[]{:S(2)}) collective-permute-start(bf16[2,160,512]{2,1,0:T(8,128)(2,1)} %get-tuple-element.89), channel_id=1, source_target_pairs={{0,2},{1,3},{2,0},{3,1},{4,6},{5,7},{6,4},{7,5},{8,10},{9,11},{10,... | collective-permute-start | bytes 983048 | tf_op jit(solution)/shard_map/ppermute | solution.py:361
  8.3 28.3 %collective-permute-start.8 = (bf16[24,1280]{1,0:T(8,128)(2,1)S(1)}, bf16[24,1280]{1,0:T(8,128)(2,1)S(1)}, u32[]{:S(2)}, u32[]{:S(2)}) collective-permute-start(bf16[24,1280]{1,0:T(8,128)(2,1)S(1)} %bitcast.111), channel_id=1, source_target_pairs={{0,2},{1,3},{2,0},{3,1},{4,6},{5,7},{6,4},{7,5},{8,10},{9,11},{10,... | collective-permute-start | bytes 184328 | tf_op jit(solution)/shard_map/ppermute | solution.py:361
  10.2 26.5 %collective-permute-start.7 = (bf16[24,1280]{1,0:T(8,128)(2,1)S(1)}, bf16[24,1280]{1,0:T(8,128)(2,1)S(1)}, u32[]{:S(2)}, u32[]{:S(2)}) collective-permute-start(bf16[24,1280]{1,0:T(8,128)(2,1)S(1)} %bitcast.112), channel_id=1, source_target_pairs={{0,1},{1,0},{2,3},{3,2},{4,5},{5,4},{6,7},{7,6},{8,9},{9,8},{10,11... | collective-permute-start | bytes 184328 | tf_op jit(solution)/shard_map/ppermute | solution.py:361
  27.7 14.2 %collective-permute-start.2 = (bf16[192,1280]{1,0:T(8,128)(2,1)S(1)}, bf16[192,1280]{1,0:T(8,128)(2,1)S(1)}, u32[]{:S(2)}, u32[]{:S(2)}) collective-permute-start(bf16[192,1280]{1,0:T(8,128)(2,1)S(1)} %bitcast.104), channel_id=1, source_target_pairs={{0,2},{1,3},{2,0},{3,1},{4,6},{5,7},{6,4},{7,5},{8,10},{9,11},{10,... | collective-permute-start | bytes 1474568 | tf_op jit(solution)/shard_map/ppermute | solution.py:361
  29.5 13.0 %collective-permute-start.4 = (bf16[400,640]{1,0:T(8,128)(2,1)S(1)}, bf16[400,640]{1,0:T(8,128)(2,1)S(1)}, u32[]{:S(2)}, u32[]{:S(2)}) collective-permute-start(bf16[400,640]{1,0:T(8,128)(2,1)S(1)} %collective-permute-done.3.refs_6_), channel_id=1, source_target_pairs={{0,4},{4,0},{8,12},{12,8},{16,20},{20,16},{24,28},{28,24},{1,5},{5... | collective-permute-start | bytes 1536008 | tf_op jit(solution)/shard_map/ppermute | solution.py:361
  31.0 11.5 %collective-permute-start.5 = (bf16[400,640]{1,0:T(8,128)(2,1)S(1)}, bf16[400,640]{1,0:T(8,128)(2,1)S(1)}, u32[]{:S(2)}, u32[]{:S(2)}) collective-permute-start(bf16[400,640]{1,0:T(8,128)(2,1)S(1)} %collective-permute-done.3.refs_6_), channel_id=1, source_target_pairs={{0,8},{4,12},{8,0},{12,4},{16,24},{20,28},{24,16},{28,20},{1,9},{5... | collective-permute-start | bytes 1536008 | tf_op jit(solution)/shard_map/ppermute | solution.py:361
  36.6 4.1 %collective-permute-start.10 = (bf16[320,512]{1,0:T(8,128)(2,1)}, bf16[320,512]{1,0:T(8,128)(2,1)S(1)}, u32[]{:S(2)}, u32[]{:S(2)}) collective-permute-start(bf16[320,512]{1,0:T(8,128)(2,1)} %get-tuple-element.94), channel_id=1, source_target_pairs={{0,1},{1,0},{2,3},{3,2},{4,5},{5,4},{6,7},{7,6},{8,9},{9,8},{10,11... | collective-permute-start | bytes 983048 | tf_op jit(solution)/shard_map/ppermute | solution.py:361
  36.7 1.7 collective-permute-start.9
  38.4 1.5 collective-permute-start.24
  40.6 3.0 %collective-permute-start = (bf16[192,1280]{1,0:T(8,128)(2,1)S(1)}, bf16[192,1280]{1,0:T(8,128)(2,1)S(1)}, u32[]{:S(2)}, u32[]{:S(2)}) collective-permute-start(bf16[192,1280]{1,0:T(8,128)(2,1)S(1)} %bitcast.105), channel_id=1, source_target_pairs={{0,1},{1,0},{2,3},{3,2},{4,5},{5,4},{6,7},{7,6},{8,9},{9,8},{10,11... | collective-permute-start | bytes 1474568 | tf_op jit(solution)/shard_map/ppermute | solution.py:361
  41.4 36.9 %collective-permute-start.18 = (bf16[1600,640]{1,0:T(8,128)(2,1)}, bf16[1600,640]{1,0:T(8,128)(2,1)}, u32[]{:S(2)}, u32[]{:S(2)}) collective-permute-start(bf16[1600,640]{1,0:T(8,128)(2,1)} %get-tuple-element.103.refs_4_), channel_id=1, source_target_pairs={{0,1},{1,0},{2,3},{3,2},{4,5},{5,4},{6,7},{7,6},{8,9},{9,8},{10,11... | collective-permute-start | bytes 6144008 | tf_op jit(solution)/shard_map/ppermute | solution.py:361
  41.9 10.1 %collective-permute-start.11 = (bf16[2,160,512]{2,1,0:T(8,128)(2,1)}, bf16[2,160,512]{2,1,0:T(8,128)(2,1)}, u32[]{:S(2)}, u32[]{:S(2)}) collective-permute-start(bf16[2,160,512]{2,1,0:T(8,128)(2,1)} %copy-done.9), channel_id=1, source_target_pairs={{0,4},{4,0},{8,12},{12,8},{16,20},{20,16},{24,28},{28,24},{1,5},{5... | collective-permute-start | bytes 983048 | tf_op jit(solution)/shard_map/ppermute | solution.py:361
  42.4 10.1 %collective-permute-start.12 = (bf16[2,160,512]{2,1,0:T(8,128)(2,1)}, bf16[2,160,512]{2,1,0:T(8,128)(2,1)}, u32[]{:S(2)}, u32[]{:S(2)}) collective-permute-start(bf16[2,160,512]{2,1,0:T(8,128)(2,1)} %copy-done.9), channel_id=1, source_target_pairs={{0,1},{1,0},{2,3},{3,2},{4,5},{5,4},{6,7},{7,6},{8,9},{9,8},{10,11... | collective-permute-start | bytes 983048 | tf_op jit(solution)/shard_map/ppermute | solution.py:361
  42.4 9.5 %collective-permute-start.14 = (bf16[2,48,1280]{2,1,0:T(8,128)(2,1)}, bf16[2,48,1280]{2,1,0:T(8,128)(2,1)S(1)}, u32[]{:S(2)}, u32[]{:S(2)}) collective-permute-start(bf16[2,48,1280]{2,1,0:T(8,128)(2,1)} %get-tuple-element.98), channel_id=1, source_target_pairs={{0,2},{1,3},{2,0},{3,1},{4,6},{5,7},{6,4},{7,5},{8,10},{9,11},{10,... | collective-permute-start | bytes 737288 | tf_op jit(solution)/shard_map/ppermute | solution.py:361
  43.5 10.8 %collective-permute-start.6 = (bf16[192,1280]{1,0:T(8,128)(2,1)S(1)}, bf16[192,1280]{1,0:T(8,128)(2,1)S(1)}, u32[]{:S(2)}, u32[]{:S(2)}) collective-permute-start(bf16[192,1280]{1,0:T(8,128)(2,1)S(1)} %collective-permute-done.2.refs_2_), channel_id=1, source_target_pairs={{0,1},{1,0},{2,3},{3,2},{4,5},{5,4},{6,7},{7,6},{8,9},{9,8},{10,11... | collective-permute-start | bytes 1474568 | tf_op jit(solution)/shard_map/ppermute | solution.py:361
  52.0 1.8 collective-permute-start.13
  52.0 2.0 collective-permute-start.25
  52.5 18.5 %collective-permute-start.19 = (bf16[400,640]{1,0:T(8,128)(2,1)S(1)}, bf16[400,640]{1,0:T(8,128)(2,1)S(1)}, u32[]{:S(2)}, u32[]{:S(2)}) collective-permute-start(bf16[400,640]{1,0:T(8,128)(2,1)S(1)} %collective-permute-done.4.refs_7_), channel_id=1, source_target_pairs={{0,8},{4,12},{8,0},{12,4},{16,24},{20,28},{24,16},{28,20},{1,9},{5... | collective-permute-start | bytes 1536008 | tf_op jit(solution)/shard_map/ppermute | solution.py:361
  53.8 17.6 %collective-permute-start.20 = (bf16[400,640]{1,0:T(8,128)(2,1)S(1)}, bf16[400,640]{1,0:T(8,128)(2,1)S(1)}, u32[]{:S(2)}, u32[]{:S(2)}) collective-permute-start(bf16[400,640]{1,0:T(8,128)(2,1)S(1)} %collective-permute-done.3.refs_6_), channel_id=1, source_target_pairs={{0,1},{1,0},{2,3},{3,2},{4,5},{5,4},{6,7},{7,6},{8,9},{9,8},{10,11... | collective-permute-start | bytes 1536008 | tf_op jit(solution)/shard_map/ppermute | solution.py:361
  54.0 17.7 %collective-permute-start.21 = (bf16[400,640]{1,0:T(8,128)(2,1)S(1)}, bf16[400,640]{1,0:T(8,128)(2,1)S(1)}, u32[]{:S(2)}, u32[]{:S(2)}) collective-permute-start(bf16[400,640]{1,0:T(8,128)(2,1)S(1)} %collective-permute-done.4.refs_7_), channel_id=1, source_target_pairs={{0,1},{1,0},{2,3},{3,2},{4,5},{5,4},{6,7},{7,6},{8,9},{9,8},{10,11... | collective-permute-start | bytes 1536008 | tf_op jit(solution)/shard_map/ppermute | solution.py:361
  54.3 18.1 %collective-permute-start.22 = (bf16[400,640]{1,0:T(8,128)(2,1)S(1)}, bf16[400,640]{1,0:T(8,128)(2,1)S(1)}, u32[]{:S(2)}, u32[]{:S(2)}) collective-permute-start(bf16[400,640]{1,0:T(8,128)(2,1)S(1)} %collective-permute-done.5.refs_8_), channel_id=1, source_target_pairs={{0,1},{1,0},{2,3},{3,2},{4,5},{5,4},{6,7},{7,6},{8,9},{9,8},{10,11... | collective-permute-start | bytes 1536008 | tf_op jit(solution)/shard_map/ppermute | solution.py:361
  71.0 7.3 %collective-permute-start.23 = (bf16[400,640]{1,0:T(8,128)(2,1)S(1)}, bf16[400,640]{1,0:T(8,128)(2,1)S(1)}, u32[]{:S(2)}, u32[]{:S(2)}) collective-permute-start(bf16[400,640]{1,0:T(8,128)(2,1)S(1)} %collective-permute-done.19.refs_9_), channel_id=1, source_target_pairs={{0,1},{1,0},{2,3},{3,2},{4,5},{5,4},{6,7},{7,6},{8,9},{9,8},{10,11... | collective-permute-start | bytes 1536008 | tf_op jit(solution)/shard_map/ppermute | solution.py:361
  71.5 2.0 collective-permute-start.15
  71.7 5.6 %collective-permute-start.16 = (bf16[192,256]{1,0:T(8,128)(2,1)S(1)}, bf16[192,256]{1,0:T(8,128)(2,1)S(1)}, u32[]{:S(2)}, u32[]{:S(2)}) collective-permute-start(bf16[192,256]{1,0:T(8,128)(2,1)S(1)} %get-tuple-element.101), channel_id=1, source_target_pairs={{0,2},{1,3},{2,0},{3,1},{4,6},{5,7},{6,4},{7,5},{8,10},{9,11},{10,... | collective-permute-start | bytes 294920 | tf_op jit(solution)/shard_map/ppermute | solution.py:361
  72.4 5.9 %collective-permute-start.17 = (bf16[192,256]{1,0:T(8,128)(2,1)S(1)}, bf16[192,256]{1,0:T(8,128)(2,1)S(1)}, u32[]{:S(2)}, u32[]{:S(2)}) collective-permute-start(bf16[192,256]{1,0:T(8,128)(2,1)S(1)} %get-tuple-element.102), channel_id=1, source_target_pairs={{0,3},{1,2},{2,1},{3,0},{4,7},{5,6},{6,5},{7,4},{8,11},{9,10},{10,... | collective-permute-start | bytes 294920 | tf_op jit(solution)/shard_map/ppermute | solution.py:361
  100.9 13.6 %collective-permute-start.31 = (bf16[2,8,3,40,640]{4,3,2,1,0:T(8,128)(2,1)}, bf16[2,8,3,40,640]{4,3,2,1,0:T(8,128)(2,1)}, u32[]{:S(2)}, u32[]{:S(2)}) collective-permute-start(bf16[2,8,3,40,640]{4,3,2,1,0:T(8,128)(2,1)} %get-tuple-element.124), channel_id=1, source_target_pairs={{0,1},{1,0},{2,3},{3,2},{4,5},{5,4},{6,7},{7,6},{8,9},{9,8},{10,11... | collective-permute-start | bytes 7372808 | tf_op jit(solution)/shard_map/ppermute | solution.py:361
  101.2 7.0 %collective-permute-start.32 = (bf16[2,8,80,640]{3,2,1,0:T(8,128)(2,1)}, bf16[2,8,80,640]{3,2,1,0:T(8,128)(2,1)}, u32[]{:S(2)}, u32[]{:S(2)}) collective-permute-start(bf16[2,8,80,640]{3,2,1,0:T(8,128)(2,1)} %get-tuple-element.126), channel_id=1, source_target_pairs={{0,1},{1,0},{2,3},{3,2},{4,5},{5,4},{6,7},{7,6},{8,9},{9,8},{10,11... | collective-permute-start | bytes 4915208 | tf_op jit(solution)/shard_map/ppermute | solution.py:361
  101.4 13.1 %collective-permute-start.26 = (bf16[192,256]{1,0:T(8,128)(2,1)}, bf16[192,256]{1,0:T(8,128)(2,1)}, u32[]{:S(2)}, u32[]{:S(2)}) collective-permute-start(bf16[192,256]{1,0:T(8,128)(2,1)} %copy-done.23), channel_id=1, source_target_pairs={{0,2},{1,3},{2,0},{3,1},{4,6},{5,7},{6,4},{7,5},{8,10},{9,11},{10,... | collective-permute-start | bytes 294920 | tf_op jit(solution)/shard_map/ppermute | solution.py:361
  112.7 20.8 %collective-permute-start.44 = (bf16[2,2,2,80,640]{4,3,2,1,0:T(8,128)(2,1)}, bf16[2,2,2,80,640]{4,3,2,1,0:T(8,128)(2,1)}, u32[]{:S(2)}, u32[]{:S(2)}) collective-permute-start(bf16[2,2,2,80,640]{4,3,2,1,0:T(8,128)(2,1)} %dynamic-slice_bitcast_fusion), channel_id=1, source_target_pairs={{0,8},{4,12},{8,0},{12,4},{16,24},{20,28},{24,16},{28,20},{1,9},{5... | collective-permute-start | bytes 2457608 | tf_op jit(solution)/shard_map/ppermute | solution.py:361
  113.6 3.5 %collective-permute-start.30 = (bf16[192,256]{1,0:T(8,128)(2,1)}, bf16[192,256]{1,0:T(8,128)(2,1)S(1)}, u32[]{:S(2)}, u32[]{:S(2)}) collective-permute-start(bf16[192,256]{1,0:T(8,128)(2,1)} %copy-done.22), channel_id=1, source_target_pairs={{0,1},{1,0},{2,3},{3,2},{4,5},{5,4},{6,7},{7,6},{8,9},{9,8},{10,11... | collective-permute-start | bytes 294920 | tf_op jit(solution)/shard_map/ppermute | solution.py:361
  113.6 4.5 %collective-permute-start.33 = (bf16[192,256]{1,0:T(8,128)(2,1)S(1)}, bf16[192,256]{1,0:T(8,128)(2,1)S(1)}, u32[]{:S(2)}, u32[]{:S(2)}) collective-permute-start(bf16[192,256]{1,0:T(8,128)(2,1)S(1)} %get-tuple-element.128), channel_id=1, source_target_pairs={{0,3},{1,2},{2,1},{3,0},{4,7},{5,6},{6,5},{7,4},{8,11},{9,10},{10,... | collective-permute-start | bytes 294920 | tf_op jit(solution)/shard_map/ppermute | solution.py:361
  125.9 17.6 %collective-permute-start.36 = (bf16[4,4,40,512]{3,2,1,0:T(8,128)(2,1)S(1)}, bf16[4,4,40,512]{3,2,1,0:T(8,128)(2,1)S(1)}, u32[]{:S(2)}, u32[]{:S(2)}) collective-permute-start(bf16[4,4,40,512]{3,2,1,0:T(8,128)(2,1)S(1)} %get-tuple-element.141), channel_id=1, source_target_pairs={{0,4},{4,0},{8,12},{12,8},{16,20},{20,16},{24,28},{28,24},{1,5},{5... | collective-permute-start | bytes 1966088 | tf_op jit(solution)/shard_map/ppermute | solution.py:361
  134.9 12.6 %collective-permute-start.45 = (bf16[2,2,80,640]{3,2,1,0:T(8,128)(2,1)S(1)}, bf16[2,2,80,640]{3,2,1,0:T(8,128)(2,1)S(1)}, u32[]{:S(2)}, u32[]{:S(2)}) collective-permute-start(bf16[2,2,80,640]{3,2,1,0:T(8,128)(2,1)S(1)} %slice_bitcast_fusion.4), channel_id=1, source_target_pairs={{0,2},{1,3},{2,0},{3,1},{4,6},{5,7},{6,4},{7,5},{8,10},{9,11},{10,... | collective-permute-start | bytes 1228808 | tf_op jit(solution)/shard_map/ppermute | solution.py:361
  135.8 39.8 %collective-permute-start.50 = (bf16[8,3,40,640]{3,2,1,0:T(8,128)(2,1)S(1)}, bf16[8,3,40,640]{3,2,1,0:T(8,128)(2,1)S(1)}, u32[]{:S(2)}, u32[]{:S(2)}) collective-permute-start(bf16[8,3,40,640]{3,2,1,0:T(8,128)(2,1)S(1)} %slice_bitcast_fusion), channel_id=1, source_target_pairs={{0,2},{1,3},{2,0},{3,1},{4,6},{5,7},{6,4},{7,5},{8,10},{9,11},{10,... | collective-permute-start | bytes 3686408 | tf_op jit(solution)/shard_map/ppermute | solution.py:361
  137.2 41.5 %collective-permute-start.34 = (bf16[2,216,1280]{2,1,0:T(8,128)(2,1)S(1)}, bf16[2,216,1280]{2,1,0:T(8,128)(2,1)S(1)}, u32[]{:S(2)}, u32[]{:S(2)}) collective-permute-start(bf16[2,216,1280]{2,1,0:T(8,128)(2,1)S(1)} %get-tuple-element.136), channel_id=1, source_target_pairs={{0,1},{1,0},{2,3},{3,2},{4,5},{5,4},{6,7},{7,6},{8,9},{9,8},{10,11... | collective-permute-start | bytes 3317768 | tf_op jit(solution)/shard_map/ppermute | solution.py:361
  143.7 12.3 %collective-permute-start.38 = (bf16[4,40,512]{2,1,0:T(8,128)(2,1)S(1)}, bf16[4,40,512]{2,1,0:T(8,128)(2,1)S(1)}, u32[]{:S(2)}, u32[]{:S(2)}) collective-permute-start(bf16[4,40,512]{2,1,0:T(8,128)(2,1)S(1)} %get-tuple-element.171), channel_id=1, source_target_pairs={{0,16},{4,20},{8,24},{12,28},{16,0},{20,4},{24,8},{28,12},{1,17},{... | collective-permute-start | bytes 491528 | tf_op jit(solution)/shard_map/ppermute | solution.py:361
  146.3 10.2 %collective-permute-start.37 = (bf16[4,40,512]{2,1,0:T(8,128)(2,1)S(1)}, bf16[4,40,512]{2,1,0:T(8,128)(2,1)S(1)}, u32[]{:S(2)}, u32[]{:S(2)}) collective-permute-start(bf16[4,40,512]{2,1,0:T(8,128)(2,1)S(1)} %get-tuple-element.169), channel_id=1, source_target_pairs={{0,8},{4,12},{8,0},{12,4},{16,24},{20,28},{24,16},{28,20},{1,9},{5... | collective-permute-start | bytes 491528 | tf_op jit(solution)/shard_map/ppermute | solution.py:361
  147.5 11.0 %collective-permute-start.39 = (bf16[4,40,512]{2,1,0:T(8,128)(2,1)S(1)}, bf16[4,40,512]{2,1,0:T(8,128)(2,1)S(1)}, u32[]{:S(2)}, u32[]{:S(2)}) collective-permute-start(bf16[4,40,512]{2,1,0:T(8,128)(2,1)S(1)} %get-tuple-element.170), channel_id=1, source_target_pairs={{0,24},{4,28},{8,16},{12,20},{16,8},{20,12},{24,0},{28,4},{1,25},{... | collective-permute-start | bytes 491528 | tf_op jit(solution)/shard_map/ppermute | solution.py:361
  155.9 5.8 %collective-permute-start.46 = (bf16[2,80,640]{2,1,0:T(8,128)(2,1)S(1)}, bf16[2,80,640]{2,1,0:T(8,128)(2,1)S(1)}, u32[]{:S(2)}, u32[]{:S(2)}) collective-permute-start(bf16[2,80,640]{2,1,0:T(8,128)(2,1)S(1)} %dynamic-slice_bitcast_fusion.2), channel_id=1, source_target_pairs={{0,4},{4,0},{8,12},{12,8},{16,20},{20,16},{24,28},{28,24},{1,5},{5... | collective-permute-start | bytes 614408 | tf_op jit(solution)/shard_map/ppermute | solution.py:361
  158.9 2.9 %collective-permute-start.40 = (bf16[40,512]{1,0:T(8,128)(2,1)S(1)}, bf16[40,512]{1,0:T(8,128)(2,1)S(1)}, u32[]{:S(2)}, u32[]{:S(2)}) collective-permute-start(bf16[40,512]{1,0:T(8,128)(2,1)S(1)} %get-tuple-element.182), channel_id=1, source_target_pairs={{0,1},{1,0},{2,3},{3,2},{4,5},{5,4},{6,7},{7,6},{8,9},{9,8},{10,11... | collective-permute-start | bytes 122888 | tf_op jit(solution)/shard_map/ppermute | solution.py:361
  159.0 15.6 %collective-permute-start.41 = (bf16[40,512]{1,0:T(8,128)(2,1)S(1)}, bf16[40,512]{1,0:T(8,128)(2,1)S(1)}, u32[]{:S(2)}, u32[]{:S(2)}) collective-permute-start(bf16[40,512]{1,0:T(8,128)(2,1)S(1)} %get-tuple-element.181), channel_id=1, source_target_pairs={{0,2},{1,3},{2,0},{3,1},{4,6},{5,7},{6,4},{7,5},{8,10},{9,11},{10,... | collective-permute-start | bytes 122888 | tf_op jit(solution)/shard_map/ppermute | solution.py:361
  161.7 13.6 %collective-permute-start.42 = (bf16[40,512]{1,0:T(8,128)(2,1)S(1)}, bf16[40,512]{1,0:T(8,128)(2,1)S(1)}, u32[]{:S(2)}, u32[]{:S(2)}) collective-permute-start(bf16[40,512]{1,0:T(8,128)(2,1)S(1)} %get-tuple-element.180), channel_id=1, source_target_pairs={{0,3},{1,2},{2,1},{3,0},{4,7},{5,6},{6,5},{7,4},{8,11},{9,10},{10,... | collective-permute-start | bytes 122888 | tf_op jit(solution)/shard_map/ppermute | solution.py:361
  161.8 18.7 %collective-permute-start.29 = (bf16[96,1280]{1,0:T(8,128)(2,1)S(1)}, bf16[96,1280]{1,0:T(8,128)(2,1)S(1)}, u32[]{:S(2)}, u32[]{:S(2)}) collective-permute-start(bf16[96,1280]{1,0:T(8,128)(2,1)S(1)} %copy-done.16), channel_id=1, source_target_pairs={{0,3},{1,2},{2,1},{3,0},{4,7},{5,6},{6,5},{7,4},{8,11},{9,10},{10,... | collective-permute-start | bytes 737288 | tf_op jit(solution)/shard_map/ppermute | solution.py:361
  174.6 11.1 %collective-permute-start.28 = (bf16[96,1280]{1,0:T(8,128)(2,1)S(1)}, bf16[96,1280]{1,0:T(8,128)(2,1)S(1)}, u32[]{:S(2)}, u32[]{:S(2)}) collective-permute-start(bf16[96,1280]{1,0:T(8,128)(2,1)S(1)} %copy-done.14), channel_id=1, source_target_pairs={{0,2},{1,3},{2,0},{3,1},{4,6},{5,7},{6,4},{7,5},{8,10},{9,11},{10,... | collective-permute-start | bytes 737288 | tf_op jit(solution)/shard_map/ppermute | solution.py:361
  175.3 10.3 %collective-permute-start.27 = (bf16[96,1280]{1,0:T(8,128)(2,1)S(1)}, bf16[96,1280]{1,0:T(8,128)(2,1)S(1)}, u32[]{:S(2)}, u32[]{:S(2)}) collective-permute-start(bf16[96,1280]{1,0:T(8,128)(2,1)S(1)} %get-tuple-element.109), channel_id=1, source_target_pairs={{0,1},{1,0},{2,3},{3,2},{4,5},{5,4},{6,7},{7,6},{8,9},{9,8},{10,11... | collective-permute-start | bytes 737288 | tf_op jit(solution)/shard_map/ppermute | solution.py:361
  175.6 10.5 %collective-permute-start.47 = (bf16[80,640]{1,0:T(8,128)(2,1)S(1)}, bf16[80,640]{1,0:T(8,128)(2,1)S(1)}, u32[]{:S(2)}, u32[]{:S(2)}) collective-permute-start(bf16[80,640]{1,0:T(8,128)(2,1)S(1)} %dynamic-slice_bitcast_fusion.9), channel_id=1, source_target_pairs={{0,16},{4,20},{8,24},{12,28},{16,0},{20,4},{24,8},{28,12},{1,17},{... | collective-permute-start | bytes 307208 | tf_op jit(solution)/shard_map/ppermute | solution.py:361
  178.8 15.8 %collective-permute-start.51 = (bf16[4,3,40,640]{3,2,1,0:T(8,128)(2,1)S(1)}, bf16[4,3,40,640]{3,2,1,0:T(8,128)(2,1)S(1)}, u32[]{:S(2)}, u32[]{:S(2)}) collective-permute-start(bf16[4,3,40,640]{3,2,1,0:T(8,128)(2,1)S(1)} %dynamic-slice_bitcast_fusion.1), channel_id=1, source_target_pairs={{0,4},{4,0},{8,12},{12,8},{16,20},{20,16},{24,28},{28,24},{1,5},{5... | collective-permute-start | bytes 1843208 | tf_op jit(solution)/shard_map/ppermute | solution.py:361
  180.5 34.0 %collective-permute-start.35 = (bf16[216,1280]{1,0:T(8,128)(2,1)}, bf16[216,1280]{1,0:T(8,128)(2,1)S(1)}, u32[]{:S(2)}, u32[]{:S(2)}) collective-permute-start(bf16[216,1280]{1,0:T(8,128)(2,1)} %get-tuple-element.167), channel_id=1, source_target_pairs={{0,2},{1,3},{2,0},{3,1},{4,6},{5,7},{6,4},{7,5},{8,10},{9,11},{10,... | collective-permute-start | bytes 1658888 | tf_op jit(solution)/shard_map/ppermute | solution.py:361
  185.7 10.7 %collective-permute-start.43 = (bf16[4,40,512]{2,1,0:T(8,128)(2,1)S(1)}, bf16[4,40,512]{2,1,0:T(8,128)(2,1)S(1)}, u32[]{:S(2)}, u32[]{:S(2)}) collective-permute-start(bf16[4,40,512]{2,1,0:T(8,128)(2,1)S(1)} %pad_maximum_fusion.4), channel_id=1, source_target_pairs={{0,8},{4,12},{8,0},{12,4},{16,24},{20,28},{24,16},{28,20},{1,9},{5... | collective-permute-start | bytes 491528 | tf_op jit(solution)/shard_map/ppermute | solution.py:361
  186.1 14.3 %collective-permute-start.48 = (bf16[4,40,512]{2,1,0:T(8,128)(2,1)S(1)}, bf16[4,40,512]{2,1,0:T(8,128)(2,1)S(1)}, u32[]{:S(2)}, u32[]{:S(2)}) collective-permute-start(bf16[4,40,512]{2,1,0:T(8,128)(2,1)S(1)} %pad_maximum_fusion.4), channel_id=1, source_target_pairs={{0,16},{4,20},{8,24},{12,28},{16,0},{20,4},{24,8},{28,12},{1,17},{... | collective-permute-start | bytes 491528 | tf_op jit(solution)/shard_map/ppermute | solution.py:361
  188.7 15.0 %collective-permute-start.49 = (bf16[4,40,512]{2,1,0:T(8,128)(2,1)S(1)}, bf16[4,40,512]{2,1,0:T(8,128)(2,1)S(1)}, u32[]{:S(2)}, u32[]{:S(2)}) collective-permute-start(bf16[4,40,512]{2,1,0:T(8,128)(2,1)S(1)} %pad_maximum_fusion.4), channel_id=1, source_target_pairs={{0,24},{4,28},{8,16},{12,20},{16,8},{20,12},{24,0},{28,4},{1,25},{... | collective-permute-start | bytes 491528 | tf_op jit(solution)/shard_map/ppermute | solution.py:361
  195.6 9.0 %collective-permute-start.53 = (bf16[3,40,640]{2,1,0:T(8,128)(2,1)}, bf16[3,40,640]{2,1,0:T(8,128)(2,1)}, u32[]{:S(2)}, u32[]{:S(2)}) collective-permute-start(bf16[3,40,640]{2,1,0:T(8,128)(2,1)} %get-tuple-element.151), channel_id=1, source_target_pairs={{0,8},{4,12},{8,0},{12,4},{16,24},{20,28},{24,16},{28,20},{1,9},{5... | collective-permute-start | bytes 460808 | tf_op jit(solution)/shard_map/ppermute | solution.py:361
  196.4 16.9 %collective-permute-start.55 = (bf16[3,40,640]{2,1,0:T(8,128)(2,1)}, bf16[3,40,640]{2,1,0:T(8,128)(2,1)}, u32[]{:S(2)}, u32[]{:S(2)}) collective-permute-start(bf16[3,40,640]{2,1,0:T(8,128)(2,1)} %get-tuple-element.153), channel_id=1, source_target_pairs={{0,16},{4,20},{8,24},{12,28},{16,0},{20,4},{24,8},{28,12},{1,17},{... | collective-permute-start | bytes 460808 | tf_op jit(solution)/shard_map/ppermute | solution.py:361
  200.4 12.9 %collective-permute-start.57 = (bf16[3,40,640]{2,1,0:T(8,128)(2,1)}, bf16[3,40,640]{2,1,0:T(8,128)(2,1)}, u32[]{:S(2)}, u32[]{:S(2)}) collective-permute-start(bf16[3,40,640]{2,1,0:T(8,128)(2,1)} %get-tuple-element.173), channel_id=1, source_target_pairs={{0,24},{4,28},{8,16},{12,20},{16,8},{20,12},{24,0},{28,4},{1,25},{... | collective-permute-start | bytes 460808 | tf_op jit(solution)/shard_map/ppermute | solution.py:361
  203.8 32.1 %collective-permute-start.52 = (bf16[4,4,40,512]{3,2,1,0:T(8,128)(2,1)S(1)}, bf16[4,4,40,512]{3,2,1,0:T(8,128)(2,1)S(1)}, u32[]{:S(2)}, u32[]{:S(2)}) collective-permute-start(bf16[4,4,40,512]{3,2,1,0:T(8,128)(2,1)S(1)} %pad_maximum_fusion.near), channel_id=1, source_target_pairs={{0,4},{4,0},{8,12},{12,8},{16,20},{20,16},{24,28},{28,24},{1,5},{5... | collective-permute-start | bytes 1966088 | tf_op jit(solution)/shard_map/ppermute | solution.py:361
  214.5 7.1 %collective-permute-start.60 = (bf16[3,40,640]{2,1,0:T(8,128)(2,1)S(1)}, bf16[3,40,640]{2,1,0:T(8,128)(2,1)S(1)}, u32[]{:S(2)}, u32[]{:S(2)}) collective-permute-start(bf16[3,40,640]{2,1,0:T(8,128)(2,1)S(1)} %fusion.10), channel_id=1, source_target_pairs={{0,8},{4,12},{8,0},{12,4},{16,24},{20,28},{24,16},{28,20},{1,9},{5... | collective-permute-start | bytes 460808 | tf_op jit(solution)/shard_map/ppermute | solution.py:361
  216.8 15.8 %collective-permute-start.61 = (bf16[3,40,640]{2,1,0:T(8,128)(2,1)S(1)}, bf16[3,40,640]{2,1,0:T(8,128)(2,1)S(1)}, u32[]{:S(2)}, u32[]{:S(2)}) collective-permute-start(bf16[3,40,640]{2,1,0:T(8,128)(2,1)S(1)} %fusion.10), channel_id=1, source_target_pairs={{0,16},{4,20},{8,24},{12,28},{16,0},{20,4},{24,8},{28,12},{1,17},{... | collective-permute-start | bytes 460808 | tf_op jit(solution)/shard_map/ppermute | solution.py:361
  218.4 17.4 %collective-permute-start.62 = (bf16[3,40,640]{2,1,0:T(8,128)(2,1)S(1)}, bf16[3,40,640]{2,1,0:T(8,128)(2,1)S(1)}, u32[]{:S(2)}, u32[]{:S(2)}) collective-permute-start(bf16[3,40,640]{2,1,0:T(8,128)(2,1)S(1)} %fusion.10), channel_id=1, source_target_pairs={{0,24},{4,28},{8,16},{12,20},{16,8},{20,12},{24,0},{28,4},{1,25},{... | collective-permute-start | bytes 460808 | tf_op jit(solution)/shard_map/ppermute | solution.py:361
  220.7 15.7 %collective-permute-start.54 = (bf16[80,640]{1,0:T(8,128)(2,1)S(1)}, bf16[80,640]{1,0:T(8,128)(2,1)S(1)}, u32[]{:S(2)}, u32[]{:S(2)}) collective-permute-start(bf16[80,640]{1,0:T(8,128)(2,1)S(1)} %fusion.11), channel_id=1, source_target_pairs={{0,8},{4,12},{8,0},{12,4},{16,24},{20,28},{24,16},{28,20},{1,9},{5... | collective-permute-start | bytes 307208 | tf_op jit(solution)/shard_map/ppermute | solution.py:361
  221.6 18.1 %collective-permute-start.56 = (bf16[80,640]{1,0:T(8,128)(2,1)S(1)}, bf16[80,640]{1,0:T(8,128)(2,1)S(1)}, u32[]{:S(2)}, u32[]{:S(2)}) collective-permute-start(bf16[80,640]{1,0:T(8,128)(2,1)S(1)} %fusion.11), channel_id=1, source_target_pairs={{0,16},{4,20},{8,24},{12,28},{16,0},{20,4},{24,8},{28,12},{1,17},{... | collective-permute-start | bytes 307208 | tf_op jit(solution)/shard_map/ppermute | solution.py:361
  232.5 7.2 %collective-permute-start.58 = (bf16[80,640]{1,0:T(8,128)(2,1)S(1)}, bf16[80,640]{1,0:T(8,128)(2,1)S(1)}, u32[]{:S(2)}, u32[]{:S(2)}) collective-permute-start(bf16[80,640]{1,0:T(8,128)(2,1)S(1)} %fusion.11), channel_id=1, source_target_pairs={{0,24},{4,28},{8,16},{12,20},{16,8},{20,12},{24,0},{28,4},{1,25},{... | collective-permute-start | bytes 307208 | tf_op jit(solution)/shard_map/ppermute | solution.py:361
  235.9 19.5 %collective-permute-start.63 = (bf16[4,3,40,640]{3,2,1,0:T(8,128)(2,1)S(1)}, bf16[4,3,40,640]{3,2,1,0:T(8,128)(2,1)S(1)}, u32[]{:S(2)}, u32[]{:S(2)}) collective-permute-start(bf16[4,3,40,640]{3,2,1,0:T(8,128)(2,1)S(1)} %pad_maximum_fusion.1.near), channel_id=1, source_target_pairs={{0,4},{4,0},{8,12},{12,8},{16,20},{20,16},{24,28},{28,24},{1,5},{5... | collective-permute-start | bytes 1843208 | tf_op jit(solution)/shard_map/ppermute | solution.py:361
  239.8 13.7 %collective-permute-start.59 = (bf16[4,80,640]{2,1,0:T(8,128)(2,1)S(1)}, bf16[4,80,640]{2,1,0:T(8,128)(2,1)S(1)}, u32[]{:S(2)}, u32[]{:S(2)}) collective-permute-start(bf16[4,80,640]{2,1,0:T(8,128)(2,1)S(1)} %pad_maximum_fusion.3.near), channel_id=1, source_target_pairs={{0,4},{4,0},{8,12},{12,8},{16,20},{20,16},{24,28},{28,24},{1,5},{5... | collective-permute-start | bytes 1228808 | tf_op jit(solution)/shard_map/ppermute | solution.py:361
  (43 other events, 362.7 us)

commit v3 on v2

--- a/solution.py
+++ b/solution.py
@@ -1,6 +1,7 @@
 import math
 
 import functools
+import itertools
 
 import jax
 import jax.numpy as jnp
@@ -334,22 +335,26 @@
     return lax.dot_general(left, right, (((0,), (0,)), ((), ())), preferred_element_type=F32)
 
 
-def wide_call(body, name, out_shape, scratch, limit_mb, flops, num_in, kept=0, out_kept=()):
-    return pl.pallas_call(
-        body,
+def wide_call(body, name, out_shape, scratch, limit_mb, flops, num_in, kept=0, late=()):
+    def with_late(idx, *refs):
+        body(idx, *refs[: num_in - 1], *refs[num_in - 1 + len(late) :])
+
+    call = pl.pallas_call(
+        with_late,
         name=name,
         out_shape=out_shape,
         in_specs=[pl.BlockSpec(memory_space=pltpu.SMEM)]
         + [pl.BlockSpec(memory_space=pltpu.HBM)] * kept
-        + [pl.BlockSpec(memory_space=pltpu.VMEM)] * (num_in - 1 - kept),
-        out_specs=tuple(
-            pl.BlockSpec(memory_space=pltpu.HBM if i in out_kept else pltpu.VMEM)
-            for i in range(len(out_shape))
-        ),
+        + [pl.BlockSpec(memory_space=pltpu.VMEM)] * (num_in - 1 - kept)
+        + [pl.BlockSpec(memory_space=pl.ANY)] * len(late),
+        out_specs=tuple(pl.BlockSpec(memory_space=pltpu.VMEM) for _ in out_shape),
         scratch_shapes=scratch,
         compiler_params=pltpu.CompilerParams(vmem_limit_bytes=limit_mb * 1024 * 1024),
-        cost_estimate=pl.CostEstimate(flops=flops, bytes_accessed=8_000_000, transcendentals=0),
-    )
+        cost_estimate=pl.CostEstimate(
+            flops=max(flops, 1), bytes_accessed=8_000_000 if flops > 1 else 1, transcendentals=0
+        ),
+    )
+    return lambda *operands: call(*operands, *late)
 
 
 def struct(*shape, dtype=BF16):
@@ -362,7 +367,8 @@
 
 
 def after(value, *others):
-    return lax.optimization_barrier((value,) + others)[0]
+    corners = [o[(slice(0, 1),) * (o.ndim - 2) + (slice(0, 8), slice(0, 128))] for o in others]
+    return lax.optimization_barrier((value, *corners))[0]
 
 
 def load(sources, held, sems):
@@ -372,9 +378,9 @@
     return copies
 
 
-def pack_body(heads, idx, *refs):
-    sources, near, (far, quarter), packs = refs[:8], refs[8:10], refs[10:12], refs[12]
-    held, sems = refs[13:21], refs[21]
+def pack_body(heads, n, per, idx, *refs):
+    sources, near, (far, first, grad_own, grad_near, across) = refs[:10], refs[10:12], refs[12:17]
+    packs, held, (wide, few, sems) = refs[17], refs[18:28], refs[28:]
     me, side, mine = idx[0], idx[1] & 1, idx[1] & 3
     half = far.shape[1]
     depth, inner = held[0].shape
@@ -395,47 +401,41 @@
         copy.wait()
     at = pl.ds(pl.multiple_of(mine * part, part), part)
     for i in range(3):
-        quarter[i * part : (i + 1) * part, :] = held[3 + i][at, :]
+        first[i * part : (i + 1) * part, :] = held[3 + i][at, :]
     for v in range(4):
 
         @pl.when(mine == v)
         def _(v=v):
-            quarter[3 * part :, :] = held[6 + (v >> 1)][:, (v & 1) * inner : (v & 1) * inner + inner]
-
-
-def block_body(n, per, idx, *refs):
-    sources, block, near, across = refs[:6], refs[6], refs[7:9], refs[9]
-    held, (wide, few, sems) = refs[10:16], refs[16:]
-    me = idx[0]
-    depth, inner = held[1].shape
-    low = held[4].shape[0]
-    copies = load(sources, held, sems)
-    copies[0].wait()
-    wide[...] = held[0][...].astype(F32)
-    share = few.shape[0] // per
+            first[3 * part :, :] = held[6 + (v >> 1)][:, (v & 1) * inner : (v & 1) * inner + inner]
+
+    wide[...] = held[8][...].astype(F32)
+    count = few.shape[0]
+    share = count // per
     tokens = wide.shape[0] // per
     for r in range(n):
-        first = pl.multiple_of((me ^ r) * share, share)
+        start = pl.multiple_of((me ^ r) * share, share)
         for j in range(per):
-            few[j * share : (j + 1) * share, :] = wide[pl.ds(j * tokens + first, share), :]
-        if r < 2:
-            near[r][...] = few[...].astype(BF16)
+            few[j * share : (j + 1) * share, :] = wide[pl.ds(j * tokens + start, share), :]
+        if r == 0:
+            grad_own[...] = few[...].astype(BF16)
+        elif r == 1:
+            grad_near[:count, :] = few[...].astype(BF16)
         else:
-            across[r - 2] = few[...].astype(BF16)
-    for copy in copies[1:]:
-        copy.wait()
-    for i in range(3):
-        block[i * depth : (i + 1) * depth, :] = held[1 + i][...]
-    for v in range(4):
-        at = 3 * depth + v * low
-        block[at : at + low, :] = held[4 + (v >> 1)][:, (v & 1) * inner : (v & 1) * inner + inner]
+            across[(r - 2) * count : (r - 1) * count, :] = few[...].astype(BF16)
+    grad_near[count:, :] = held[9][...]
+    across[2 * count :, :] = held[9][...]
 
 
 def spatial_forward_body(n, tokens, width, idx, *refs):
-    frames, refer, refs = refs[:n], refs[n : 2 * n], refs[2 * n :]
-    near, far = refs[:2], ((refs[2], refs[3]), (refs[4], refs[5]))
-    x_out, w_out, q_out, k_out, v_out, p_out, o_out = refs[6:13]
-    mixed, turn, few = refs[13:]
+    sources, refs = refs[: 2 * n + 8], refs[2 * n + 8 :]
+    x_out, w_out, q_out, k_out, v_out, p_out = refs[:6]
+    o_outs, (token_out, tall_out, flat_out) = refs[6 : n + 6], refs[n + 6 : n + 9]
+    mixed, turn, few, wide, spread, sems = refs[n + 9 : n + 15]
+    held = refs[n + 15 :]
+    cut = tall_out.shape[0]
+    copies = load(sources, held, sems)
+    frames, refer, packs = held[:n], held[n : 2 * n], held[2 * n :]
+    near, far = packs[:2], ((packs[2], packs[3]), (packs[4], packs[5]))
     me, side = idx[0], idx[1] & 1
     share = tokens // n
     rows = frames[0].shape[0]
@@ -444,22 +444,35 @@
     lanes = q_out.shape[1]
     room = w_out.shape[1]
     total = n * rows
+    for r in range(n):
+        copies[r].wait()
+
+        def norm(i, _, r=r):
+            at = pl.multiple_of(i * CHUNK, CHUNK)
+            centred, _ = layer_stats(frames[r][pl.ds(at, CHUNK), :])
+            x_out[pl.ds(r * rows + at, CHUNK), :] = centred.astype(BF16)
+            return 0
+
+        lax.fori_loop(0, rows // CHUNK, norm, 0)
+        wide[...] = frames[r][...].astype(F32)
+        first = pl.multiple_of(me * share, share)
+        for j in range(rows // tokens):
+            at = r * (rows // tokens) * share + j * share
+            spread[at : at + share, :] = wide[pl.ds(j * tokens + first, share), :]
+        copies[n + r].wait()
+        few[r * share : (r + 1) * share, :] = refer[r][refer[r].shape[0] - share :, :].astype(F32)
+    x_out[total:, :] = few[...].astype(BF16)
+    token_out[...] = spread[...].astype(BF16)
+    for copy in copies[2 * n :]:
+        copy.wait()
     for r in range(2):
         w_out[pl.ds(pl.multiple_of((me ^ r) * depth, depth), depth), :] = near[r][...]
         for k in range(2):
             at = pl.multiple_of((me ^ (r + 2)) * depth + (side ^ k) * half, half)
             w_out[pl.ds(at, half), :] = far[r][k][r]
-    for r in range(n):
-
-        def norm(i, _, r=r):
-            at = pl.multiple_of(i * CHUNK, CHUNK)
-            centred, _ = layer_stats(frames[r][pl.ds(at, CHUNK), :])
-            x_out[pl.ds(r * rows + at, CHUNK), :] = centred.astype(BF16)
-            return 0
-
-        lax.fori_loop(0, rows // CHUNK, norm, 0)
-        few[r * share : (r + 1) * share, :] = refer[r][...].astype(F32)
-    x_out[total:, :] = few[...].astype(BF16)
+    second, third = packs[6:8]
+    tall_out[...] = third[:cut, :]
+    flat_out[...] = second[cut:, :]
     for start, count in [(r * rows, rows) for r in range(n)] + [(total, tokens)]:
         three = mm(x_out[start : start + count, :], w_out[...])
         keep = lax.broadcasted_iota(jnp.int32, (count, lanes), 1) < width
@@ -485,7 +498,7 @@
         for b in range(total // tokens):
             to = ((b // per) ^ r) * per + b % per
             turn[to * share : (to + 1) * share, :] = mixed[pl.ds(b * tokens + first, share), :]
-        o_out[r] = turn[...].astype(BF16)
+        o_outs[r][...] = turn[...].astype(BF16)
 
 
 def spatial_backward_body(n, tokens, width, idx, *refs):
@@ -554,15 +567,20 @@
                 out[k, j] = term[pl.ds(at, piece), :].astype(BF16)
 
 
+def parts_of(ref, dim, inner):
+    starts = [0, dim, 2 * dim] + [3 * dim + i * inner for i in range(4)]
+    parts = [ref.at[:, a : a + (dim if i < 3 else inner)] for i, a in enumerate(starts)]
+    first, lanes = 3 * dim + 4 * inner, (ref.shape[1] - 3 * dim - 4 * inner) // 2
+    return parts + [ref.at[:, first + i * lanes : first + (i + 1) * lanes] for i in range(2)]
+
+
 def temporal_body(n, heads, per, idx, *refs):
-    mixed, refs = refs[:n], refs[n:]
-    near, far, refs = refs[:2], (refs[2:6], refs[6:10]), refs[10:]
-    frames, table = refs[0], refs[n + 1]
-    cotangents = refs[1 : n + 1]
-    refs = refs[n + 2 :]
-    grad_outs, back_outs, refs = refs[:n], refs[n : 2 * n], refs[2 * n :]
-    gh_out, n2_out, gq_out, gk_out, gv_out, o2_out, cotangent = refs[:7]
-    so, tq, tk, tv, to, hidden, centred, inverse, wide, qs, gos = refs[7:]
+    mixed_in, near, far, refs = refs[:n], (refs[n : n + 5], refs[n + 5 : n + 10]), refs[n + 10 :][:10], refs[n + 20 :]
+    far = (far[:5], far[5:])
+    frames_in, cotangents, table_in, refs = refs[0], refs[1 : n + 1], refs[n + 1], refs[n + 2 :]
+    grad_outs, back_outs, kept, refs = refs[:n], refs[n : 2 * n], refs[2 * n], refs[2 * n + 1 :]
+    so, tq, tk, tv, to, hidden, centred, inverse, wide, qs, gos = refs[:11]
+    mixed, frames, table, sems = refs[11 : n + 11], *refs[n + 11 :]
     me, quarter = idx[0], idx[1] & 3
     rows, dim = frames.shape
     inner = tq.shape[1]
@@ -571,37 +589,65 @@
     part = depth // 4
     few = rows // n
     share = few // per
+    gh_out, n2_out, cotangent, gq_out, gk_out, gv_out, o2_out, *o_outs = parts_of(kept, dim, inner)
+    first, second, chosen = [], [], []
+
+    def bring(source, to_ref, group):
+        group.append(pltpu.make_async_copy(source, to_ref, sems.at[len(first) + len(second) + len(chosen)]))
+
+    def low_rows(r):
+        return pl.ds(pl.multiple_of((me ^ r) * low, low), low)
+
     for r in range(n):
-        cotangent[r * few : (r + 1) * few, :] = cotangents[r][...] if r < 2 else cotangents[r][r - 2]
-        base = (me ^ r) * depth
-        low_at = pl.ds(pl.multiple_of((me ^ r) * low, low), low)
-
-        def put(v, source, r=r, low_at=low_at):
-            lanes = slice((v & 1) * inner, (v & 1) * inner + inner)
-            if v < 2:
-                so[r, :low, lanes] = source
-            else:
-                to[low_at, lanes] = source
-
+        bring(mixed_in[r], mixed[r], first)
         if r < 2:
-            for i, whole in enumerate((tq, tk, tv)):
-                whole[pl.ds(pl.multiple_of(base, depth), depth), :] = near[r][i * depth : (i + 1) * depth, :]
+            bring(near[r][3], so.at[r, pl.ds(0, low), :], first)
+    bring(frames_in, frames, first)
+    bring(table_in, table, first)
+    for r in range(2, n):
+        for s in range(4):
+            flat, start = (far[r - 2][s], 3 * part) if s < 3 else (far[r - 2][4], 0)
+            place = len(first) + len(second) + len(chosen)
+            cases = []
             for v in range(4):
-                at = 3 * depth + v * low
-                put(v, near[r][at : at + low, :])
-        else:
+                lanes = pl.ds((v & 1) * inner, inner)
+                target = so.at[r, pl.ds(0, low), lanes] if v < 2 else to.at[low_rows(r), lanes]
+                source = flat.at[pl.ds(start, low), :]
+                cases.append((v, pltpu.make_async_copy(source, target, sems.at[place])))
+            chosen.append((quarter ^ s, cases))
+    for r in range(n):
+        if r < 2:
+            bring(near[r][4], to.at[low_rows(r), :], second)
+        for i, whole in enumerate((tq, tk, tv)):
+            if r < 2:
+                at = pl.ds(pl.multiple_of((me ^ r) * depth, depth), depth)
+                bring(near[r][i], whole.at[at, :], second)
+                continue
             for s in range(4):
-                source = far[r - 2][s]
-                at = pl.ds(pl.multiple_of(base + (quarter ^ s) * part, part), part)
-                for i, whole in enumerate((tq, tk, tv)):
-                    whole[at, :] = source[i * part : (i + 1) * part, :]
-                for v in range(4):
-
-                    @pl.when((quarter ^ s) == v)
-                    def _(v=v, source=source, put=put):
-                        put(v, source[3 * part :, :])
-
-        so[r, low:, :] = jnp.zeros((so.shape[1] - low, dim), BF16)
+                at = pl.ds(pl.multiple_of((me ^ r) * depth + (quarter ^ s) * part, part), part)
+                bring(far[r - 2][s].at[pl.ds(i * part, part), :], whole.at[at, :], second)
+        source = cotangents[r].at[pl.ds(few if r == 3 else 0, few), :]
+        bring(source, cotangent.at[pl.ds(r * few, few), :], second)
+
+    def choose(act):
+        for which, cases in chosen:
+            for v, copy in cases:
+
+                @pl.when(which == v)
+                def _(copy=copy):
+                    act(copy)
+
+    for copy in first:
+        copy.start()
+    choose(lambda copy: copy.start())
+    for copy in second:
+        copy.start()
+    so[:, low:, :] = jnp.zeros((n, so.shape[1] - low, dim), BF16)
+    for copy in first:
+        copy.wait()
+    choose(lambda copy: copy.wait())
+    for i in range(2):
+        o_outs[i][...] = mixed[2 * i + 1][...]
     step = dim // 5
     for j in range(5):
         at = slice(j * step, (j + 1) * step)
@@ -620,6 +666,8 @@
 
     lax.fori_loop(0, rows // share, norm, 0)
     n2_out[...] = wide[...].astype(BF16)
+    for copy in second:
+        copy.wait()
 
     def token(axis):
         place = lax.broadcasted_iota(jnp.int32, (rows, rows), axis).astype(F32)
@@ -686,35 +734,38 @@
 
 
 def terms_body(n, idx, *refs):
-    mixed = refs[:n]
-    gh, n2, gq, gk, gv, o2, cotangent = refs[n : n + 7]
-    talls, flats = refs[n + 7 : n + 9], refs[n + 9 : n + 11]
-    tall, flat = refs[n + 11 :]
-    me = idx[0]
-    dim, inner = tall.shape
-    depth, low = dim // n, inner // n
-    pieces, piece = talls[0].shape[1], talls[0].shape[3]
-    for i, grad in enumerate((gq, gk, gv)):
-        for j in range(5):
-            at = slice(j * (dim // 5), (j + 1) * (dim // 5))
-            tall[at, :] = mm_at(n2[:, at], grad[...])
-        for r in range(n):
+    held, refs = refs[:4], refs[4:]
+    tall_keep, tall_send, flat_keep, flat_send = refs[:4]
+    n2_turned, o2_turned, tall, so = refs[4:]
+    me, bit = idx[0], (idx[1] >> 1) & 1
+    rows = held[0].shape[0]
+    depth, inner = tall.shape
+    dim, low = depth * n, inner // n
+    pieces, _, piece = tall_keep.shape[:3]
+    both = [parts_of(ref, dim, inner) for ref in held[:2]]
+    for i in range(2):
+        n2_turned[:, i * rows : (i + 1) * rows] = both[i][1][...].T
+        o2_turned[:, i * rows : (i + 1) * rows] = both[i][6][...].T
+    ours, theirs = both
+    mixed = [*held[2:], *theirs[7:]]
+    for i in range(3):
+        grad = jnp.concatenate([ours[3 + i][...], theirs[3 + i][...]], 0)
+        for k, out in enumerate((tall_keep, tall_send)):
+            at = pl.multiple_of((me ^ (2 * k)) * depth, depth)
+            tall[...] = mm(n2_turned[pl.ds(at, depth), :], grad)
             for p in range(pieces):
-                at = pl.multiple_of((me ^ r) * depth + p * piece, piece)
-                talls[r & 1][r >> 1, p, i] = tall[pl.ds(at, piece), :].astype(BF16)
-    for j in range(5):
-        at = slice(j * (inner // 5), (j + 1) * (inner // 5))
-        flat[at, :] = mm_at(o2[:, at], cotangent[...]).astype(BF16)
+                out[p, i] = tall[p * piece : (p + 1) * piece, :].astype(BF16)
     half = low // 2
-    for r in range(n):
-        out = flats[r & 1]
-        mine = mm_at(mixed[r][...], gh[...])[:low].astype(BF16)
-        for j in range(2):
-            lanes = slice(j * inner, (j + 1) * inner)
-            for k in range(2):
-                at = pl.multiple_of((me ^ r) * low + k * half, half)
-                out[r >> 1, 2 * j + k] = mine[k * half : (k + 1) * half, lanes]
-                out[r >> 1, 4 + 2 * j + k] = flat[pl.ds(at, half), lanes]
+    for k in range(2):
+        so[0] = (mm_at(mixed[k][...], ours[0][...]) + mm_at(mixed[2 + k][...], theirs[0][...]))[:low]
+        at = pl.multiple_of((me ^ (2 * k)) * low, low)
+        grad = jnp.concatenate([ours[2][...], theirs[2][...]], 0)
+        so[1] = mm(o2_turned[pl.ds(at, low), :], grad)
+        for i in range(2):
+            for j in range(2):
+                for out, part in ((flat_keep, bit), (flat_send, 1 - bit)):
+                    at = pl.multiple_of(part * half, half)
+                    out[k, i, j] = so[i, pl.ds(at, half), j * inner : (j + 1) * inner].astype(BF16)
 
 
 def finish_body(n, per, idx, frames, *refs):
@@ -745,65 +796,110 @@
 
 
 def place_body(idx, near, far, *outs):
-    side, level = idx[1] & 1, idx[1] >> 1
-    count, _, piece = near.shape[:3]
-    for source, half in ((near, side), (far, 1 - side)):
-        for k in range(count):
-            at = pl.multiple_of((half * count + (level ^ k)) * piece, piece)
+    side, low_bit = idx[1] & 1, (idx[1] >> 1) & 1
+    piece = near.shape[3]
+    for low, source in enumerate((near, far)):
+        for high, other in itertools.product(range(2), range(2)):
+            place = (side ^ other) * 4 + 2 * high + (low_bit ^ low)
+            at = pl.multiple_of(place * piece, piece)
             for i, out in enumerate(outs):
-                out[pl.ds(at, piece), :] = source[k, i].astype(F32)
-
-
-def place_flat_body(idx, near, far, *outs):
-    side, level = idx[1] & 1, idx[1] >> 1
-    count, piece, inner = near.shape
-    for source, half in ((near, side), (far, 1 - side)):
-        for k in range(count):
-            place = level ^ k
-            at = pl.multiple_of((place & 1) * piece, piece)
-            for i, out in enumerate(outs):
-                for j in range(2):
-
-                    @pl.when((half == i) & ((place >> 1) == j))
-                    def _(source=source, k=k, at=at, out=out, j=j):
-                        out[pl.ds(at, piece), j * inner : (j + 1) * inner] = source[k].astype(F32)
+                out[pl.ds(at, piece), :] = source[high, other, i].astype(F32)
 
 
 def place_heads_body(width, idx, near, far, *outs):
-    me, side, level = idx[0], idx[1] & 1, idx[1] >> 1
-    count, n, piece = near.shape[:3]
-    for source, half in ((near, side), (far, 1 - side)):
-        for k in range(count):
-            at = pl.multiple_of((half * count + (level ^ k)) * piece, piece)
-            heads = [source[k, me ^ h].astype(F32) for h in range(n)]
+    me, side, low_bit = idx[0], idx[1] & 1, (idx[1] >> 1) & 1
+    _, _, n, piece, _ = near.shape
+    for low, source in enumerate((near, far)):
+        for high, other in itertools.product(range(2), range(2)):
+            place = (side ^ other) * 4 + 2 * high + (low_bit ^ low)
+            at = pl.multiple_of(place * piece, piece)
+            heads = [source[high, other, me ^ h].astype(F32) for h in range(n)]
             for i, out in enumerate(outs):
                 parts = [h[:, i * width : (i + 1) * width] for h in heads]
                 out[pl.ds(at, piece), :] = jnp.concatenate(parts, 1)
 
 
-def add(*parts):
-    total = parts[0].astype(F32)
-    for part in parts[1:]:
-        total = total + part.astype(F32)
-    return total.astype(BF16)
+def place_flat_body(idx, near, far, *outs):
+    side, low_bit = idx[1] & 1, (idx[1] >> 1) & 1
+    piece, inner = near.shape[2:]
+    for source, half in ((near, side), (far, 1 - side)):
+        for high, low in itertools.product(range(2), range(2)):
+            at = pl.multiple_of((low_bit ^ low) * piece, piece)
+            for i, out in enumerate(outs):
+
+                @pl.when(half == i)
+                def _(source=source, high=high, low=low, at=at, out=out):
+                    lanes = slice(high * inner, (high + 1) * inner)
+                    out[pl.ds(at, piece), lanes] = source[high, low].astype(F32)
+
+
+def merge_body(axis, place, spread, idx, kept, moved, *outs):
+    shape = kept.shape
+    bit = None if axis is None else (idx[1] >> place) & 1
+    for at in itertools.product(*map(range, shape[:-2])):
+        if axis is not None:
+            if at[axis]:
+                continue
+            rest = at[:axis] + at[axis + 1 :]
+            for out, half in ((outs[0], bit), (outs[1], 1 - bit)):
+                here = at[:axis] + (half,) + at[axis + 1 :]
+                out[rest] = (kept[here].astype(F32) + moved[here].astype(F32)).astype(BF16)
+        elif spread:
+            here = (at[0], idx[0] ^ at[1])
+            outs[at[1]][at[0]] = (kept[here].astype(F32) + moved[here].astype(F32)).astype(BF16)
+        else:
+            outs[0][at] = (kept[at].astype(F32) + moved[at].astype(F32)).astype(BF16)
+
+
+def join_body(axis, idx, *refs):
+    out = refs[-1]
+    for i, part in enumerate(refs[:-1]):
+        for at in itertools.product(*map(range, part.shape[:-2])):
+            out[at[:axis] + (i,) + at[axis:]] = part[at]
 
 
 def pick(value, index, axis=0):
     return lax.dynamic_index_in_dim(value, index, axis, keepdims=False)
 
 
-class Links:
-    def __init__(self, window):
-        self.window = window
-        self.past = {}
-
-    def send(self, link, value, axis, bit):
-        past = self.past.setdefault(link, [])
-        if len(past) >= self.window:
-            value = after(value, past[-self.window])
-        got = flip(value, axis, bit)
-        past.append(got)
-        return got
+class Steps:
+    def __init__(self, idx):
+        self.idx, self.last = idx, ()
+
+    def call(self, body, name, out_shape, operands, scratch=(), limit_mb=12):
+        def marked(idx, *refs):
+            ends = len(operands) + len(out_shape)
+            body(idx, *refs[:ends], *refs[ends + 1 :])
+            refs[ends][...] = jnp.zeros(refs[ends].shape, F32)
+
+        *outs, mark = wide_call(
+            marked,
+            name,
+            list(out_shape) + [struct(8, 128, dtype=F32)],
+            list(scratch),
+            limit_mb,
+            0,
+            len(operands) + 1,
+            0,
+            self.last,
+        )(self.idx, *operands)
+        self.last = (mark,)
+        return outs
+
+    def merge(self, kept, moved, axis=None, place=0, spread=False):
+        shape = kept.shape
+        if axis is not None:
+            shapes = [shape[:axis] + shape[axis + 1 :]] * 2
+        else:
+            shapes = [shape[:1] + shape[2:]] * shape[1] if spread else [shape]
+        body = functools.partial(merge_body, axis, place, spread)
+        outs = self.call(body, "merge", [struct(*one) for one in shapes], [kept, moved])
+        return outs if len(outs) > 1 else outs[0]
+
+    def join(self, *parts, axis=0):
+        shape = parts[0].shape
+        shape = shape[:axis] + (len(parts),) + shape[axis:]
+        return self.call(functools.partial(join_body, axis), "join", [struct(*shape)], parts)[0]
 
 
 def per_device(
@@ -838,7 +934,7 @@
     token_rows = n * few
     count, piece = clips // 2, depth // clips
     frames = frames_in.reshape(rows, dim)
-    links = Links(2)
+    steps = Steps(idx)
 
     def exchange(parts):
         return [parts[0]] + [flip(parts[r], "frame", r) for r in range(1, n)]
@@ -847,63 +943,54 @@
         far = flip(value, "frame", 2)
         return [value, flip(value, "frame", 1), far, flip(far, "frame", 1)]
 
-    own, near, far_pack, quarter = wide_call(
-        functools.partial(pack_body, HEADS),
+    others = (time_query, time_key, time_value, space_output, time_output)
+    own, near, far_pack, first, grad_own, grad_near, across = wide_call(
+        functools.partial(pack_body, HEADS, n, per),
         "pack_heads",
         [
             struct(depth, room),
             struct(depth, room),
             struct(2, depth // 2, room),
             struct(3 * depth // 4 + low, inner),
+            struct(few, dim),
+            struct(few + share, dim),
+            struct(2 * few + share, dim),
         ],
         [pltpu.VMEM((HEADS, depth, room), BF16)]
         + [pltpu.VMEM((depth, inner), BF16)] * 6
         + [pltpu.VMEM((low, dim), BF16)] * 2
-        + [pltpu.SemaphoreType.DMA((8,))],
+        + [
+            pltpu.VMEM((rows, dim), BF16),
+            pltpu.VMEM((share, dim), BF16),
+            pltpu.VMEM((rows, dim), F32),
+            pltpu.VMEM((few, dim), F32),
+            pltpu.SemaphoreType.DMA((10,)),
+        ],
         60,
         0,
-        9,
-        8,
-    )(idx, space_query, space_key, space_value, time_query, time_key, time_value, space_output, time_output)
+        11,
+        10,
+    )(idx, space_query, space_key, space_value, *others, out_grad.reshape(rows, dim), ref_feats[0])
+    first = flip(first, "frame", 2)
     far_pack = flip(far_pack, "frame", 2)
-    first = flip(quarter, "frame", 2)
     far_frames = flip(after(frames, far_pack), "frame", 2)
-    all_refer = gather(ref_feats[0])
+    across = flip(after(across, far_pack), "frame", 2)
     side_pack = flip(far_pack, "clip", 1)
-    packs = [own, flip(near, "frame", 1), far_pack, side_pack]
-    packs = packs + [flip(p, "frame", 1) for p in packs[2:]]
     second, third = flip(first, "clip", 1), flip(first, "clip", 2)
-    far = [first, second, third, flip(second, "clip", 2)]
-    far_frames = after(far_frames, second, third)
-    all_frames = [frames, flip(frames, "frame", 1), far_frames, flip(far_frames, "frame", 1)]
-    far = far + [flip(p, "frame", 1) for p in far]
-    block, grad_own, grad_near, across = wide_call(
-        functools.partial(block_body, n, per),
-        "weight_block",
-        [struct(3 * depth + 4 * low, inner)] + [struct(few, dim)] * 2 + [struct(2, few, dim)],
-        [pltpu.VMEM((rows, dim), BF16)]
-        + [pltpu.VMEM((depth, inner), BF16)] * 3
-        + [pltpu.VMEM((low, dim), BF16)] * 2
-        + [pltpu.VMEM((rows, dim), F32), pltpu.VMEM((few, dim), F32), pltpu.SemaphoreType.DMA((6,))],
-        60,
-        0,
-        7,
-        6,
-    )(idx, after(out_grad.reshape(rows, dim), own), time_query, time_key, time_value, space_output, time_output)
-    blocks = [block, flip(block, "frame", 1)] + far
-    across = flip(after(across, first), "frame", 2)
-    token_grad = [grad_own, flip(grad_near, "frame", 1), across, flip(across, "frame", 1)]
-    token_frames = jnp.concatenate(
-        [
-            lax.dynamic_slice_in_dim(f.reshape(per, tokens, dim), me * share, share, 1).reshape(few, dim)
-            for f in all_frames
-        ],
-        0,
-    )
+    near, grad_near, near_frames = (flip(v, "frame", 1) for v in (near, grad_near, frames))
+    packs = [own, near, far_pack, side_pack, flip(far_pack, "frame", 1), flip(side_pack, "frame", 1)]
+    all_frames = [frames, near_frames, far_frames, flip(far_frames, "frame", 1)]
+    across_near = flip(across, "frame", 1)
+    all_refer = [ref_feats[0], grad_near, across, across_near]
+    token_grad = [grad_own, grad_near, across, across_near]
+    far = [first, second, third]
+    far_near = [flip(p, "frame", 1) for p in far]
+    others_near = [flip(p, "frame", 1) for p in others]
     frame_ids = jnp.concatenate([(me ^ r) * per + jnp.arange(per) for r in range(n)])
     table = position_rows(frame_ids, dim)
 
-    x_all, w_all, q_all, k_all, v_all, probs, mixed = wide_call(
+    cut = 3 * depth // 4
+    x_all, w_all, q_all, k_all, v_all, probs, *mixed, token_frames, tall_part, flat_part = wide_call(
         functools.partial(spatial_forward_body, n, tokens, width),
         "spatial_forward",
         [
@@ -913,27 +1000,40 @@
             struct(total + tokens, lanes),
             struct(total + tokens, lanes),
             struct(total, 2 * tokens, dtype=F32),
-            struct(n, token_rows, lanes),
+            *[struct(token_rows, lanes)] * n,
+            struct(token_rows, dim),
+            struct(cut, inner),
+            struct(low, inner),
         ],
         [
             pltpu.VMEM((total, lanes), F32),
             pltpu.VMEM((token_rows, lanes), F32),
             pltpu.VMEM((tokens, dim), F32),
-        ],
-        26,
+            pltpu.VMEM((rows, dim), F32),
+            pltpu.VMEM((token_rows, dim), F32),
+            pltpu.SemaphoreType.DMA((2 * n + 8,)),
+        ]
+        + [pltpu.VMEM((rows, dim), BF16)] * n
+        + [pltpu.VMEM(one.shape, BF16) for one in all_refer]
+        + [pltpu.VMEM((depth, room), BF16)] * 2
+        + [pltpu.VMEM((2, depth // 2, room), BF16)] * 4
+        + [pltpu.VMEM((cut + low, inner), BF16)] * 2,
+        60,
         2_000_000_000,
-        2 * n + 7,
-    )(idx, *all_frames, *all_refer, *packs)
-    mixed = exchange(list(after([mixed[r] for r in range(n)], across)))
-
+        2 * n + 9,
+        2 * n + 8,
+        (*far_near, *others_near),
+    )(idx, *all_frames, *all_refer, *packs, second, third)
+    mixed = exchange(mixed)
+    fourth = [flip(tall_part, "clip", 1), flip(flat_part, "clip", 2)]
+    fourth_near = [flip(p, "frame", 1) for p in fourth]
+    blocks = [*others, *others_near, *far, *fourth, *far_near, *fourth_near]
     outs = wide_call(
         functools.partial(temporal_body, n, HEADS, per),
         "temporal",
         [struct(token_rows, lanes)] * n
         + [struct(2 * few, dim)] * n
-        + [struct(token_rows, dim)] * 2
-        + [struct(token_rows, inner)] * 4
-        + [struct(token_rows, dim)],
+        + [struct(token_rows, 3 * dim + 4 * inner + 2 * lanes)],
         [
             pltpu.VMEM((n, lanes, dim), BF16),
             pltpu.VMEM((dim, inner), BF16),
@@ -946,29 +1046,41 @@
             pltpu.VMEM((token_rows, dim), F32),
             pltpu.VMEM((HEADS * token_rows, inner), BF16),
             pltpu.VMEM((HEADS * token_rows, inner), BF16),
+        ]
+        + [pltpu.VMEM((token_rows, lanes), BF16)] * n
+        + [
+            pltpu.VMEM((token_rows, dim), BF16),
+            pltpu.VMEM(table.shape, F32),
+            pltpu.SemaphoreType.DMA((60,)),
         ],
-        36,
+        60,
         5_000_000_000,
-        2 * n + 13,
+        2 * n + 23,
+        2 * n + 22,
     )(idx, *mixed, *blocks, token_frames, *token_grad, table)
     mixed_grads = exchange(list(outs[:n]))
     backs = outs[n : 2 * n]
-    hidden_grad, n2, gq, gk, gv, o2, token_grad = outs[2 * n :]
-
+
+    ours = outs[2 * n]
     keep_tall, send_tall, keep_flat, send_flat = wide_call(
         functools.partial(terms_body, n),
         "temporal_terms",
-        [struct(n // 2, clips, 3, piece, inner)] * 2 + [struct(n // 2, clips, low // 2, inner)] * 2,
-        [pltpu.VMEM((dim, inner), F32), pltpu.VMEM((inner, dim), BF16)],
-        26,
-        3_000_000_000,
-        n + 8,
-    )(idx, *mixed, hidden_grad, n2, gq, gk, gv, o2, token_grad)
-
-    tall = add(keep_tall, flip(send_tall, "frame", 1))
-    flat = add(keep_flat, flip(send_flat, "frame", 1))
-    backs = exchange([backs[0]] + [after(t, mixed_grads[2]) for t in backs[1:]])
-    mixed_grads[1] = after(mixed_grads[1], tall, flat)
+        [struct(clips, 3, piece, inner)] * 2 + [struct(2, 2, 2, low // 2, inner)] * 2,
+        [
+            pltpu.VMEM((dim, 2 * token_rows), BF16),
+            pltpu.VMEM((inner, 2 * token_rows), BF16),
+            pltpu.VMEM((depth, inner), F32),
+            pltpu.VMEM((2, low, dim), F32),
+        ],
+        18,
+        1,
+        5,
+        0,
+        tuple(mixed_grads[1:]),
+    )(idx, ours, flip(ours, "frame", 1), mixed[0], mixed[2])
+    flat_a = flip(send_flat, "clip", 2)
+    tall_y = flip(send_tall, "frame", 2)
+
     keep_out, send_out, keep_term, send_term = wide_call(
         functools.partial(spatial_backward_body, n, tokens, width),
         "spatial_backward",
@@ -979,72 +1091,67 @@
             pltpu.VMEM((total + tokens, room), BF16),
             pltpu.VMEM((dim, room), F32),
         ],
-        26,
-        4_000_000_000,
+        20,
+        1,
         n + 7,
+        0,
+        (send_flat, send_tall),
     )(idx, *mixed_grads, x_all, w_all, q_all, k_all, v_all, probs)
 
-    def over_x(value):
-        moved = links.send("x", pick(value, 1 - side), "clip", 1)
-        return add(pick(value, side), moved)
-
-    def over_y(value):
-        return add(value[0], links.send("y", value[1], "frame", 2))
-
-    def over_z(value):
-        moved = [links.send(f"z{k}", pick(value, level ^ k), "clip", 2 * k) for k in range(1, count)]
-        return add(pick(value, level), *moved)
-
-    def spread_z(value):
-        return jnp.stack([value] + [links.send(f"z{k}", value, "clip", 2 * k) for k in range(1, count)])
-
-    def spread_x(value):
-        return value, links.send("x", value, "clip", 1)
-
-    bit = level & 1
-    flat = flat.reshape(n // 2, 2, 2, 2, low // 2, inner)
-    flat = add(pick(flat, bit, 3), links.send("z1", pick(flat, 1 - bit, 3), "clip", 2))
-    tall = over_y(tall).reshape(2, count, 3, piece, inner)
-    head = add(keep_term, links.send("x", send_term, "clip", 1))
-    flat = over_y(flat)
-    head = over_z(head)
-    tall = over_x(tall)
-    flat = over_x(flat)
-    head = jnp.stack(exchange([pick(head, me ^ r) for r in range(n)]))
-    high = level >> 1
-    flat = add(pick(flat, high), links.send("z2", pick(flat, 1 - high), "clip", 4))
-    tall = over_z(tall)
-    near = add(keep_out, flip(send_out, "frame", 1))
-    head = after(head, near, *backs)
-    partial_far = flip(near[1], "frame", 2)
-    head = spread_z(head)
-    flat = spread_z(flat)
-    tall = spread_z(after(tall, partial_far))
-    head = spread_x(head)
-    flat = spread_x(flat)
-    tall = spread_x(tall)
-
-    output, frames_grad, refer_grad = wide_call(
+    def to_clip(value, bit):
+        return flip(value, "clip", bit)
+
+    head_got = to_clip(send_term, 1)
+    out_got = flip(send_out, "frame", 1)
+    flat, flat_out = steps.merge(keep_flat, flat_a, 0, 7)
+    halves = (2, 2, 2, 3, piece, inner)
+    tall, tall_out = steps.merge(keep_tall.reshape(halves), tall_y.reshape(halves), 0, 0)
+    tall_got = to_clip(tall_out, 1)
+    flat_got = flip(flat_out, "frame", 2)
+    halves = (2, 2, n, piece, room)
+    head, head_out = steps.merge(keep_term.reshape(halves), head_got.reshape(halves), 1, 1)
+    head_got = to_clip(head_out, 2)
+    partial, partial_out = steps.merge(keep_out, out_got, 0, 7)
+    head = steps.merge(head, head_got)
+    head_got = to_clip(head, 4)
+    flat, flat_out = steps.merge(flat, flat_got, 0, 0)
+    flat_got = to_clip(flat_out, 1)
+    tall, tall_out = steps.merge(tall, tall_got, 1, 1)
+    tall_got = to_clip(tall_out, 2)
+    head_f = exchange(steps.merge(head, head_got, spread=True))
+    flat = steps.merge(flat, flat_got)
+    flat_got = to_clip(flat, 4)
+    tall = steps.merge(tall, tall_got)
+    tall_got = to_clip(tall, 4)
+    head = steps.join(*head_f, axis=1)
+    head_got = to_clip(head, 1)
+    backs = exchange(list(backs))
+    partial_got = flip(partial_out, "frame", 2)
+    head = steps.join(head, head_got, axis=1)
+    head_got = to_clip(head, 2)
+    output, frames_grad, refer_grad = steps.call(
         functools.partial(finish_body, n, per),
         "finish",
         [struct(rows, dim)] * 2 + [struct(share, dim)],
+        [frames, *backs, partial, partial_got],
         [pltpu.VMEM((2 * few, dim), F32), pltpu.VMEM((2, rows, dim), F32)],
-        16,
-        0,
-        n + 4,
-    )(idx, frames, *backs, near[0], partial_far)
-
-    head_grads = wide_call(
+    )
+    flat = steps.merge(flat, flat_got)
+    flat_got = to_clip(flat, 2)
+    tall = steps.merge(tall, tall_got)
+    tall_got = to_clip(tall, 1)
+    head_grads = steps.call(
         functools.partial(place_heads_body, width),
         "place_heads",
         [struct(depth, inner, dtype=F32)] * 3,
-        [],
-        24,
-        0,
-        3,
-    )(idx, *head)
-    tall_grads = wide_call(place_body, "place_tall", [struct(depth, inner, dtype=F32)] * 3, [], 24, 0, 3)(idx, *tall)
-    flat_grads = wide_call(place_flat_body, "place_flat", [struct(low, dim, dtype=F32)] * 2, [], 24, 0, 3)(idx, *flat)
+        [head, head_got],
+    )
+    flat = steps.join(flat, flat_got, axis=1)
+    flat_got = to_clip(flat, 1)
+    tall = steps.join(tall, tall_got, axis=1)
+    tall_got = to_clip(tall, 2)
+    flat_grads = steps.call(place_flat_body, "place_flat", [struct(low, dim, dtype=F32)] * 2, [flat, flat_got])
+    tall_grads = steps.call(place_body, "place_tall", [struct(depth, inner, dtype=F32)] * 3, [tall, tall_got])
     return (
         output.reshape(frames_in.shape),
         frames_grad.reshape(frames_in.shape),

time: 261 us -> 239 us (0.916); the launches traced: 258 us -> 239 us
  starting transfers between devices: 60.8 us -> 43.8 us
  other arithmetic: 11.1 us -> 1.6 us
  local copies, waits for them, and re-layouts: 15 us -> 6.18 us
  Pallas kernels: 55.3 us -> 64 us
  waiting for transfers between devices: 114 us -> 122 us
    ppermute x64 -> x58, starting transfers between devices: 60.8 us -> 43.8 us  [flip(): return lax.ppermute(value, axis, [(i, i ^ bit) for i in range(size)])]
    convert_element_type x12 -> x0, other arithmetic: 9.89 us -> none  [add(): return total.astype(BF16)]
    pallas_call x10 -> x25, Pallas kernels: 55.3 us -> 64 us  [wide_call(): return lambda *operands: call(*operands, *late)]
    ppermute x64 -> x58, waiting for transfers between devices: 114 us -> 122 us  [flip(): return lax.ppermute(value, axis, [(i, i ^ bit) for i in range(size)])]
    unnamed x86 -> x90, local copies, waits for them, and re-layouts: 11.9 us -> 6.18 us
    squeeze x10 -> x0, local copies, waits for them, and re-layouts: 3.05 us -> none  [the longest x6 2 us: pick(): return lax.dynamic_index_in_dim(value, index, axis, keepdims=False)]
  transfers between devices with their start and end apart: 64 -> 58, of which waited for: 23 -> 26; matrix products, arithmetic and copies ran while one was open for 5% -> 0% of each run, Pallas kernels for 11% -> 10%
where the time goes in v3:
time: 239 us
  waiting for transfers between devices  122 us (51%)
  Pallas kernels  64 us (27%)
  starting transfers between devices  43.8 us (18%)
  local copies, waits for them, and re-layouts  6.18 us (3%)
    ppermute x58, waiting for transfers between devices, flip(): return lax.ppermute(value, axis, [(i, i ^ bit) for i in range(size)])  122 us
    pallas_call x25, Pallas kernels, wide_call(): return lambda *operands: call(*operands, *late)  64 us
    ppermute x58, starting transfers between devices, flip(): return lax.ppermute(value, axis, [(i, i ^ bit) for i in range(size)])  43.8 us
    unnamed x90, local copies, waits for them, and re-layouts  6.18 us
  transfers between devices with their start and end apart: 58, of which 26 were waited for; matrix products, arithmetic and copies ran while one was open for 0% of the time, Pallas kernels for 10%

profile of v3, /device:TPU:0, one launch (start us, length us, event | category | flops | bytes accessed | tf_op | source)
XLA Modules:
  0.0 238.7 jit_solution(5614256320162952168)
XLA Ops:
  1.3 4.3 %pack_heads.1 = (bf16[320,512]{1,0:T(8,128)(2,1)}, bf16[320,512]{1,0:T(8,128)(2,1)}, bf16[2,160,512]{2,1,0:T(8,128)(2,1)}, bf16[400,640]{1,0:T(8,128)(2,1)}, bf1...) custom-call(s32[2]{0:T(128)} %pad_add_fusion.idx, bf16[320,640]{1,0:T(8,128)(2,1)} %refs_0_.1, ...), custom_call_target="tpu_custom_call" | custom-call | flops 1 | bytes 1 | tf_op jit(solution)/shard_map/pack_heads/pallas_call | solution.py:357
  5.6 3.0 %collective-permute-start.1 = (bf16[2,160,512]{2,1,0:T(8,128)(2,1)}, bf16[2,160,512]{2,1,0:T(8,128)(2,1)S(1)}, u32[]{:S(2)}, u32[]{:S(2)}) collective-permute-start(bf16[2,160,512]{2,1,0:T(8,128)(2,1)} %get-tuple-element.105), channel_id=1, source_target_pairs={{0,2},{1,3},{2,0},{3,1},{4,6},{5,7},{6,4},{7,5},{8,10},{9,11},{10,... | collective-permute-start | bytes 983048 | tf_op jit(solution)/shard_map/ppermute | solution.py:366
  9.7 2.0 collective-permute-done.4.refs_5_.refs_26_
  12.1 4.5 %collective-permute-done.1.refs_10_ = bf16[2,160,512]{2,1,0:T(8,128)(2,1)S(1)} collective-permute-done((bf16[2,160,512]{2,1,0:T(8,128)(2,1)}, bf16[2,160,512]{2,1,0:T(8,128)(2,1)S(1)}, u32[]{:S(2)}, u32[]{:S(2)}) %collective-permute-start.1) | collective-permute-done | bytes 327712 | tf_op jit(solution)/shard_map/ppermute | solution.py:366
  16.6 1.7 collective-permute-start.11
  19.5 12.0 %collective-permute-done.11.refs_14_ = bf16[400,640]{1,0:T(8,128)(2,1)} collective-permute-done((bf16[400,640]{1,0:T(8,128)(2,1)}, bf16[400,640]{1,0:T(8,128)(2,1)}, u32[]{:S(2)}, u32[]{:S(2)}) %collective-permute-start.11) | collective-permute-done | bytes 512032 | tf_op jit(solution)/shard_map/ppermute | solution.py:366
  31.5 1.8 collective-permute-start.13
  33.3 1.5 collective-permute-start.12
  34.8 1.5 collective-permute-start.2
  36.3 1.7 collective-permute-done.5.refs_6_.refs_27_
  38.0 1.7 collective-permute-start.8
  39.7 0.7 copy-done.33
  40.4 9.5 %collective-permute-done.8.refs_11_ = bf16[2,160,512]{2,1,0:T(8,128)(2,1)} collective-permute-done((bf16[2,160,512]{2,1,0:T(8,128)(2,1)S(1)}, bf16[2,160,512]{2,1,0:T(8,128)(2,1)}, u32[]{:S(2)}, u32[]{:S(2)}) %collective-permute-start.8) | collective-permute-done | bytes 327712 | tf_op jit(solution)/shard_map/ppermute | solution.py:366
  51.1 0.7 copy-done.35
  51.9 2.9 %collective-permute-done.10.refs_13_ = bf16[2,160,512]{2,1,0:T(8,128)(2,1)} collective-permute-done((bf16[2,160,512]{2,1,0:T(8,128)(2,1)}, bf16[2,160,512]{2,1,0:T(8,128)(2,1)}, u32[]{:S(2)}, u32[]{:S(2)}) %collective-permute-start.10) | collective-permute-done | bytes 327712 | tf_op jit(solution)/shard_map/ppermute | solution.py:366
  54.9 0.7 copy-done.17
  56.0 12.0 %spatial_forward.1 = (bf16[864,1280]{1,0:T(8,128)(2,1)}, bf16[1280,512]{1,0:T(8,128)(2,1)}, bf16[864,256]{1,0:T(8,128)(2,1)}, bf16[864,256]{1,0:T(8,128)(2,1)}, ...) custom-call(s32[2]{0:T(128)} %pad_add_fusion.idx, ...), custom_call_target="tpu_custom_call" | custom-call | flops 2000000000 | bytes 8000000 | tf_op jit(solution)/shard_map/spatial_forward/pallas_call | solution.py:357
  68.1 1.6 collective-permute-start.25
  70.3 1.6 collective-permute-start.23
  72.1 4.6 %collective-permute-done.26.refs_18_ = bf16[160,640]{1,0:T(8,128)(2,1)S(1)} collective-permute-done((bf16[160,640]{1,0:T(8,128)(2,1)}, bf16[160,640]{1,0:T(8,128)(2,1)S(1)}, u32[]{:S(2)}, u32[]{:S(2)}) %collective-permute-start.26) | collective-permute-done | bytes 204832 | tf_op jit(solution)/shard_map/ppermute | solution.py:366
  76.7 1.0 collective-permute-done.25.refs_17_
  77.7 0.8 fusion.refs_29_
  78.6 0.7 collective-permute-done.27.refs_22_
  80.0 16.4 %temporal.1 = (bf16[192,256]{1,0:T(8,128)(2,1)}, bf16[192,256]{1,0:T(8,128)(2,1)}, bf16[192,256]{1,0:T(8,128)(2,1)}, bf16[192,256]{1,0:T(8,128)(2,1)}, bf16[96,1...) custom-call(s32[2]{0:T(128)} %pad_add_fusion.idx, ...), custom_call_target="tpu_custom_call" | custom-call | flops 5000000000 | bytes 8000000 | tf_op jit(solution)/shard_map/temporal/pallas_call | solution.py:357
  97.0 1.5 collective-permute-start.33
  98.6 3.3 %collective-permute-done.32.refs_4_.refs_1_ = bf16[192,256]{1,0:T(8,128)(2,1)S(1)} collective-permute-done((bf16[192,256]{1,0:T(8,128)(2,1)}, bf16[192,256]{1,0:T(8,128)(2,1)S(1)}, u32[]{:S(2)}, u32[]{:S(2)}) %collective-permute-start.32) | collective-permute-done | bytes 98336 | tf_op jit(solution)/shard_map/ppermute | solution.py:366
  102.4 1.5 collective-permute-done.34.refs_6_.refs_3_
  103.9 1.7 copy-done
  105.6 0.9 copy-done.14
  106.5 4.1 %temporal_terms.1 = (bf16[8,3,40,640]{3,2,1,0:T(8,128)(2,1)S(1)}, bf16[8,3,40,640]{3,2,1,0:T(8,128)(2,1)S(1)}, bf16[2,2,2,80,640]{4,3,2,1,0:T(8,128)(2,1)S(1)}, bf16[2,2,2,80,640]{4,3,2,1,0:T(8,128)(2,1)S(1)}) custom-call(s32[2]{0:T(128)S(1)} %copy-done.9, bf16[192,6912]{1,0:T(8,128)(2,1)S(1)} %copy-done, ...), custom_call_target="tpu_custom_call" | custom-call | flops 1 | bytes 1 | tf_op jit(solution)/shard_map/temporal_terms/pallas_call | solution.py:357
  110.6 1.1 collective-permute-start.38
  112.3 7.1 %spatial_backward.1 = (bf16[2,216,1280]{2,1,0:T(8,128)(2,1)S(1)}, bf16[2,216,1280]{2,1,0:T(8,128)(2,1)S(1)}, bf16[4,4,40,512]{3,2,1,0:T(8,128)(2,1)S(1)}, bf16[4,4,40,512]{3,2,1,0:T(8,128)(2,1)S(1)}) custom-call(s32[2]{0:T(128)S(1)} %copy-done.9, bf16[192,256]{1,0:T(8,128)(2,1)S(1)} %copy-done.11, ...), custom_call_target="tpu_custom_call" | custom-call | flops 1 | bytes 1 | tf_op jit(solution)/shard_map/spatial_backward/pallas_call | solution.py:357
  119.5 1.5 collective-permute-start.37
  121.0 11.3 %collective-permute-done.39.refs_1_ = bf16[2,2,2,80,640]{4,3,2,1,0:T(8,128)(2,1)S(1)} collective-permute-done((bf16[2,2,2,80,640]{4,3,2,1,0:T(8,128)(2,1)S(1)}, bf16[2,2,2,80,640]{4,3,2,1,0:T(8,128)(2,1)S(1)}, u32[]{:S(2)}, u32[]{:S(2)}) %collective-permute-start.39) | collective-permute-done | bytes 819232 | tf_op jit(solution)/shard_map/ppermute | solution.py:366
  132.3 0.7 merge.12
  133.0 6.8 %collective-permute-done.38 = bf16[8,3,40,640]{3,2,1,0:T(8,128)(2,1)S(1)} collective-permute-done((bf16[8,3,40,640]{3,2,1,0:T(8,128)(2,1)S(1)}, bf16[8,3,40,640]{3,2,1,0:T(8,128)(2,1)S(1)}, u32[]{:S(2)}, u32[]{:S(2)}) %collective-permute-start.38) | collective-permute-done | bytes 1228832 | tf_op jit(solution)/shard_map/ppermute | solution.py:366
  139.8 0.8 merge.13
  140.6 1.6 collective-permute-start.43
  142.2 0.7 merge.14
  143.4 1.5 collective-permute-start.44
  144.9 0.8 merge.15
  145.7 5.9 %collective-permute-done.41.refs_1_ = bf16[2,4,40,512]{3,2,1,0:T(8,128)(2,1)S(1)} collective-permute-done((bf16[2,4,40,512]{3,2,1,0:T(8,128)(2,1)S(1)}, bf16[2,4,40,512]{3,2,1,0:T(8,128)(2,1)S(1)}, u32[]{:S(2)}, u32[]{:S(2)}) %collective-permute-start.41) | collective-permute-done | bytes 327712 | tf_op jit(solution)/shard_map/ppermute | solution.py:366
  152.3 2.7 %collective-permute-start.42 = (bf16[2,4,40,512]{3,2,1,0:T(8,128)(2,1)S(1)}, bf16[2,4,40,512]{3,2,1,0:T(8,128)(2,1)S(1)}, u32[]{:S(2)}, u32[]{:S(2)}) collective-permute-start(bf16[2,4,40,512]{3,2,1,0:T(8,128)(2,1)S(1)} %get-tuple-element.152.refs_0_), channel_id=1, source_target_pairs={{0,16},{4,20},{8,24},{12,28},{16,0},{20,4},{24,8},{28,12},{1,17},{... | collective-permute-start | bytes 983048 | tf_op jit(solution)/shard_map/ppermute | solution.py:366
  155.8 0.7 merge.18
  156.5 1.4 collective-permute-start.48
  158.5 9.5 %collective-permute-done.42.refs_1_ = bf16[2,4,40,512]{3,2,1,0:T(8,128)(2,1)S(1)} collective-permute-done((bf16[2,4,40,512]{3,2,1,0:T(8,128)(2,1)S(1)}, bf16[2,4,40,512]{3,2,1,0:T(8,128)(2,1)S(1)}, u32[]{:S(2)}, u32[]{:S(2)}) %collective-permute-start.42) | collective-permute-done | bytes 327712 | tf_op jit(solution)/shard_map/ppermute | solution.py:366
  168.7 2.6 %collective-permute-start.46 = (bf16[2,40,512]{2,1,0:T(8,128)(2,1)S(1)}, bf16[2,40,512]{2,1,0:T(8,128)(2,1)S(1)}, u32[]{:S(2)}, u32[]{:S(2)}) collective-permute-start(bf16[2,40,512]{2,1,0:T(8,128)(2,1)S(1)} %get-tuple-element.162), channel_id=1, source_target_pairs={{0,2},{1,3},{2,0},{3,1},{4,6},{5,7},{6,4},{7,5},{8,10},{9,11},{10,... | collective-permute-start | bytes 245768 | tf_op jit(solution)/shard_map/ppermute | solution.py:366
  172.6 1.7 collective-permute-done.46.refs_2_
  174.3 1.5 collective-permute-done.47.refs_3_
  176.9 1.6 collective-permute-start.40
  179.0 7.1 %collective-permute-done.50.refs_1_ = bf16[2,4,40,512]{3,2,1,0:T(8,128)(2,1)S(1)} collective-permute-done((bf16[2,4,40,512]{3,2,1,0:T(8,128)(2,1)S(1)}, bf16[2,4,40,512]{3,2,1,0:T(8,128)(2,1)S(1)}, u32[]{:S(2)}, u32[]{:S(2)}) %collective-permute-start.50) | collective-permute-done | bytes 327712 | tf_op jit(solution)/shard_map/ppermute | solution.py:366
  186.8 3.1 %collective-permute-start.52 = (bf16[2,3,40,640]{3,2,1,0:T(8,128)(2,1)S(1)}, bf16[2,3,40,640]{3,2,1,0:T(8,128)(2,1)S(1)}, u32[]{:S(2)}, u32[]{:S(2)}) collective-permute-start(bf16[2,3,40,640]{3,2,1,0:T(8,128)(2,1)S(1)} %get-tuple-element.178.refs_0_), channel_id=1, source_target_pairs={{0,16},{4,20},{8,24},{12,28},{16,0},{20,4},{24,8},{28,12},{1,17},{... | collective-permute-start | bytes 921608 | tf_op jit(solution)/shard_map/ppermute | solution.py:366
  190.2 7.4 %collective-permute-done.30.refs_3_ = bf16[96,1280]{1,0:T(8,128)(2,1)S(1)} collective-permute-done((bf16[96,1280]{1,0:T(8,128)(2,1)S(1)}, bf16[96,1280]{1,0:T(8,128)(2,1)S(1)}, u32[]{:S(2)}, u32[]{:S(2)}) %collective-permute-start.30) | collective-permute-done | bytes 245792 | tf_op jit(solution)/shard_map/ppermute | solution.py:366
  197.6 3.4 %collective-permute-done.31.refs_4_ = bf16[96,1280]{1,0:T(8,128)(2,1)S(1)} collective-permute-done((bf16[96,1280]{1,0:T(8,128)(2,1)S(1)}, bf16[96,1280]{1,0:T(8,128)(2,1)S(1)}, u32[]{:S(2)}, u32[]{:S(2)}) %collective-permute-start.31) | collective-permute-done | bytes 245792 | tf_op jit(solution)/shard_map/ppermute | solution.py:366
  201.0 3.3 %finish.1 = (bf16[192,1280]{1,0:T(8,128)(2,1)}, bf16[192,1280]{1,0:T(8,128)(2,1)}, bf16[24,1280]{1,0:T(8,128)(2,1)}, f32[8,128]{1,0:T(8,128)S(1)}) custom-call(s32[2]{0:T(128)S(1)} %copy-done.9, bf16[192,1280]{1,0:T(8,128)(2,1)S(1)} %bitcast.15, bf16[96,1280]{1,0:T(8,128)(2,1)S(1)} %copy-done.10, bf16[96,1280]{1,0:T(8,128)(2,1)S(1)} %collective-permute-done.29.refs_2_, ...), custom_call_target="tpu_custom_call" | custom-call | flops 1 | bytes 1 | tf_op jit(solution)/shard_map/finish/pallas_call | solution.py:357
  204.3 10.9 %collective-permute-done.53.refs_1_ = bf16[2,80,640]{2,1,0:T(8,128)(2,1)S(1)} collective-permute-done((bf16[2,80,640]{2,1,0:T(8,128)(2,1)S(1)}, bf16[2,80,640]{2,1,0:T(8,128)(2,1)S(1)}, u32[]{:S(2)}, u32[]{:S(2)}) %collective-permute-start.53) | collective-permute-done | bytes 204832 | tf_op jit(solution)/shard_map/ppermute | solution.py:366
  216.4 1.1 collective-permute-start.56
  217.5 2.4 %place_heads.1 = (f32[320,640]{1,0:T(8,128)}, f32[320,640]{1,0:T(8,128)}, f32[320,640]{1,0:T(8,128)}, f32[8,128]{1,0:T(8,128)S(1)}) custom-call(s32[2]{0:T(128)S(1)} %copy-done.9, bf16[2,2,4,40,512]{4,3,2,1,0:T(8,128)(2,1)S(1)} %get-tuple-element.177.refs_0_, bf16[2,2,4,40,512]{4,3,2,1,0:T(8,128)(2,1)S(1)} %collective-permute-done.51.refs_1_, ...), custom_call_target="tpu_custom_call" | custom-call | flops 1 | bytes 1 | tf_op jit(solution)/shard_map/place_heads/pallas_call | solution.py:357
  219.9 3.3 %collective-permute-done.54.refs_1_ = bf16[2,80,640]{2,1,0:T(8,128)(2,1)S(1)} collective-permute-done((bf16[2,80,640]{2,1,0:T(8,128)(2,1)S(1)}, bf16[2,80,640]{2,1,0:T(8,128)(2,1)S(1)}, u32[]{:S(2)}, u32[]{:S(2)}) %collective-permute-start.54) | collective-permute-done | bytes 204832 | tf_op jit(solution)/shard_map/ppermute | solution.py:366
  224.9 1.1 collective-permute-start.55
  225.9 7.7 %collective-permute-done.55.refs_1_ = bf16[2,2,80,640]{3,2,1,0:T(8,128)(2,1)S(1)} collective-permute-done((bf16[2,2,80,640]{3,2,1,0:T(8,128)(2,1)S(1)}, bf16[2,2,80,640]{3,2,1,0:T(8,128)(2,1)S(1)}, u32[]{:S(2)}, u32[]{:S(2)}) %collective-permute-start.55) | collective-permute-done | bytes 409632 | tf_op jit(solution)/shard_map/ppermute | solution.py:366
  233.7 1.9 place_flat.1
  235.5 1.1 collective-permute-done.57.refs_1_
  236.6 2.1 place_tall.1
  (174 shorter events, 18.4 us)
Async XLA Ops:
  5.6 11.0 %collective-permute-start.1 = (bf16[2,160,512]{2,1,0:T(8,128)(2,1)}, bf16[2,160,512]{2,1,0:T(8,128)(2,1)S(1)}, u32[]{:S(2)}, u32[]{:S(2)}) collective-permute-start(bf16[2,160,512]{2,1,0:T(8,128)(2,1)} %get-tuple-element.105), channel_id=1, source_target_pairs={{0,2},{1,3},{2,0},{3,1},{4,6},{5,7},{6,4},{7,5},{8,10},{9,11},{10,... | collective-permute-start | bytes 983048 | tf_op jit(solution)/shard_map/ppermute | solution.py:366
  8.7 9.7 %collective-permute-start.20 = (bf16[160,1280]{1,0:T(8,128)(2,1)S(1)}, bf16[160,1280]{1,0:T(8,128)(2,1)S(1)}, u32[]{:S(2)}, u32[]{:S(2)}) collective-permute-start(bf16[160,1280]{1,0:T(8,128)(2,1)S(1)} %copy-done.25), channel_id=1, source_target_pairs={{0,1},{1,0},{2,3},{3,2},{4,5},{5,4},{6,7},{7,6},{8,9},{9,8},{10,11... | collective-permute-start | bytes 1228808 | tf_op jit(solution)/shard_map/ppermute | solution.py:366
  8.7 10.4 %collective-permute-start.17 = (bf16[320,640]{1,0:T(8,128)(2,1)S(1)}, bf16[320,640]{1,0:T(8,128)(2,1)S(1)}, u32[]{:S(2)}, u32[]{:S(2)}) collective-permute-start(bf16[320,640]{1,0:T(8,128)(2,1)S(1)} %copy-done.22), channel_id=1, source_target_pairs={{0,1},{1,0},{2,3},{3,2},{4,5},{5,4},{6,7},{7,6},{8,9},{9,8},{10,11... | collective-permute-start | bytes 1228808 | tf_op jit(solution)/shard_map/ppermute | solution.py:366
  9.2 9.2 %collective-permute-start.7 = (bf16[320,512]{1,0:T(8,128)(2,1)}, bf16[320,512]{1,0:T(8,128)(2,1)S(1)}, u32[]{:S(2)}, u32[]{:S(2)}) collective-permute-start(bf16[320,512]{1,0:T(8,128)(2,1)} %get-tuple-element.111), channel_id=1, source_target_pairs={{0,1},{1,0},{2,3},{3,2},{4,5},{5,4},{6,7},{7,6},{8,9},{9,8},{10,11... | collective-permute-start | bytes 983048 | tf_op jit(solution)/shard_map/ppermute | solution.py:366
  9.2 2.5 %collective-permute-start.4 = (bf16[72,1280]{1,0:T(8,128)(2,1)}, bf16[72,1280]{1,0:T(8,128)(2,1)}, u32[]{:S(2)}, u32[]{:S(2)}) collective-permute-start(bf16[72,1280]{1,0:T(8,128)(2,1)} %get-tuple-element.107), channel_id=1, source_target_pairs={{0,1},{1,0},{2,3},{3,2},{4,5},{5,4},{6,7},{7,6},{8,9},{9,8},{10,11... | collective-permute-start | bytes 552968 | tf_op jit(solution)/shard_map/ppermute | solution.py:366
  11.7 7.4 %collective-permute-start.18 = (bf16[320,640]{1,0:T(8,128)(2,1)S(1)}, bf16[320,640]{1,0:T(8,128)(2,1)S(1)}, u32[]{:S(2)}, u32[]{:S(2)}) collective-permute-start(bf16[320,640]{1,0:T(8,128)(2,1)S(1)} %copy-done.23), channel_id=1, source_target_pairs={{0,1},{1,0},{2,3},{3,2},{4,5},{5,4},{6,7},{7,6},{8,9},{9,8},{10,11... | collective-permute-start | bytes 1228808 | tf_op jit(solution)/shard_map/ppermute | solution.py:366
  16.6 34.5 %copy-start.31 = (bf16[2,160,512]{2,1,0:T(8,128)(2,1)}, bf16[2,160,512]{2,1,0:T(8,128)(2,1)S(1)}, u32[]{:S(2)}) copy-start(bf16[2,160,512]{2,1,0:T(8,128)(2,1)S(1)} %collective-permute-done.1.refs_10_) | copy-start | bytes 983044
  16.6 14.9 %collective-permute-start.11 = (bf16[400,640]{1,0:T(8,128)(2,1)}, bf16[400,640]{1,0:T(8,128)(2,1)}, u32[]{:S(2)}, u32[]{:S(2)}) collective-permute-start(bf16[400,640]{1,0:T(8,128)(2,1)} %get-tuple-element.112), channel_id=1, source_target_pairs={{0,2},{1,3},{2,0},{3,1},{4,6},{5,7},{6,4},{7,5},{8,10},{9,11},{10,... | collective-permute-start | bytes 1536008 | tf_op jit(solution)/shard_map/ppermute | solution.py:366
  18.3 18.0 %collective-permute-start = (bf16[192,1280]{1,0:T(8,128)(2,1)S(1)}, bf16[192,1280]{1,0:T(8,128)(2,1)S(1)}, u32[]{:S(2)}, u32[]{:S(2)}) collective-permute-start(bf16[192,1280]{1,0:T(8,128)(2,1)S(1)} %bitcast.13), channel_id=1, source_target_pairs={{0,1},{1,0},{2,3},{3,2},{4,5},{5,4},{6,7},{7,6},{8,9},{9,8},{10,11... | collective-permute-start | bytes 1474568 | tf_op jit(solution)/shard_map/ppermute | solution.py:366
  18.4 31.5 %copy-start.27 = (bf16[160,1280]{1,0:T(8,128)(2,1)}, bf16[160,1280]{1,0:T(8,128)(2,1)S(1)}, u32[]{:S(2)}) copy-start(bf16[160,1280]{1,0:T(8,128)(2,1)S(1)} %collective-permute-done.20.refs_22_.refs_12_) | copy-start | bytes 1228804
  18.4 14.9 %collective-permute-start.19 = (bf16[320,640]{1,0:T(8,128)(2,1)S(1)}, bf16[320,640]{1,0:T(8,128)(2,1)}, u32[]{:S(2)}, u32[]{:S(2)}) collective-permute-start(bf16[320,640]{1,0:T(8,128)(2,1)S(1)} %copy-done.24), channel_id=1, source_target_pairs={{0,1},{1,0},{2,3},{3,2},{4,5},{5,4},{6,7},{7,6},{8,9},{9,8},{10,11... | collective-permute-start | bytes 1228808 | tf_op jit(solution)/shard_map/ppermute | solution.py:366
  19.1 31.4 %copy-start.28 = (bf16[320,640]{1,0:T(8,128)(2,1)}, bf16[320,640]{1,0:T(8,128)(2,1)S(1)}, u32[]{:S(2)}) copy-start(bf16[320,640]{1,0:T(8,128)(2,1)S(1)} %collective-permute-done.17.refs_19_.refs_9_) | copy-start | bytes 1228804
  19.1 15.7 %collective-permute-start.21 = (bf16[160,1280]{1,0:T(8,128)(2,1)S(1)}, bf16[160,1280]{1,0:T(8,128)(2,1)S(1)}, u32[]{:S(2)}, u32[]{:S(2)}) collective-permute-start(bf16[160,1280]{1,0:T(8,128)(2,1)S(1)} %copy-done.26), channel_id=1, source_target_pairs={{0,1},{1,0},{2,3},{3,2},{4,5},{5,4},{6,7},{7,6},{8,9},{9,8},{10,11... | collective-permute-start | bytes 1228808 | tf_op jit(solution)/shard_map/ppermute | solution.py:366
  19.1 31.4 %copy-start.29 = (bf16[320,640]{1,0:T(8,128)(2,1)}, bf16[320,640]{1,0:T(8,128)(2,1)S(1)}, u32[]{:S(2)}) copy-start(bf16[320,640]{1,0:T(8,128)(2,1)S(1)} %collective-permute-done.18.refs_20_.refs_10_) | copy-start | bytes 1228804
  19.2 18.8 %collective-permute-start.5 = (bf16[120,1280]{1,0:T(8,128)(2,1)}, bf16[120,1280]{1,0:T(8,128)(2,1)S(1)}, u32[]{:S(2)}, u32[]{:S(2)}) collective-permute-start(bf16[120,1280]{1,0:T(8,128)(2,1)} %get-tuple-element.109), channel_id=1, source_target_pairs={{0,2},{1,3},{2,0},{3,1},{4,6},{5,7},{6,4},{7,5},{8,10},{9,11},{10,... | collective-permute-start | bytes 921608 | tf_op jit(solution)/shard_map/ppermute | solution.py:366
  31.5 18.4 %collective-permute-start.13 = (bf16[400,640]{1,0:T(8,128)(2,1)}, bf16[400,640]{1,0:T(8,128)(2,1)S(1)}, u32[]{:S(2)}, u32[]{:S(2)}) collective-permute-start(bf16[400,640]{1,0:T(8,128)(2,1)} %collective-permute-done.11.refs_14_), channel_id=1, source_target_pairs={{0,8},{4,12},{8,0},{12,4},{16,24},{20,28},{24,16},{28,20},{1,9},{5... | collective-permute-start | bytes 1536008 | tf_op jit(solution)/shard_map/ppermute | solution.py:366
  33.3 17.2 %collective-permute-start.12 = (bf16[400,640]{1,0:T(8,128)(2,1)}, bf16[400,640]{1,0:T(8,128)(2,1)S(1)}, u32[]{:S(2)}, u32[]{:S(2)}) collective-permute-start(bf16[400,640]{1,0:T(8,128)(2,1)} %collective-permute-done.11.refs_14_), channel_id=1, source_target_pairs={{0,4},{4,0},{8,12},{12,8},{16,20},{20,16},{24,28},{28,24},{1,5},{5... | collective-permute-start | bytes 1536008 | tf_op jit(solution)/shard_map/ppermute | solution.py:366
  34.8 15.8 %collective-permute-start.2 = (bf16[192,1280]{1,0:T(8,128)(2,1)S(1)}, bf16[192,1280]{1,0:T(8,128)(2,1)}, u32[]{:S(2)}, u32[]{:S(2)}) collective-permute-start(bf16[192,1280]{1,0:T(8,128)(2,1)S(1)} %bitcast.14), channel_id=1, source_target_pairs={{0,2},{1,3},{2,0},{3,1},{4,6},{5,7},{6,4},{7,5},{8,10},{9,11},{10,... | collective-permute-start | bytes 1474568 | tf_op jit(solution)/shard_map/ppermute | solution.py:366
  36.3 3.4 %collective-permute-start.9 = (bf16[2,160,512]{2,1,0:T(8,128)(2,1)S(1)}, bf16[2,160,512]{2,1,0:T(8,128)(2,1)S(1)}, u32[]{:S(2)}, u32[]{:S(2)}) collective-permute-start(bf16[2,160,512]{2,1,0:T(8,128)(2,1)S(1)} %collective-permute-done.1.refs_10_), channel_id=1, source_target_pairs={{0,1},{1,0},{2,3},{3,2},{4,5},{5,4},{6,7},{7,6},{8,9},{9,8},{10,11... | collective-permute-start | bytes 983048 | tf_op jit(solution)/shard_map/ppermute | solution.py:366
  38.0 11.9 %collective-permute-start.8 = (bf16[2,160,512]{2,1,0:T(8,128)(2,1)S(1)}, bf16[2,160,512]{2,1,0:T(8,128)(2,1)}, u32[]{:S(2)}, u32[]{:S(2)}) collective-permute-start(bf16[2,160,512]{2,1,0:T(8,128)(2,1)S(1)} %collective-permute-done.1.refs_10_), channel_id=1, source_target_pairs={{0,4},{4,0},{8,12},{12,8},{16,20},{20,16},{24,28},{28,24},{1,5},{5... | collective-permute-start | bytes 983048 | tf_op jit(solution)/shard_map/ppermute | solution.py:366
  39.7 11.4 %collective-permute-start.6 = (bf16[120,1280]{1,0:T(8,128)(2,1)S(1)}, bf16[120,1280]{1,0:T(8,128)(2,1)S(1)}, u32[]{:S(2)}, u32[]{:S(2)}) collective-permute-start(bf16[120,1280]{1,0:T(8,128)(2,1)S(1)} %collective-permute-done.5.refs_6_.refs_27_), channel_id=1, source_target_pairs={{0,1},{1,0},{2,3},{3,2},{4,5},{5,4},{6,7},{7,6},{8,9},{9,8},{10,11... | collective-permute-start | bytes 921608 | tf_op jit(solution)/shard_map/ppermute | solution.py:366
  49.9 4.9 %collective-permute-start.14 = (bf16[400,640]{1,0:T(8,128)(2,1)}, bf16[400,640]{1,0:T(8,128)(2,1)S(1)}, u32[]{:S(2)}, u32[]{:S(2)}) collective-permute-start(bf16[400,640]{1,0:T(8,128)(2,1)} %collective-permute-done.11.refs_14_), channel_id=1, source_target_pairs={{0,1},{1,0},{2,3},{3,2},{4,5},{5,4},{6,7},{7,6},{8,9},{9,8},{10,11... | collective-permute-start | bytes 1536008 | tf_op jit(solution)/shard_map/ppermute | solution.py:366
  49.9 4.9 %collective-permute-start.16 = (bf16[400,640]{1,0:T(8,128)(2,1)S(1)}, bf16[400,640]{1,0:T(8,128)(2,1)S(1)}, u32[]{:S(2)}, u32[]{:S(2)}) collective-permute-start(bf16[400,640]{1,0:T(8,128)(2,1)S(1)} %collective-permute-done.13.refs_15_.refs_16_), channel_id=1, source_target_pairs={{0,1},{1,0},{2,3},{3,2},{4,5},{5,4},{6,7},{7,6},{8,9},{9,8},{10,11... | collective-permute-start | bytes 1536008 | tf_op jit(solution)/shard_map/ppermute | solution.py:366
  50.5 4.3 %collective-permute-start.15 = (bf16[400,640]{1,0:T(8,128)(2,1)S(1)}, bf16[400,640]{1,0:T(8,128)(2,1)S(1)}, u32[]{:S(2)}, u32[]{:S(2)}) collective-permute-start(bf16[400,640]{1,0:T(8,128)(2,1)S(1)} %collective-permute-done.12.refs_14_.refs_15_), channel_id=1, source_target_pairs={{0,1},{1,0},{2,3},{3,2},{4,5},{5,4},{6,7},{7,6},{8,9},{9,8},{10,11... | collective-permute-start | bytes 1536008 | tf_op jit(solution)/shard_map/ppermute | solution.py:366
  50.6 4.2 %collective-permute-start.3 = (bf16[192,1280]{1,0:T(8,128)(2,1)}, bf16[192,1280]{1,0:T(8,128)(2,1)S(1)}, u32[]{:S(2)}, u32[]{:S(2)}) collective-permute-start(bf16[192,1280]{1,0:T(8,128)(2,1)} %collective-permute-done.2.refs_2_), channel_id=1, source_target_pairs={{0,1},{1,0},{2,3},{3,2},{4,5},{5,4},{6,7},{7,6},{8,9},{9,8},{10,11... | collective-permute-start | bytes 1474568 | tf_op jit(solution)/shard_map/ppermute | solution.py:366
  51.8 3.0 %collective-permute-start.10 = (bf16[2,160,512]{2,1,0:T(8,128)(2,1)}, bf16[2,160,512]{2,1,0:T(8,128)(2,1)}, u32[]{:S(2)}, u32[]{:S(2)}) collective-permute-start(bf16[2,160,512]{2,1,0:T(8,128)(2,1)} %collective-permute-done.8.refs_11_), channel_id=1, source_target_pairs={{0,1},{1,0},{2,3},{3,2},{4,5},{5,4},{6,7},{7,6},{8,9},{9,8},{10,11... | collective-permute-start | bytes 983048 | tf_op jit(solution)/shard_map/ppermute | solution.py:366
  68.1 9.6 %collective-permute-start.25 = (bf16[240,640]{1,0:T(8,128)(2,1)}, bf16[240,640]{1,0:T(8,128)(2,1)S(1)}, u32[]{:S(2)}, u32[]{:S(2)}) collective-permute-start(bf16[240,640]{1,0:T(8,128)(2,1)} %get-tuple-element.117), channel_id=1, source_target_pairs={{0,4},{4,0},{8,12},{12,8},{16,20},{20,16},{24,28},{28,24},{1,5},{5... | collective-permute-start | bytes 921608 | tf_op jit(solution)/shard_map/ppermute | solution.py:366
  69.7 7.0 %collective-permute-start.26 = (bf16[160,640]{1,0:T(8,128)(2,1)}, bf16[160,640]{1,0:T(8,128)(2,1)S(1)}, u32[]{:S(2)}, u32[]{:S(2)}) collective-permute-start(bf16[160,640]{1,0:T(8,128)(2,1)} %get-tuple-element.118), channel_id=1, source_target_pairs={{0,8},{4,12},{8,0},{12,4},{16,24},{20,28},{24,16},{28,20},{1,9},{5... | collective-permute-start | bytes 614408 | tf_op jit(solution)/shard_map/ppermute | solution.py:366
  70.2 8.3 %collective-permute-start.22 = (bf16[192,256]{1,0:T(8,128)(2,1)}, bf16[192,256]{1,0:T(8,128)(2,1)S(1)}, u32[]{:S(2)}, u32[]{:S(2)}) collective-permute-start(bf16[192,256]{1,0:T(8,128)(2,1)} %get-tuple-element.114), channel_id=1, source_target_pairs={{0,1},{1,0},{2,3},{3,2},{4,5},{5,4},{6,7},{7,6},{8,9},{9,8},{10,11... | collective-permute-start | bytes 294920 | tf_op jit(solution)/shard_map/ppermute | solution.py:366
  70.3 8.3 %collective-permute-start.23 = (bf16[192,256]{1,0:T(8,128)(2,1)}, bf16[192,256]{1,0:T(8,128)(2,1)S(1)}, u32[]{:S(2)}, u32[]{:S(2)}) collective-permute-start(bf16[192,256]{1,0:T(8,128)(2,1)} %get-tuple-element.115), channel_id=1, source_target_pairs={{0,2},{1,3},{2,0},{3,1},{4,6},{5,7},{6,4},{7,5},{8,10},{9,11},{10,... | collective-permute-start | bytes 294920 | tf_op jit(solution)/shard_map/ppermute | solution.py:366
  71.9 6.7 %collective-permute-start.24 = (bf16[192,256]{1,0:T(8,128)(2,1)}, bf16[192,256]{1,0:T(8,128)(2,1)S(1)}, u32[]{:S(2)}, u32[]{:S(2)}) collective-permute-start(bf16[192,256]{1,0:T(8,128)(2,1)} %get-tuple-element.116), channel_id=1, source_target_pairs={{0,3},{1,2},{2,1},{3,0},{4,7},{5,6},{6,5},{7,4},{8,11},{9,10},{10,... | collective-permute-start | bytes 294920 | tf_op jit(solution)/shard_map/ppermute | solution.py:366
  76.7 1.9 collective-permute-start.28
  77.7 1.6 collective-permute-start.27
  96.4 7.4 %collective-permute-start.35 = (bf16[192,6912]{1,0:T(8,128)(2,1)}, bf16[192,6912]{1,0:T(8,128)(2,1)S(1)}, u32[]{:S(2)}, u32[]{:S(2)}) collective-permute-start(bf16[192,6912]{1,0:T(8,128)(2,1)} %get-tuple-element.135.refs_0_), channel_id=1, source_target_pairs={{0,1},{1,0},{2,3},{3,2},{4,5},{5,4},{6,7},{7,6},{8,9},{9,8},{10,11... | collective-permute-start | bytes 7962632 | tf_op jit(solution)/shard_map/ppermute | solution.py:366
  96.6 5.2 %collective-permute-start.32 = (bf16[192,256]{1,0:T(8,128)(2,1)}, bf16[192,256]{1,0:T(8,128)(2,1)S(1)}, u32[]{:S(2)}, u32[]{:S(2)}) collective-permute-start(bf16[192,256]{1,0:T(8,128)(2,1)} %get-tuple-element.126), channel_id=1, source_target_pairs={{0,1},{1,0},{2,3},{3,2},{4,5},{5,4},{6,7},{7,6},{8,9},{9,8},{10,11... | collective-permute-start | bytes 294920 | tf_op jit(solution)/shard_map/ppermute | solution.py:366
  97.0 5.4 %collective-permute-start.33 = (bf16[192,256]{1,0:T(8,128)(2,1)}, bf16[192,256]{1,0:T(8,128)(2,1)S(1)}, u32[]{:S(2)}, u32[]{:S(2)}) collective-permute-start(bf16[192,256]{1,0:T(8,128)(2,1)} %get-tuple-element.127), channel_id=1, source_target_pairs={{0,2},{1,3},{2,0},{3,1},{4,6},{5,7},{6,4},{7,5},{8,10},{9,11},{10,... | collective-permute-start | bytes 294920 | tf_op jit(solution)/shard_map/ppermute | solution.py:366
  98.5 5.3 %collective-permute-start.34 = (bf16[192,256]{1,0:T(8,128)(2,1)}, bf16[192,256]{1,0:T(8,128)(2,1)S(1)}, u32[]{:S(2)}, u32[]{:S(2)}) collective-permute-start(bf16[192,256]{1,0:T(8,128)(2,1)} %get-tuple-element.128), channel_id=1, source_target_pairs={{0,3},{1,2},{2,1},{3,0},{4,7},{5,6},{6,5},{7,4},{8,11},{9,10},{10,... | collective-permute-start | bytes 294920 | tf_op jit(solution)/shard_map/ppermute | solution.py:366
  110.6 29.2 %collective-permute-start.38 = (bf16[8,3,40,640]{3,2,1,0:T(8,128)(2,1)S(1)}, bf16[8,3,40,640]{3,2,1,0:T(8,128)(2,1)S(1)}, u32[]{:S(2)}, u32[]{:S(2)}) collective-permute-start(bf16[8,3,40,640]{3,2,1,0:T(8,128)(2,1)S(1)} %get-tuple-element.137.refs_11_), channel_id=1, source_target_pairs={{0,2},{1,3},{2,0},{3,1},{4,6},{5,7},{6,4},{7,5},{8,10},{9,11},{10,... | collective-permute-start | bytes 3686408 | tf_op jit(solution)/shard_map/ppermute | solution.py:366
  111.8 20.5 %collective-permute-start.39 = (bf16[2,2,2,80,640]{4,3,2,1,0:T(8,128)(2,1)S(1)}, bf16[2,2,2,80,640]{4,3,2,1,0:T(8,128)(2,1)S(1)}, u32[]{:S(2)}, u32[]{:S(2)}) collective-permute-start(bf16[2,2,2,80,640]{4,3,2,1,0:T(8,128)(2,1)S(1)} %get-tuple-element.136.refs_10_), channel_id=1, source_target_pairs={{0,8},{4,12},{8,0},{12,4},{16,24},{20,28},{24,16},{28,20},{1,9},{5... | collective-permute-start | bytes 2457608 | tf_op jit(solution)/shard_map/ppermute | solution.py:366
  119.4 25.6 %collective-permute-start.36 = (bf16[2,216,1280]{2,1,0:T(8,128)(2,1)S(1)}, bf16[2,216,1280]{2,1,0:T(8,128)(2,1)S(1)}, u32[]{:S(2)}, u32[]{:S(2)}) collective-permute-start(bf16[2,216,1280]{2,1,0:T(8,128)(2,1)S(1)} %get-tuple-element.139), channel_id=1, source_target_pairs={{0,1},{1,0},{2,3},{3,2},{4,5},{5,4},{6,7},{7,6},{8,9},{9,8},{10,11... | collective-permute-start | bytes 3317768 | tf_op jit(solution)/shard_map/ppermute | solution.py:366
  119.5 22.7 %collective-permute-start.37 = (bf16[4,4,40,512]{3,2,1,0:T(8,128)(2,1)S(1)}, bf16[4,4,40,512]{3,2,1,0:T(8,128)(2,1)S(1)}, u32[]{:S(2)}, u32[]{:S(2)}) collective-permute-start(bf16[4,4,40,512]{3,2,1,0:T(8,128)(2,1)S(1)} %get-tuple-element.141), channel_id=1, source_target_pairs={{0,4},{4,0},{8,12},{12,8},{16,20},{20,16},{24,28},{28,24},{1,5},{5... | collective-permute-start | bytes 1966088 | tf_op jit(solution)/shard_map/ppermute | solution.py:366
  140.6 15.2 %collective-permute-start.43 = (bf16[2,2,3,40,640]{4,3,2,1,0:T(8,128)(2,1)S(1)}, bf16[2,2,3,40,640]{4,3,2,1,0:T(8,128)(2,1)S(1)}, u32[]{:S(2)}, u32[]{:S(2)}) collective-permute-start(bf16[2,2,3,40,640]{4,3,2,1,0:T(8,128)(2,1)S(1)} %get-tuple-element.154), channel_id=1, source_target_pairs={{0,4},{4,0},{8,12},{12,8},{16,20},{20,16},{24,28},{28,24},{1,5},{5... | collective-permute-start | bytes 1843208 | tf_op jit(solution)/shard_map/ppermute | solution.py:366
  142.9 8.7 %collective-permute-start.41 = (bf16[2,4,40,512]{3,2,1,0:T(8,128)(2,1)S(1)}, bf16[2,4,40,512]{3,2,1,0:T(8,128)(2,1)S(1)}, u32[]{:S(2)}, u32[]{:S(2)}) collective-permute-start(bf16[2,4,40,512]{3,2,1,0:T(8,128)(2,1)S(1)} %get-tuple-element.150), channel_id=1, source_target_pairs={{0,8},{4,12},{8,0},{12,4},{16,24},{20,28},{24,16},{28,20},{1,9},{5... | collective-permute-start | bytes 983048 | tf_op jit(solution)/shard_map/ppermute | solution.py:366
  143.4 11.5 %collective-permute-start.44 = (bf16[2,2,80,640]{3,2,1,0:T(8,128)(2,1)S(1)}, bf16[2,2,80,640]{3,2,1,0:T(8,128)(2,1)S(1)}, u32[]{:S(2)}, u32[]{:S(2)}) collective-permute-start(bf16[2,2,80,640]{3,2,1,0:T(8,128)(2,1)S(1)} %get-tuple-element.156), channel_id=1, source_target_pairs={{0,2},{1,3},{2,0},{3,1},{4,6},{5,7},{6,4},{7,5},{8,10},{9,11},{10,... | collective-permute-start | bytes 1228808 | tf_op jit(solution)/shard_map/ppermute | solution.py:366
  152.3 15.7 %collective-permute-start.42 = (bf16[2,4,40,512]{3,2,1,0:T(8,128)(2,1)S(1)}, bf16[2,4,40,512]{3,2,1,0:T(8,128)(2,1)S(1)}, u32[]{:S(2)}, u32[]{:S(2)}) collective-permute-start(bf16[2,4,40,512]{3,2,1,0:T(8,128)(2,1)S(1)} %get-tuple-element.152.refs_0_), channel_id=1, source_target_pairs={{0,16},{4,20},{8,24},{12,28},{16,0},{20,4},{24,8},{28,12},{1,17},{... | collective-permute-start | bytes 983048 | tf_op jit(solution)/shard_map/ppermute | solution.py:366
  156.5 15.4 %collective-permute-start.48 = (bf16[2,3,40,640]{3,2,1,0:T(8,128)(2,1)S(1)}, bf16[2,3,40,640]{3,2,1,0:T(8,128)(2,1)S(1)}, u32[]{:S(2)}, u32[]{:S(2)}) collective-permute-start(bf16[2,3,40,640]{3,2,1,0:T(8,128)(2,1)S(1)} %get-tuple-element.165), channel_id=1, source_target_pairs={{0,8},{4,12},{8,0},{12,4},{16,24},{20,28},{24,16},{28,20},{1,9},{5... | collective-permute-start | bytes 921608 | tf_op jit(solution)/shard_map/ppermute | solution.py:366
  157.9 13.4 %collective-permute-start.49 = (bf16[2,80,640]{2,1,0:T(8,128)(2,1)S(1)}, bf16[2,80,640]{2,1,0:T(8,128)(2,1)S(1)}, u32[]{:S(2)}, u32[]{:S(2)}) collective-permute-start(bf16[2,80,640]{2,1,0:T(8,128)(2,1)S(1)} %get-tuple-element.167), channel_id=1, source_target_pairs={{0,4},{4,0},{8,12},{12,8},{16,20},{20,16},{24,28},{28,24},{1,5},{5... | collective-permute-start | bytes 614408 | tf_op jit(solution)/shard_map/ppermute | solution.py:366
  168.0 33.0 %copy-start.3 = (bf16[1,2,96,1280]{3,2,1,0:T(8,128)(2,1)S(1)}, bf16[1,2,96,1280]{3,2,1,0:T(8,128)(2,1)}, u32[]{:S(2)}) copy-start(bf16[1,2,96,1280]{3,2,1,0:T(8,128)(2,1)} %param.11) | copy-start | bytes 1474564
  168.0 33.0 %copy-start.10 = (bf16[96,1280]{1,0:T(8,128)(2,1)S(1)}, bf16[96,1280]{1,0:T(8,128)(2,1)}, u32[]{:S(2)}) copy-start(bf16[96,1280]{1,0:T(8,128)(2,1)} %get-tuple-element.121.refs_1_) | copy-start | bytes 737284
  168.6 4.0 %collective-permute-start.45 = (bf16[2,40,512]{2,1,0:T(8,128)(2,1)S(1)}, bf16[2,40,512]{2,1,0:T(8,128)(2,1)S(1)}, u32[]{:S(2)}, u32[]{:S(2)}) collective-permute-start(bf16[2,40,512]{2,1,0:T(8,128)(2,1)S(1)} %get-tuple-element.161), channel_id=1, source_target_pairs={{0,1},{1,0},{2,3},{3,2},{4,5},{5,4},{6,7},{7,6},{8,9},{9,8},{10,11... | collective-permute-start | bytes 245768 | tf_op jit(solution)/shard_map/ppermute | solution.py:366
  168.7 5.6 %collective-permute-start.46 = (bf16[2,40,512]{2,1,0:T(8,128)(2,1)S(1)}, bf16[2,40,512]{2,1,0:T(8,128)(2,1)S(1)}, u32[]{:S(2)}, u32[]{:S(2)}) collective-permute-start(bf16[2,40,512]{2,1,0:T(8,128)(2,1)S(1)} %get-tuple-element.162), channel_id=1, source_target_pairs={{0,2},{1,3},{2,0},{3,1},{4,6},{5,7},{6,4},{7,5},{8,10},{9,11},{10,... | collective-permute-start | bytes 245768 | tf_op jit(solution)/shard_map/ppermute | solution.py:366
  171.2 4.5 %collective-permute-start.47 = (bf16[2,40,512]{2,1,0:T(8,128)(2,1)S(1)}, bf16[2,40,512]{2,1,0:T(8,128)(2,1)S(1)}, u32[]{:S(2)}, u32[]{:S(2)}) collective-permute-start(bf16[2,40,512]{2,1,0:T(8,128)(2,1)S(1)} %get-tuple-element.163), channel_id=1, source_target_pairs={{0,3},{1,2},{2,1},{3,0},{4,7},{5,6},{6,5},{7,4},{8,11},{9,10},{10,... | collective-permute-start | bytes 245768 | tf_op jit(solution)/shard_map/ppermute | solution.py:366
  176.3 9.8 %collective-permute-start.50 = (bf16[2,4,40,512]{3,2,1,0:T(8,128)(2,1)S(1)}, bf16[2,4,40,512]{3,2,1,0:T(8,128)(2,1)S(1)}, u32[]{:S(2)}, u32[]{:S(2)}) collective-permute-start(bf16[2,4,40,512]{3,2,1,0:T(8,128)(2,1)S(1)} %get-tuple-element.171.refs_0_), channel_id=1, source_target_pairs={{0,4},{4,0},{8,12},{12,8},{16,20},{20,16},{24,28},{28,24},{1,5},{5... | collective-permute-start | bytes 983048 | tf_op jit(solution)/shard_map/ppermute | solution.py:366
  176.9 24.1 %collective-permute-start.40 = (bf16[216,1280]{1,0:T(8,128)(2,1)S(1)}, bf16[216,1280]{1,0:T(8,128)(2,1)S(1)}, u32[]{:S(2)}, u32[]{:S(2)}) collective-permute-start(bf16[216,1280]{1,0:T(8,128)(2,1)S(1)} %get-tuple-element.148), channel_id=1, source_target_pairs={{0,2},{1,3},{2,0},{3,1},{4,6},{5,7},{6,4},{7,5},{8,10},{9,11},{10,... | collective-permute-start | bytes 1658888 | tf_op jit(solution)/shard_map/ppermute | solution.py:366
  178.5 11.4 %collective-permute-start.29 = (bf16[96,1280]{1,0:T(8,128)(2,1)S(1)}, bf16[96,1280]{1,0:T(8,128)(2,1)S(1)}, u32[]{:S(2)}, u32[]{:S(2)}) collective-permute-start(bf16[96,1280]{1,0:T(8,128)(2,1)S(1)} %copy-done.40), channel_id=1, source_target_pairs={{0,1},{1,0},{2,3},{3,2},{4,5},{5,4},{6,7},{7,6},{8,9},{9,8},{10,11... | collective-permute-start | bytes 737288 | tf_op jit(solution)/shard_map/ppermute | solution.py:366
  178.5 19.1 %collective-permute-start.30 = (bf16[96,1280]{1,0:T(8,128)(2,1)S(1)}, bf16[96,1280]{1,0:T(8,128)(2,1)S(1)}, u32[]{:S(2)}, u32[]{:S(2)}) collective-permute-start(bf16[96,1280]{1,0:T(8,128)(2,1)S(1)} %copy-done.39), channel_id=1, source_target_pairs={{0,2},{1,3},{2,0},{3,1},{4,6},{5,7},{6,4},{7,5},{8,10},{9,11},{10,... | collective-permute-start | bytes 737288 | tf_op jit(solution)/shard_map/ppermute | solution.py:366
  186.7 30.8 %collective-permute-start.51 = (bf16[2,2,4,40,512]{4,3,2,1,0:T(8,128)(2,1)S(1)}, bf16[2,2,4,40,512]{4,3,2,1,0:T(8,128)(2,1)S(1)}, u32[]{:S(2)}, u32[]{:S(2)}) collective-permute-start(bf16[2,2,4,40,512]{4,3,2,1,0:T(8,128)(2,1)S(1)} %get-tuple-element.177.refs_0_), channel_id=1, source_target_pairs={{0,8},{4,12},{8,0},{12,4},{16,24},{20,28},{24,16},{28,20},{1,9},{5... | collective-permute-start | bytes 1966088 | tf_op jit(solution)/shard_map/ppermute | solution.py:366
  186.8 29.0 %collective-permute-start.52 = (bf16[2,3,40,640]{3,2,1,0:T(8,128)(2,1)S(1)}, bf16[2,3,40,640]{3,2,1,0:T(8,128)(2,1)S(1)}, u32[]{:S(2)}, u32[]{:S(2)}) collective-permute-start(bf16[2,3,40,640]{3,2,1,0:T(8,128)(2,1)S(1)} %get-tuple-element.178.refs_0_), channel_id=1, source_target_pairs={{0,16},{4,20},{8,24},{12,28},{16,0},{20,4},{24,8},{28,12},{1,17},{... | collective-permute-start | bytes 921608 | tf_op jit(solution)/shard_map/ppermute | solution.py:366
  189.9 11.1 %collective-permute-start.31 = (bf16[96,1280]{1,0:T(8,128)(2,1)S(1)}, bf16[96,1280]{1,0:T(8,128)(2,1)S(1)}, u32[]{:S(2)}, u32[]{:S(2)}) collective-permute-start(bf16[96,1280]{1,0:T(8,128)(2,1)S(1)} %copy-done.38), channel_id=1, source_target_pairs={{0,3},{1,2},{2,1},{3,0},{4,7},{5,6},{6,5},{7,4},{8,11},{9,10},{10,... | collective-permute-start | bytes 737288 | tf_op jit(solution)/shard_map/ppermute | solution.py:366
  197.6 17.6 %collective-permute-start.53 = (bf16[2,80,640]{2,1,0:T(8,128)(2,1)S(1)}, bf16[2,80,640]{2,1,0:T(8,128)(2,1)S(1)}, u32[]{:S(2)}, u32[]{:S(2)}) collective-permute-start(bf16[2,80,640]{2,1,0:T(8,128)(2,1)S(1)} %get-tuple-element.179.refs_0_), channel_id=1, source_target_pairs={{0,16},{4,20},{8,24},{12,28},{16,0},{20,4},{24,8},{28,12},{1,17},{... | collective-permute-start | bytes 614408 | tf_op jit(solution)/shard_map/ppermute | solution.py:366
  216.4 7.4 %collective-permute-start.56 = (bf16[2,3,40,640]{3,2,1,0:T(8,128)(2,1)S(1)}, bf16[2,3,40,640]{3,2,1,0:T(8,128)(2,1)S(1)}, u32[]{:S(2)}, u32[]{:S(2)}) collective-permute-start(bf16[2,3,40,640]{3,2,1,0:T(8,128)(2,1)S(1)} %get-tuple-element.189.refs_0_), channel_id=1, source_target_pairs={{0,4},{4,0},{8,12},{12,8},{16,20},{20,16},{24,28},{28,24},{1,5},{5... | collective-permute-start | bytes 921608 | tf_op jit(solution)/shard_map/ppermute | solution.py:366
  217.5 5.8 %collective-permute-start.54 = (bf16[2,80,640]{2,1,0:T(8,128)(2,1)S(1)}, bf16[2,80,640]{2,1,0:T(8,128)(2,1)S(1)}, u32[]{:S(2)}, u32[]{:S(2)}) collective-permute-start(bf16[2,80,640]{2,1,0:T(8,128)(2,1)S(1)} %get-tuple-element.186.refs_0_), channel_id=1, source_target_pairs={{0,8},{4,12},{8,0},{12,4},{16,24},{20,28},{24,16},{28,20},{1,9},{5... | collective-permute-start | bytes 614408 | tf_op jit(solution)/shard_map/ppermute | solution.py:366
  224.5 12.1 %collective-permute-start.57 = (bf16[2,2,3,40,640]{4,3,2,1,0:T(8,128)(2,1)S(1)}, bf16[2,2,3,40,640]{4,3,2,1,0:T(8,128)(2,1)S(1)}, u32[]{:S(2)}, u32[]{:S(2)}) collective-permute-start(bf16[2,2,3,40,640]{4,3,2,1,0:T(8,128)(2,1)S(1)} %get-tuple-element.193.refs_0_), channel_id=1, source_target_pairs={{0,8},{4,12},{8,0},{12,4},{16,24},{20,28},{24,16},{28,20},{1,9},{5... | collective-permute-start | bytes 1843208 | tf_op jit(solution)/shard_map/ppermute | solution.py:366
  224.9 8.8 %collective-permute-start.55 = (bf16[2,2,80,640]{3,2,1,0:T(8,128)(2,1)S(1)}, bf16[2,2,80,640]{3,2,1,0:T(8,128)(2,1)S(1)}, u32[]{:S(2)}, u32[]{:S(2)}) collective-permute-start(bf16[2,2,80,640]{3,2,1,0:T(8,128)(2,1)S(1)} %get-tuple-element.188.refs_0_), channel_id=1, source_target_pairs={{0,4},{4,0},{8,12},{12,8},{16,20},{20,16},{24,28},{28,24},{1,5},{5... | collective-permute-start | bytes 1228808 | tf_op jit(solution)/shard_map/ppermute | solution.py:366
  (39 other events, 304.6 us)

commit v4 on v3

--- a/solution.py
+++ b/solution.py
@@ -1129,6 +1129,8 @@
     partial_got = flip(partial_out, "frame", 2)
     head = steps.join(head, head_got, axis=1)
     head_got = to_clip(head, 2)
+    flat = steps.merge(flat, flat_got)
+    flat_got = to_clip(flat, 2)
     output, frames_grad, refer_grad = steps.call(
         functools.partial(finish_body, n, per),
         "finish",
@@ -1136,8 +1138,6 @@
         [frames, *backs, partial, partial_got],
         [pltpu.VMEM((2 * few, dim), F32), pltpu.VMEM((2, rows, dim), F32)],
     )
-    flat = steps.merge(flat, flat_got)
-    flat_got = to_clip(flat, 2)
     tall = steps.merge(tall, tall_got)
     tall_got = to_clip(tall, 1)
     head_grads = steps.call(

time: 239 us -> 234 us (0.979)
  waiting for transfers between devices: 122 us -> 111 us
  starting transfers between devices: 43.8 us -> 49.4 us
    ppermute x58, waiting for transfers between devices: 122 us -> 111 us  [flip(): return lax.ppermute(value, axis, [(i, i ^ bit) for i in range(size)])]
    ppermute x58, starting transfers between devices: 43.8 us -> 49.4 us  [flip(): return lax.ppermute(value, axis, [(i, i ^ bit) for i in range(size)])]
where the time goes in v4:
time: 234 us
  waiting for transfers between devices  111 us (47%)
  Pallas kernels  64 us (27%)
  starting transfers between devices  49.4 us (21%)
  local copies, waits for them, and re-layouts  6.18 us (3%)
    ppermute x58, waiting for transfers between devices, flip(): return lax.ppermute(value, axis, [(i, i ^ bit) for i in range(size)])  111 us
    pallas_call x25, Pallas kernels, wide_call(): return lambda *operands: call(*operands, *late)  64 us
    ppermute x58, starting transfers between devices, flip(): return lax.ppermute(value, axis, [(i, i ^ bit) for i in range(size)])  49.4 us
    unnamed x90, local copies, waits for them, and re-layouts  6.18 us
  transfers between devices with their start and end apart: 58, of which 26 were waited for; matrix products, arithmetic and copies ran while one was open for 0% of the time, Pallas kernels for 10%

profile of v4, /device:TPU:0, one launch (start us, length us, event | category | flops | bytes accessed | tf_op | source)
XLA Modules:
  0.0 233.8 jit_solution(11935267025386772875)
XLA Ops:
  1.3 4.3 %pack_heads.1 = (bf16[320,512]{1,0:T(8,128)(2,1)}, bf16[320,512]{1,0:T(8,128)(2,1)}, bf16[2,160,512]{2,1,0:T(8,128)(2,1)}, bf16[400,640]{1,0:T(8,128)(2,1)}, bf1...) custom-call(s32[2]{0:T(128)} %pad_add_fusion.idx, bf16[320,640]{1,0:T(8,128)(2,1)} %refs_0_.1, ...), custom_call_target="tpu_custom_call" | custom-call | flops 1 | bytes 1 | tf_op jit(solution)/shard_map/pack_heads/pallas_call | solution.py:357
  5.6 3.0 %collective-permute-start.1 = (bf16[2,160,512]{2,1,0:T(8,128)(2,1)}, bf16[2,160,512]{2,1,0:T(8,128)(2,1)S(1)}, u32[]{:S(2)}, u32[]{:S(2)}) collective-permute-start(bf16[2,160,512]{2,1,0:T(8,128)(2,1)} %get-tuple-element.105), channel_id=1, source_target_pairs={{0,2},{1,3},{2,0},{3,1},{4,6},{5,7},{6,4},{7,5},{8,10},{9,11},{10,... | collective-permute-start | bytes 983048 | tf_op jit(solution)/shard_map/ppermute | solution.py:366
  9.7 2.0 collective-permute-done.4.refs_5_.refs_26_
  12.1 4.5 %collective-permute-done.1.refs_10_ = bf16[2,160,512]{2,1,0:T(8,128)(2,1)S(1)} collective-permute-done((bf16[2,160,512]{2,1,0:T(8,128)(2,1)}, bf16[2,160,512]{2,1,0:T(8,128)(2,1)S(1)}, u32[]{:S(2)}, u32[]{:S(2)}) %collective-permute-start.1) | collective-permute-done | bytes 327712 | tf_op jit(solution)/shard_map/ppermute | solution.py:366
  16.6 1.7 collective-permute-start.11
  19.5 12.0 %collective-permute-done.11.refs_14_ = bf16[400,640]{1,0:T(8,128)(2,1)} collective-permute-done((bf16[400,640]{1,0:T(8,128)(2,1)}, bf16[400,640]{1,0:T(8,128)(2,1)}, u32[]{:S(2)}, u32[]{:S(2)}) %collective-permute-start.11) | collective-permute-done | bytes 512032 | tf_op jit(solution)/shard_map/ppermute | solution.py:366
  31.5 1.8 collective-permute-start.13
  33.3 1.5 collective-permute-start.12
  34.8 1.5 collective-permute-start.2
  36.3 1.7 collective-permute-done.5.refs_6_.refs_27_
  38.0 1.7 collective-permute-start.8
  39.7 0.7 copy-done.33
  40.4 9.5 %collective-permute-done.8.refs_11_ = bf16[2,160,512]{2,1,0:T(8,128)(2,1)} collective-permute-done((bf16[2,160,512]{2,1,0:T(8,128)(2,1)S(1)}, bf16[2,160,512]{2,1,0:T(8,128)(2,1)}, u32[]{:S(2)}, u32[]{:S(2)}) %collective-permute-start.8) | collective-permute-done | bytes 327712 | tf_op jit(solution)/shard_map/ppermute | solution.py:366
  51.1 0.7 copy-done.35
  51.9 2.9 %collective-permute-done.10.refs_13_ = bf16[2,160,512]{2,1,0:T(8,128)(2,1)} collective-permute-done((bf16[2,160,512]{2,1,0:T(8,128)(2,1)}, bf16[2,160,512]{2,1,0:T(8,128)(2,1)}, u32[]{:S(2)}, u32[]{:S(2)}) %collective-permute-start.10) | collective-permute-done | bytes 327712 | tf_op jit(solution)/shard_map/ppermute | solution.py:366
  54.9 0.7 copy-done.17
  56.0 12.0 %spatial_forward.1 = (bf16[864,1280]{1,0:T(8,128)(2,1)}, bf16[1280,512]{1,0:T(8,128)(2,1)}, bf16[864,256]{1,0:T(8,128)(2,1)}, bf16[864,256]{1,0:T(8,128)(2,1)}, ...) custom-call(s32[2]{0:T(128)} %pad_add_fusion.idx, ...), custom_call_target="tpu_custom_call" | custom-call | flops 2000000000 | bytes 8000000 | tf_op jit(solution)/shard_map/spatial_forward/pallas_call | solution.py:357
  68.1 1.6 collective-permute-start.25
  70.3 1.6 collective-permute-start.23
  72.1 4.6 %collective-permute-done.26.refs_18_ = bf16[160,640]{1,0:T(8,128)(2,1)S(1)} collective-permute-done((bf16[160,640]{1,0:T(8,128)(2,1)}, bf16[160,640]{1,0:T(8,128)(2,1)S(1)}, u32[]{:S(2)}, u32[]{:S(2)}) %collective-permute-start.26) | collective-permute-done | bytes 204832 | tf_op jit(solution)/shard_map/ppermute | solution.py:366
  76.7 1.0 collective-permute-done.25.refs_17_
  77.7 0.8 fusion.refs_29_
  80.0 16.4 %temporal.1 = (bf16[192,256]{1,0:T(8,128)(2,1)}, bf16[192,256]{1,0:T(8,128)(2,1)}, bf16[192,256]{1,0:T(8,128)(2,1)}, bf16[192,256]{1,0:T(8,128)(2,1)}, bf16[96,1...) custom-call(s32[2]{0:T(128)} %pad_add_fusion.idx, ...), custom_call_target="tpu_custom_call" | custom-call | flops 5000000000 | bytes 8000000 | tf_op jit(solution)/shard_map/temporal/pallas_call | solution.py:357
  97.0 1.5 collective-permute-start.33
  98.6 3.3 %collective-permute-done.32.refs_4_.refs_1_ = bf16[192,256]{1,0:T(8,128)(2,1)S(1)} collective-permute-done((bf16[192,256]{1,0:T(8,128)(2,1)}, bf16[192,256]{1,0:T(8,128)(2,1)S(1)}, u32[]{:S(2)}, u32[]{:S(2)}) %collective-permute-start.32) | collective-permute-done | bytes 98336 | tf_op jit(solution)/shard_map/ppermute | solution.py:366
  102.4 1.5 collective-permute-done.34.refs_6_.refs_3_
  103.9 1.7 copy-done
  105.6 0.9 copy-done.14
  106.5 4.1 %temporal_terms.1 = (bf16[8,3,40,640]{3,2,1,0:T(8,128)(2,1)S(1)}, bf16[8,3,40,640]{3,2,1,0:T(8,128)(2,1)S(1)}, bf16[2,2,2,80,640]{4,3,2,1,0:T(8,128)(2,1)S(1)}, bf16[2,2,2,80,640]{4,3,2,1,0:T(8,128)(2,1)S(1)}) custom-call(s32[2]{0:T(128)S(1)} %copy-done.9, bf16[192,6912]{1,0:T(8,128)(2,1)S(1)} %copy-done, ...), custom_call_target="tpu_custom_call" | custom-call | flops 1 | bytes 1 | tf_op jit(solution)/shard_map/temporal_terms/pallas_call | solution.py:357
  110.6 1.1 collective-permute-start.38
  112.3 7.1 %spatial_backward.1 = (bf16[2,216,1280]{2,1,0:T(8,128)(2,1)S(1)}, bf16[2,216,1280]{2,1,0:T(8,128)(2,1)S(1)}, bf16[4,4,40,512]{3,2,1,0:T(8,128)(2,1)S(1)}, bf16[4,4,40,512]{3,2,1,0:T(8,128)(2,1)S(1)}) custom-call(s32[2]{0:T(128)S(1)} %copy-done.9, bf16[192,256]{1,0:T(8,128)(2,1)S(1)} %copy-done.11, ...), custom_call_target="tpu_custom_call" | custom-call | flops 1 | bytes 1 | tf_op jit(solution)/shard_map/spatial_backward/pallas_call | solution.py:357
  119.5 1.5 collective-permute-start.37
  121.0 11.3 %collective-permute-done.39.refs_1_ = bf16[2,2,2,80,640]{4,3,2,1,0:T(8,128)(2,1)S(1)} collective-permute-done((bf16[2,2,2,80,640]{4,3,2,1,0:T(8,128)(2,1)S(1)}, bf16[2,2,2,80,640]{4,3,2,1,0:T(8,128)(2,1)S(1)}, u32[]{:S(2)}, u32[]{:S(2)}) %collective-permute-start.39) | collective-permute-done | bytes 819232 | tf_op jit(solution)/shard_map/ppermute | solution.py:366
  132.3 0.7 merge.12
  133.0 6.8 %collective-permute-done.38 = bf16[8,3,40,640]{3,2,1,0:T(8,128)(2,1)S(1)} collective-permute-done((bf16[8,3,40,640]{3,2,1,0:T(8,128)(2,1)S(1)}, bf16[8,3,40,640]{3,2,1,0:T(8,128)(2,1)S(1)}, u32[]{:S(2)}, u32[]{:S(2)}) %collective-permute-start.38) | collective-permute-done | bytes 1228832 | tf_op jit(solution)/shard_map/ppermute | solution.py:366
  139.8 0.8 merge.13
  140.6 1.6 collective-permute-start.45
  142.2 0.7 merge.14
  143.4 1.5 collective-permute-start.41
  144.9 0.8 merge.15
  145.7 5.9 %collective-permute-done.42.refs_1_ = bf16[2,4,40,512]{3,2,1,0:T(8,128)(2,1)S(1)} collective-permute-done((bf16[2,4,40,512]{3,2,1,0:T(8,128)(2,1)S(1)}, bf16[2,4,40,512]{3,2,1,0:T(8,128)(2,1)S(1)}, u32[]{:S(2)}, u32[]{:S(2)}) %collective-permute-start.42) | collective-permute-done | bytes 327712 | tf_op jit(solution)/shard_map/ppermute | solution.py:366
  152.3 2.7 %collective-permute-start.44 = (bf16[2,4,40,512]{3,2,1,0:T(8,128)(2,1)S(1)}, bf16[2,4,40,512]{3,2,1,0:T(8,128)(2,1)S(1)}, u32[]{:S(2)}, u32[]{:S(2)}) collective-permute-start(bf16[2,4,40,512]{3,2,1,0:T(8,128)(2,1)S(1)} %get-tuple-element.157.refs_0_), channel_id=1, source_target_pairs={{0,16},{4,20},{8,24},{12,28},{16,0},{20,4},{24,8},{28,12},{1,17},{... | collective-permute-start | bytes 983048 | tf_op jit(solution)/shard_map/ppermute | solution.py:366
  155.8 0.7 merge.18
  156.5 1.4 collective-permute-start.50
  158.5 9.5 %collective-permute-done.44.refs_1_ = bf16[2,4,40,512]{3,2,1,0:T(8,128)(2,1)S(1)} collective-permute-done((bf16[2,4,40,512]{3,2,1,0:T(8,128)(2,1)S(1)}, bf16[2,4,40,512]{3,2,1,0:T(8,128)(2,1)S(1)}, u32[]{:S(2)}, u32[]{:S(2)}) %collective-permute-start.44) | collective-permute-done | bytes 327712 | tf_op jit(solution)/shard_map/ppermute | solution.py:366
  168.7 2.6 %collective-permute-start.48 = (bf16[2,40,512]{2,1,0:T(8,128)(2,1)S(1)}, bf16[2,40,512]{2,1,0:T(8,128)(2,1)S(1)}, u32[]{:S(2)}, u32[]{:S(2)}) collective-permute-start(bf16[2,40,512]{2,1,0:T(8,128)(2,1)S(1)} %get-tuple-element.166), channel_id=1, source_target_pairs={{0,2},{1,3},{2,0},{3,1},{4,6},{5,7},{6,4},{7,5},{8,10},{9,11},{10,... | collective-permute-start | bytes 245768 | tf_op jit(solution)/shard_map/ppermute | solution.py:366
  172.6 1.7 collective-permute-done.48.refs_2_
  174.3 1.5 collective-permute-done.49.refs_3_
  176.9 1.6 collective-permute-start.40
  178.5 7.6 %collective-permute-done.51.refs_1_ = bf16[2,4,40,512]{3,2,1,0:T(8,128)(2,1)S(1)} collective-permute-done((bf16[2,4,40,512]{3,2,1,0:T(8,128)(2,1)S(1)}, bf16[2,4,40,512]{3,2,1,0:T(8,128)(2,1)S(1)}, u32[]{:S(2)}, u32[]{:S(2)}) %collective-permute-start.51) | collective-permute-done | bytes 327712 | tf_op jit(solution)/shard_map/ppermute | solution.py:366
  186.8 3.1 %collective-permute-start.53 = (bf16[2,3,40,640]{3,2,1,0:T(8,128)(2,1)S(1)}, bf16[2,3,40,640]{3,2,1,0:T(8,128)(2,1)S(1)}, u32[]{:S(2)}, u32[]{:S(2)}) collective-permute-start(bf16[2,3,40,640]{3,2,1,0:T(8,128)(2,1)S(1)} %get-tuple-element.180.refs_0_), channel_id=1, source_target_pairs={{0,16},{4,20},{8,24},{12,28},{16,0},{20,4},{24,8},{28,12},{1,17},{... | collective-permute-start | bytes 921608 | tf_op jit(solution)/shard_map/ppermute | solution.py:366
  189.9 1.8 collective-permute-start.30
  192.3 6.4 %collective-permute-done.30.refs_3_ = bf16[96,1280]{1,0:T(8,128)(2,1)S(1)} collective-permute-done((bf16[96,1280]{1,0:T(8,128)(2,1)S(1)}, bf16[96,1280]{1,0:T(8,128)(2,1)S(1)}, u32[]{:S(2)}, u32[]{:S(2)}) %collective-permute-start.30) | collective-permute-done | bytes 245792 | tf_op jit(solution)/shard_map/ppermute | solution.py:366
  198.7 2.5 %collective-permute-done.31.refs_4_ = bf16[96,1280]{1,0:T(8,128)(2,1)S(1)} collective-permute-done((bf16[96,1280]{1,0:T(8,128)(2,1)S(1)}, bf16[96,1280]{1,0:T(8,128)(2,1)S(1)}, u32[]{:S(2)}, u32[]{:S(2)}) %collective-permute-start.31) | collective-permute-done | bytes 245792 | tf_op jit(solution)/shard_map/ppermute | solution.py:366
  201.2 3.3 %finish.1 = (bf16[192,1280]{1,0:T(8,128)(2,1)}, bf16[192,1280]{1,0:T(8,128)(2,1)}, bf16[24,1280]{1,0:T(8,128)(2,1)}, f32[8,128]{1,0:T(8,128)S(1)}) custom-call(s32[2]{0:T(128)S(1)} %copy-done.9, bf16[192,1280]{1,0:T(8,128)(2,1)S(1)} %bitcast.15, bf16[96,1280]{1,0:T(8,128)(2,1)S(1)} %copy-done.10, bf16[96,1280]{1,0:T(8,128)(2,1)S(1)} %collective-permute-done.29.refs_2_, ...), custom_call_target="tpu_custom_call" | custom-call | flops 1 | bytes 1 | tf_op jit(solution)/shard_map/finish/pallas_call | solution.py:357
  204.5 2.6 %collective-permute-done.53.refs_1_ = bf16[2,3,40,640]{3,2,1,0:T(8,128)(2,1)S(1)} collective-permute-done((bf16[2,3,40,640]{3,2,1,0:T(8,128)(2,1)S(1)}, bf16[2,3,40,640]{3,2,1,0:T(8,128)(2,1)S(1)}, u32[]{:S(2)}, u32[]{:S(2)}) %collective-permute-start.53) | collective-permute-done | bytes 307232 | tf_op jit(solution)/shard_map/ppermute | solution.py:366
  208.3 3.5 %collective-permute-start.54 = (bf16[2,80,640]{2,1,0:T(8,128)(2,1)S(1)}, bf16[2,80,640]{2,1,0:T(8,128)(2,1)S(1)}, u32[]{:S(2)}, u32[]{:S(2)}) collective-permute-start(bf16[2,80,640]{2,1,0:T(8,128)(2,1)S(1)} %get-tuple-element.186.refs_0_), channel_id=1, source_target_pairs={{0,8},{4,12},{8,0},{12,4},{16,24},{20,28},{24,16},{28,20},{1,9},{5... | collective-permute-start | bytes 614408 | tf_op jit(solution)/shard_map/ppermute | solution.py:366
  211.9 2.4 %place_heads.1 = (f32[320,640]{1,0:T(8,128)}, f32[320,640]{1,0:T(8,128)}, f32[320,640]{1,0:T(8,128)}, f32[8,128]{1,0:T(8,128)S(1)}) custom-call(s32[2]{0:T(128)S(1)} %copy-done.9, bf16[2,2,4,40,512]{4,3,2,1,0:T(8,128)(2,1)S(1)} %get-tuple-element.179.refs_0_, bf16[2,2,4,40,512]{4,3,2,1,0:T(8,128)(2,1)S(1)} %collective-permute-done.52.refs_1_, ...), custom_call_target="tpu_custom_call" | custom-call | flops 1 | bytes 1 | tf_op jit(solution)/shard_map/place_heads/pallas_call | solution.py:357
  214.3 1.9 collective-permute-done.54.refs_1_
  217.4 2.5 %collective-permute-start.57 = (bf16[2,2,3,40,640]{4,3,2,1,0:T(8,128)(2,1)S(1)}, bf16[2,2,3,40,640]{4,3,2,1,0:T(8,128)(2,1)S(1)}, u32[]{:S(2)}, u32[]{:S(2)}) collective-permute-start(bf16[2,2,3,40,640]{4,3,2,1,0:T(8,128)(2,1)S(1)} %get-tuple-element.193.refs_0_), channel_id=1, source_target_pairs={{0,8},{4,12},{8,0},{12,4},{16,24},{20,28},{24,16},{28,20},{1,9},{5... | collective-permute-start | bytes 1843208 | tf_op jit(solution)/shard_map/ppermute | solution.py:366
  220.4 8.3 %collective-permute-done.55.refs_1_ = bf16[2,2,80,640]{3,2,1,0:T(8,128)(2,1)S(1)} collective-permute-done((bf16[2,2,80,640]{3,2,1,0:T(8,128)(2,1)S(1)}, bf16[2,2,80,640]{3,2,1,0:T(8,128)(2,1)S(1)}, u32[]{:S(2)}, u32[]{:S(2)}) %collective-permute-start.55) | collective-permute-done | bytes 409632 | tf_op jit(solution)/shard_map/ppermute | solution.py:366
  228.7 1.9 place_flat.1
  230.5 1.1 collective-permute-done.57.refs_1_
  231.7 2.1 place_tall.1
  (174 shorter events, 19.1 us)
Async XLA Ops:
  5.6 11.0 %collective-permute-start.1 = (bf16[2,160,512]{2,1,0:T(8,128)(2,1)}, bf16[2,160,512]{2,1,0:T(8,128)(2,1)S(1)}, u32[]{:S(2)}, u32[]{:S(2)}) collective-permute-start(bf16[2,160,512]{2,1,0:T(8,128)(2,1)} %get-tuple-element.105), channel_id=1, source_target_pairs={{0,2},{1,3},{2,0},{3,1},{4,6},{5,7},{6,4},{7,5},{8,10},{9,11},{10,... | collective-permute-start | bytes 983048 | tf_op jit(solution)/shard_map/ppermute | solution.py:366
  8.7 9.7 %collective-permute-start.20 = (bf16[160,1280]{1,0:T(8,128)(2,1)S(1)}, bf16[160,1280]{1,0:T(8,128)(2,1)S(1)}, u32[]{:S(2)}, u32[]{:S(2)}) collective-permute-start(bf16[160,1280]{1,0:T(8,128)(2,1)S(1)} %copy-done.25), channel_id=1, source_target_pairs={{0,1},{1,0},{2,3},{3,2},{4,5},{5,4},{6,7},{7,6},{8,9},{9,8},{10,11... | collective-permute-start | bytes 1228808 | tf_op jit(solution)/shard_map/ppermute | solution.py:366
  8.7 10.4 %collective-permute-start.17 = (bf16[320,640]{1,0:T(8,128)(2,1)S(1)}, bf16[320,640]{1,0:T(8,128)(2,1)S(1)}, u32[]{:S(2)}, u32[]{:S(2)}) collective-permute-start(bf16[320,640]{1,0:T(8,128)(2,1)S(1)} %copy-done.22), channel_id=1, source_target_pairs={{0,1},{1,0},{2,3},{3,2},{4,5},{5,4},{6,7},{7,6},{8,9},{9,8},{10,11... | collective-permute-start | bytes 1228808 | tf_op jit(solution)/shard_map/ppermute | solution.py:366
  9.2 9.2 %collective-permute-start.7 = (bf16[320,512]{1,0:T(8,128)(2,1)}, bf16[320,512]{1,0:T(8,128)(2,1)S(1)}, u32[]{:S(2)}, u32[]{:S(2)}) collective-permute-start(bf16[320,512]{1,0:T(8,128)(2,1)} %get-tuple-element.111), channel_id=1, source_target_pairs={{0,1},{1,0},{2,3},{3,2},{4,5},{5,4},{6,7},{7,6},{8,9},{9,8},{10,11... | collective-permute-start | bytes 983048 | tf_op jit(solution)/shard_map/ppermute | solution.py:366
  9.2 2.5 %collective-permute-start.4 = (bf16[72,1280]{1,0:T(8,128)(2,1)}, bf16[72,1280]{1,0:T(8,128)(2,1)}, u32[]{:S(2)}, u32[]{:S(2)}) collective-permute-start(bf16[72,1280]{1,0:T(8,128)(2,1)} %get-tuple-element.107), channel_id=1, source_target_pairs={{0,1},{1,0},{2,3},{3,2},{4,5},{5,4},{6,7},{7,6},{8,9},{9,8},{10,11... | collective-permute-start | bytes 552968 | tf_op jit(solution)/shard_map/ppermute | solution.py:366
  11.7 7.4 %collective-permute-start.18 = (bf16[320,640]{1,0:T(8,128)(2,1)S(1)}, bf16[320,640]{1,0:T(8,128)(2,1)S(1)}, u32[]{:S(2)}, u32[]{:S(2)}) collective-permute-start(bf16[320,640]{1,0:T(8,128)(2,1)S(1)} %copy-done.23), channel_id=1, source_target_pairs={{0,1},{1,0},{2,3},{3,2},{4,5},{5,4},{6,7},{7,6},{8,9},{9,8},{10,11... | collective-permute-start | bytes 1228808 | tf_op jit(solution)/shard_map/ppermute | solution.py:366
  16.6 34.5 %copy-start.31 = (bf16[2,160,512]{2,1,0:T(8,128)(2,1)}, bf16[2,160,512]{2,1,0:T(8,128)(2,1)S(1)}, u32[]{:S(2)}) copy-start(bf16[2,160,512]{2,1,0:T(8,128)(2,1)S(1)} %collective-permute-done.1.refs_10_) | copy-start | bytes 983044
  16.6 14.9 %collective-permute-start.11 = (bf16[400,640]{1,0:T(8,128)(2,1)}, bf16[400,640]{1,0:T(8,128)(2,1)}, u32[]{:S(2)}, u32[]{:S(2)}) collective-permute-start(bf16[400,640]{1,0:T(8,128)(2,1)} %get-tuple-element.112), channel_id=1, source_target_pairs={{0,2},{1,3},{2,0},{3,1},{4,6},{5,7},{6,4},{7,5},{8,10},{9,11},{10,... | collective-permute-start | bytes 1536008 | tf_op jit(solution)/shard_map/ppermute | solution.py:366
  18.3 18.0 %collective-permute-start = (bf16[192,1280]{1,0:T(8,128)(2,1)S(1)}, bf16[192,1280]{1,0:T(8,128)(2,1)S(1)}, u32[]{:S(2)}, u32[]{:S(2)}) collective-permute-start(bf16[192,1280]{1,0:T(8,128)(2,1)S(1)} %bitcast.13), channel_id=1, source_target_pairs={{0,1},{1,0},{2,3},{3,2},{4,5},{5,4},{6,7},{7,6},{8,9},{9,8},{10,11... | collective-permute-start | bytes 1474568 | tf_op jit(solution)/shard_map/ppermute | solution.py:366
  18.4 31.5 %copy-start.27 = (bf16[160,1280]{1,0:T(8,128)(2,1)}, bf16[160,1280]{1,0:T(8,128)(2,1)S(1)}, u32[]{:S(2)}) copy-start(bf16[160,1280]{1,0:T(8,128)(2,1)S(1)} %collective-permute-done.20.refs_22_.refs_12_) | copy-start | bytes 1228804
  18.4 14.9 %collective-permute-start.19 = (bf16[320,640]{1,0:T(8,128)(2,1)S(1)}, bf16[320,640]{1,0:T(8,128)(2,1)}, u32[]{:S(2)}, u32[]{:S(2)}) collective-permute-start(bf16[320,640]{1,0:T(8,128)(2,1)S(1)} %copy-done.24), channel_id=1, source_target_pairs={{0,1},{1,0},{2,3},{3,2},{4,5},{5,4},{6,7},{7,6},{8,9},{9,8},{10,11... | collective-permute-start | bytes 1228808 | tf_op jit(solution)/shard_map/ppermute | solution.py:366
  19.1 31.4 %copy-start.28 = (bf16[320,640]{1,0:T(8,128)(2,1)}, bf16[320,640]{1,0:T(8,128)(2,1)S(1)}, u32[]{:S(2)}) copy-start(bf16[320,640]{1,0:T(8,128)(2,1)S(1)} %collective-permute-done.17.refs_19_.refs_9_) | copy-start | bytes 1228804
  19.1 15.7 %collective-permute-start.21 = (bf16[160,1280]{1,0:T(8,128)(2,1)S(1)}, bf16[160,1280]{1,0:T(8,128)(2,1)S(1)}, u32[]{:S(2)}, u32[]{:S(2)}) collective-permute-start(bf16[160,1280]{1,0:T(8,128)(2,1)S(1)} %copy-done.26), channel_id=1, source_target_pairs={{0,1},{1,0},{2,3},{3,2},{4,5},{5,4},{6,7},{7,6},{8,9},{9,8},{10,11... | collective-permute-start | bytes 1228808 | tf_op jit(solution)/shard_map/ppermute | solution.py:366
  19.1 31.4 %copy-start.29 = (bf16[320,640]{1,0:T(8,128)(2,1)}, bf16[320,640]{1,0:T(8,128)(2,1)S(1)}, u32[]{:S(2)}) copy-start(bf16[320,640]{1,0:T(8,128)(2,1)S(1)} %collective-permute-done.18.refs_20_.refs_10_) | copy-start | bytes 1228804
  19.2 18.8 %collective-permute-start.5 = (bf16[120,1280]{1,0:T(8,128)(2,1)}, bf16[120,1280]{1,0:T(8,128)(2,1)S(1)}, u32[]{:S(2)}, u32[]{:S(2)}) collective-permute-start(bf16[120,1280]{1,0:T(8,128)(2,1)} %get-tuple-element.109), channel_id=1, source_target_pairs={{0,2},{1,3},{2,0},{3,1},{4,6},{5,7},{6,4},{7,5},{8,10},{9,11},{10,... | collective-permute-start | bytes 921608 | tf_op jit(solution)/shard_map/ppermute | solution.py:366
  31.5 18.4 %collective-permute-start.13 = (bf16[400,640]{1,0:T(8,128)(2,1)}, bf16[400,640]{1,0:T(8,128)(2,1)S(1)}, u32[]{:S(2)}, u32[]{:S(2)}) collective-permute-start(bf16[400,640]{1,0:T(8,128)(2,1)} %collective-permute-done.11.refs_14_), channel_id=1, source_target_pairs={{0,8},{4,12},{8,0},{12,4},{16,24},{20,28},{24,16},{28,20},{1,9},{5... | collective-permute-start | bytes 1536008 | tf_op jit(solution)/shard_map/ppermute | solution.py:366
  33.3 17.2 %collective-permute-start.12 = (bf16[400,640]{1,0:T(8,128)(2,1)}, bf16[400,640]{1,0:T(8,128)(2,1)S(1)}, u32[]{:S(2)}, u32[]{:S(2)}) collective-permute-start(bf16[400,640]{1,0:T(8,128)(2,1)} %collective-permute-done.11.refs_14_), channel_id=1, source_target_pairs={{0,4},{4,0},{8,12},{12,8},{16,20},{20,16},{24,28},{28,24},{1,5},{5... | collective-permute-start | bytes 1536008 | tf_op jit(solution)/shard_map/ppermute | solution.py:366
  34.8 15.8 %collective-permute-start.2 = (bf16[192,1280]{1,0:T(8,128)(2,1)S(1)}, bf16[192,1280]{1,0:T(8,128)(2,1)}, u32[]{:S(2)}, u32[]{:S(2)}) collective-permute-start(bf16[192,1280]{1,0:T(8,128)(2,1)S(1)} %bitcast.14), channel_id=1, source_target_pairs={{0,2},{1,3},{2,0},{3,1},{4,6},{5,7},{6,4},{7,5},{8,10},{9,11},{10,... | collective-permute-start | bytes 1474568 | tf_op jit(solution)/shard_map/ppermute | solution.py:366
  36.3 3.4 %collective-permute-start.9 = (bf16[2,160,512]{2,1,0:T(8,128)(2,1)S(1)}, bf16[2,160,512]{2,1,0:T(8,128)(2,1)S(1)}, u32[]{:S(2)}, u32[]{:S(2)}) collective-permute-start(bf16[2,160,512]{2,1,0:T(8,128)(2,1)S(1)} %collective-permute-done.1.refs_10_), channel_id=1, source_target_pairs={{0,1},{1,0},{2,3},{3,2},{4,5},{5,4},{6,7},{7,6},{8,9},{9,8},{10,11... | collective-permute-start | bytes 983048 | tf_op jit(solution)/shard_map/ppermute | solution.py:366
  38.0 11.9 %collective-permute-start.8 = (bf16[2,160,512]{2,1,0:T(8,128)(2,1)S(1)}, bf16[2,160,512]{2,1,0:T(8,128)(2,1)}, u32[]{:S(2)}, u32[]{:S(2)}) collective-permute-start(bf16[2,160,512]{2,1,0:T(8,128)(2,1)S(1)} %collective-permute-done.1.refs_10_), channel_id=1, source_target_pairs={{0,4},{4,0},{8,12},{12,8},{16,20},{20,16},{24,28},{28,24},{1,5},{5... | collective-permute-start | bytes 983048 | tf_op jit(solution)/shard_map/ppermute | solution.py:366
  39.7 11.4 %collective-permute-start.6 = (bf16[120,1280]{1,0:T(8,128)(2,1)S(1)}, bf16[120,1280]{1,0:T(8,128)(2,1)S(1)}, u32[]{:S(2)}, u32[]{:S(2)}) collective-permute-start(bf16[120,1280]{1,0:T(8,128)(2,1)S(1)} %collective-permute-done.5.refs_6_.refs_27_), channel_id=1, source_target_pairs={{0,1},{1,0},{2,3},{3,2},{4,5},{5,4},{6,7},{7,6},{8,9},{9,8},{10,11... | collective-permute-start | bytes 921608 | tf_op jit(solution)/shard_map/ppermute | solution.py:366
  49.9 4.9 %collective-permute-start.14 = (bf16[400,640]{1,0:T(8,128)(2,1)}, bf16[400,640]{1,0:T(8,128)(2,1)S(1)}, u32[]{:S(2)}, u32[]{:S(2)}) collective-permute-start(bf16[400,640]{1,0:T(8,128)(2,1)} %collective-permute-done.11.refs_14_), channel_id=1, source_target_pairs={{0,1},{1,0},{2,3},{3,2},{4,5},{5,4},{6,7},{7,6},{8,9},{9,8},{10,11... | collective-permute-start | bytes 1536008 | tf_op jit(solution)/shard_map/ppermute | solution.py:366
  49.9 4.9 %collective-permute-start.16 = (bf16[400,640]{1,0:T(8,128)(2,1)S(1)}, bf16[400,640]{1,0:T(8,128)(2,1)S(1)}, u32[]{:S(2)}, u32[]{:S(2)}) collective-permute-start(bf16[400,640]{1,0:T(8,128)(2,1)S(1)} %collective-permute-done.13.refs_15_.refs_16_), channel_id=1, source_target_pairs={{0,1},{1,0},{2,3},{3,2},{4,5},{5,4},{6,7},{7,6},{8,9},{9,8},{10,11... | collective-permute-start | bytes 1536008 | tf_op jit(solution)/shard_map/ppermute | solution.py:366
  50.5 4.3 %collective-permute-start.15 = (bf16[400,640]{1,0:T(8,128)(2,1)S(1)}, bf16[400,640]{1,0:T(8,128)(2,1)S(1)}, u32[]{:S(2)}, u32[]{:S(2)}) collective-permute-start(bf16[400,640]{1,0:T(8,128)(2,1)S(1)} %collective-permute-done.12.refs_14_.refs_15_), channel_id=1, source_target_pairs={{0,1},{1,0},{2,3},{3,2},{4,5},{5,4},{6,7},{7,6},{8,9},{9,8},{10,11... | collective-permute-start | bytes 1536008 | tf_op jit(solution)/shard_map/ppermute | solution.py:366
  50.6 4.2 %collective-permute-start.3 = (bf16[192,1280]{1,0:T(8,128)(2,1)}, bf16[192,1280]{1,0:T(8,128)(2,1)S(1)}, u32[]{:S(2)}, u32[]{:S(2)}) collective-permute-start(bf16[192,1280]{1,0:T(8,128)(2,1)} %collective-permute-done.2.refs_2_), channel_id=1, source_target_pairs={{0,1},{1,0},{2,3},{3,2},{4,5},{5,4},{6,7},{7,6},{8,9},{9,8},{10,11... | collective-permute-start | bytes 1474568 | tf_op jit(solution)/shard_map/ppermute | solution.py:366
  51.8 3.0 %collective-permute-start.10 = (bf16[2,160,512]{2,1,0:T(8,128)(2,1)}, bf16[2,160,512]{2,1,0:T(8,128)(2,1)}, u32[]{:S(2)}, u32[]{:S(2)}) collective-permute-start(bf16[2,160,512]{2,1,0:T(8,128)(2,1)} %collective-permute-done.8.refs_11_), channel_id=1, source_target_pairs={{0,1},{1,0},{2,3},{3,2},{4,5},{5,4},{6,7},{7,6},{8,9},{9,8},{10,11... | collective-permute-start | bytes 983048 | tf_op jit(solution)/shard_map/ppermute | solution.py:366
  68.1 9.6 %collective-permute-start.25 = (bf16[240,640]{1,0:T(8,128)(2,1)}, bf16[240,640]{1,0:T(8,128)(2,1)S(1)}, u32[]{:S(2)}, u32[]{:S(2)}) collective-permute-start(bf16[240,640]{1,0:T(8,128)(2,1)} %get-tuple-element.117), channel_id=1, source_target_pairs={{0,4},{4,0},{8,12},{12,8},{16,20},{20,16},{24,28},{28,24},{1,5},{5... | collective-permute-start | bytes 921608 | tf_op jit(solution)/shard_map/ppermute | solution.py:366
  69.7 7.0 %collective-permute-start.26 = (bf16[160,640]{1,0:T(8,128)(2,1)}, bf16[160,640]{1,0:T(8,128)(2,1)S(1)}, u32[]{:S(2)}, u32[]{:S(2)}) collective-permute-start(bf16[160,640]{1,0:T(8,128)(2,1)} %get-tuple-element.118), channel_id=1, source_target_pairs={{0,8},{4,12},{8,0},{12,4},{16,24},{20,28},{24,16},{28,20},{1,9},{5... | collective-permute-start | bytes 614408 | tf_op jit(solution)/shard_map/ppermute | solution.py:366
  70.2 8.3 %collective-permute-start.22 = (bf16[192,256]{1,0:T(8,128)(2,1)}, bf16[192,256]{1,0:T(8,128)(2,1)S(1)}, u32[]{:S(2)}, u32[]{:S(2)}) collective-permute-start(bf16[192,256]{1,0:T(8,128)(2,1)} %get-tuple-element.114), channel_id=1, source_target_pairs={{0,1},{1,0},{2,3},{3,2},{4,5},{5,4},{6,7},{7,6},{8,9},{9,8},{10,11... | collective-permute-start | bytes 294920 | tf_op jit(solution)/shard_map/ppermute | solution.py:366
  70.3 8.3 %collective-permute-start.23 = (bf16[192,256]{1,0:T(8,128)(2,1)}, bf16[192,256]{1,0:T(8,128)(2,1)S(1)}, u32[]{:S(2)}, u32[]{:S(2)}) collective-permute-start(bf16[192,256]{1,0:T(8,128)(2,1)} %get-tuple-element.115), channel_id=1, source_target_pairs={{0,2},{1,3},{2,0},{3,1},{4,6},{5,7},{6,4},{7,5},{8,10},{9,11},{10,... | collective-permute-start | bytes 294920 | tf_op jit(solution)/shard_map/ppermute | solution.py:366
  71.9 6.7 %collective-permute-start.24 = (bf16[192,256]{1,0:T(8,128)(2,1)}, bf16[192,256]{1,0:T(8,128)(2,1)S(1)}, u32[]{:S(2)}, u32[]{:S(2)}) collective-permute-start(bf16[192,256]{1,0:T(8,128)(2,1)} %get-tuple-element.116), channel_id=1, source_target_pairs={{0,3},{1,2},{2,1},{3,0},{4,7},{5,6},{6,5},{7,4},{8,11},{9,10},{10,... | collective-permute-start | bytes 294920 | tf_op jit(solution)/shard_map/ppermute | solution.py:366
  76.7 1.9 collective-permute-start.28
  77.7 1.6 collective-permute-start.27
  96.4 7.4 %collective-permute-start.35 = (bf16[192,6912]{1,0:T(8,128)(2,1)}, bf16[192,6912]{1,0:T(8,128)(2,1)S(1)}, u32[]{:S(2)}, u32[]{:S(2)}) collective-permute-start(bf16[192,6912]{1,0:T(8,128)(2,1)} %get-tuple-element.135.refs_0_), channel_id=1, source_target_pairs={{0,1},{1,0},{2,3},{3,2},{4,5},{5,4},{6,7},{7,6},{8,9},{9,8},{10,11... | collective-permute-start | bytes 7962632 | tf_op jit(solution)/shard_map/ppermute | solution.py:366
  96.6 5.2 %collective-permute-start.32 = (bf16[192,256]{1,0:T(8,128)(2,1)}, bf16[192,256]{1,0:T(8,128)(2,1)S(1)}, u32[]{:S(2)}, u32[]{:S(2)}) collective-permute-start(bf16[192,256]{1,0:T(8,128)(2,1)} %get-tuple-element.126), channel_id=1, source_target_pairs={{0,1},{1,0},{2,3},{3,2},{4,5},{5,4},{6,7},{7,6},{8,9},{9,8},{10,11... | collective-permute-start | bytes 294920 | tf_op jit(solution)/shard_map/ppermute | solution.py:366
  97.0 5.4 %collective-permute-start.33 = (bf16[192,256]{1,0:T(8,128)(2,1)}, bf16[192,256]{1,0:T(8,128)(2,1)S(1)}, u32[]{:S(2)}, u32[]{:S(2)}) collective-permute-start(bf16[192,256]{1,0:T(8,128)(2,1)} %get-tuple-element.127), channel_id=1, source_target_pairs={{0,2},{1,3},{2,0},{3,1},{4,6},{5,7},{6,4},{7,5},{8,10},{9,11},{10,... | collective-permute-start | bytes 294920 | tf_op jit(solution)/shard_map/ppermute | solution.py:366
  98.5 5.3 %collective-permute-start.34 = (bf16[192,256]{1,0:T(8,128)(2,1)}, bf16[192,256]{1,0:T(8,128)(2,1)S(1)}, u32[]{:S(2)}, u32[]{:S(2)}) collective-permute-start(bf16[192,256]{1,0:T(8,128)(2,1)} %get-tuple-element.128), channel_id=1, source_target_pairs={{0,3},{1,2},{2,1},{3,0},{4,7},{5,6},{6,5},{7,4},{8,11},{9,10},{10,... | collective-permute-start | bytes 294920 | tf_op jit(solution)/shard_map/ppermute | solution.py:366
  110.6 29.2 %collective-permute-start.38 = (bf16[8,3,40,640]{3,2,1,0:T(8,128)(2,1)S(1)}, bf16[8,3,40,640]{3,2,1,0:T(8,128)(2,1)S(1)}, u32[]{:S(2)}, u32[]{:S(2)}) collective-permute-start(bf16[8,3,40,640]{3,2,1,0:T(8,128)(2,1)S(1)} %get-tuple-element.137.refs_11_), channel_id=1, source_target_pairs={{0,2},{1,3},{2,0},{3,1},{4,6},{5,7},{6,4},{7,5},{8,10},{9,11},{10,... | collective-permute-start | bytes 3686408 | tf_op jit(solution)/shard_map/ppermute | solution.py:366
  111.8 20.5 %collective-permute-start.39 = (bf16[2,2,2,80,640]{4,3,2,1,0:T(8,128)(2,1)S(1)}, bf16[2,2,2,80,640]{4,3,2,1,0:T(8,128)(2,1)S(1)}, u32[]{:S(2)}, u32[]{:S(2)}) collective-permute-start(bf16[2,2,2,80,640]{4,3,2,1,0:T(8,128)(2,1)S(1)} %get-tuple-element.136.refs_10_), channel_id=1, source_target_pairs={{0,8},{4,12},{8,0},{12,4},{16,24},{20,28},{24,16},{28,20},{1,9},{5... | collective-permute-start | bytes 2457608 | tf_op jit(solution)/shard_map/ppermute | solution.py:366
  119.4 25.6 %collective-permute-start.36 = (bf16[2,216,1280]{2,1,0:T(8,128)(2,1)S(1)}, bf16[2,216,1280]{2,1,0:T(8,128)(2,1)S(1)}, u32[]{:S(2)}, u32[]{:S(2)}) collective-permute-start(bf16[2,216,1280]{2,1,0:T(8,128)(2,1)S(1)} %get-tuple-element.139), channel_id=1, source_target_pairs={{0,1},{1,0},{2,3},{3,2},{4,5},{5,4},{6,7},{7,6},{8,9},{9,8},{10,11... | collective-permute-start | bytes 3317768 | tf_op jit(solution)/shard_map/ppermute | solution.py:366
  119.5 22.7 %collective-permute-start.37 = (bf16[4,4,40,512]{3,2,1,0:T(8,128)(2,1)S(1)}, bf16[4,4,40,512]{3,2,1,0:T(8,128)(2,1)S(1)}, u32[]{:S(2)}, u32[]{:S(2)}) collective-permute-start(bf16[4,4,40,512]{3,2,1,0:T(8,128)(2,1)S(1)} %get-tuple-element.141), channel_id=1, source_target_pairs={{0,4},{4,0},{8,12},{12,8},{16,20},{20,16},{24,28},{28,24},{1,5},{5... | collective-permute-start | bytes 1966088 | tf_op jit(solution)/shard_map/ppermute | solution.py:366
  140.6 15.2 %collective-permute-start.45 = (bf16[2,2,3,40,640]{4,3,2,1,0:T(8,128)(2,1)S(1)}, bf16[2,2,3,40,640]{4,3,2,1,0:T(8,128)(2,1)S(1)}, u32[]{:S(2)}, u32[]{:S(2)}) collective-permute-start(bf16[2,2,3,40,640]{4,3,2,1,0:T(8,128)(2,1)S(1)} %get-tuple-element.159), channel_id=1, source_target_pairs={{0,4},{4,0},{8,12},{12,8},{16,20},{20,16},{24,28},{28,24},{1,5},{5... | collective-permute-start | bytes 1843208 | tf_op jit(solution)/shard_map/ppermute | solution.py:366
  142.9 8.7 %collective-permute-start.42 = (bf16[2,4,40,512]{3,2,1,0:T(8,128)(2,1)S(1)}, bf16[2,4,40,512]{3,2,1,0:T(8,128)(2,1)S(1)}, u32[]{:S(2)}, u32[]{:S(2)}) collective-permute-start(bf16[2,4,40,512]{3,2,1,0:T(8,128)(2,1)S(1)} %get-tuple-element.152), channel_id=1, source_target_pairs={{0,8},{4,12},{8,0},{12,4},{16,24},{20,28},{24,16},{28,20},{1,9},{5... | collective-permute-start | bytes 983048 | tf_op jit(solution)/shard_map/ppermute | solution.py:366
  143.4 11.5 %collective-permute-start.41 = (bf16[2,2,80,640]{3,2,1,0:T(8,128)(2,1)S(1)}, bf16[2,2,80,640]{3,2,1,0:T(8,128)(2,1)S(1)}, u32[]{:S(2)}, u32[]{:S(2)}) collective-permute-start(bf16[2,2,80,640]{3,2,1,0:T(8,128)(2,1)S(1)} %get-tuple-element.150), channel_id=1, source_target_pairs={{0,2},{1,3},{2,0},{3,1},{4,6},{5,7},{6,4},{7,5},{8,10},{9,11},{10,... | collective-permute-start | bytes 1228808 | tf_op jit(solution)/shard_map/ppermute | solution.py:366
  152.3 15.7 %collective-permute-start.44 = (bf16[2,4,40,512]{3,2,1,0:T(8,128)(2,1)S(1)}, bf16[2,4,40,512]{3,2,1,0:T(8,128)(2,1)S(1)}, u32[]{:S(2)}, u32[]{:S(2)}) collective-permute-start(bf16[2,4,40,512]{3,2,1,0:T(8,128)(2,1)S(1)} %get-tuple-element.157.refs_0_), channel_id=1, source_target_pairs={{0,16},{4,20},{8,24},{12,28},{16,0},{20,4},{24,8},{28,12},{1,17},{... | collective-permute-start | bytes 983048 | tf_op jit(solution)/shard_map/ppermute | solution.py:366
  156.5 15.4 %collective-permute-start.50 = (bf16[2,3,40,640]{3,2,1,0:T(8,128)(2,1)S(1)}, bf16[2,3,40,640]{3,2,1,0:T(8,128)(2,1)S(1)}, u32[]{:S(2)}, u32[]{:S(2)}) collective-permute-start(bf16[2,3,40,640]{3,2,1,0:T(8,128)(2,1)S(1)} %get-tuple-element.169), channel_id=1, source_target_pairs={{0,8},{4,12},{8,0},{12,4},{16,24},{20,28},{24,16},{28,20},{1,9},{5... | collective-permute-start | bytes 921608 | tf_op jit(solution)/shard_map/ppermute | solution.py:366
  157.9 13.4 %collective-permute-start.43 = (bf16[2,80,640]{2,1,0:T(8,128)(2,1)S(1)}, bf16[2,80,640]{2,1,0:T(8,128)(2,1)S(1)}, u32[]{:S(2)}, u32[]{:S(2)}) collective-permute-start(bf16[2,80,640]{2,1,0:T(8,128)(2,1)S(1)} %get-tuple-element.156), channel_id=1, source_target_pairs={{0,4},{4,0},{8,12},{12,8},{16,20},{20,16},{24,28},{28,24},{1,5},{5... | collective-permute-start | bytes 614408 | tf_op jit(solution)/shard_map/ppermute | solution.py:366
  168.6 4.0 %collective-permute-start.47 = (bf16[2,40,512]{2,1,0:T(8,128)(2,1)S(1)}, bf16[2,40,512]{2,1,0:T(8,128)(2,1)S(1)}, u32[]{:S(2)}, u32[]{:S(2)}) collective-permute-start(bf16[2,40,512]{2,1,0:T(8,128)(2,1)S(1)} %get-tuple-element.165), channel_id=1, source_target_pairs={{0,1},{1,0},{2,3},{3,2},{4,5},{5,4},{6,7},{7,6},{8,9},{9,8},{10,11... | collective-permute-start | bytes 245768 | tf_op jit(solution)/shard_map/ppermute | solution.py:366
  168.7 5.6 %collective-permute-start.48 = (bf16[2,40,512]{2,1,0:T(8,128)(2,1)S(1)}, bf16[2,40,512]{2,1,0:T(8,128)(2,1)S(1)}, u32[]{:S(2)}, u32[]{:S(2)}) collective-permute-start(bf16[2,40,512]{2,1,0:T(8,128)(2,1)S(1)} %get-tuple-element.166), channel_id=1, source_target_pairs={{0,2},{1,3},{2,0},{3,1},{4,6},{5,7},{6,4},{7,5},{8,10},{9,11},{10,... | collective-permute-start | bytes 245768 | tf_op jit(solution)/shard_map/ppermute | solution.py:366
  171.2 4.5 %collective-permute-start.49 = (bf16[2,40,512]{2,1,0:T(8,128)(2,1)S(1)}, bf16[2,40,512]{2,1,0:T(8,128)(2,1)S(1)}, u32[]{:S(2)}, u32[]{:S(2)}) collective-permute-start(bf16[2,40,512]{2,1,0:T(8,128)(2,1)S(1)} %get-tuple-element.167), channel_id=1, source_target_pairs={{0,3},{1,2},{2,1},{3,0},{4,7},{5,6},{6,5},{7,4},{8,11},{9,10},{10,... | collective-permute-start | bytes 245768 | tf_op jit(solution)/shard_map/ppermute | solution.py:366
  171.3 29.9 %copy-start.3 = (bf16[1,2,96,1280]{3,2,1,0:T(8,128)(2,1)S(1)}, bf16[1,2,96,1280]{3,2,1,0:T(8,128)(2,1)}, u32[]{:S(2)}) copy-start(bf16[1,2,96,1280]{3,2,1,0:T(8,128)(2,1)} %param.11) | copy-start | bytes 1474564
  171.3 29.9 %copy-start.10 = (bf16[96,1280]{1,0:T(8,128)(2,1)S(1)}, bf16[96,1280]{1,0:T(8,128)(2,1)}, u32[]{:S(2)}) copy-start(bf16[96,1280]{1,0:T(8,128)(2,1)} %get-tuple-element.121.refs_1_) | copy-start | bytes 737284
  176.3 9.8 %collective-permute-start.51 = (bf16[2,4,40,512]{3,2,1,0:T(8,128)(2,1)S(1)}, bf16[2,4,40,512]{3,2,1,0:T(8,128)(2,1)S(1)}, u32[]{:S(2)}, u32[]{:S(2)}) collective-permute-start(bf16[2,4,40,512]{3,2,1,0:T(8,128)(2,1)S(1)} %get-tuple-element.172.refs_0_), channel_id=1, source_target_pairs={{0,4},{4,0},{8,12},{12,8},{16,20},{20,16},{24,28},{28,24},{1,5},{5... | collective-permute-start | bytes 983048 | tf_op jit(solution)/shard_map/ppermute | solution.py:366
  176.9 24.3 %collective-permute-start.40 = (bf16[216,1280]{1,0:T(8,128)(2,1)S(1)}, bf16[216,1280]{1,0:T(8,128)(2,1)S(1)}, u32[]{:S(2)}, u32[]{:S(2)}) collective-permute-start(bf16[216,1280]{1,0:T(8,128)(2,1)S(1)} %get-tuple-element.148), channel_id=1, source_target_pairs={{0,2},{1,3},{2,0},{3,1},{4,6},{5,7},{6,4},{7,5},{8,10},{9,11},{10,... | collective-permute-start | bytes 1658888 | tf_op jit(solution)/shard_map/ppermute | solution.py:366
  178.5 11.4 %collective-permute-start.29 = (bf16[96,1280]{1,0:T(8,128)(2,1)S(1)}, bf16[96,1280]{1,0:T(8,128)(2,1)S(1)}, u32[]{:S(2)}, u32[]{:S(2)}) collective-permute-start(bf16[96,1280]{1,0:T(8,128)(2,1)S(1)} %copy-done.40), channel_id=1, source_target_pairs={{0,1},{1,0},{2,3},{3,2},{4,5},{5,4},{6,7},{7,6},{8,9},{9,8},{10,11... | collective-permute-start | bytes 737288 | tf_op jit(solution)/shard_map/ppermute | solution.py:366
  178.5 13.2 %collective-permute-start.46 = (bf16[2,80,640]{2,1,0:T(8,128)(2,1)S(1)}, bf16[2,80,640]{2,1,0:T(8,128)(2,1)S(1)}, u32[]{:S(2)}, u32[]{:S(2)}) collective-permute-start(bf16[2,80,640]{2,1,0:T(8,128)(2,1)S(1)} %get-tuple-element.163.refs_0_), channel_id=1, source_target_pairs={{0,16},{4,20},{8,24},{12,28},{16,0},{20,4},{24,8},{28,12},{1,17},{... | collective-permute-start | bytes 614408 | tf_op jit(solution)/shard_map/ppermute | solution.py:366
  186.7 25.2 %collective-permute-start.52 = (bf16[2,2,4,40,512]{4,3,2,1,0:T(8,128)(2,1)S(1)}, bf16[2,2,4,40,512]{4,3,2,1,0:T(8,128)(2,1)S(1)}, u32[]{:S(2)}, u32[]{:S(2)}) collective-permute-start(bf16[2,2,4,40,512]{4,3,2,1,0:T(8,128)(2,1)S(1)} %get-tuple-element.179.refs_0_), channel_id=1, source_target_pairs={{0,8},{4,12},{8,0},{12,4},{16,24},{20,28},{24,16},{28,20},{1,9},{5... | collective-permute-start | bytes 1966088 | tf_op jit(solution)/shard_map/ppermute | solution.py:366
  186.8 20.3 %collective-permute-start.53 = (bf16[2,3,40,640]{3,2,1,0:T(8,128)(2,1)S(1)}, bf16[2,3,40,640]{3,2,1,0:T(8,128)(2,1)S(1)}, u32[]{:S(2)}, u32[]{:S(2)}) collective-permute-start(bf16[2,3,40,640]{3,2,1,0:T(8,128)(2,1)S(1)} %get-tuple-element.180.refs_0_), channel_id=1, source_target_pairs={{0,16},{4,20},{8,24},{12,28},{16,0},{20,4},{24,8},{28,12},{1,17},{... | collective-permute-start | bytes 921608 | tf_op jit(solution)/shard_map/ppermute | solution.py:366
  189.9 8.8 %collective-permute-start.30 = (bf16[96,1280]{1,0:T(8,128)(2,1)S(1)}, bf16[96,1280]{1,0:T(8,128)(2,1)S(1)}, u32[]{:S(2)}, u32[]{:S(2)}) collective-permute-start(bf16[96,1280]{1,0:T(8,128)(2,1)S(1)} %copy-done.39), channel_id=1, source_target_pairs={{0,2},{1,3},{2,0},{3,1},{4,6},{5,7},{6,4},{7,5},{8,10},{9,11},{10,... | collective-permute-start | bytes 737288 | tf_op jit(solution)/shard_map/ppermute | solution.py:366
  191.7 9.5 %collective-permute-start.31 = (bf16[96,1280]{1,0:T(8,128)(2,1)S(1)}, bf16[96,1280]{1,0:T(8,128)(2,1)S(1)}, u32[]{:S(2)}, u32[]{:S(2)}) collective-permute-start(bf16[96,1280]{1,0:T(8,128)(2,1)S(1)} %copy-done.38), channel_id=1, source_target_pairs={{0,3},{1,2},{2,1},{3,0},{4,7},{5,6},{6,5},{7,4},{8,11},{9,10},{10,... | collective-permute-start | bytes 737288 | tf_op jit(solution)/shard_map/ppermute | solution.py:366
  207.7 9.1 %collective-permute-start.56 = (bf16[2,3,40,640]{3,2,1,0:T(8,128)(2,1)S(1)}, bf16[2,3,40,640]{3,2,1,0:T(8,128)(2,1)S(1)}, u32[]{:S(2)}, u32[]{:S(2)}) collective-permute-start(bf16[2,3,40,640]{3,2,1,0:T(8,128)(2,1)S(1)} %get-tuple-element.189.refs_0_), channel_id=1, source_target_pairs={{0,4},{4,0},{8,12},{12,8},{16,20},{20,16},{24,28},{28,24},{1,5},{5... | collective-permute-start | bytes 921608 | tf_op jit(solution)/shard_map/ppermute | solution.py:366
  208.3 7.9 %collective-permute-start.54 = (bf16[2,80,640]{2,1,0:T(8,128)(2,1)S(1)}, bf16[2,80,640]{2,1,0:T(8,128)(2,1)S(1)}, u32[]{:S(2)}, u32[]{:S(2)}) collective-permute-start(bf16[2,80,640]{2,1,0:T(8,128)(2,1)S(1)} %get-tuple-element.186.refs_0_), channel_id=1, source_target_pairs={{0,8},{4,12},{8,0},{12,4},{16,24},{20,28},{24,16},{28,20},{1,9},{5... | collective-permute-start | bytes 614408 | tf_op jit(solution)/shard_map/ppermute | solution.py:366
  217.4 14.3 %collective-permute-start.57 = (bf16[2,2,3,40,640]{4,3,2,1,0:T(8,128)(2,1)S(1)}, bf16[2,2,3,40,640]{4,3,2,1,0:T(8,128)(2,1)S(1)}, u32[]{:S(2)}, u32[]{:S(2)}) collective-permute-start(bf16[2,2,3,40,640]{4,3,2,1,0:T(8,128)(2,1)S(1)} %get-tuple-element.193.refs_0_), channel_id=1, source_target_pairs={{0,8},{4,12},{8,0},{12,4},{16,24},{20,28},{24,16},{28,20},{1,9},{5... | collective-permute-start | bytes 1843208 | tf_op jit(solution)/shard_map/ppermute | solution.py:366
  219.8 8.8 %collective-permute-start.55 = (bf16[2,2,80,640]{3,2,1,0:T(8,128)(2,1)S(1)}, bf16[2,2,80,640]{3,2,1,0:T(8,128)(2,1)S(1)}, u32[]{:S(2)}, u32[]{:S(2)}) collective-permute-start(bf16[2,2,80,640]{3,2,1,0:T(8,128)(2,1)S(1)} %get-tuple-element.188.refs_0_), channel_id=1, source_target_pairs={{0,4},{4,0},{8,12},{12,8},{16,20},{20,16},{24,28},{28,24},{1,5},{5... | collective-permute-start | bytes 1228808 | tf_op jit(solution)/shard_map/ppermute | solution.py:366
  (39 other events, 306.3 us)

commit v5 on v4

--- a/solution.py
+++ b/solution.py
@@ -1022,7 +1022,7 @@
         2_000_000_000,
         2 * n + 9,
         2 * n + 8,
-        (*far_near, *others_near),
+        tuple(far_near),
     )(idx, *all_frames, *all_refer, *packs, second, third)
     mixed = exchange(mixed)
     fourth = [flip(tall_part, "clip", 1), flip(flat_part, "clip", 2)]

time: 234 us -> 232 us (level)
    unnamed x90 -> x76, local copies, waits for them, and re-layouts: 6.18 us -> 4.3 us
  transfers between devices with their start and end apart: 58 -> 58, of which waited for: 26 -> 27; matrix products, arithmetic and copies ran while one was open for 0% -> 0% of each run, Pallas kernels for 10% -> 16%
where the time goes in v5:
time: 232 us
  waiting for transfers between devices  113 us (49%)
  Pallas kernels  64.2 us (28%)
  starting transfers between devices  48.3 us (21%)
  local copies, waits for them, and re-layouts  4.3 us (2%)
    ppermute x58, waiting for transfers between devices, flip(): return lax.ppermute(value, axis, [(i, i ^ bit) for i in range(size)])  113 us
    pallas_call x25, Pallas kernels, wide_call(): return lambda *operands: call(*operands, *late)  64.2 us
    ppermute x58, starting transfers between devices, flip(): return lax.ppermute(value, axis, [(i, i ^ bit) for i in range(size)])  48.3 us
  transfers between devices with their start and end apart: 58, of which 27 were waited for; matrix products, arithmetic and copies ran while one was open for 0% of the time, Pallas kernels for 16%

profile of v5, /device:TPU:0, one launch (start us, length us, event | category | flops | bytes accessed | tf_op | source)
XLA Modules:
  0.0 232.2 jit_solution(4550510733721206716)
XLA Ops:
  1.3 4.3 %pack_heads.1 = (bf16[320,512]{1,0:T(8,128)(2,1)}, bf16[320,512]{1,0:T(8,128)(2,1)}, bf16[2,160,512]{2,1,0:T(8,128)(2,1)}, bf16[400,640]{1,0:T(8,128)(2,1)}, bf1...) custom-call(s32[2]{0:T(128)} %pad_add_fusion.idx, bf16[320,640]{1,0:T(8,128)(2,1)} %refs_0_.1, ...), custom_call_target="tpu_custom_call" | custom-call | flops 1 | bytes 1 | tf_op jit(solution)/shard_map/pack_heads/pallas_call | solution.py:357
  5.6 3.0 %collective-permute-start.1 = (bf16[2,160,512]{2,1,0:T(8,128)(2,1)}, bf16[2,160,512]{2,1,0:T(8,128)(2,1)S(1)}, u32[]{:S(2)}, u32[]{:S(2)}) collective-permute-start(bf16[2,160,512]{2,1,0:T(8,128)(2,1)} %get-tuple-element.105), channel_id=1, source_target_pairs={{0,2},{1,3},{2,0},{3,1},{4,6},{5,7},{6,4},{7,5},{8,10},{9,11},{10,... | collective-permute-start | bytes 983048 | tf_op jit(solution)/shard_map/ppermute | solution.py:366
  9.2 8.2 %collective-permute-done.1.refs_10_ = bf16[2,160,512]{2,1,0:T(8,128)(2,1)S(1)} collective-permute-done((bf16[2,160,512]{2,1,0:T(8,128)(2,1)}, bf16[2,160,512]{2,1,0:T(8,128)(2,1)S(1)}, u32[]{:S(2)}, u32[]{:S(2)}) %collective-permute-start.1) | collective-permute-done | bytes 327712 | tf_op jit(solution)/shard_map/ppermute | solution.py:366
  17.4 2.1 collective-permute-start.5
  19.6 8.7 %collective-permute-done.11.refs_14_ = bf16[400,640]{1,0:T(8,128)(2,1)S(1)} collective-permute-done((bf16[400,640]{1,0:T(8,128)(2,1)}, bf16[400,640]{1,0:T(8,128)(2,1)S(1)}, u32[]{:S(2)}, u32[]{:S(2)}) %collective-permute-start.11) | collective-permute-done | bytes 512032 | tf_op jit(solution)/shard_map/ppermute | solution.py:366
  28.3 2.1 collective-permute-start.13
  30.5 1.5 collective-permute-start.12
  31.9 3.0 %collective-permute-done.5.refs_6_.refs_27_ = bf16[120,1280]{1,0:T(8,128)(2,1)S(1)} collective-permute-done((bf16[120,1280]{1,0:T(8,128)(2,1)}, bf16[120,1280]{1,0:T(8,128)(2,1)S(1)}, u32[]{:S(2)}, u32[]{:S(2)}) %collective-permute-start.5) | collective-permute-done | bytes 307232 | tf_op jit(solution)/shard_map/ppermute | solution.py:366
  34.9 2.0 collective-permute-start.8
  37.0 11.7 %collective-permute-done.8.refs_11_ = bf16[2,160,512]{2,1,0:T(8,128)(2,1)} collective-permute-done((bf16[2,160,512]{2,1,0:T(8,128)(2,1)S(1)}, bf16[2,160,512]{2,1,0:T(8,128)(2,1)}, u32[]{:S(2)}, u32[]{:S(2)}) %collective-permute-start.8) | collective-permute-done | bytes 327712 | tf_op jit(solution)/shard_map/ppermute | solution.py:366
  49.8 0.7 copy-done.28
  51.8 1.6 collective-permute-done.3.refs_3_
  54.2 12.0 %spatial_forward.1 = (bf16[864,1280]{1,0:T(8,128)(2,1)}, bf16[1280,512]{1,0:T(8,128)(2,1)}, bf16[864,256]{1,0:T(8,128)(2,1)}, bf16[864,256]{1,0:T(8,128)(2,1)}, ...) custom-call(s32[2]{0:T(128)} %pad_add_fusion.idx, ...), custom_call_target="tpu_custom_call" | custom-call | flops 2000000000 | bytes 8000000 | tf_op jit(solution)/shard_map/spatial_forward/pallas_call | solution.py:357
  66.2 1.6 collective-permute-start.25
  68.5 1.6 collective-permute-start.18
  70.3 4.7 %collective-permute-done.26.refs_18_ = bf16[160,640]{1,0:T(8,128)(2,1)S(1)} collective-permute-done((bf16[160,640]{1,0:T(8,128)(2,1)}, bf16[160,640]{1,0:T(8,128)(2,1)S(1)}, u32[]{:S(2)}, u32[]{:S(2)}) %collective-permute-start.26) | collective-permute-done | bytes 204832 | tf_op jit(solution)/shard_map/ppermute | solution.py:366
  75.0 1.0 collective-permute-done.25.refs_17_
  76.0 0.8 fusion.refs_29_
  76.9 0.7 collective-permute-done.27.refs_22_
  77.6 0.7 copy-done.30
  78.3 16.5 %temporal.1 = (bf16[192,256]{1,0:T(8,128)(2,1)}, bf16[192,256]{1,0:T(8,128)(2,1)}, bf16[192,256]{1,0:T(8,128)(2,1)}, bf16[192,256]{1,0:T(8,128)(2,1)}, bf16[96,1...) custom-call(s32[2]{0:T(128)} %pad_add_fusion.idx, ...), custom_call_target="tpu_custom_call" | custom-call | flops 5000000000 | bytes 8000000 | tf_op jit(solution)/shard_map/temporal/pallas_call | solution.py:357
  95.3 1.5 collective-permute-start.33
  96.9 3.3 %collective-permute-done.32.refs_4_.refs_1_ = bf16[192,256]{1,0:T(8,128)(2,1)S(1)} collective-permute-done((bf16[192,256]{1,0:T(8,128)(2,1)}, bf16[192,256]{1,0:T(8,128)(2,1)S(1)}, u32[]{:S(2)}, u32[]{:S(2)}) %collective-permute-start.32) | collective-permute-done | bytes 98336 | tf_op jit(solution)/shard_map/ppermute | solution.py:366
  100.7 1.5 collective-permute-done.34.refs_6_.refs_3_
  102.2 1.7 copy-done
  103.9 0.9 copy-done.14
  104.8 4.1 %temporal_terms.1 = (bf16[8,3,40,640]{3,2,1,0:T(8,128)(2,1)S(1)}, bf16[8,3,40,640]{3,2,1,0:T(8,128)(2,1)S(1)}, bf16[2,2,2,80,640]{4,3,2,1,0:T(8,128)(2,1)S(1)}, bf16[2,2,2,80,640]{4,3,2,1,0:T(8,128)(2,1)S(1)}) custom-call(s32[2]{0:T(128)S(1)} %copy-done.9, bf16[192,6912]{1,0:T(8,128)(2,1)S(1)} %copy-done, ...), custom_call_target="tpu_custom_call" | custom-call | flops 1 | bytes 1 | tf_op jit(solution)/shard_map/temporal_terms/pallas_call | solution.py:357
  109.0 1.1 collective-permute-start.38
  110.6 7.2 %spatial_backward.1 = (bf16[2,216,1280]{2,1,0:T(8,128)(2,1)S(1)}, bf16[2,216,1280]{2,1,0:T(8,128)(2,1)S(1)}, bf16[4,4,40,512]{3,2,1,0:T(8,128)(2,1)S(1)}, bf16[4,4,40,512]{3,2,1,0:T(8,128)(2,1)S(1)}) custom-call(s32[2]{0:T(128)S(1)} %copy-done.9, bf16[192,256]{1,0:T(8,128)(2,1)S(1)} %copy-done.11, ...), custom_call_target="tpu_custom_call" | custom-call | flops 1 | bytes 1 | tf_op jit(solution)/shard_map/spatial_backward/pallas_call | solution.py:357
  117.9 1.5 collective-permute-start.37
  119.4 11.2 %collective-permute-done.39.refs_1_ = bf16[2,2,2,80,640]{4,3,2,1,0:T(8,128)(2,1)S(1)} collective-permute-done((bf16[2,2,2,80,640]{4,3,2,1,0:T(8,128)(2,1)S(1)}, bf16[2,2,2,80,640]{4,3,2,1,0:T(8,128)(2,1)S(1)}, u32[]{:S(2)}, u32[]{:S(2)}) %collective-permute-start.39) | collective-permute-done | bytes 819232 | tf_op jit(solution)/shard_map/ppermute | solution.py:366
  130.6 0.7 merge.12
  131.3 6.8 %collective-permute-done.38 = bf16[8,3,40,640]{3,2,1,0:T(8,128)(2,1)S(1)} collective-permute-done((bf16[8,3,40,640]{3,2,1,0:T(8,128)(2,1)S(1)}, bf16[8,3,40,640]{3,2,1,0:T(8,128)(2,1)S(1)}, u32[]{:S(2)}, u32[]{:S(2)}) %collective-permute-start.38) | collective-permute-done | bytes 1228832 | tf_op jit(solution)/shard_map/ppermute | solution.py:366
  138.1 0.8 merge.13
  139.0 1.5 collective-permute-start.45
  140.5 0.7 merge.14
  141.7 1.5 collective-permute-start.41
  143.3 0.8 merge.15
  144.1 5.9 %collective-permute-done.42.refs_1_ = bf16[2,4,40,512]{3,2,1,0:T(8,128)(2,1)S(1)} collective-permute-done((bf16[2,4,40,512]{3,2,1,0:T(8,128)(2,1)S(1)}, bf16[2,4,40,512]{3,2,1,0:T(8,128)(2,1)S(1)}, u32[]{:S(2)}, u32[]{:S(2)}) %collective-permute-start.42) | collective-permute-done | bytes 327712 | tf_op jit(solution)/shard_map/ppermute | solution.py:366
  150.5 2.7 %collective-permute-start.44 = (bf16[2,4,40,512]{3,2,1,0:T(8,128)(2,1)S(1)}, bf16[2,4,40,512]{3,2,1,0:T(8,128)(2,1)S(1)}, u32[]{:S(2)}, u32[]{:S(2)}) collective-permute-start(bf16[2,4,40,512]{3,2,1,0:T(8,128)(2,1)S(1)} %get-tuple-element.157.refs_0_), channel_id=1, source_target_pairs={{0,16},{4,20},{8,24},{12,28},{16,0},{20,4},{24,8},{28,12},{1,17},{... | collective-permute-start | bytes 983048 | tf_op jit(solution)/shard_map/ppermute | solution.py:366
  153.2 0.7 merge.17
  154.1 0.7 merge.18
  154.8 0.8 collective-permute-start.50
  155.6 1.2 collective-permute-start.43
  156.8 9.5 %collective-permute-done.44.refs_1_ = bf16[2,4,40,512]{3,2,1,0:T(8,128)(2,1)S(1)} collective-permute-done((bf16[2,4,40,512]{3,2,1,0:T(8,128)(2,1)S(1)}, bf16[2,4,40,512]{3,2,1,0:T(8,128)(2,1)S(1)}, u32[]{:S(2)}, u32[]{:S(2)}) %collective-permute-start.44) | collective-permute-done | bytes 327712 | tf_op jit(solution)/shard_map/ppermute | solution.py:366
  167.0 2.6 %collective-permute-start.48 = (bf16[2,40,512]{2,1,0:T(8,128)(2,1)S(1)}, bf16[2,40,512]{2,1,0:T(8,128)(2,1)S(1)}, u32[]{:S(2)}, u32[]{:S(2)}) collective-permute-start(bf16[2,40,512]{2,1,0:T(8,128)(2,1)S(1)} %get-tuple-element.166), channel_id=1, source_target_pairs={{0,2},{1,3},{2,0},{3,1},{4,6},{5,7},{6,4},{7,5},{8,10},{9,11},{10,... | collective-permute-start | bytes 245768 | tf_op jit(solution)/shard_map/ppermute | solution.py:366
  170.9 1.7 collective-permute-done.48.refs_2_
  172.6 1.5 collective-permute-done.49.refs_3_
  175.2 1.6 collective-permute-start.40
  176.9 7.6 %collective-permute-done.51.refs_1_ = bf16[2,4,40,512]{3,2,1,0:T(8,128)(2,1)S(1)} collective-permute-done((bf16[2,4,40,512]{3,2,1,0:T(8,128)(2,1)S(1)}, bf16[2,4,40,512]{3,2,1,0:T(8,128)(2,1)S(1)}, u32[]{:S(2)}, u32[]{:S(2)}) %collective-permute-start.51) | collective-permute-done | bytes 327712 | tf_op jit(solution)/shard_map/ppermute | solution.py:366
  185.1 3.1 %collective-permute-start.53 = (bf16[2,3,40,640]{3,2,1,0:T(8,128)(2,1)S(1)}, bf16[2,3,40,640]{3,2,1,0:T(8,128)(2,1)S(1)}, u32[]{:S(2)}, u32[]{:S(2)}) collective-permute-start(bf16[2,3,40,640]{3,2,1,0:T(8,128)(2,1)S(1)} %get-tuple-element.180.refs_0_), channel_id=1, source_target_pairs={{0,16},{4,20},{8,24},{12,28},{16,0},{20,4},{24,8},{28,12},{1,17},{... | collective-permute-start | bytes 921608 | tf_op jit(solution)/shard_map/ppermute | solution.py:366
  188.2 1.8 collective-permute-start.30
  190.6 6.4 %collective-permute-done.30.refs_3_ = bf16[96,1280]{1,0:T(8,128)(2,1)S(1)} collective-permute-done((bf16[96,1280]{1,0:T(8,128)(2,1)S(1)}, bf16[96,1280]{1,0:T(8,128)(2,1)S(1)}, u32[]{:S(2)}, u32[]{:S(2)}) %collective-permute-start.30) | collective-permute-done | bytes 245792 | tf_op jit(solution)/shard_map/ppermute | solution.py:366
  197.0 2.5 %collective-permute-done.31.refs_4_ = bf16[96,1280]{1,0:T(8,128)(2,1)S(1)} collective-permute-done((bf16[96,1280]{1,0:T(8,128)(2,1)S(1)}, bf16[96,1280]{1,0:T(8,128)(2,1)S(1)}, u32[]{:S(2)}, u32[]{:S(2)}) %collective-permute-start.31) | collective-permute-done | bytes 245792 | tf_op jit(solution)/shard_map/ppermute | solution.py:366
  199.6 3.3 %finish.1 = (bf16[192,1280]{1,0:T(8,128)(2,1)}, bf16[192,1280]{1,0:T(8,128)(2,1)}, bf16[24,1280]{1,0:T(8,128)(2,1)}, f32[8,128]{1,0:T(8,128)S(1)}) custom-call(s32[2]{0:T(128)S(1)} %copy-done.9, bf16[192,1280]{1,0:T(8,128)(2,1)S(1)} %bitcast.19, bf16[96,1280]{1,0:T(8,128)(2,1)S(1)} %copy-done.10, bf16[96,1280]{1,0:T(8,128)(2,1)S(1)} %collective-permute-done.29.refs_2_, ...), custom_call_target="tpu_custom_call" | custom-call | flops 1 | bytes 1 | tf_op jit(solution)/shard_map/finish/pallas_call | solution.py:357
  202.8 2.6 %collective-permute-done.53.refs_1_ = bf16[2,3,40,640]{3,2,1,0:T(8,128)(2,1)S(1)} collective-permute-done((bf16[2,3,40,640]{3,2,1,0:T(8,128)(2,1)S(1)}, bf16[2,3,40,640]{3,2,1,0:T(8,128)(2,1)S(1)}, u32[]{:S(2)}, u32[]{:S(2)}) %collective-permute-start.53) | collective-permute-done | bytes 307232 | tf_op jit(solution)/shard_map/ppermute | solution.py:366
  206.6 3.6 %collective-permute-start.54 = (bf16[2,80,640]{2,1,0:T(8,128)(2,1)S(1)}, bf16[2,80,640]{2,1,0:T(8,128)(2,1)S(1)}, u32[]{:S(2)}, u32[]{:S(2)}) collective-permute-start(bf16[2,80,640]{2,1,0:T(8,128)(2,1)S(1)} %get-tuple-element.186.refs_0_), channel_id=1, source_target_pairs={{0,8},{4,12},{8,0},{12,4},{16,24},{20,28},{24,16},{28,20},{1,9},{5... | collective-permute-start | bytes 614408 | tf_op jit(solution)/shard_map/ppermute | solution.py:366
  210.3 2.4 %place_heads.1 = (f32[320,640]{1,0:T(8,128)}, f32[320,640]{1,0:T(8,128)}, f32[320,640]{1,0:T(8,128)}, f32[8,128]{1,0:T(8,128)S(1)}) custom-call(s32[2]{0:T(128)S(1)} %copy-done.9, bf16[2,2,4,40,512]{4,3,2,1,0:T(8,128)(2,1)S(1)} %get-tuple-element.179.refs_0_, bf16[2,2,4,40,512]{4,3,2,1,0:T(8,128)(2,1)S(1)} %collective-permute-done.52.refs_1_, ...), custom_call_target="tpu_custom_call" | custom-call | flops 1 | bytes 1 | tf_op jit(solution)/shard_map/place_heads/pallas_call | solution.py:357
  212.7 1.9 collective-permute-done.54.refs_1_
  215.7 2.4 %collective-permute-start.57 = (bf16[2,2,3,40,640]{4,3,2,1,0:T(8,128)(2,1)S(1)}, bf16[2,2,3,40,640]{4,3,2,1,0:T(8,128)(2,1)S(1)}, u32[]{:S(2)}, u32[]{:S(2)}) collective-permute-start(bf16[2,2,3,40,640]{4,3,2,1,0:T(8,128)(2,1)S(1)} %get-tuple-element.193.refs_0_), channel_id=1, source_target_pairs={{0,8},{4,12},{8,0},{12,4},{16,24},{20,28},{24,16},{28,20},{1,9},{5... | collective-permute-start | bytes 1843208 | tf_op jit(solution)/shard_map/ppermute | solution.py:366
  218.7 8.3 %collective-permute-done.55.refs_1_ = bf16[2,2,80,640]{3,2,1,0:T(8,128)(2,1)S(1)} collective-permute-done((bf16[2,2,80,640]{3,2,1,0:T(8,128)(2,1)S(1)}, bf16[2,2,80,640]{3,2,1,0:T(8,128)(2,1)S(1)}, u32[]{:S(2)}, u32[]{:S(2)}) %collective-permute-start.55) | collective-permute-done | bytes 409632 | tf_op jit(solution)/shard_map/ppermute | solution.py:366
  227.0 1.9 place_flat.1
  228.9 1.2 collective-permute-done.57.refs_1_
  230.0 2.1 place_tall.1
  (160 shorter events, 16.1 us)
Async XLA Ops:
  1.3 50.0 %copy-start.18 = (bf16[160,1280]{1,0:T(8,128)(2,1)S(1)}, bf16[160,1280]{1,0:T(8,128)(2,1)}, u32[]{:S(2)}) copy-start(bf16[160,1280]{1,0:T(8,128)(2,1)} %refs_7_.3) | copy-start | bytes 1228804
  1.3 50.2 %copy-start.15 = (bf16[320,640]{1,0:T(8,128)(2,1)S(1)}, bf16[320,640]{1,0:T(8,128)(2,1)}, u32[]{:S(2)}) copy-start(bf16[320,640]{1,0:T(8,128)(2,1)} %refs_4_.3) | copy-start | bytes 1228804
  1.3 52.1 %copy-start.16 = (bf16[320,640]{1,0:T(8,128)(2,1)S(1)}, bf16[320,640]{1,0:T(8,128)(2,1)}, u32[]{:S(2)}) copy-start(bf16[320,640]{1,0:T(8,128)(2,1)} %refs_5_.3) | copy-start | bytes 1228804
  1.3 52.3 %copy-start.17 = (bf16[320,640]{1,0:T(8,128)(2,1)S(1)}, bf16[320,640]{1,0:T(8,128)(2,1)}, u32[]{:S(2)}) copy-start(bf16[320,640]{1,0:T(8,128)(2,1)} %refs_6_.3) | copy-start | bytes 1228804
  1.3 52.6 %copy-start.19 = (bf16[160,1280]{1,0:T(8,128)(2,1)S(1)}, bf16[160,1280]{1,0:T(8,128)(2,1)}, u32[]{:S(2)}) copy-start(bf16[160,1280]{1,0:T(8,128)(2,1)} %refs_8_.1) | copy-start | bytes 1228804
  5.6 11.8 %collective-permute-start.1 = (bf16[2,160,512]{2,1,0:T(8,128)(2,1)}, bf16[2,160,512]{2,1,0:T(8,128)(2,1)S(1)}, u32[]{:S(2)}, u32[]{:S(2)}) collective-permute-start(bf16[2,160,512]{2,1,0:T(8,128)(2,1)} %get-tuple-element.105), channel_id=1, source_target_pairs={{0,2},{1,3},{2,0},{3,1},{4,6},{5,7},{6,4},{7,5},{8,10},{9,11},{10,... | collective-permute-start | bytes 983048 | tf_op jit(solution)/shard_map/ppermute | solution.py:366
  8.6 19.7 %collective-permute-start.11 = (bf16[400,640]{1,0:T(8,128)(2,1)}, bf16[400,640]{1,0:T(8,128)(2,1)S(1)}, u32[]{:S(2)}, u32[]{:S(2)}) collective-permute-start(bf16[400,640]{1,0:T(8,128)(2,1)} %get-tuple-element.112), channel_id=1, source_target_pairs={{0,2},{1,3},{2,0},{3,1},{4,6},{5,7},{6,4},{7,5},{8,10},{9,11},{10,... | collective-permute-start | bytes 1536008 | tf_op jit(solution)/shard_map/ppermute | solution.py:366
  8.7 21.8 %collective-permute-start = (bf16[192,1280]{1,0:T(8,128)(2,1)S(1)}, bf16[192,1280]{1,0:T(8,128)(2,1)S(1)}, u32[]{:S(2)}, u32[]{:S(2)}) collective-permute-start(bf16[192,1280]{1,0:T(8,128)(2,1)S(1)} %bitcast.17), channel_id=1, source_target_pairs={{0,1},{1,0},{2,3},{3,2},{4,5},{5,4},{6,7},{7,6},{8,9},{9,8},{10,11... | collective-permute-start | bytes 1474568 | tf_op jit(solution)/shard_map/ppermute | solution.py:366
  8.7 10.7 %collective-permute-start.7 = (bf16[320,512]{1,0:T(8,128)(2,1)}, bf16[320,512]{1,0:T(8,128)(2,1)S(1)}, u32[]{:S(2)}, u32[]{:S(2)}) collective-permute-start(bf16[320,512]{1,0:T(8,128)(2,1)} %get-tuple-element.111), channel_id=1, source_target_pairs={{0,1},{1,0},{2,3},{3,2},{4,5},{5,4},{6,7},{7,6},{8,9},{9,8},{10,11... | collective-permute-start | bytes 983048 | tf_op jit(solution)/shard_map/ppermute | solution.py:366
  9.2 10.2 %collective-permute-start.4 = (bf16[72,1280]{1,0:T(8,128)(2,1)}, bf16[72,1280]{1,0:T(8,128)(2,1)}, u32[]{:S(2)}, u32[]{:S(2)}) collective-permute-start(bf16[72,1280]{1,0:T(8,128)(2,1)} %get-tuple-element.107), channel_id=1, source_target_pairs={{0,1},{1,0},{2,3},{3,2},{4,5},{5,4},{6,7},{7,6},{8,9},{9,8},{10,11... | collective-permute-start | bytes 552968 | tf_op jit(solution)/shard_map/ppermute | solution.py:366
  17.4 17.6 %collective-permute-start.5 = (bf16[120,1280]{1,0:T(8,128)(2,1)}, bf16[120,1280]{1,0:T(8,128)(2,1)S(1)}, u32[]{:S(2)}, u32[]{:S(2)}) collective-permute-start(bf16[120,1280]{1,0:T(8,128)(2,1)} %get-tuple-element.109), channel_id=1, source_target_pairs={{0,2},{1,3},{2,0},{3,1},{4,6},{5,7},{6,4},{7,5},{8,10},{9,11},{10,... | collective-permute-start | bytes 921608 | tf_op jit(solution)/shard_map/ppermute | solution.py:366
  19.4 17.5 %collective-permute-start.9 = (bf16[2,160,512]{2,1,0:T(8,128)(2,1)S(1)}, bf16[2,160,512]{2,1,0:T(8,128)(2,1)S(1)}, u32[]{:S(2)}, u32[]{:S(2)}) collective-permute-start(bf16[2,160,512]{2,1,0:T(8,128)(2,1)S(1)} %collective-permute-done.1.refs_10_), channel_id=1, source_target_pairs={{0,1},{1,0},{2,3},{3,2},{4,5},{5,4},{6,7},{7,6},{8,9},{9,8},{10,11... | collective-permute-start | bytes 983048 | tf_op jit(solution)/shard_map/ppermute | solution.py:366
  19.5 29.2 %collective-permute-start.2 = (bf16[192,1280]{1,0:T(8,128)(2,1)S(1)}, bf16[192,1280]{1,0:T(8,128)(2,1)}, u32[]{:S(2)}, u32[]{:S(2)}) collective-permute-start(bf16[192,1280]{1,0:T(8,128)(2,1)S(1)} %bitcast.18), channel_id=1, source_target_pairs={{0,2},{1,3},{2,0},{3,1},{4,6},{5,7},{6,4},{7,5},{8,10},{9,11},{10,... | collective-permute-start | bytes 1474568 | tf_op jit(solution)/shard_map/ppermute | solution.py:366
  28.3 37.9 %copy-start.20 = (bf16[400,640]{1,0:T(8,128)(2,1)}, bf16[400,640]{1,0:T(8,128)(2,1)S(1)}, u32[]{:S(2)}) copy-start(bf16[400,640]{1,0:T(8,128)(2,1)S(1)} %collective-permute-done.11.refs_14_) | copy-start | bytes 1536004
  28.3 20.9 %collective-permute-start.13 = (bf16[400,640]{1,0:T(8,128)(2,1)S(1)}, bf16[400,640]{1,0:T(8,128)(2,1)}, u32[]{:S(2)}, u32[]{:S(2)}) collective-permute-start(bf16[400,640]{1,0:T(8,128)(2,1)S(1)} %collective-permute-done.11.refs_14_), channel_id=1, source_target_pairs={{0,8},{4,12},{8,0},{12,4},{16,24},{20,28},{24,16},{28,20},{1,9},{5... | collective-permute-start | bytes 1536008 | tf_op jit(solution)/shard_map/ppermute | solution.py:366
  30.5 18.8 %collective-permute-start.12 = (bf16[400,640]{1,0:T(8,128)(2,1)S(1)}, bf16[400,640]{1,0:T(8,128)(2,1)}, u32[]{:S(2)}, u32[]{:S(2)}) collective-permute-start(bf16[400,640]{1,0:T(8,128)(2,1)S(1)} %collective-permute-done.11.refs_14_), channel_id=1, source_target_pairs={{0,4},{4,0},{8,12},{12,8},{16,20},{20,16},{24,28},{28,24},{1,5},{5... | collective-permute-start | bytes 1536008 | tf_op jit(solution)/shard_map/ppermute | solution.py:366
  34.9 13.8 %collective-permute-start.8 = (bf16[2,160,512]{2,1,0:T(8,128)(2,1)S(1)}, bf16[2,160,512]{2,1,0:T(8,128)(2,1)}, u32[]{:S(2)}, u32[]{:S(2)}) collective-permute-start(bf16[2,160,512]{2,1,0:T(8,128)(2,1)S(1)} %collective-permute-done.1.refs_10_), channel_id=1, source_target_pairs={{0,4},{4,0},{8,12},{12,8},{16,20},{20,16},{24,28},{28,24},{1,5},{5... | collective-permute-start | bytes 983048 | tf_op jit(solution)/shard_map/ppermute | solution.py:366
  37.0 12.8 %collective-permute-start.6 = (bf16[120,1280]{1,0:T(8,128)(2,1)S(1)}, bf16[120,1280]{1,0:T(8,128)(2,1)S(1)}, u32[]{:S(2)}, u32[]{:S(2)}) collective-permute-start(bf16[120,1280]{1,0:T(8,128)(2,1)S(1)} %collective-permute-done.5.refs_6_.refs_27_), channel_id=1, source_target_pairs={{0,1},{1,0},{2,3},{3,2},{4,5},{5,4},{6,7},{7,6},{8,9},{9,8},{10,11... | collective-permute-start | bytes 921608 | tf_op jit(solution)/shard_map/ppermute | solution.py:366
  48.7 2.7 %collective-permute-start.14 = (bf16[400,640]{1,0:T(8,128)(2,1)S(1)}, bf16[400,640]{1,0:T(8,128)(2,1)}, u32[]{:S(2)}, u32[]{:S(2)}) collective-permute-start(bf16[400,640]{1,0:T(8,128)(2,1)S(1)} %collective-permute-done.11.refs_14_), channel_id=1, source_target_pairs={{0,1},{1,0},{2,3},{3,2},{4,5},{5,4},{6,7},{7,6},{8,9},{9,8},{10,11... | collective-permute-start | bytes 1536008 | tf_op jit(solution)/shard_map/ppermute | solution.py:366
  48.7 2.5 %collective-permute-start.10 = (bf16[2,160,512]{2,1,0:T(8,128)(2,1)}, bf16[2,160,512]{2,1,0:T(8,128)(2,1)}, u32[]{:S(2)}, u32[]{:S(2)}) collective-permute-start(bf16[2,160,512]{2,1,0:T(8,128)(2,1)} %collective-permute-done.8.refs_11_), channel_id=1, source_target_pairs={{0,1},{1,0},{2,3},{3,2},{4,5},{5,4},{6,7},{7,6},{8,9},{9,8},{10,11... | collective-permute-start | bytes 983048 | tf_op jit(solution)/shard_map/ppermute | solution.py:366
  49.2 4.3 %collective-permute-start.16 = (bf16[400,640]{1,0:T(8,128)(2,1)}, bf16[400,640]{1,0:T(8,128)(2,1)}, u32[]{:S(2)}, u32[]{:S(2)}) collective-permute-start(bf16[400,640]{1,0:T(8,128)(2,1)} %collective-permute-done.13.refs_15_.refs_16_), channel_id=1, source_target_pairs={{0,1},{1,0},{2,3},{3,2},{4,5},{5,4},{6,7},{7,6},{8,9},{9,8},{10,11... | collective-permute-start | bytes 1536008 | tf_op jit(solution)/shard_map/ppermute | solution.py:366
  49.3 4.6 %collective-permute-start.15 = (bf16[400,640]{1,0:T(8,128)(2,1)}, bf16[400,640]{1,0:T(8,128)(2,1)}, u32[]{:S(2)}, u32[]{:S(2)}) collective-permute-start(bf16[400,640]{1,0:T(8,128)(2,1)} %collective-permute-done.12.refs_14_.refs_15_), channel_id=1, source_target_pairs={{0,1},{1,0},{2,3},{3,2},{4,5},{5,4},{6,7},{7,6},{8,9},{9,8},{10,11... | collective-permute-start | bytes 1536008 | tf_op jit(solution)/shard_map/ppermute | solution.py:366
  50.5 2.9 %collective-permute-start.3 = (bf16[192,1280]{1,0:T(8,128)(2,1)}, bf16[192,1280]{1,0:T(8,128)(2,1)S(1)}, u32[]{:S(2)}, u32[]{:S(2)}) collective-permute-start(bf16[192,1280]{1,0:T(8,128)(2,1)} %collective-permute-done.2.refs_2_), channel_id=1, source_target_pairs={{0,1},{1,0},{2,3},{3,2},{4,5},{5,4},{6,7},{7,6},{8,9},{9,8},{10,11... | collective-permute-start | bytes 1474568 | tf_op jit(solution)/shard_map/ppermute | solution.py:366
  51.2 15.0 %collective-permute-start.23 = (bf16[160,1280]{1,0:T(8,128)(2,1)S(1)}, bf16[160,1280]{1,0:T(8,128)(2,1)S(1)}, u32[]{:S(2)}, u32[]{:S(2)}) collective-permute-start(bf16[160,1280]{1,0:T(8,128)(2,1)S(1)} %copy-done.18), channel_id=1, source_target_pairs={{0,1},{1,0},{2,3},{3,2},{4,5},{5,4},{6,7},{7,6},{8,9},{9,8},{10,11... | collective-permute-start | bytes 1228808 | tf_op jit(solution)/shard_map/ppermute | solution.py:366
  51.4 16.4 %collective-permute-start.20 = (bf16[320,640]{1,0:T(8,128)(2,1)S(1)}, bf16[320,640]{1,0:T(8,128)(2,1)}, u32[]{:S(2)}, u32[]{:S(2)}) collective-permute-start(bf16[320,640]{1,0:T(8,128)(2,1)S(1)} %copy-done.15), channel_id=1, source_target_pairs={{0,1},{1,0},{2,3},{3,2},{4,5},{5,4},{6,7},{7,6},{8,9},{9,8},{10,11... | collective-permute-start | bytes 1228808 | tf_op jit(solution)/shard_map/ppermute | solution.py:366
  53.4 14.9 %collective-permute-start.21 = (bf16[320,640]{1,0:T(8,128)(2,1)S(1)}, bf16[320,640]{1,0:T(8,128)(2,1)}, u32[]{:S(2)}, u32[]{:S(2)}) collective-permute-start(bf16[320,640]{1,0:T(8,128)(2,1)S(1)} %copy-done.16), channel_id=1, source_target_pairs={{0,1},{1,0},{2,3},{3,2},{4,5},{5,4},{6,7},{7,6},{8,9},{9,8},{10,11... | collective-permute-start | bytes 1228808 | tf_op jit(solution)/shard_map/ppermute | solution.py:366
  53.5 14.9 %collective-permute-start.22 = (bf16[320,640]{1,0:T(8,128)(2,1)S(1)}, bf16[320,640]{1,0:T(8,128)(2,1)}, u32[]{:S(2)}, u32[]{:S(2)}) collective-permute-start(bf16[320,640]{1,0:T(8,128)(2,1)S(1)} %copy-done.17), channel_id=1, source_target_pairs={{0,1},{1,0},{2,3},{3,2},{4,5},{5,4},{6,7},{7,6},{8,9},{9,8},{10,11... | collective-permute-start | bytes 1228808 | tf_op jit(solution)/shard_map/ppermute | solution.py:366
  53.9 16.1 %collective-permute-start.24 = (bf16[160,1280]{1,0:T(8,128)(2,1)S(1)}, bf16[160,1280]{1,0:T(8,128)(2,1)}, u32[]{:S(2)}, u32[]{:S(2)}) collective-permute-start(bf16[160,1280]{1,0:T(8,128)(2,1)S(1)} %copy-done.19), channel_id=1, source_target_pairs={{0,1},{1,0},{2,3},{3,2},{4,5},{5,4},{6,7},{7,6},{8,9},{9,8},{10,11... | collective-permute-start | bytes 1228808 | tf_op jit(solution)/shard_map/ppermute | solution.py:366
  66.2 9.7 %collective-permute-start.25 = (bf16[240,640]{1,0:T(8,128)(2,1)}, bf16[240,640]{1,0:T(8,128)(2,1)S(1)}, u32[]{:S(2)}, u32[]{:S(2)}) collective-permute-start(bf16[240,640]{1,0:T(8,128)(2,1)} %get-tuple-element.117), channel_id=1, source_target_pairs={{0,4},{4,0},{8,12},{12,8},{16,20},{20,16},{24,28},{28,24},{1,5},{5... | collective-permute-start | bytes 921608 | tf_op jit(solution)/shard_map/ppermute | solution.py:366
  67.8 7.2 %collective-permute-start.26 = (bf16[160,640]{1,0:T(8,128)(2,1)}, bf16[160,640]{1,0:T(8,128)(2,1)S(1)}, u32[]{:S(2)}, u32[]{:S(2)}) collective-permute-start(bf16[160,640]{1,0:T(8,128)(2,1)} %get-tuple-element.118), channel_id=1, source_target_pairs={{0,8},{4,12},{8,0},{12,4},{16,24},{20,28},{24,16},{28,20},{1,9},{5... | collective-permute-start | bytes 614408 | tf_op jit(solution)/shard_map/ppermute | solution.py:366
  68.4 8.5 %collective-permute-start.17 = (bf16[192,256]{1,0:T(8,128)(2,1)}, bf16[192,256]{1,0:T(8,128)(2,1)S(1)}, u32[]{:S(2)}, u32[]{:S(2)}) collective-permute-start(bf16[192,256]{1,0:T(8,128)(2,1)} %get-tuple-element.114), channel_id=1, source_target_pairs={{0,1},{1,0},{2,3},{3,2},{4,5},{5,4},{6,7},{7,6},{8,9},{9,8},{10,11... | collective-permute-start | bytes 294920 | tf_op jit(solution)/shard_map/ppermute | solution.py:366
  68.5 8.4 %collective-permute-start.18 = (bf16[192,256]{1,0:T(8,128)(2,1)}, bf16[192,256]{1,0:T(8,128)(2,1)S(1)}, u32[]{:S(2)}, u32[]{:S(2)}) collective-permute-start(bf16[192,256]{1,0:T(8,128)(2,1)} %get-tuple-element.115), channel_id=1, source_target_pairs={{0,2},{1,3},{2,0},{3,1},{4,6},{5,7},{6,4},{7,5},{8,10},{9,11},{10,... | collective-permute-start | bytes 294920 | tf_op jit(solution)/shard_map/ppermute | solution.py:366
  70.0 6.8 %collective-permute-start.19 = (bf16[192,256]{1,0:T(8,128)(2,1)}, bf16[192,256]{1,0:T(8,128)(2,1)S(1)}, u32[]{:S(2)}, u32[]{:S(2)}) collective-permute-start(bf16[192,256]{1,0:T(8,128)(2,1)} %get-tuple-element.116), channel_id=1, source_target_pairs={{0,3},{1,2},{2,1},{3,0},{4,7},{5,6},{6,5},{7,4},{8,11},{9,10},{10,... | collective-permute-start | bytes 294920 | tf_op jit(solution)/shard_map/ppermute | solution.py:366
  75.0 1.9 collective-permute-start.28
  76.0 1.6 collective-permute-start.27
  94.8 7.4 %collective-permute-start.35 = (bf16[192,6912]{1,0:T(8,128)(2,1)}, bf16[192,6912]{1,0:T(8,128)(2,1)S(1)}, u32[]{:S(2)}, u32[]{:S(2)}) collective-permute-start(bf16[192,6912]{1,0:T(8,128)(2,1)} %get-tuple-element.135.refs_0_), channel_id=1, source_target_pairs={{0,1},{1,0},{2,3},{3,2},{4,5},{5,4},{6,7},{7,6},{8,9},{9,8},{10,11... | collective-permute-start | bytes 7962632 | tf_op jit(solution)/shard_map/ppermute | solution.py:366
  94.9 5.2 %collective-permute-start.32 = (bf16[192,256]{1,0:T(8,128)(2,1)}, bf16[192,256]{1,0:T(8,128)(2,1)S(1)}, u32[]{:S(2)}, u32[]{:S(2)}) collective-permute-start(bf16[192,256]{1,0:T(8,128)(2,1)} %get-tuple-element.126), channel_id=1, source_target_pairs={{0,1},{1,0},{2,3},{3,2},{4,5},{5,4},{6,7},{7,6},{8,9},{9,8},{10,11... | collective-permute-start | bytes 294920 | tf_op jit(solution)/shard_map/ppermute | solution.py:366
  95.3 5.3 %collective-permute-start.33 = (bf16[192,256]{1,0:T(8,128)(2,1)}, bf16[192,256]{1,0:T(8,128)(2,1)S(1)}, u32[]{:S(2)}, u32[]{:S(2)}) collective-permute-start(bf16[192,256]{1,0:T(8,128)(2,1)} %get-tuple-element.127), channel_id=1, source_target_pairs={{0,2},{1,3},{2,0},{3,1},{4,6},{5,7},{6,4},{7,5},{8,10},{9,11},{10,... | collective-permute-start | bytes 294920 | tf_op jit(solution)/shard_map/ppermute | solution.py:366
  96.8 5.3 %collective-permute-start.34 = (bf16[192,256]{1,0:T(8,128)(2,1)}, bf16[192,256]{1,0:T(8,128)(2,1)S(1)}, u32[]{:S(2)}, u32[]{:S(2)}) collective-permute-start(bf16[192,256]{1,0:T(8,128)(2,1)} %get-tuple-element.128), channel_id=1, source_target_pairs={{0,3},{1,2},{2,1},{3,0},{4,7},{5,6},{6,5},{7,4},{8,11},{9,10},{10,... | collective-permute-start | bytes 294920 | tf_op jit(solution)/shard_map/ppermute | solution.py:366
  109.0 29.1 %collective-permute-start.38 = (bf16[8,3,40,640]{3,2,1,0:T(8,128)(2,1)S(1)}, bf16[8,3,40,640]{3,2,1,0:T(8,128)(2,1)S(1)}, u32[]{:S(2)}, u32[]{:S(2)}) collective-permute-start(bf16[8,3,40,640]{3,2,1,0:T(8,128)(2,1)S(1)} %get-tuple-element.137.refs_11_), channel_id=1, source_target_pairs={{0,2},{1,3},{2,0},{3,1},{4,6},{5,7},{6,4},{7,5},{8,10},{9,11},{10,... | collective-permute-start | bytes 3686408 | tf_op jit(solution)/shard_map/ppermute | solution.py:366
  110.1 20.5 %collective-permute-start.39 = (bf16[2,2,2,80,640]{4,3,2,1,0:T(8,128)(2,1)S(1)}, bf16[2,2,2,80,640]{4,3,2,1,0:T(8,128)(2,1)S(1)}, u32[]{:S(2)}, u32[]{:S(2)}) collective-permute-start(bf16[2,2,2,80,640]{4,3,2,1,0:T(8,128)(2,1)S(1)} %get-tuple-element.136.refs_10_), channel_id=1, source_target_pairs={{0,8},{4,12},{8,0},{12,4},{16,24},{20,28},{24,16},{28,20},{1,9},{5... | collective-permute-start | bytes 2457608 | tf_op jit(solution)/shard_map/ppermute | solution.py:366
  117.8 25.5 %collective-permute-start.36 = (bf16[2,216,1280]{2,1,0:T(8,128)(2,1)S(1)}, bf16[2,216,1280]{2,1,0:T(8,128)(2,1)S(1)}, u32[]{:S(2)}, u32[]{:S(2)}) collective-permute-start(bf16[2,216,1280]{2,1,0:T(8,128)(2,1)S(1)} %get-tuple-element.139), channel_id=1, source_target_pairs={{0,1},{1,0},{2,3},{3,2},{4,5},{5,4},{6,7},{7,6},{8,9},{9,8},{10,11... | collective-permute-start | bytes 3317768 | tf_op jit(solution)/shard_map/ppermute | solution.py:366
  117.9 22.6 %collective-permute-start.37 = (bf16[4,4,40,512]{3,2,1,0:T(8,128)(2,1)S(1)}, bf16[4,4,40,512]{3,2,1,0:T(8,128)(2,1)S(1)}, u32[]{:S(2)}, u32[]{:S(2)}) collective-permute-start(bf16[4,4,40,512]{3,2,1,0:T(8,128)(2,1)S(1)} %get-tuple-element.141), channel_id=1, source_target_pairs={{0,4},{4,0},{8,12},{12,8},{16,20},{20,16},{24,28},{28,24},{1,5},{5... | collective-permute-start | bytes 1966088 | tf_op jit(solution)/shard_map/ppermute | solution.py:366
  139.0 15.1 %collective-permute-start.45 = (bf16[2,2,3,40,640]{4,3,2,1,0:T(8,128)(2,1)S(1)}, bf16[2,2,3,40,640]{4,3,2,1,0:T(8,128)(2,1)S(1)}, u32[]{:S(2)}, u32[]{:S(2)}) collective-permute-start(bf16[2,2,3,40,640]{4,3,2,1,0:T(8,128)(2,1)S(1)} %get-tuple-element.159), channel_id=1, source_target_pairs={{0,4},{4,0},{8,12},{12,8},{16,20},{20,16},{24,28},{28,24},{1,5},{5... | collective-permute-start | bytes 1843208 | tf_op jit(solution)/shard_map/ppermute | solution.py:366
  141.2 8.7 %collective-permute-start.42 = (bf16[2,4,40,512]{3,2,1,0:T(8,128)(2,1)S(1)}, bf16[2,4,40,512]{3,2,1,0:T(8,128)(2,1)S(1)}, u32[]{:S(2)}, u32[]{:S(2)}) collective-permute-start(bf16[2,4,40,512]{3,2,1,0:T(8,128)(2,1)S(1)} %get-tuple-element.152), channel_id=1, source_target_pairs={{0,8},{4,12},{8,0},{12,4},{16,24},{20,28},{24,16},{28,20},{1,9},{5... | collective-permute-start | bytes 983048 | tf_op jit(solution)/shard_map/ppermute | solution.py:366
  141.7 11.5 %collective-permute-start.41 = (bf16[2,2,80,640]{3,2,1,0:T(8,128)(2,1)S(1)}, bf16[2,2,80,640]{3,2,1,0:T(8,128)(2,1)S(1)}, u32[]{:S(2)}, u32[]{:S(2)}) collective-permute-start(bf16[2,2,80,640]{3,2,1,0:T(8,128)(2,1)S(1)} %get-tuple-element.150), channel_id=1, source_target_pairs={{0,2},{1,3},{2,0},{3,1},{4,6},{5,7},{6,4},{7,5},{8,10},{9,11},{10,... | collective-permute-start | bytes 1228808 | tf_op jit(solution)/shard_map/ppermute | solution.py:366
  150.5 15.8 %collective-permute-start.44 = (bf16[2,4,40,512]{3,2,1,0:T(8,128)(2,1)S(1)}, bf16[2,4,40,512]{3,2,1,0:T(8,128)(2,1)S(1)}, u32[]{:S(2)}, u32[]{:S(2)}) collective-permute-start(bf16[2,4,40,512]{3,2,1,0:T(8,128)(2,1)S(1)} %get-tuple-element.157.refs_0_), channel_id=1, source_target_pairs={{0,16},{4,20},{8,24},{12,28},{16,0},{20,4},{24,8},{28,12},{1,17},{... | collective-permute-start | bytes 983048 | tf_op jit(solution)/shard_map/ppermute | solution.py:366
  154.8 15.4 %collective-permute-start.50 = (bf16[2,3,40,640]{3,2,1,0:T(8,128)(2,1)S(1)}, bf16[2,3,40,640]{3,2,1,0:T(8,128)(2,1)S(1)}, u32[]{:S(2)}, u32[]{:S(2)}) collective-permute-start(bf16[2,3,40,640]{3,2,1,0:T(8,128)(2,1)S(1)} %get-tuple-element.169), channel_id=1, source_target_pairs={{0,8},{4,12},{8,0},{12,4},{16,24},{20,28},{24,16},{28,20},{1,9},{5... | collective-permute-start | bytes 921608 | tf_op jit(solution)/shard_map/ppermute | solution.py:366
  155.6 14.0 %collective-permute-start.43 = (bf16[2,80,640]{2,1,0:T(8,128)(2,1)S(1)}, bf16[2,80,640]{2,1,0:T(8,128)(2,1)S(1)}, u32[]{:S(2)}, u32[]{:S(2)}) collective-permute-start(bf16[2,80,640]{2,1,0:T(8,128)(2,1)S(1)} %get-tuple-element.156), channel_id=1, source_target_pairs={{0,4},{4,0},{8,12},{12,8},{16,20},{20,16},{24,28},{28,24},{1,5},{5... | collective-permute-start | bytes 614408 | tf_op jit(solution)/shard_map/ppermute | solution.py:366
  166.9 3.9 %collective-permute-start.47 = (bf16[2,40,512]{2,1,0:T(8,128)(2,1)S(1)}, bf16[2,40,512]{2,1,0:T(8,128)(2,1)S(1)}, u32[]{:S(2)}, u32[]{:S(2)}) collective-permute-start(bf16[2,40,512]{2,1,0:T(8,128)(2,1)S(1)} %get-tuple-element.165), channel_id=1, source_target_pairs={{0,1},{1,0},{2,3},{3,2},{4,5},{5,4},{6,7},{7,6},{8,9},{9,8},{10,11... | collective-permute-start | bytes 245768 | tf_op jit(solution)/shard_map/ppermute | solution.py:366
  167.0 5.6 %collective-permute-start.48 = (bf16[2,40,512]{2,1,0:T(8,128)(2,1)S(1)}, bf16[2,40,512]{2,1,0:T(8,128)(2,1)S(1)}, u32[]{:S(2)}, u32[]{:S(2)}) collective-permute-start(bf16[2,40,512]{2,1,0:T(8,128)(2,1)S(1)} %get-tuple-element.166), channel_id=1, source_target_pairs={{0,2},{1,3},{2,0},{3,1},{4,6},{5,7},{6,4},{7,5},{8,10},{9,11},{10,... | collective-permute-start | bytes 245768 | tf_op jit(solution)/shard_map/ppermute | solution.py:366
  169.6 4.5 %collective-permute-start.49 = (bf16[2,40,512]{2,1,0:T(8,128)(2,1)S(1)}, bf16[2,40,512]{2,1,0:T(8,128)(2,1)S(1)}, u32[]{:S(2)}, u32[]{:S(2)}) collective-permute-start(bf16[2,40,512]{2,1,0:T(8,128)(2,1)S(1)} %get-tuple-element.167), channel_id=1, source_target_pairs={{0,3},{1,2},{2,1},{3,0},{4,7},{5,6},{6,5},{7,4},{8,11},{9,10},{10,... | collective-permute-start | bytes 245768 | tf_op jit(solution)/shard_map/ppermute | solution.py:366
  174.6 9.8 %collective-permute-start.51 = (bf16[2,4,40,512]{3,2,1,0:T(8,128)(2,1)S(1)}, bf16[2,4,40,512]{3,2,1,0:T(8,128)(2,1)S(1)}, u32[]{:S(2)}, u32[]{:S(2)}) collective-permute-start(bf16[2,4,40,512]{3,2,1,0:T(8,128)(2,1)S(1)} %get-tuple-element.172.refs_0_), channel_id=1, source_target_pairs={{0,4},{4,0},{8,12},{12,8},{16,20},{20,16},{24,28},{28,24},{1,5},{5... | collective-permute-start | bytes 983048 | tf_op jit(solution)/shard_map/ppermute | solution.py:366
  175.2 24.3 %collective-permute-start.40 = (bf16[216,1280]{1,0:T(8,128)(2,1)S(1)}, bf16[216,1280]{1,0:T(8,128)(2,1)S(1)}, u32[]{:S(2)}, u32[]{:S(2)}) collective-permute-start(bf16[216,1280]{1,0:T(8,128)(2,1)S(1)} %get-tuple-element.148), channel_id=1, source_target_pairs={{0,2},{1,3},{2,0},{3,1},{4,6},{5,7},{6,4},{7,5},{8,10},{9,11},{10,... | collective-permute-start | bytes 1658888 | tf_op jit(solution)/shard_map/ppermute | solution.py:366
  176.8 11.4 %collective-permute-start.29 = (bf16[96,1280]{1,0:T(8,128)(2,1)S(1)}, bf16[96,1280]{1,0:T(8,128)(2,1)S(1)}, u32[]{:S(2)}, u32[]{:S(2)}) collective-permute-start(bf16[96,1280]{1,0:T(8,128)(2,1)S(1)} %copy-done.33), channel_id=1, source_target_pairs={{0,1},{1,0},{2,3},{3,2},{4,5},{5,4},{6,7},{7,6},{8,9},{9,8},{10,11... | collective-permute-start | bytes 737288 | tf_op jit(solution)/shard_map/ppermute | solution.py:366
  176.8 13.1 %collective-permute-start.46 = (bf16[2,80,640]{2,1,0:T(8,128)(2,1)S(1)}, bf16[2,80,640]{2,1,0:T(8,128)(2,1)S(1)}, u32[]{:S(2)}, u32[]{:S(2)}) collective-permute-start(bf16[2,80,640]{2,1,0:T(8,128)(2,1)S(1)} %get-tuple-element.163.refs_0_), channel_id=1, source_target_pairs={{0,16},{4,20},{8,24},{12,28},{16,0},{20,4},{24,8},{28,12},{1,17},{... | collective-permute-start | bytes 614408 | tf_op jit(solution)/shard_map/ppermute | solution.py:366
  185.0 25.2 %collective-permute-start.52 = (bf16[2,2,4,40,512]{4,3,2,1,0:T(8,128)(2,1)S(1)}, bf16[2,2,4,40,512]{4,3,2,1,0:T(8,128)(2,1)S(1)}, u32[]{:S(2)}, u32[]{:S(2)}) collective-permute-start(bf16[2,2,4,40,512]{4,3,2,1,0:T(8,128)(2,1)S(1)} %get-tuple-element.179.refs_0_), channel_id=1, source_target_pairs={{0,8},{4,12},{8,0},{12,4},{16,24},{20,28},{24,16},{28,20},{1,9},{5... | collective-permute-start | bytes 1966088 | tf_op jit(solution)/shard_map/ppermute | solution.py:366
  185.1 20.3 %collective-permute-start.53 = (bf16[2,3,40,640]{3,2,1,0:T(8,128)(2,1)S(1)}, bf16[2,3,40,640]{3,2,1,0:T(8,128)(2,1)S(1)}, u32[]{:S(2)}, u32[]{:S(2)}) collective-permute-start(bf16[2,3,40,640]{3,2,1,0:T(8,128)(2,1)S(1)} %get-tuple-element.180.refs_0_), channel_id=1, source_target_pairs={{0,16},{4,20},{8,24},{12,28},{16,0},{20,4},{24,8},{28,12},{1,17},{... | collective-permute-start | bytes 921608 | tf_op jit(solution)/shard_map/ppermute | solution.py:366
  188.2 8.8 %collective-permute-start.30 = (bf16[96,1280]{1,0:T(8,128)(2,1)S(1)}, bf16[96,1280]{1,0:T(8,128)(2,1)S(1)}, u32[]{:S(2)}, u32[]{:S(2)}) collective-permute-start(bf16[96,1280]{1,0:T(8,128)(2,1)S(1)} %copy-done.32), channel_id=1, source_target_pairs={{0,2},{1,3},{2,0},{3,1},{4,6},{5,7},{6,4},{7,5},{8,10},{9,11},{10,... | collective-permute-start | bytes 737288 | tf_op jit(solution)/shard_map/ppermute | solution.py:366
  190.0 9.5 %collective-permute-start.31 = (bf16[96,1280]{1,0:T(8,128)(2,1)S(1)}, bf16[96,1280]{1,0:T(8,128)(2,1)S(1)}, u32[]{:S(2)}, u32[]{:S(2)}) collective-permute-start(bf16[96,1280]{1,0:T(8,128)(2,1)S(1)} %copy-done.31), channel_id=1, source_target_pairs={{0,3},{1,2},{2,1},{3,0},{4,7},{5,6},{6,5},{7,4},{8,11},{9,10},{10,... | collective-permute-start | bytes 737288 | tf_op jit(solution)/shard_map/ppermute | solution.py:366
  206.0 9.1 %collective-permute-start.56 = (bf16[2,3,40,640]{3,2,1,0:T(8,128)(2,1)S(1)}, bf16[2,3,40,640]{3,2,1,0:T(8,128)(2,1)S(1)}, u32[]{:S(2)}, u32[]{:S(2)}) collective-permute-start(bf16[2,3,40,640]{3,2,1,0:T(8,128)(2,1)S(1)} %get-tuple-element.189.refs_0_), channel_id=1, source_target_pairs={{0,4},{4,0},{8,12},{12,8},{16,20},{20,16},{24,28},{28,24},{1,5},{5... | collective-permute-start | bytes 921608 | tf_op jit(solution)/shard_map/ppermute | solution.py:366
  206.6 7.9 %collective-permute-start.54 = (bf16[2,80,640]{2,1,0:T(8,128)(2,1)S(1)}, bf16[2,80,640]{2,1,0:T(8,128)(2,1)S(1)}, u32[]{:S(2)}, u32[]{:S(2)}) collective-permute-start(bf16[2,80,640]{2,1,0:T(8,128)(2,1)S(1)} %get-tuple-element.186.refs_0_), channel_id=1, source_target_pairs={{0,8},{4,12},{8,0},{12,4},{16,24},{20,28},{24,16},{28,20},{1,9},{5... | collective-permute-start | bytes 614408 | tf_op jit(solution)/shard_map/ppermute | solution.py:366
  215.7 14.3 %collective-permute-start.57 = (bf16[2,2,3,40,640]{4,3,2,1,0:T(8,128)(2,1)S(1)}, bf16[2,2,3,40,640]{4,3,2,1,0:T(8,128)(2,1)S(1)}, u32[]{:S(2)}, u32[]{:S(2)}) collective-permute-start(bf16[2,2,3,40,640]{4,3,2,1,0:T(8,128)(2,1)S(1)} %get-tuple-element.193.refs_0_), channel_id=1, source_target_pairs={{0,8},{4,12},{8,0},{12,4},{16,24},{20,28},{24,16},{28,20},{1,9},{5... | collective-permute-start | bytes 1843208 | tf_op jit(solution)/shard_map/ppermute | solution.py:366
  218.2 8.8 %collective-permute-start.55 = (bf16[2,2,80,640]{3,2,1,0:T(8,128)(2,1)S(1)}, bf16[2,2,80,640]{3,2,1,0:T(8,128)(2,1)S(1)}, u32[]{:S(2)}, u32[]{:S(2)}) collective-permute-start(bf16[2,2,80,640]{3,2,1,0:T(8,128)(2,1)S(1)} %get-tuple-element.188.refs_0_), channel_id=1, source_target_pairs={{0,4},{4,0},{8,12},{12,8},{16,20},{20,16},{24,28},{28,24},{1,5},{5... | collective-permute-start | bytes 1228808 | tf_op jit(solution)/shard_map/ppermute | solution.py:366
  (32 other events, 350.9 us)
